TPU v7x, 32 devices: a whole 2x2x4 slice. The times are simulated.
32 devices in a mesh: rows: 4 (over x, core), cols: 8 (over z, y).
Axes of the slice: x: 2, y: 2, z: 4, core: 2. Of those that a mesh axis runs over, the one named last changes fastest.
Arguments:
- kernels: float32 [10240, 128, 128], P(('rows', 'cols')), may hold values from -0.1875 to 0.1875
- pick_index: int32 [10240], P(('rows', 'cols')), may hold values from 0 to 127
- cell_index: int32 [10240], P(('rows', 'cols')), may hold values from 0 to 511
- counts: int32 [4, 8], P('rows', 'cols'), may hold values from 80 to 320, as said below
- data: float32 [128, 512], P('cols', 'rows'), may hold values from -6 to 6
Outputs:
- model: float32 [512, 1024], P('rows', 'cols')
- search: float32 [512, 1024], P('rows', 'cols')
Inputs may be any that keep to these rules, and one draw needn't show every extreme that they name: `counts`: every device has at least 80 live tiles, and some device has all 320 slots live.
All inputs are finite; a program needn't handle non-finite values.
Results may differ from a plain program's by a relative error of at most 0.0003.
Values sent between devices are 32-bit elements; how exact they have to be, the bound alone decides.
No kernel may reach another device: no remote copies, remote signals or barrier semaphores. Data moves between devices by JAX's collectives and lax.ppermute only.
A program may use at most 64 MiB of HBM per device.

v0:
```python
import jax
import jax.numpy as jnp
from jax import lax
from jax.sharding import PartitionSpec as P

PBLK = 128
CBLK = 512
ITERS = 2
HIGHEST = lax.Precision.HIGHEST


def swapped(block, axis, size, bit):
    return lax.ppermute(block, axis, [(i, i ^ bit) for i in range(size)])


def pairwise_sum(block, axis, size):
    bit = 1
    while bit < size:
        block = block + swapped(block, axis, size, bit)
        bit *= 2
    return block


def gather_blocks(block, axis, size):
    copies = jnp.broadcast_to(block[None], (size,) + block.shape)
    got = lax.all_to_all(copies, axis, split_axis=0, concat_axis=0, tiled=True)
    return got.reshape(size * block.shape[0], -1)


def with_tail(block, extra):
    return jnp.concatenate([block, jnp.full((8, block.shape[1]), extra)], axis=0)


def scatter_sum(whole, extra, axis, size):
    rows = whole.shape[0] // size
    parts = whole.reshape(size, rows, -1)
    tail = jnp.full((size, 8, whole.shape[1]), extra)
    parts = jnp.concatenate([parts, tail], axis=1)
    total = lax.all_to_all(parts, axis, split_axis=0, concat_axis=0, tiled=True).sum(axis=0)
    return total[:rows], total[rows, 0]


def per_device(n_rows, n_cols, kernels, pick_index, cell_index, counts, data):
    slots = kernels.shape[0]
    live = (lax.iota(jnp.int32, slots) < counts[0, 0]).astype(jnp.float32)
    pick_table = (pick_index[None, :] == lax.iota(jnp.int32, PBLK)[:, None]).astype(
        jnp.float32
    ) * live[None, :]
    cell_table = (cell_index[None, :] == lax.iota(jnp.int32, CBLK)[:, None]).astype(
        jnp.float32
    ) * live[None, :]

    def adjoint(group):
        product = jnp.einsum("kij,ki->kj", kernels, group[pick_index], precision=HIGHEST)
        whole = jnp.dot(cell_table, product, precision=HIGHEST)
        return scatter_sum(whole, jnp.sum(group * group), "rows", n_rows)

    def forward(owned):
        group = gather_blocks(owned, "rows", n_rows)
        product = jnp.einsum("kij,kj->ki", kernels, group[cell_index], precision=HIGHEST)
        whole = jnp.dot(pick_table, product, precision=HIGHEST)
        total = pairwise_sum(with_tail(whole, jnp.sum(group * group)), "cols", n_cols)
        return total[:PBLK], total[PBLK, 0]

    upick = gather_blocks(data, "cols", n_cols)
    product, square = adjoint(upick)
    beta = jnp.sqrt(square)
    vcell = product / beta
    phibar = beta
    rhobar = None
    model = jnp.zeros_like(vcell)
    search = None
    for step in range(ITERS):
        product, square = forward(vcell)
        alpha = jnp.sqrt(square)
        if step == 0:
            rhobar = alpha
            search = vcell / alpha
        else:
            theta = sine * alpha
            rhobar = -cosine * alpha
            search = vcell / alpha - theta / rho * search
        upick = product / alpha - alpha * (upick / beta)
        product, square = adjoint(upick)
        beta = jnp.sqrt(square)
        vcell = product / beta - beta * (vcell / alpha)
        rho = jnp.sqrt(rhobar * rhobar + beta * beta)
        cosine = rhobar / rho
        sine = beta / rho
        phi = cosine * phibar
        phibar = sine * phibar
        model = model + phi / rho * search
    square = jnp.full((8, 128), jnp.sum(vcell * vcell))
    square = pairwise_sum(square, "rows", n_rows)
    square = pairwise_sum(square, "cols", n_cols)
    alpha = jnp.sqrt(square[0, 0])
    search = vcell / alpha - sine * alpha / rho * search
    return (model, search)


def solution(mesh):
    def run(*args):
        return per_device(mesh.shape["rows"], mesh.shape["cols"], *args)

    return jax.shard_map(
        run,
        mesh=mesh,
        in_specs=(
            P(("rows", "cols"), None, None),
            P(("rows", "cols")),
            P(("rows", "cols")),
            P("rows", "cols"),
            P("cols", "rows"),
        ),
        out_specs=(P("rows", "cols"), P("rows", "cols")),
        check_vma=False,
    )
```

profile of v0, /device:TPU:0, one launch (start us, length us, event | category | flops | bytes accessed | tf_op | source)
XLA Modules:
  0.0 267.4 jit_solution(10922020019581617724)
XLA Ops:
  0.6 1.3 broadcast_in_dim.12
  2.0 7.3 %all-to-all-start = ((f32[8,16,128]{2,1,0:T(8,128)}), f32[8,16,128]{2,1,0:T(8,128)S(1)}, u32[]{:S(2)}, u32[]{:S(2)}) async-start(f32[8,16,128]{2,1,0:T(8,128)} %broadcast_in_dim.12), calls=%async_computation | async-start | bytes 131072 | tf_op jit(solution)/shard_map/all_to_all | solution.py:26
  9.9 0.7 compare_select_fusion.1
  10.6 5.6 %all-to-all-done = f32[8,16,128]{2,1,0:T(8,128)S(1)} async-done(((f32[8,16,128]{2,1,0:T(8,128)}), f32[8,16,128]{2,1,0:T(8,128)S(1)}, u32[]{:S(2)}, u32[]{:S(2)}) %all-to-all-start) | async-done | bytes 65568 | tf_op jit(solution)/shard_map/all_to_all | solution.py:26
  16.2 1.1 gather_fusion
  17.2 20.4 %fusion.37 = f32[320,1,128]{2,1,0:T(1,128)S(1)} fusion(f32[320,128,1]{1,2,0:T(1,128)S(1)} %bitcast.63, f32[320,128,128]{2,1,0:T(8,128)} %param.5), kind=kOutput, calls=%fused_computation.66 | convolution fusion | flops 62914560 | bytes 21299200 | tf_op jit(solution)/shard_map/kij,ki->kj/dot_general | solution.py:54
  37.6 0.9 fusion.4
  39.1 0.7 concatenate.15
  39.8 8.8 %all_to_all.30 = f32[4,136,128]{2,1,0:T(8,128)S(1)} all-to-all(f32[4,136,128]{2,1,0:T(8,128)S(1)} %concatenate.15), channel_id=1, replica_groups=mesh['rows'=4,'cols'=8] {'rows'}, dimensions={0} | all-to-all | bytes 557056 | tf_op jit(solution)/shard_map/all_to_all | solution.py:39
  49.8 0.7 broadcast_in_dim.14
  50.5 3.6 %all-to-all-start.2 = ((f32[4,128,128]{2,1,0:T(8,128)}), f32[4,128,128]{2,1,0:T(8,128)S(1)}, u32[]{:S(2)}, u32[]{:S(2)}) async-start(f32[4,128,128]{2,1,0:T(8,128)} %broadcast_in_dim.14), calls=%async_computation.2 | async-start | bytes 524288 | tf_op jit(solution)/shard_map/all_to_all | solution.py:26
  54.1 5.8 %all-to-all-done.2 = f32[4,128,128]{2,1,0:T(8,128)S(1)} async-done(((f32[4,128,128]{2,1,0:T(8,128)}), f32[4,128,128]{2,1,0:T(8,128)S(1)}, u32[]{:S(2)}, u32[]{:S(2)}) %all-to-all-start.2) | async-done | bytes 262176 | tf_op jit(solution)/shard_map/all_to_all | solution.py:26
  59.9 1.1 gather_fusion.1
  61.0 35.4 %fusion.38 = f32[320,1,128]{2,1,0:T(1,128)S(1)} fusion(f32[320,128,1]{1,2,0:T(1,128)S(1)} %bitcast.64, f32[320,128,128]{2,1,0:T(8,128)} %param.5), kind=kOutput, calls=%fused_computation.67 | convolution fusion | flops 62914560 | bytes 21299200 | tf_op jit(solution)/shard_map/kij,kj->ki/dot_general | solution.py:60
  96.7 0.7 multiply_reduce_fusion.1
  97.4 0.7 concatenate.16
  98.5 3.9 %collective-permute-done = f32[136,128]{1,0:T(8,128)S(1)} collective-permute-done((f32[136,128]{1,0:T(8,128)S(1)}, f32[136,128]{1,0:T(8,128)S(1)}, u32[]{:S(2)}, u32[]{:S(2)}) %collective-permute-start) | collective-permute-done | bytes 69664 | tf_op jit(solution)/shard_map/ppermute | solution.py:13
  102.4 0.7 pad_add_fusion.1
  103.4 4.1 %collective-permute-done.1 = f32[136,128]{1,0:T(8,128)S(1)} collective-permute-done((f32[136,128]{1,0:T(8,128)S(1)}, f32[136,128]{1,0:T(8,128)S(1)}, u32[]{:S(2)}, u32[]{:S(2)}) %collective-permute-start.1) | collective-permute-done | bytes 69664 | tf_op jit(solution)/shard_map/ppermute | solution.py:13
  108.0 5.1 %collective-permute-done.2 = f32[136,128]{1,0:T(8,128)S(1)} collective-permute-done((f32[136,128]{1,0:T(8,128)S(1)}, f32[136,128]{1,0:T(8,128)S(1)}, u32[]{:S(2)}, u32[]{:S(2)}) %collective-permute-start.2) | collective-permute-done | bytes 69664 | tf_op jit(solution)/shard_map/ppermute | solution.py:13
  114.4 0.7 multiply_reduce_fusion.4
  115.0 1.1 gather_fusion.2
  116.1 20.6 %fusion.39 = f32[320,1,128]{2,1,0:T(1,128)S(1)} fusion(f32[320,128,1]{1,2,0:T(1,128)S(1)} %bitcast.65, f32[320,128,128]{2,1,0:T(8,128)} %param.5), kind=kOutput, calls=%fused_computation.68 | convolution fusion | flops 62914560 | bytes 21299200 | tf_op jit(solution)/shard_map/kij,ki->kj/dot_general | solution.py:54
  136.7 0.9 fusion.2
  137.6 1.4 concatenate.17
  139.0 3.4 %all-to-all-start.3 = ((f32[4,136,128]{2,1,0:T(8,128)}), f32[4,136,128]{2,1,0:T(8,128)S(1)}, u32[]{:S(2)}, u32[]{:S(2)}) async-start(f32[4,136,128]{2,1,0:T(8,128)} %concatenate.17), calls=%async_computation.3 | async-start | bytes 557056 | tf_op jit(solution)/shard_map/all_to_all | solution.py:39
  142.4 6.2 %all-to-all-done.3 = f32[4,136,128]{2,1,0:T(8,128)S(1)} async-done(((f32[4,136,128]{2,1,0:T(8,128)}), f32[4,136,128]{2,1,0:T(8,128)S(1)}, u32[]{:S(2)}, u32[]{:S(2)}) %all-to-all-start.3) | async-done | bytes 278560 | tf_op jit(solution)/shard_map/all_to_all | solution.py:39
  150.0 8.4 %all_to_all.31 = f32[4,128,128]{2,1,0:T(8,128)S(1)} all-to-all(f32[4,128,128]{2,1,0:T(8,128)S(1)} %broadcast_in_dim.16), channel_id=1, replica_groups=mesh['rows'=4,'cols'=8] {'rows'}, dimensions={0} | all-to-all | bytes 524288 | tf_op jit(solution)/shard_map/all_to_all | solution.py:26
  158.4 1.1 gather_fusion.3
  159.5 35.4 %fusion.40 = f32[320,1,128]{2,1,0:T(1,128)S(1)} fusion(f32[320,128,1]{1,2,0:T(1,128)S(1)} %bitcast.62, f32[320,128,128]{2,1,0:T(8,128)} %param.5), kind=kOutput, calls=%fused_computation.69 | convolution fusion | flops 62914560 | bytes 21299200 | tf_op jit(solution)/shard_map/kij,kj->ki/dot_general | solution.py:60
  195.2 0.7 multiply_reduce_fusion
  196.5 4.3 %collective-permute-done.3 = f32[136,128]{1,0:T(8,128)S(1)} collective-permute-done((f32[136,128]{1,0:T(8,128)S(1)}, f32[136,128]{1,0:T(8,128)S(1)}, u32[]{:S(2)}, u32[]{:S(2)}) %collective-permute-start.3) | collective-permute-done | bytes 69664 | tf_op jit(solution)/shard_map/ppermute | solution.py:13
  201.5 4.3 %collective-permute-done.4 = f32[136,128]{1,0:T(8,128)S(1)} collective-permute-done((f32[136,128]{1,0:T(8,128)S(1)}, f32[136,128]{1,0:T(8,128)S(1)}, u32[]{:S(2)}, u32[]{:S(2)}) %collective-permute-start.4) | collective-permute-done | bytes 69664 | tf_op jit(solution)/shard_map/ppermute | solution.py:13
  205.9 5.3 %collective-permute-done.5 = f32[136,128]{1,0:T(8,128)S(1)} collective-permute-done((f32[136,128]{1,0:T(8,128)S(1)}, f32[136,128]{1,0:T(8,128)S(1)}, u32[]{:S(2)}, u32[]{:S(2)}) %collective-permute-start.5) | collective-permute-done | bytes 69664 | tf_op jit(solution)/shard_map/ppermute | solution.py:13
  212.4 0.7 multiply_reduce_fusion.3
  213.0 1.1 gather_fusion.4
  214.1 20.7 %fusion.41 = f32[320,1,128]{2,1,0:T(1,128)S(1)} fusion(f32[320,128,1]{1,2,0:T(1,128)S(1)} %bitcast.61, f32[320,128,128]{2,1,0:T(8,128)} %param.5), kind=kOutput, calls=%fused_computation.70 | convolution fusion | flops 62914560 | bytes 21299200 | tf_op jit(solution)/shard_map/kij,ki->kj/dot_general | solution.py:54
  234.8 0.9 fusion
  235.7 0.7 concatenate.19
  236.3 8.6 %all_to_all.32 = f32[4,136,128]{2,1,0:T(8,128)S(1)} all-to-all(f32[4,136,128]{2,1,0:T(8,128)S(1)} %concatenate.19), channel_id=1, replica_groups=mesh['rows'=4,'cols'=8] {'rows'}, dimensions={0} | all-to-all | bytes 557056 | tf_op jit(solution)/shard_map/all_to_all | solution.py:39
  246.1 0.7 multiply_reduce_fusion.2
  247.6 1.1 collective-permute-done.6
  249.8 3.2 %collective-permute-done.7 = f32[8,128]{1,0:T(8,128)S(1)} collective-permute-done((f32[8,128]{1,0:T(8,128)S(1)}, f32[8,128]{1,0:T(8,128)S(1)}, u32[]{:S(2)}, u32[]{:S(2)}) %collective-permute-start.7) | collective-permute-done | bytes 4128 | tf_op jit(solution)/shard_map/ppermute | solution.py:13
  253.0 0.6 fusion.57
  253.7 3.6 %collective-permute-done.8 = f32[8,128]{1,0:T(8,128)S(1)} collective-permute-done((f32[8,128]{1,0:T(8,128)S(1)}, f32[8,128]{1,0:T(8,128)S(1)}, u32[]{:S(2)}, u32[]{:S(2)}) %collective-permute-start.8) | collective-permute-done | bytes 4128 | tf_op jit(solution)/shard_map/ppermute | solution.py:13
  257.3 3.6 %collective-permute-done.9 = f32[8,128]{1,0:T(8,128)S(1)} collective-permute-done((f32[8,128]{1,0:T(8,128)S(1)}, f32[8,128]{1,0:T(8,128)S(1)}, u32[]{:S(2)}, u32[]{:S(2)}) %collective-permute-start.9) | collective-permute-done | bytes 4128 | tf_op jit(solution)/shard_map/ppermute | solution.py:13
  261.3 4.1 %collective-permute-done.10 = f32[8,128]{1,0:T(8,128)S(1)} collective-permute-done((f32[8,128]{1,0:T(8,128)S(1)}, f32[8,128]{1,0:T(8,128)S(1)}, u32[]{:S(2)}, u32[]{:S(2)}) %collective-permute-start.10) | collective-permute-done | bytes 4128 | tf_op jit(solution)/shard_map/ppermute | solution.py:13
  266.7 0.7 multiply_subtract_fusion
  (45 shorter events, 9.2 us)
Async XLA Ops:
  0.6 37.0 %copy-start.1 = (s32[320]{0:T(512)S(1)}, s32[320]{0:T(512)}, u32[]{:S(2)}) copy-start(s32[320]{0:T(512)} %param.7) | copy-start | bytes 3844
  2.0 14.2 %all-to-all-start = ((f32[8,16,128]{2,1,0:T(8,128)}), f32[8,16,128]{2,1,0:T(8,128)S(1)}, u32[]{:S(2)}, u32[]{:S(2)}) async-start(f32[8,16,128]{2,1,0:T(8,128)} %broadcast_in_dim.12), calls=%async_computation | async-start | bytes 131072 | tf_op jit(solution)/shard_map/all_to_all | solution.py:26
  39.8 56.6 %copy-start = (s32[320]{0:T(512)S(1)}, s32[320]{0:T(512)}, u32[]{:S(2)}) copy-start(s32[320]{0:T(512)} %param.6) | copy-start | bytes 3844
  50.5 9.4 %all-to-all-start.2 = ((f32[4,128,128]{2,1,0:T(8,128)}), f32[4,128,128]{2,1,0:T(8,128)S(1)}, u32[]{:S(2)}, u32[]{:S(2)}) async-start(f32[4,128,128]{2,1,0:T(8,128)} %broadcast_in_dim.14), calls=%async_computation.2 | async-start | bytes 524288 | tf_op jit(solution)/shard_map/all_to_all | solution.py:26
  98.1 4.4 %collective-permute-start = (f32[136,128]{1,0:T(8,128)S(1)}, f32[136,128]{1,0:T(8,128)S(1)}, u32[]{:S(2)}, u32[]{:S(2)}) collective-permute-start(f32[136,128]{1,0:T(8,128)S(1)} %concatenate.16), channel_id=1, source_target_pairs={{0,1},{1,0},{2,3},{3,2},{4,5},{5,4},{6,7},{7,6},{8,9},{9,8},{10,11... | collective-permute-start | bytes 208904 | tf_op jit(solution)/shard_map/ppermute | solution.py:13
  103.1 4.4 %collective-permute-start.1 = (f32[136,128]{1,0:T(8,128)S(1)}, f32[136,128]{1,0:T(8,128)S(1)}, u32[]{:S(2)}, u32[]{:S(2)}) collective-permute-start(f32[136,128]{1,0:T(8,128)S(1)} %pad_add_fusion.1), channel_id=1, source_target_pairs={{0,2},{1,3},{2,0},{3,1},{4,6},{5,7},{6,4},{7,5},{8,10},{9,11},{10,... | collective-permute-start | bytes 208904 | tf_op jit(solution)/shard_map/ppermute | solution.py:13
  107.5 5.7 %collective-permute-start.2 = (f32[136,128]{1,0:T(8,128)S(1)}, f32[136,128]{1,0:T(8,128)S(1)}, u32[]{:S(2)}, u32[]{:S(2)}) collective-permute-start(f32[136,128]{1,0:T(8,128)S(1)} %add.64), channel_id=1, source_target_pairs={{0,4},{1,5},{2,6},{3,7},{4,0},{5,1},{6,2},{7,3},{8,12},{9,13},{10,... | collective-permute-start | bytes 208904 | tf_op jit(solution)/shard_map/ppermute | solution.py:13
  139.0 9.6 %all-to-all-start.3 = ((f32[4,136,128]{2,1,0:T(8,128)}), f32[4,136,128]{2,1,0:T(8,128)S(1)}, u32[]{:S(2)}, u32[]{:S(2)}) async-start(f32[4,136,128]{2,1,0:T(8,128)} %concatenate.17), calls=%async_computation.3 | async-start | bytes 557056 | tf_op jit(solution)/shard_map/all_to_all | solution.py:39
  196.4 4.4 %collective-permute-start.3 = (f32[136,128]{1,0:T(8,128)S(1)}, f32[136,128]{1,0:T(8,128)S(1)}, u32[]{:S(2)}, u32[]{:S(2)}) collective-permute-start(f32[136,128]{1,0:T(8,128)S(1)} %concatenate.18), channel_id=1, source_target_pairs={{0,1},{1,0},{2,3},{3,2},{4,5},{5,4},{6,7},{7,6},{8,9},{9,8},{10,11... | collective-permute-start | bytes 208904 | tf_op jit(solution)/shard_map/ppermute | solution.py:13
  201.4 4.4 %collective-permute-start.4 = (f32[136,128]{1,0:T(8,128)S(1)}, f32[136,128]{1,0:T(8,128)S(1)}, u32[]{:S(2)}, u32[]{:S(2)}) collective-permute-start(f32[136,128]{1,0:T(8,128)S(1)} %pad_add_fusion), channel_id=1, source_target_pairs={{0,2},{1,3},{2,0},{3,1},{4,6},{5,7},{6,4},{7,5},{8,10},{9,11},{10,... | collective-permute-start | bytes 208904 | tf_op jit(solution)/shard_map/ppermute | solution.py:13
  205.8 5.5 %collective-permute-start.5 = (f32[136,128]{1,0:T(8,128)S(1)}, f32[136,128]{1,0:T(8,128)S(1)}, u32[]{:S(2)}, u32[]{:S(2)}) collective-permute-start(f32[136,128]{1,0:T(8,128)S(1)} %add.68), channel_id=1, source_target_pairs={{0,4},{1,5},{2,6},{3,7},{4,0},{5,1},{6,2},{7,3},{8,12},{9,13},{10,... | collective-permute-start | bytes 208904 | tf_op jit(solution)/shard_map/ppermute | solution.py:13
  247.5 1.2 collective-permute-start.6
  249.3 3.7 %collective-permute-start.7 = (f32[8,128]{1,0:T(8,128)S(1)}, f32[8,128]{1,0:T(8,128)S(1)}, u32[]{:S(2)}, u32[]{:S(2)}) collective-permute-start(f32[8,128]{1,0:T(8,128)S(1)} %broadcast_add_fusion), channel_id=1, source_target_pairs={{0,16},{8,24},{16,0},{24,8},{1,17},{9,25},{17,1},{25,9},{2,18},{10... | collective-permute-start | bytes 12296 | tf_op jit(solution)/shard_map/ppermute | solution.py:13
  253.6 3.7 %collective-permute-start.8 = (f32[8,128]{1,0:T(8,128)S(1)}, f32[8,128]{1,0:T(8,128)S(1)}, u32[]{:S(2)}, u32[]{:S(2)}) collective-permute-start(f32[8,128]{1,0:T(8,128)S(1)} %fusion.57), channel_id=1, source_target_pairs={{0,1},{1,0},{2,3},{3,2},{4,5},{5,4},{6,7},{7,6},{8,9},{9,8},{10,11... | collective-permute-start | bytes 12296 | tf_op jit(solution)/shard_map/ppermute | solution.py:13
  257.3 3.6 %collective-permute-start.9 = (f32[8,128]{1,0:T(8,128)S(1)}, f32[8,128]{1,0:T(8,128)S(1)}, u32[]{:S(2)}, u32[]{:S(2)}) collective-permute-start(f32[8,128]{1,0:T(8,128)S(1)} %add.74), channel_id=1, source_target_pairs={{0,2},{1,3},{2,0},{3,1},{4,6},{5,7},{6,4},{7,5},{8,10},{9,11},{10,... | collective-permute-start | bytes 12296 | tf_op jit(solution)/shard_map/ppermute | solution.py:13
  260.9 4.5 %collective-permute-start.10 = (f32[8,128]{1,0:T(8,128)S(1)}, f32[8,128]{1,0:T(8,128)S(1)}, u32[]{:S(2)}, u32[]{:S(2)}) collective-permute-start(f32[8,128]{1,0:T(8,128)S(1)} %add.75), channel_id=1, source_target_pairs={{0,4},{1,5},{2,6},{3,7},{4,0},{5,1},{6,2},{7,3},{8,12},{9,13},{10,... | collective-permute-start | bytes 12296 | tf_op jit(solution)/shard_map/ppermute | solution.py:13
where the time goes:
time: 268 us; the launch traced here: 267 us
  matrix products  136 us (51%)
  waiting for transfers between devices  60.3 us (22%)
  blocking collectives  25.8 us (10%)
  starting transfers between devices  16.5 us (6%)
  local copies, waits for them, and re-layouts  15.1 us (6%)
  other arithmetic  7.96 us (3%)
  between operations  6.12 us (2%)
    dot_general x2, matrix products, forward(): jnp.einsum('kij,kj->ki', kernels, group[cell_index], precision=HIGHEST)  70.7 us
    dot_general x3, matrix products, adjoint(): jnp.einsum('kij,ki->kj', kernels, group[pick_index], precision=HIGHEST)  61.7 us
    ppermute x11, waiting for transfers between devices, swapped(): return lax.ppermute(block, axis, [(i, i ^ bit) for i in range(size)])  42.7 us
    all_to_all x2, blocking collectives, scatter_sum(): lax.all_to_all(parts, axis, split_axis=0, concat_axis=0, tiled=True)  17.3 us
    all_to_all x2, waiting for transfers between devices, gather_blocks(): got = lax.all_to_all(copies, axis, split_axis=0, concat_axis=0, tiled=True)  11.4 us
    all_to_all x2, starting transfers between devices, gather_blocks(): got = lax.all_to_all(copies, axis, split_axis=0, concat_axis=0, tiled=True)  10.9 us
    all_to_all x1, blocking collectives, gather_blocks(): got = lax.all_to_all(copies, axis, split_axis=0, concat_axis=0, tiled=True)  8.42 us
    all_to_all x1, waiting for transfers between devices, scatter_sum(): lax.all_to_all(parts, axis, split_axis=0, concat_axis=0, tiled=True)  6.17 us
  transfers between devices with their start and end apart: 14, of which 14 were waited for; matrix products, arithmetic and copies ran while one was open for 0% of the time, Pallas kernels for 0%

commit v1 on v0

v1 whole, which is shorter than its diff:
```python
import functools

import jax
import jax.numpy as jnp
from jax import lax
from jax.experimental import pallas as pl
from jax.experimental.pallas import tpu as pltpu
from jax.sharding import PartitionSpec as P

PBLK = 128
CBLK = 512
ITERS = 2
B = 128
SUB = 8
GROUP = 8
FOLDS = (1, 2, 4, 8)
TAIL = 8


def tile_transposed(tile, turned, pick):
    column = jnp.take_along_axis(turned, jnp.full((B, B), pick, jnp.int32), axis=1)
    return (tile * column).reshape(B // SUB, SUB, B).sum(axis=0)


def tile_forward(tile, row, masks):
    parts = [tile[SUB * q : SUB * (q + 1)] * row for q in range(B // SUB)]
    for bit, mask in zip(FOLDS, masks):
        parts = [
            jnp.where(mask, a, b) + pltpu.roll(jnp.where(mask, b, a), B - bit, 1)
            for a, b in zip(parts[::2], parts[1::2])
        ]
    return parts[0]


def over_tiles(slots, live, partial, target, spare, acc_ref):
    def some(group, carry):
        base = group * GROUP
        parts = [partial(base + k) for k in range(GROUP)]
        for k in range(GROUP):
            block = jnp.where(base + k < live, target(base + k), spare)
            where = pl.ds(pl.multiple_of(block * SUB, SUB), SUB)
            acc_ref[where, :] += parts[k]
        return carry

    acc_ref[...] = jnp.zeros_like(acc_ref)
    lax.fori_loop(0, (live + GROUP - 1) // GROUP, some, 0)


def strided_sum(ref, blocks):
    return sum(ref[pl.ds(k, blocks, stride=SUB), :] for k in range(SUB))


def halves(n_rows, cells):
    size = cells // n_rows
    return size, [range(core, n_rows, 2) for core in range(2)]


def adjoint_tail(n_rows, tiles, pick, cell, counts, u, keep, send, acc):
    turned = u.T
    over_tiles(
        tiles.shape[0],
        counts[0, 0],
        lambda s: tile_transposed(tiles[s], turned, pick[s]),
        lambda s: cell[s],
        CBLK,
        acc,
    )
    whole = strided_sum(acc, CBLK)
    square = jnp.full((TAIL, B), jnp.sum(u * u))
    size, _ = halves(n_rows, CBLK)
    core = lax.rem(lax.axis_index("rows"), 2)
    for block in range(n_rows):
        part = whole[block * size : (block + 1) * size]
        place = pl.ds(block // 2 * size, size)

        @pl.when(core == block % 2)
        def _():
            keep[place, :] = part

        @pl.when(core != block % 2)
        def _():
            send[place, :] = part

    keep[pl.ds(CBLK // 2, TAIL), :] = square
    send[pl.ds(CBLK // 2, TAIL), :] = square


def first_adjoint(n_rows, n_cols, tiles, pick, cell, counts, *rest):
    pieces, (u_out, keep, send, acc) = rest[:-4], rest[-4:]
    me = lax.axis_index("cols")
    offset = 0
    for piece in pieces:
        rows = PBLK // n_cols
        for at in range(piece.shape[0] // rows):
            owner = jnp.bitwise_xor(me, offset)
            u_out[pl.ds(pl.multiple_of(owner * rows, rows), rows), :] = piece[pl.ds(at * rows, rows), :]
            offset += 1
    adjoint_tail(n_rows, tiles, pick, cell, counts, u_out[...], keep, send, acc)


def next_adjoint(n_rows, tiles, pick, cell, counts, mine, other, u_old, beta_old, u_out, alpha_out, keep, send, acc):
    total = mine[...] + other[...]
    alpha = jnp.sqrt(total[PBLK:])
    alpha_out[...] = alpha
    u = total[:PBLK] / alpha[:1] - alpha[:1] * (u_old[...] / beta_old[:1])
    u_out[...] = u
    adjoint_tail(n_rows, tiles, pick, cell, counts, u, keep, send, acc)


def forward(first, n_rows, tiles, pick, cell, counts, mine, other, *rest):
    if first:
        v_out, beta_out, own_out, out, acc = rest
    else:
        v_old, alpha_old, v_out, beta_out, own_out, out, acc = rest
    size, _ = halves(n_rows, CBLK)
    me = lax.axis_index("rows")
    core = lax.rem(me, 2)
    beta = jnp.sqrt(mine[pl.ds(CBLK // 2, TAIL), :])
    beta_out[...] = beta
    for block in range(n_rows):
        place = pl.ds(block // 2 * size, size)
        part = jnp.where(core == block % 2, mine[place, :], other[place, :]) / beta[:1]
        here = pl.ds(block * size, size)
        if not first:
            part = part - beta[:1] * (v_old[here, :] / alpha_old[:1])
        v_out[here, :] = part
    own_out[...] = v_out[pl.ds(pl.multiple_of(me * size, size), size), :]
    lane = lax.broadcasted_iota(jnp.int32, (SUB, B), 1)
    masks = [jnp.bitwise_and(lane, bit) == 0 for bit in FOLDS]
    over_tiles(
        tiles.shape[0],
        counts[0, 0],
        lambda s: tile_forward(
            tiles[s], jnp.broadcast_to(v_out[pl.ds(cell[s], 1), :], (SUB, B)), masks
        ),
        lambda s: pick[s],
        PBLK,
        acc,
    )
    source = lax.broadcasted_iota(jnp.int32, (B, B), 0)
    column = lax.broadcasted_iota(jnp.int32, (B, B), 1)
    collect = (lax.rem(source, B // SUB) == lax.div(column, SUB)).astype(jnp.float32)
    sums = jnp.dot(
        acc[: PBLK * SUB, :],
        collect,
        precision=lax.Precision.HIGHEST,
        preferred_element_type=jnp.float32,
    )
    row = lax.rem(lax.broadcasted_iota(jnp.int32, (PBLK * SUB, B), 0), SUB)
    column = lax.rem(lax.broadcasted_iota(jnp.int32, (PBLK * SUB, B), 1), SUB)
    acc[: PBLK * SUB, :] = jnp.where(row == column, sums, 0.0)
    out[:PBLK, :] = strided_sum(acc, PBLK)
    v = v_out[...]
    out[pl.ds(PBLK, TAIL), :] = jnp.full((TAIL, B), jnp.sum(v * v))


def swapped(block, axis, size, bit):
    return lax.ppermute(block, axis, [(i, i ^ bit) for i in range(size)])


def pairwise_sum(block, axis, size, bit=1):
    while bit < size:
        block = block + swapped(block, axis, size, bit)
        bit *= 2
    return block


def shape(*dims):
    return jax.ShapeDtypeStruct(dims, jnp.float32)


def call(kernel, outs, blocks, scalars, arrays):
    vector = pl.BlockSpec(memory_space=pltpu.VMEM)
    scalar = pl.BlockSpec(memory_space=pltpu.SMEM)
    return pl.pallas_call(
        kernel,
        out_shape=outs,
        in_specs=[vector] + [scalar] * len(scalars) + [vector] * (len(arrays) - 1),
        out_specs=[vector] * len(outs),
        scratch_shapes=[pltpu.VMEM(((blocks + 1) * SUB, B), jnp.float32)],
        compiler_params=pltpu.CompilerParams(vmem_limit_bytes=24 << 20),
    )(arrays[0], *scalars, *arrays[1:])


def per_device(n_rows, n_cols, kernels, pick_index, cell_index, counts, data):
    tiles = pltpu.with_memory_space_constraint(kernels, pltpu.VMEM)
    scalars = (pick_index, cell_index, counts)
    half = CBLK // 2 + TAIL
    own = CBLK // n_rows

    def sum_cells(keep, send):
        return pairwise_sum(keep + swapped(send, "rows", n_rows, 1), "rows", n_rows, 2)

    pair = jnp.concatenate([data, swapped(data, "cols", n_cols, 1)], axis=0)
    pieces = [pair] + [swapped(pair, "cols", n_cols, bit) for bit in range(2, n_cols, 2)]
    upick, keep, send = call(
        functools.partial(first_adjoint, n_rows, n_cols),
        [shape(PBLK, B), shape(half, B), shape(half, B)],
        CBLK,
        scalars,
        [tiles] + pieces,
    )
    vcell = alpha = None
    blocks, alphas, betas = [], [], []
    for step in range(ITERS):
        mine = sum_cells(keep, send)
        other = swapped(mine, "rows", n_rows, 1)
        vcell, beta, block, product = call(
            functools.partial(forward, step == 0, n_rows),
            [shape(CBLK, B), shape(TAIL, B), shape(own, B), shape(PBLK + TAIL, B)],
            PBLK,
            scalars,
            [tiles, mine, other] + ([] if step == 0 else [vcell, alpha]),
        )
        blocks.append(block)
        betas.append(beta[0, 0])
        bit = 1
        while 2 * bit < n_cols:
            product = product + swapped(product, "cols", n_cols, bit)
            bit *= 2
        upick, alpha, keep, send = call(
            functools.partial(next_adjoint, n_rows),
            [shape(PBLK, B), shape(TAIL, B), shape(half, B), shape(half, B)],
            CBLK,
            scalars,
            [tiles, product, swapped(product, "cols", n_cols, bit), upick, beta],
        )
        alphas.append(alpha[0, 0])
    mine = sum_cells(keep, send)
    beta = jnp.sqrt(mine[CBLK // 2, 0])
    betas.append(beta)
    me = lax.axis_index("rows")
    old = vcell.reshape(n_rows // 2, 2, own, B)
    old = lax.dynamic_index_in_dim(old, lax.rem(me, 2), axis=1, keepdims=False)
    kept = mine[: CBLK // 2] / beta - beta * (old.reshape(CBLK // 2, B) / alphas[-1])
    square = jnp.full((TAIL, B), jnp.sum(kept * kept))
    square = square + swapped(square, "rows", n_rows, 1)
    square = pairwise_sum(square, "cols", n_cols)
    alphas.append(jnp.sqrt(square[0, 0]))
    blocks.append(lax.dynamic_slice_in_dim(kept, lax.div(me, 2) * own, own, axis=0))

    phibar, rhobar = betas[0], alphas[0]
    search = blocks[0] / alphas[0]
    model = jnp.zeros_like(search)
    for step in range(ITERS):
        beta, alpha = betas[step + 1], alphas[step + 1]
        rho = jnp.sqrt(rhobar * rhobar + beta * beta)
        cosine = rhobar / rho
        sine = beta / rho
        theta = sine * alpha
        rhobar = -cosine * alpha
        phi = cosine * phibar
        phibar = sine * phibar
        model = model + phi / rho * search
        search = blocks[step + 1] / alpha - theta / rho * search
    return (model, search)


def solution(mesh):
    def run(*args):
        return per_device(mesh.shape["rows"], mesh.shape["cols"], *args)

    return jax.shard_map(
        run,
        mesh=mesh,
        in_specs=(
            P(("rows", "cols"), None, None),
            P(("rows", "cols")),
            P(("rows", "cols")),
            P("rows", "cols"),
            P("cols", "rows"),
        ),
        out_specs=(P("rows", "cols"), P("rows", "cols")),
        check_vma=False,
    )
```

time: 268 us -> 163 us (0.61); the launches traced: 267 us -> 165 us
  matrix products: 136 us -> 0 us
  Pallas kernels: 0 us -> 42.5 us
  starting transfers between devices: 16.5 us -> 54.1 us
  blocking collectives: 25.8 us -> 0 us
  waiting for transfers between devices: 60.3 us -> 41.8 us
  between operations: 6.12 us -> 9.59 us
  other arithmetic: 7.96 us -> 4.68 us
    dot_general x10 -> x0, matrix products: 136 us -> none  [the longest x2 70.7 us: forward(): jnp.einsum('kij,kj->ki', kernels, group[cell_index], precision=HIGHEST)]
    ppermute x11 -> x22, starting transfers between devices: 2.15 us -> 54.1 us  [swapped(): return lax.ppermute(block, axis, [(i, i ^ bit) for i in range(size)])]
    pallas_call x0 -> x5, Pallas kernels: none -> 42.5 us  [call(): pl.pallas_call(kernel, out_shape=outs, in_specs=[vector] + [scalar] * len...]
    all_to_all x3 -> x0, blocking collectives: 25.8 us -> none  [the longest x2 17.3 us: scatter_sum(): lax.all_to_all(parts, axis, split_axis=0, concat_axis=0, tiled=True)]
    all_to_all x3 -> x0, waiting for transfers between devices: 17.5 us -> none  [the longest x2 11.4 us: gather_blocks(): got = lax.all_to_all(copies, axis, split_axis=0, concat_axis=0, tiled=True)]
    all_to_all x3 -> x0, starting transfers between devices: 14.3 us -> none  [the longest x2 10.9 us: gather_blocks(): got = lax.all_to_all(copies, axis, split_axis=0, concat_axis=0, tiled=True)]
    unnamed x4 -> x7, local copies, waits for them, and re-layouts: 0.01 us -> 9.06 us
    gather x5 -> x0, local copies, waits for them, and re-layouts: 5.37 us -> none  [the longest x3 3.22 us: adjoint(): group[pick_index]]
  transfers between devices with their start and end apart: 14 -> 22, of which waited for: 14 -> 20; matrix products, arithmetic and copies ran while one was open for 0% -> 2% of each run, Pallas kernels for 0% -> 0%
where the time goes in v1:
time: 163 us; the launch traced here: 165 us
  starting transfers between devices  54.1 us (33%)
  Pallas kernels  42.5 us (26%)
  waiting for transfers between devices  41.8 us (26%)
  local copies, waits for them, and re-layouts  12.9 us (8%)
  between operations  9.59 us (6%)
  other arithmetic  4.68 us (3%)
    ppermute x22, starting transfers between devices, swapped(): return lax.ppermute(block, axis, [(i, i ^ bit) for i in range(size)])  54.1 us
    pallas_call x5, Pallas kernels, call(): pl.pallas_call(kernel, out_shape=outs, in_specs=[vector] + [scalar] * len...  42.5 us
    ppermute x22, waiting for transfers between devices, swapped(): return lax.ppermute(block, axis, [(i, i ^ bit) for i in range(size)])  41.8 us
    unnamed x7, local copies, waits for them, and re-layouts  9.06 us
  transfers between devices with their start and end apart: 22, of which 20 were waited for; matrix products, arithmetic and copies ran while one was open for 2% of the time, Pallas kernels for 0%

profile of v1, /device:TPU:0, one launch (start us, length us, event | category | flops | bytes accessed | tf_op | source)
XLA Modules:
  0.0 165.5 jit_solution(5233532514349696333)
XLA Ops:
  0.6 3.0 %collective-permute-start = (f32[16,128]{1,0:T(8,128)}, f32[16,128]{1,0:T(8,128)S(1)}, u32[]{:S(2)}, u32[]{:S(2)}) collective-permute-start(f32[16,128]{1,0:T(8,128)} %param.9), channel_id=1, source_target_pairs={{0,1},{1,0},{2,3},{3,2},{4,5},{5,4},{6,7},{7,6},{8,9},{9,8},{10,11... | collective-permute-start | bytes 24584 | tf_op jit(solution)/shard_map/ppermute | solution.py:158
  3.7 0.7 constant_dynamic-update-slice_fusion.1
  4.4 1.1 collective-permute-done
  5.5 4.1 %collective-permute-start.3 = (f32[32,128]{1,0:T(8,128)S(1)}, f32[32,128]{1,0:T(8,128)S(1)}, u32[]{:S(2)}, u32[]{:S(2)}) collective-permute-start(f32[32,128]{1,0:T(8,128)S(1)} %constant_dynamic-update-slice_fusion.rest_0_), channel_id=1, source_target_pairs={{0,6},{1,7},{2,4},{3,5},{4,2},{5,3},{6,0},{7,1},{8,14},{9,15},{10,... | collective-permute-start | bytes 49160 | tf_op jit(solution)/shard_map/ppermute | solution.py:158
  11.3 2.9 %collective-permute-done.2.rest_2_ = f32[32,128]{1,0:T(8,128)S(1)} collective-permute-done((f32[32,128]{1,0:T(8,128)S(1)}, f32[32,128]{1,0:T(8,128)S(1)}, u32[]{:S(2)}, u32[]{:S(2)}) %collective-permute-start.2) | collective-permute-done | bytes 16416 | tf_op jit(solution)/shard_map/ppermute | solution.py:158
  14.3 7.0 %copy-done = f32[320,128,128]{2,1,0:T(8,128)S(1)} copy-done((f32[320,128,128]{2,1,0:T(8,128)S(1)}, f32[320,128,128]{2,1,0:T(8,128)}, u32[]{:S(2)}) %copy-start) | copy-done | bytes 20971544
  21.2 0.7 copy-done.1
  21.9 0.7 copy-done.2
  22.6 7.3 %shard_map.68 = (f32[128,128]{1,0:T(8,128)S(1)}, f32[264,128]{1,0:T(8,128)S(1)}, f32[264,128]{1,0:T(8,128)S(1)}) custom-call(f32[320,128,128]{2,1,0:T(8,128)S(1)} %copy-done, s32[320]{0:T(512)S(1)} %copy-done.1, s32[320]{0:T(512)S(1)} %copy-done.2, s32[1,1]{1,0:T(1,128)S(6)} %copy.10.counts, f32[32,128]{1,0:T(8,128)S(1)} %constant_dynamic-update-slice_fusion.rest_0_, ...), custom_call_target="tpu_custom_call" | custom-call | tf_op jit(solution)/shard_map/pallas_call | solution.py:175
  30.0 1.3 collective-permute-done.4
  31.3 4.1 %collective-permute-start.5 = (f32[264,128]{1,0:T(8,128)S(1)}, f32[264,128]{1,0:T(8,128)S(1)}, u32[]{:S(2)}, u32[]{:S(2)}) collective-permute-start(f32[264,128]{1,0:T(8,128)S(1)} %add.58), channel_id=1, source_target_pairs={{0,16},{8,24},{16,0},{24,8},{1,17},{9,25},{17,1},{25,9},{2,18},{10... | collective-permute-start | bytes 405512 | tf_op jit(solution)/shard_map/ppermute | solution.py:158
  35.4 3.9 %collective-permute-done.5 = f32[264,128]{1,0:T(8,128)S(1)} collective-permute-done((f32[264,128]{1,0:T(8,128)S(1)}, f32[264,128]{1,0:T(8,128)S(1)}, u32[]{:S(2)}, u32[]{:S(2)}) %collective-permute-start.5) | collective-permute-done | bytes 135200 | tf_op jit(solution)/shard_map/ppermute | solution.py:158
  39.4 1.3 collective-permute-done.6.other
  40.7 9.9 %shard_map.69 = (f32[512,128]{1,0:T(8,128)S(1)}, f32[8,128]{1,0:T(8,128)S(1)}, f32[128,128]{1,0:T(8,128)S(1)}, f32[136,128]{1,0:T(8,128)S(1)}) custom-call(f32[320,128,128]{2,1,0:T(8,128)S(1)} %copy-done, s32[320]{0:T(512)S(1)} %copy-done.1, s32[320]{0:T(512)S(1)} %copy-done.2, s32[1,1]{1,0:T(1,128)S(6)} %copy.10.counts, f32[264,128]{1,0:T(8,128)S(1)} %add.59.mine, ...), custom_call_target="tpu_custom_call" | custom-call | tf_op jit(solution)/shard_map/pallas_call | solution.py:175
  50.7 3.9 %collective-permute-start.7 = (f32[136,128]{1,0:T(8,128)S(1)}, f32[136,128]{1,0:T(8,128)S(1)}, u32[]{:S(2)}, u32[]{:S(2)}) collective-permute-start(f32[136,128]{1,0:T(8,128)S(1)} %get-tuple-element.22), channel_id=1, source_target_pairs={{0,1},{1,0},{2,3},{3,2},{4,5},{5,4},{6,7},{7,6},{8,9},{9,8},{10,11... | collective-permute-start | bytes 208904 | tf_op jit(solution)/shard_map/ppermute | solution.py:158
  54.6 2.3 %collective-permute-done.7 = f32[136,128]{1,0:T(8,128)S(1)} collective-permute-done((f32[136,128]{1,0:T(8,128)S(1)}, f32[136,128]{1,0:T(8,128)S(1)}, u32[]{:S(2)}, u32[]{:S(2)}) %collective-permute-start.7) | collective-permute-done | bytes 69664 | tf_op jit(solution)/shard_map/ppermute | solution.py:158
  56.9 4.8 %collective-permute-start.8 = (f32[136,128]{1,0:T(8,128)S(1)}, f32[136,128]{1,0:T(8,128)S(1)}, u32[]{:S(2)}, u32[]{:S(2)}) collective-permute-start(f32[136,128]{1,0:T(8,128)S(1)} %add.60), channel_id=1, source_target_pairs={{0,2},{1,3},{2,0},{3,1},{4,6},{5,7},{6,4},{7,5},{8,10},{9,11},{10,... | collective-permute-start | bytes 208904 | tf_op jit(solution)/shard_map/ppermute | solution.py:158
  61.7 2.5 %collective-permute-done.8 = f32[136,128]{1,0:T(8,128)S(1)} collective-permute-done((f32[136,128]{1,0:T(8,128)S(1)}, f32[136,128]{1,0:T(8,128)S(1)}, u32[]{:S(2)}, u32[]{:S(2)}) %collective-permute-start.8) | collective-permute-done | bytes 69664 | tf_op jit(solution)/shard_map/ppermute | solution.py:158
  64.2 2.2 %collective-permute-start.9 = (f32[136,128]{1,0:T(8,128)S(1)}, f32[136,128]{1,0:T(8,128)S(1)}, u32[]{:S(2)}, u32[]{:S(2)}) collective-permute-start(f32[136,128]{1,0:T(8,128)S(1)} %add.61.mine), channel_id=1, source_target_pairs={{0,4},{1,5},{2,6},{3,7},{4,0},{5,1},{6,2},{7,3},{8,12},{9,13},{10,... | collective-permute-start | bytes 208904 | tf_op jit(solution)/shard_map/ppermute | solution.py:158
  66.4 3.0 %collective-permute-done.9.other = f32[136,128]{1,0:T(8,128)S(1)} collective-permute-done((f32[136,128]{1,0:T(8,128)S(1)}, f32[136,128]{1,0:T(8,128)S(1)}, u32[]{:S(2)}, u32[]{:S(2)}) %collective-permute-start.9) | collective-permute-done | bytes 69664 | tf_op jit(solution)/shard_map/ppermute | solution.py:158
  69.5 7.3 %shard_map.70 = (f32[128,128]{1,0:T(8,128)S(1)}, f32[8,128]{1,0:T(8,128)S(1)}, f32[264,128]{1,0:T(8,128)S(1)}, f32[264,128]{1,0:T(8,128)S(1)}) custom-call(f32[320,128,128]{2,1,0:T(8,128)S(1)} %copy-done, s32[320]{0:T(512)S(1)} %copy-done.1, s32[320]{0:T(512)S(1)} %copy-done.2, s32[1,1]{1,0:T(1,128)S(6)} %copy.10.counts, f32[136,128]{1,0:T(8,128)S(1)} %add.61.mine, ...), custom_call_target="tpu_custom_call" | custom-call | tf_op jit(solution)/shard_map/pallas_call | solution.py:175
  76.9 1.3 collective-permute-done.10
  78.2 4.8 %collective-permute-start.11 = (f32[264,128]{1,0:T(8,128)S(1)}, f32[264,128]{1,0:T(8,128)S(1)}, u32[]{:S(2)}, u32[]{:S(2)}) collective-permute-start(f32[264,128]{1,0:T(8,128)S(1)} %add.62), channel_id=1, source_target_pairs={{0,16},{8,24},{16,0},{24,8},{1,17},{9,25},{17,1},{25,9},{2,18},{10... | collective-permute-start | bytes 405512 | tf_op jit(solution)/shard_map/ppermute | solution.py:158
  83.0 3.9 %collective-permute-done.11 = f32[264,128]{1,0:T(8,128)S(1)} collective-permute-done((f32[264,128]{1,0:T(8,128)S(1)}, f32[264,128]{1,0:T(8,128)S(1)}, u32[]{:S(2)}, u32[]{:S(2)}) %collective-permute-start.11) | collective-permute-done | bytes 135200 | tf_op jit(solution)/shard_map/ppermute | solution.py:158
  87.0 1.3 collective-permute-done.12.other
  88.4 10.0 %shard_map.71 = (f32[512,128]{1,0:T(8,128)S(1)}, f32[8,128]{1,0:T(8,128)S(1)}, f32[128,128]{1,0:T(8,128)S(1)}, f32[136,128]{1,0:T(8,128)S(1)}) custom-call(f32[320,128,128]{2,1,0:T(8,128)S(1)} %copy-done, s32[320]{0:T(512)S(1)} %copy-done.1, s32[320]{0:T(512)S(1)} %copy-done.2, s32[1,1]{1,0:T(1,128)S(6)} %copy.10.counts, f32[264,128]{1,0:T(8,128)S(1)} %add.63.mine, ...), custom_call_target="tpu_custom_call" | custom-call | tf_op jit(solution)/shard_map/pallas_call | solution.py:175
  98.4 4.4 %collective-permute-start.13 = (f32[136,128]{1,0:T(8,128)S(1)}, f32[136,128]{1,0:T(8,128)S(1)}, u32[]{:S(2)}, u32[]{:S(2)}) collective-permute-start(f32[136,128]{1,0:T(8,128)S(1)} %get-tuple-element.31), channel_id=1, source_target_pairs={{0,1},{1,0},{2,3},{3,2},{4,5},{5,4},{6,7},{7,6},{8,9},{9,8},{10,11... | collective-permute-start | bytes 208904 | tf_op jit(solution)/shard_map/ppermute | solution.py:158
  102.7 2.3 %collective-permute-done.13 = f32[136,128]{1,0:T(8,128)S(1)} collective-permute-done((f32[136,128]{1,0:T(8,128)S(1)}, f32[136,128]{1,0:T(8,128)S(1)}, u32[]{:S(2)}, u32[]{:S(2)}) %collective-permute-start.13) | collective-permute-done | bytes 69664 | tf_op jit(solution)/shard_map/ppermute | solution.py:158
  105.0 6.5 %collective-permute-start.14 = (f32[136,128]{1,0:T(8,128)S(1)}, f32[136,128]{1,0:T(8,128)S(1)}, u32[]{:S(2)}, u32[]{:S(2)}) collective-permute-start(f32[136,128]{1,0:T(8,128)S(1)} %add.65), channel_id=1, source_target_pairs={{0,2},{1,3},{2,0},{3,1},{4,6},{5,7},{6,4},{7,5},{8,10},{9,11},{10,... | collective-permute-start | bytes 208904 | tf_op jit(solution)/shard_map/ppermute | solution.py:158
  111.5 2.3 %collective-permute-done.14 = f32[136,128]{1,0:T(8,128)S(1)} collective-permute-done((f32[136,128]{1,0:T(8,128)S(1)}, f32[136,128]{1,0:T(8,128)S(1)}, u32[]{:S(2)}, u32[]{:S(2)}) %collective-permute-start.14) | collective-permute-done | bytes 69664 | tf_op jit(solution)/shard_map/ppermute | solution.py:158
  113.8 2.6 %collective-permute-start.15 = (f32[136,128]{1,0:T(8,128)S(1)}, f32[136,128]{1,0:T(8,128)S(1)}, u32[]{:S(2)}, u32[]{:S(2)}) collective-permute-start(f32[136,128]{1,0:T(8,128)S(1)} %add.66.mine), channel_id=1, source_target_pairs={{0,4},{1,5},{2,6},{3,7},{4,0},{5,1},{6,2},{7,3},{8,12},{9,13},{10,... | collective-permute-start | bytes 208904 | tf_op jit(solution)/shard_map/ppermute | solution.py:158
  116.4 2.6 %collective-permute-done.15.other = f32[136,128]{1,0:T(8,128)S(1)} collective-permute-done((f32[136,128]{1,0:T(8,128)S(1)}, f32[136,128]{1,0:T(8,128)S(1)}, u32[]{:S(2)}, u32[]{:S(2)}) %collective-permute-start.15) | collective-permute-done | bytes 69664 | tf_op jit(solution)/shard_map/ppermute | solution.py:158
  119.0 7.9 %shard_map.72 = (f32[128,128]{1,0:T(8,128)}, f32[8,128]{1,0:T(8,128)S(1)}, f32[264,128]{1,0:T(8,128)S(1)}, f32[264,128]{1,0:T(8,128)S(1)}) custom-call(f32[320,128,128]{2,1,0:T(8,128)S(1)} %copy-done, s32[320]{0:T(512)S(1)} %copy-done.1, s32[320]{0:T(512)S(1)} %copy-done.2, s32[1,1]{1,0:T(1,128)S(6)} %copy.10.counts, f32[136,128]{1,0:T(8,128)S(1)} %add.66.mine, ...), custom_call_target="tpu_custom_call" | custom-call | tf_op jit(solution)/shard_map/pallas_call | solution.py:175
  127.0 1.4 collective-permute-done.16
  128.4 3.8 %collective-permute-start.17 = (f32[264,128]{1,0:T(8,128)S(1)}, f32[264,128]{1,0:T(8,128)S(1)}, u32[]{:S(2)}, u32[]{:S(2)}) collective-permute-start(f32[264,128]{1,0:T(8,128)S(1)} %add.67), channel_id=1, source_target_pairs={{0,16},{8,24},{16,0},{24,8},{1,17},{9,25},{17,1},{25,9},{2,18},{10... | collective-permute-start | bytes 405512 | tf_op jit(solution)/shard_map/ppermute | solution.py:158
  132.7 3.4 %collective-permute-done.17 = f32[264,128]{1,0:T(8,128)S(1)} collective-permute-done((f32[264,128]{1,0:T(8,128)S(1)}, f32[264,128]{1,0:T(8,128)S(1)}, u32[]{:S(2)}, u32[]{:S(2)}) %collective-permute-start.17) | collective-permute-done | bytes 135200 | tf_op jit(solution)/shard_map/ppermute | solution.py:158
  137.3 0.7 fusion.1
  137.9 0.7 multiply_reduce_fusion
  138.6 0.6 broadcast_in_dim.3
  139.3 1.2 collective-permute-done.18
  140.5 0.6 broadcast_add_fusion
  141.1 2.2 %collective-permute-start.19 = (f32[8,128]{1,0:T(8,128)S(1)}, f32[8,128]{1,0:T(8,128)S(1)}, u32[]{:S(2)}, u32[]{:S(2)}) collective-permute-start(f32[8,128]{1,0:T(8,128)S(1)} %broadcast_add_fusion), channel_id=1, source_target_pairs={{0,1},{1,0},{2,3},{3,2},{4,5},{5,4},{6,7},{7,6},{8,9},{9,8},{10,11... | collective-permute-start | bytes 12296 | tf_op jit(solution)/shard_map/ppermute | solution.py:158
  143.3 1.6 collective-permute-done.19
  144.9 0.6 fusion.3
  145.5 4.0 %collective-permute-start.20 = (f32[8,128]{1,0:T(8,128)S(1)}, f32[8,128]{1,0:T(8,128)S(1)}, u32[]{:S(2)}, u32[]{:S(2)}) collective-permute-start(f32[8,128]{1,0:T(8,128)S(1)} %fusion.3), channel_id=1, source_target_pairs={{0,2},{1,3},{2,0},{3,1},{4,6},{5,7},{6,4},{7,5},{8,10},{9,11},{10,... | collective-permute-start | bytes 12296 | tf_op jit(solution)/shard_map/ppermute | solution.py:158
  149.5 1.6 collective-permute-done.20
  151.1 2.8 %collective-permute-start.21 = (f32[8,128]{1,0:T(8,128)S(1)}, f32[8,128]{1,0:T(8,128)S(1)}, u32[]{:S(2)}, u32[]{:S(2)}) collective-permute-start(f32[8,128]{1,0:T(8,128)S(1)} %add.75), channel_id=1, source_target_pairs={{0,4},{1,5},{2,6},{3,7},{4,0},{5,1},{6,2},{7,3},{8,12},{9,13},{10,... | collective-permute-start | bytes 12296 | tf_op jit(solution)/shard_map/ppermute | solution.py:158
  163.6 1.9 %multiply_subtract_fusion = (f32[128,128]{1,0:T(8,128)}, f32[128,128]{1,0:T(8,128)}) fusion(f32[256,128]{1,0:T(8,128)S(1)} %get-tuple-element.39, s32[]{:T(128)S(6)} %select_n.8, f32[]{:T(128)S(6)} %div.85, f32[]{:T(128)} %bitcast.7, f32[128,128]{1,0:T(8,128)S(1)} %get-tuple-element.30, f32[]{:T(128)} %bitcast, f32[]{:T(128)S(6)} %div.73, ...), kind=kLoop, calls=%fused_computation.5 | loop fusion | flops 163840 | bytes 327712 | tf_op jit(solution)/shard_map/sub | solution.py:255
  (33 shorter events, 4.8 us)
Async XLA Ops:
  0.6 4.9 %collective-permute-start = (f32[16,128]{1,0:T(8,128)}, f32[16,128]{1,0:T(8,128)S(1)}, u32[]{:S(2)}, u32[]{:S(2)}) collective-permute-start(f32[16,128]{1,0:T(8,128)} %param.9), channel_id=1, source_target_pairs={{0,1},{1,0},{2,3},{3,2},{4,5},{5,4},{6,7},{7,6},{8,9},{9,8},{10,11... | collective-permute-start | bytes 24584 | tf_op jit(solution)/shard_map/ppermute | solution.py:158
  5.5 5.8 %collective-permute-start.3 = (f32[32,128]{1,0:T(8,128)S(1)}, f32[32,128]{1,0:T(8,128)S(1)}, u32[]{:S(2)}, u32[]{:S(2)}) collective-permute-start(f32[32,128]{1,0:T(8,128)S(1)} %constant_dynamic-update-slice_fusion.rest_0_), channel_id=1, source_target_pairs={{0,6},{1,7},{2,4},{3,5},{4,2},{5,3},{6,0},{7,1},{8,14},{9,15},{10,... | collective-permute-start | bytes 49160 | tf_op jit(solution)/shard_map/ppermute | solution.py:158
  9.6 4.6 %collective-permute-start.2 = (f32[32,128]{1,0:T(8,128)S(1)}, f32[32,128]{1,0:T(8,128)S(1)}, u32[]{:S(2)}, u32[]{:S(2)}) collective-permute-start(f32[32,128]{1,0:T(8,128)S(1)} %constant_dynamic-update-slice_fusion.rest_0_), channel_id=1, source_target_pairs={{0,4},{1,5},{2,6},{3,7},{4,0},{5,1},{6,2},{7,3},{8,12},{9,13},{10,... | collective-permute-start | bytes 49160 | tf_op jit(solution)/shard_map/ppermute | solution.py:158
  9.6 4.6 %collective-permute-start.1 = (f32[32,128]{1,0:T(8,128)S(1)}, f32[32,128]{1,0:T(8,128)S(1)}, u32[]{:S(2)}, u32[]{:S(2)}) collective-permute-start(f32[32,128]{1,0:T(8,128)S(1)} %constant_dynamic-update-slice_fusion.rest_0_), channel_id=1, source_target_pairs={{0,2},{1,3},{2,0},{3,1},{4,6},{5,7},{6,4},{7,5},{8,10},{9,11},{10,... | collective-permute-start | bytes 49160 | tf_op jit(solution)/shard_map/ppermute | solution.py:158
  14.2 7.0 %copy-start = (f32[320,128,128]{2,1,0:T(8,128)S(1)}, f32[320,128,128]{2,1,0:T(8,128)}, u32[]{:S(2)}) copy-start(f32[320,128,128]{2,1,0:T(8,128)} %tiles.9) | copy-start | bytes 62914564
  21.2 0.7 copy-start.1
  21.9 0.7 copy-start.2
  29.9 1.4 collective-permute-start.4
  31.3 8.0 %collective-permute-start.5 = (f32[264,128]{1,0:T(8,128)S(1)}, f32[264,128]{1,0:T(8,128)S(1)}, u32[]{:S(2)}, u32[]{:S(2)}) collective-permute-start(f32[264,128]{1,0:T(8,128)S(1)} %add.58), channel_id=1, source_target_pairs={{0,16},{8,24},{16,0},{24,8},{1,17},{9,25},{17,1},{25,9},{2,18},{10... | collective-permute-start | bytes 405512 | tf_op jit(solution)/shard_map/ppermute | solution.py:158
  39.3 1.4 collective-permute-start.6
  50.7 6.2 %collective-permute-start.7 = (f32[136,128]{1,0:T(8,128)S(1)}, f32[136,128]{1,0:T(8,128)S(1)}, u32[]{:S(2)}, u32[]{:S(2)}) collective-permute-start(f32[136,128]{1,0:T(8,128)S(1)} %get-tuple-element.22), channel_id=1, source_target_pairs={{0,1},{1,0},{2,3},{3,2},{4,5},{5,4},{6,7},{7,6},{8,9},{9,8},{10,11... | collective-permute-start | bytes 208904 | tf_op jit(solution)/shard_map/ppermute | solution.py:158
  56.9 7.3 %collective-permute-start.8 = (f32[136,128]{1,0:T(8,128)S(1)}, f32[136,128]{1,0:T(8,128)S(1)}, u32[]{:S(2)}, u32[]{:S(2)}) collective-permute-start(f32[136,128]{1,0:T(8,128)S(1)} %add.60), channel_id=1, source_target_pairs={{0,2},{1,3},{2,0},{3,1},{4,6},{5,7},{6,4},{7,5},{8,10},{9,11},{10,... | collective-permute-start | bytes 208904 | tf_op jit(solution)/shard_map/ppermute | solution.py:158
  64.2 5.3 %collective-permute-start.9 = (f32[136,128]{1,0:T(8,128)S(1)}, f32[136,128]{1,0:T(8,128)S(1)}, u32[]{:S(2)}, u32[]{:S(2)}) collective-permute-start(f32[136,128]{1,0:T(8,128)S(1)} %add.61.mine), channel_id=1, source_target_pairs={{0,4},{1,5},{2,6},{3,7},{4,0},{5,1},{6,2},{7,3},{8,12},{9,13},{10,... | collective-permute-start | bytes 208904 | tf_op jit(solution)/shard_map/ppermute | solution.py:158
  76.8 1.4 collective-permute-start.10
  78.2 8.7 %collective-permute-start.11 = (f32[264,128]{1,0:T(8,128)S(1)}, f32[264,128]{1,0:T(8,128)S(1)}, u32[]{:S(2)}, u32[]{:S(2)}) collective-permute-start(f32[264,128]{1,0:T(8,128)S(1)} %add.62), channel_id=1, source_target_pairs={{0,16},{8,24},{16,0},{24,8},{1,17},{9,25},{17,1},{25,9},{2,18},{10... | collective-permute-start | bytes 405512 | tf_op jit(solution)/shard_map/ppermute | solution.py:158
  87.0 1.4 collective-permute-start.12
  98.4 6.7 %collective-permute-start.13 = (f32[136,128]{1,0:T(8,128)S(1)}, f32[136,128]{1,0:T(8,128)S(1)}, u32[]{:S(2)}, u32[]{:S(2)}) collective-permute-start(f32[136,128]{1,0:T(8,128)S(1)} %get-tuple-element.31), channel_id=1, source_target_pairs={{0,1},{1,0},{2,3},{3,2},{4,5},{5,4},{6,7},{7,6},{8,9},{9,8},{10,11... | collective-permute-start | bytes 208904 | tf_op jit(solution)/shard_map/ppermute | solution.py:158
  105.0 8.7 %collective-permute-start.14 = (f32[136,128]{1,0:T(8,128)S(1)}, f32[136,128]{1,0:T(8,128)S(1)}, u32[]{:S(2)}, u32[]{:S(2)}) collective-permute-start(f32[136,128]{1,0:T(8,128)S(1)} %add.65), channel_id=1, source_target_pairs={{0,2},{1,3},{2,0},{3,1},{4,6},{5,7},{6,4},{7,5},{8,10},{9,11},{10,... | collective-permute-start | bytes 208904 | tf_op jit(solution)/shard_map/ppermute | solution.py:158
  113.8 5.3 %collective-permute-start.15 = (f32[136,128]{1,0:T(8,128)S(1)}, f32[136,128]{1,0:T(8,128)S(1)}, u32[]{:S(2)}, u32[]{:S(2)}) collective-permute-start(f32[136,128]{1,0:T(8,128)S(1)} %add.66.mine), channel_id=1, source_target_pairs={{0,4},{1,5},{2,6},{3,7},{4,0},{5,1},{6,2},{7,3},{8,12},{9,13},{10,... | collective-permute-start | bytes 208904 | tf_op jit(solution)/shard_map/ppermute | solution.py:158
  127.0 1.4 collective-permute-start.16
  128.4 7.7 %collective-permute-start.17 = (f32[264,128]{1,0:T(8,128)S(1)}, f32[264,128]{1,0:T(8,128)S(1)}, u32[]{:S(2)}, u32[]{:S(2)}) collective-permute-start(f32[264,128]{1,0:T(8,128)S(1)} %add.67), channel_id=1, source_target_pairs={{0,16},{8,24},{16,0},{24,8},{1,17},{9,25},{17,1},{25,9},{2,18},{10... | collective-permute-start | bytes 405512 | tf_op jit(solution)/shard_map/ppermute | solution.py:158
  139.2 1.2 collective-permute-start.18
  141.1 3.8 %collective-permute-start.19 = (f32[8,128]{1,0:T(8,128)S(1)}, f32[8,128]{1,0:T(8,128)S(1)}, u32[]{:S(2)}, u32[]{:S(2)}) collective-permute-start(f32[8,128]{1,0:T(8,128)S(1)} %broadcast_add_fusion), channel_id=1, source_target_pairs={{0,1},{1,0},{2,3},{3,2},{4,5},{5,4},{6,7},{7,6},{8,9},{9,8},{10,11... | collective-permute-start | bytes 12296 | tf_op jit(solution)/shard_map/ppermute | solution.py:158
  145.5 5.6 %collective-permute-start.20 = (f32[8,128]{1,0:T(8,128)S(1)}, f32[8,128]{1,0:T(8,128)S(1)}, u32[]{:S(2)}, u32[]{:S(2)}) collective-permute-start(f32[8,128]{1,0:T(8,128)S(1)} %fusion.3), channel_id=1, source_target_pairs={{0,2},{1,3},{2,0},{3,1},{4,6},{5,7},{6,4},{7,5},{8,10},{9,11},{10,... | collective-permute-start | bytes 12296 | tf_op jit(solution)/shard_map/ppermute | solution.py:158
  151.1 11.2 %collective-permute-start.21 = (f32[8,128]{1,0:T(8,128)S(1)}, f32[8,128]{1,0:T(8,128)S(1)}, u32[]{:S(2)}, u32[]{:S(2)}) collective-permute-start(f32[8,128]{1,0:T(8,128)S(1)} %add.75), channel_id=1, source_target_pairs={{0,4},{1,5},{2,6},{3,7},{4,0},{5,1},{6,2},{7,3},{8,12},{9,13},{10,... | collective-permute-start | bytes 12296 | tf_op jit(solution)/shard_map/ppermute | solution.py:158

commit v2 on v1

v2 whole, which is shorter than its diff:
```python
import functools

import jax
import jax.numpy as jnp
from jax import lax
from jax.experimental import pallas as pl
from jax.experimental.pallas import tpu as pltpu
from jax.sharding import PartitionSpec as P

PBLK = 128
CBLK = 512
ITERS = 2
B = 128
SUB = 8
GROUP = 16
PARTS = 2
STEP = 16
BUFFERS = 4
TAIL = 8


def split(value):
    high = value.astype(jnp.bfloat16)
    return high, (value - high.astype(jnp.float32)).astype(jnp.bfloat16)


def split_tiles(start, tiles, out, held, arrived):
    steps = out.shape[0] // STEP

    def copy(step, slot):
        return pltpu.make_async_copy(
            tiles.at[pl.ds(start + step * STEP, STEP)], held.at[slot], arrived.at[slot]
        )

    for step in range(min(BUFFERS - 1, steps)):
        copy(step, step).start()
    for step in range(steps):
        slot = step % BUFFERS
        ahead = step + BUFFERS - 1
        if ahead < steps:
            copy(ahead, ahead % BUFFERS).start()
        copy(step, slot).wait()

        def one(k, carry):
            high, low = split(held[slot, k])
            out[step * STEP + k, :B, :] = high
            out[step * STEP + k, B:, :] = low
            return carry

        lax.fori_loop(0, STEP, one, 0, unroll=2)


def fill_table(table, value):
    high, low = split(value)
    blocks = value.shape[0]
    table[pl.ds(0, blocks, stride=SUB), :] = high.astype(jnp.float32)
    table[pl.ds(1, blocks, stride=SUB), :] = low.astype(jnp.float32)


def block_at(index):
    return pl.ds(pl.multiple_of(index * SUB, SUB), SUB)


def tile_transposed(tile, row):
    row = jnp.concatenate([row, row], axis=1)
    return jnp.dot(row, tile, preferred_element_type=jnp.float32)


def tile_forward(tile, row):
    both = lax.dot_general(
        row, tile, (((1,), (1,)), ((), ())), preferred_element_type=jnp.float32
    )
    return both[:, :B] + both[:, B:]


def over_tiles(parts, live, product, table, source, target, blocks, acc):
    zeros = jnp.zeros((blocks, B), jnp.float32)
    acc[pl.ds(0, blocks, stride=SUB), :] = zeros
    acc[pl.ds(1, blocks, stride=SUB), :] = zeros
    first = 0
    for tiles in parts:
        size = tiles.shape[0]
        here = jnp.clip(live - first, 0, size)

        def some(group, carry, tiles=tiles, first=first):
            base = group * GROUP
            sums = []
            for k in range(GROUP):
                row = table[block_at(source[first + base + k]), :].astype(jnp.bfloat16)
                sums.append(product(tiles[base + k], row))
            for k in range(GROUP):
                slot = first + base + k
                acc[block_at(jnp.where(slot < live, target[slot], blocks)), :] += sums[k]
            return carry

        lax.fori_loop(0, (here + GROUP - 1) // GROUP, some, 0)
        first += size
    return acc[pl.ds(0, blocks, stride=SUB), :] + acc[pl.ds(1, blocks, stride=SUB), :]


def halves(n_rows, cells):
    size = cells // n_rows
    return size, [range(core, n_rows, 2) for core in range(2)]


def adjoint_tail(n_rows, parts, pick, cell, counts, u, keep, send, table, acc):
    fill_table(table, u)
    whole = over_tiles(parts, counts[0, 0], tile_transposed, table, pick, cell, CBLK, acc)
    square = jnp.full((TAIL, B), jnp.sum(u * u))
    size, _ = halves(n_rows, CBLK)
    core = lax.rem(lax.axis_index("rows"), 2)
    for block in range(n_rows):
        part = whole[block * size : (block + 1) * size]
        place = pl.ds(block // 2 * size, size)

        @pl.when(core == block % 2)
        def _():
            keep[place, :] = part

        @pl.when(core != block % 2)
        def _():
            send[place, :] = part

    keep[pl.ds(CBLK // 2, TAIL), :] = square
    send[pl.ds(CBLK // 2, TAIL), :] = square


def first_adjoint(n_rows, n_cols, pick, cell, counts, *rest):
    parts, pieces, (u_out, keep, send, table, acc) = rest[:PARTS], rest[PARTS:-5], rest[-5:]
    me = lax.axis_index("cols")
    offset = 0
    for piece in pieces:
        rows = PBLK // n_cols
        for at in range(piece.shape[0] // rows):
            owner = jnp.bitwise_xor(me, offset)
            u_out[pl.ds(pl.multiple_of(owner * rows, rows), rows), :] = piece[pl.ds(at * rows, rows), :]
            offset += 1
    adjoint_tail(n_rows, parts, pick, cell, counts, u_out[...], keep, send, table, acc)


def next_adjoint(n_rows, pick, cell, counts, *rest):
    parts = rest[:PARTS]
    mine, other, u_old, beta_old, u_out, alpha_out, keep, send, table, acc = rest[PARTS:]
    total = mine[...] + other[...]
    alpha = jnp.sqrt(total[PBLK:])
    alpha_out[...] = alpha
    u = total[:PBLK] / alpha[:1] - alpha[:1] * (u_old[...] / beta_old[:1])
    u_out[...] = u
    adjoint_tail(n_rows, parts, pick, cell, counts, u, keep, send, table, acc)


def forward(first, n_rows, pick, cell, counts, *rest):
    parts, rest = rest[:PARTS], rest[PARTS:]
    if first:
        mine, other, v_out, beta_out, own_out, out, table, acc = rest
    else:
        mine, other, v_old, alpha_old, v_out, beta_out, own_out, out, table, acc = rest
    size, _ = halves(n_rows, CBLK)
    me = lax.axis_index("rows")
    core = lax.rem(me, 2)
    beta = jnp.sqrt(mine[pl.ds(CBLK // 2, TAIL), :])
    beta_out[...] = beta
    for block in range(n_rows):
        place = pl.ds(block // 2 * size, size)
        part = jnp.where(core == block % 2, mine[place, :], other[place, :]) / beta[:1]
        here = pl.ds(block * size, size)
        if not first:
            part = part - beta[:1] * (v_old[here, :] / alpha_old[:1])
        v_out[here, :] = part
    own_out[...] = v_out[pl.ds(pl.multiple_of(me * size, size), size), :]
    v = v_out[...]
    fill_table(table, v)
    out[:PBLK, :] = over_tiles(parts, counts[0, 0], tile_forward, table, cell, pick, PBLK, acc)
    out[pl.ds(PBLK, TAIL), :] = jnp.full((TAIL, B), jnp.sum(v * v))


def swapped(block, axis, size, bit):
    return lax.ppermute(block, axis, [(i, i ^ bit) for i in range(size)])


def pairwise_sum(block, axis, size, bit=1):
    while bit < size:
        block = block + swapped(block, axis, size, bit)
        bit *= 2
    return block


def shape(*dims):
    return jax.ShapeDtypeStruct(dims, jnp.float32)


VECTOR = pl.BlockSpec(memory_space=pltpu.VMEM)
SCALAR = pl.BlockSpec(memory_space=pltpu.SMEM)


def call(kernel, outs, sources, targets, scalars, arrays):
    return pl.pallas_call(
        kernel,
        out_shape=outs,
        in_specs=[SCALAR] * len(scalars) + [VECTOR] * len(arrays),
        out_specs=[VECTOR] * len(outs),
        scratch_shapes=[
            pltpu.VMEM((sources * SUB, B), jnp.float32),
            pltpu.VMEM(((targets + 1) * SUB, B), jnp.float32),
        ],
        compiler_params=pltpu.CompilerParams(vmem_limit_bytes=24 << 20),
    )(*scalars, *arrays)


def split_part(kernels, part):
    size = kernels.shape[0] // PARTS
    return pl.pallas_call(
        functools.partial(split_tiles, part * size),
        out_shape=pltpu.VMEM((size, 2 * B, B), jnp.bfloat16),
        in_specs=[pl.BlockSpec(memory_space=pl.ANY)],
        out_specs=VECTOR,
        scratch_shapes=[
            pltpu.VMEM((BUFFERS, STEP, B, B), jnp.float32),
            pltpu.SemaphoreType.DMA((BUFFERS,)),
        ],
        cost_estimate=pl.CostEstimate(
            flops=4 * size * B * B, bytes_accessed=4 * size * B * B, transcendentals=0
        ),
        compiler_params=pltpu.CompilerParams(vmem_limit_bytes=24 << 20),
    )(kernels)


def per_device(n_rows, n_cols, kernels, pick_index, cell_index, counts, data):
    tiles = [split_part(kernels, part) for part in range(PARTS)]
    scalars = tuple(
        pltpu.with_memory_space_constraint(x, pltpu.SMEM) for x in (pick_index, cell_index, counts)
    )
    half = CBLK // 2 + TAIL
    own = CBLK // n_rows

    def sum_cells(keep, send):
        return pairwise_sum(keep + swapped(send, "rows", n_rows, 1), "rows", n_rows, 2)

    pair = jnp.concatenate([data, swapped(data, "cols", n_cols, 1)], axis=0)
    pieces = [pair] + [swapped(pair, "cols", n_cols, bit) for bit in range(2, n_cols, 2)]
    upick, keep, send = call(
        functools.partial(first_adjoint, n_rows, n_cols),
        [shape(PBLK, B), shape(half, B), shape(half, B)],
        PBLK,
        CBLK,
        scalars,
        tiles + pieces,
    )
    vcell = alpha = None
    blocks, alphas, betas = [], [], []
    for step in range(ITERS):
        mine = sum_cells(keep, send)
        other = swapped(mine, "rows", n_rows, 1)
        vcell, beta, block, product = call(
            functools.partial(forward, step == 0, n_rows),
            [shape(CBLK, B), shape(TAIL, B), shape(own, B), shape(PBLK + TAIL, B)],
            CBLK,
            PBLK,
            scalars,
            tiles + [mine, other] + ([] if step == 0 else [vcell, alpha]),
        )
        blocks.append(block)
        betas.append(beta[0, 0])
        bit = 1
        while 2 * bit < n_cols:
            product = product + swapped(product, "cols", n_cols, bit)
            bit *= 2
        upick, alpha, keep, send = call(
            functools.partial(next_adjoint, n_rows),
            [shape(PBLK, B), shape(TAIL, B), shape(half, B), shape(half, B)],
            PBLK,
            CBLK,
            scalars,
            tiles + [product, swapped(product, "cols", n_cols, bit), upick, beta],
        )
        alphas.append(alpha[0, 0])
    mine = sum_cells(keep, send)
    beta = jnp.sqrt(mine[CBLK // 2, 0])
    betas.append(beta)
    me = lax.axis_index("rows")
    old = vcell.reshape(n_rows // 2, 2, own, B)
    old = lax.dynamic_index_in_dim(old, lax.rem(me, 2), axis=1, keepdims=False)
    kept = mine[: CBLK // 2] / beta - beta * (old.reshape(CBLK // 2, B) / alphas[-1])
    square = jnp.full((TAIL, B), jnp.sum(kept * kept))
    square = square + swapped(square, "rows", n_rows, 1)
    square = pairwise_sum(square, "cols", n_cols)
    alphas.append(jnp.sqrt(square[0, 0]))
    blocks.append(lax.dynamic_slice_in_dim(kept, lax.div(me, 2) * own, own, axis=0))

    phibar, rhobar = betas[0], alphas[0]
    search = blocks[0] / alphas[0]
    model = jnp.zeros_like(search)
    for step in range(ITERS):
        beta, alpha = betas[step + 1], alphas[step + 1]
        rho = jnp.sqrt(rhobar * rhobar + beta * beta)
        cosine = rhobar / rho
        sine = beta / rho
        theta = sine * alpha
        rhobar = -cosine * alpha
        phi = cosine * phibar
        phibar = sine * phibar
        model = model + phi / rho * search
        search = blocks[step + 1] / alpha - theta / rho * search
    return (model, search)


def solution(mesh):
    def run(*args):
        return per_device(mesh.shape["rows"], mesh.shape["cols"], *args)

    return jax.shard_map(
        run,
        mesh=mesh,
        in_specs=(
            P(("rows", "cols"), None, None),
            P(("rows", "cols")),
            P(("rows", "cols")),
            P("rows", "cols"),
            P("cols", "rows"),
        ),
        out_specs=(P("rows", "cols"), P("rows", "cols")),
        check_vma=False,
    )
```

time: 163 us -> 137 us (0.84); the launches traced: 165 us -> 136 us
  Pallas kernels: 42.5 us -> 25.9 us
  starting transfers between devices: 54.1 us -> 44.4 us
  local copies, waits for them, and re-layouts: 12.9 us -> 4.6 us
  waiting for transfers between devices: 41.8 us -> 46.7 us
    pallas_call x5 -> x7, Pallas kernels: 42.5 us -> 25.9 us  [the longest x5 16.4 us: call(): pl.pallas_call(kernel, out_shape=outs, in_specs=[SCALAR] * len(scalars) +...]
    ppermute x22, starting transfers between devices: 54.1 us -> 44.4 us  [swapped(): return lax.ppermute(block, axis, [(i, i ^ bit) for i in range(size)])]
    unnamed x7 -> x5, local copies, waits for them, and re-layouts: 9.06 us -> 0.74 us
    ppermute x22, waiting for transfers between devices: 41.8 us -> 46.7 us  [swapped(): return lax.ppermute(block, axis, [(i, i ^ bit) for i in range(size)])]
  transfers between devices with their start and end apart: 22 -> 22, of which waited for: 20 -> 18; matrix products, arithmetic and copies ran while one was open for 2% -> 2% of each run, Pallas kernels for 0% -> 7%
where the time goes in v2:
time: 137 us; the launch traced here: 136 us
  waiting for transfers between devices  46.7 us (34%)
  starting transfers between devices  44.4 us (32%)
  Pallas kernels  25.9 us (19%)
  between operations  9.71 us (7%)
  other arithmetic  4.81 us (4%)
  local copies, waits for them, and re-layouts  4.6 us (3%)
    ppermute x22, waiting for transfers between devices, swapped(): return lax.ppermute(block, axis, [(i, i ^ bit) for i in range(size)])  46.7 us
    ppermute x22, starting transfers between devices, swapped(): return lax.ppermute(block, axis, [(i, i ^ bit) for i in range(size)])  44.4 us
    pallas_call x5, Pallas kernels, call(): pl.pallas_call(kernel, out_shape=outs, in_specs=[SCALAR] * len(scalars) +...  16.4 us
    pallas_call x2, Pallas kernels, split_part(): pl.pallas_call(functools.partial(split_tiles, part * size), out_shape=plt...  9.54 us
  transfers between devices with their start and end apart: 22, of which 18 were waited for; matrix products, arithmetic and copies ran while one was open for 2% of the time, Pallas kernels for 7%

profile of v2, /device:TPU:0, one launch (start us, length us, event | category | flops | bytes accessed | tf_op | source)
XLA Modules:
  0.0 136.1 jit_solution(770748182019018796)
XLA Ops:
  0.6 3.0 %collective-permute-start = (f32[16,128]{1,0:T(8,128)}, f32[16,128]{1,0:T(8,128)S(1)}, u32[]{:S(2)}, u32[]{:S(2)}) collective-permute-start(f32[16,128]{1,0:T(8,128)} %param.9), channel_id=1, source_target_pairs={{0,1},{1,0},{2,3},{3,2},{4,5},{5,4},{6,7},{7,6},{8,9},{9,8},{10,11... | collective-permute-start | bytes 24584 | tf_op jit(solution)/shard_map/ppermute | solution.py:178
  3.7 0.7 constant_dynamic-update-slice_fusion.1
  4.4 1.1 collective-permute-done
  5.5 4.1 %collective-permute-start.3 = (f32[32,128]{1,0:T(8,128)S(1)}, f32[32,128]{1,0:T(8,128)S(1)}, u32[]{:S(2)}, u32[]{:S(2)}) collective-permute-start(f32[32,128]{1,0:T(8,128)S(1)} %constant_dynamic-update-slice_fusion.rest_2_), channel_id=1, source_target_pairs={{0,6},{1,7},{2,4},{3,5},{4,2},{5,3},{6,0},{7,1},{8,14},{9,15},{10,... | collective-permute-start | bytes 49160 | tf_op jit(solution)/shard_map/ppermute | solution.py:178
  9.6 0.6 collective-permute-start.1
  10.8 4.8 %shard_map.69.rest_1_ = bf16[160,256,128]{2,1,0:T(8,128)(2,1)S(1)} custom-call(f32[320,128,128]{2,1,0:T(8,128)} %tiles.3), custom_call_target="tpu_custom_call" | custom-call | flops 10485760 | bytes 10485760 | tf_op jit(solution)/shard_map/pallas_call | solution.py:212
  15.6 4.8 %shard_map.68.rest_0_ = bf16[160,256,128]{2,1,0:T(8,128)(2,1)S(1)} custom-call(f32[320,128,128]{2,1,0:T(8,128)} %tiles.3), custom_call_target="tpu_custom_call" | custom-call | flops 10485760 | bytes 10485760 | tf_op jit(solution)/shard_map/pallas_call | solution.py:212
  20.5 2.7 %shard_map.70 = (f32[128,128]{1,0:T(8,128)S(1)}, f32[264,128]{1,0:T(8,128)S(1)}, f32[264,128]{1,0:T(8,128)S(1)}) custom-call(s32[320]{0:T(512)S(1)} %copy-done, s32[320]{0:T(512)S(1)} %copy-done.1, s32[1,1]{1,0:T(1,128)S(6)} %copy.10.counts, bf16[160,256,128]{2,1,0:T(8,128)(2,1)S(1)} %shard_map.68.rest_0_, bf16[160,256,128]{2,1,0:T(8,128)(2,1)S(1)} %shard_map.69.rest_1_, ...), custom_call_target="tpu_custom_call" | custom-call | tf_op jit(solution)/shard_map/pallas_call | solution.py:197
  23.3 1.3 collective-permute-done.4
  24.6 3.6 %collective-permute-start.5 = (f32[264,128]{1,0:T(8,128)S(1)}, f32[264,128]{1,0:T(8,128)S(1)}, u32[]{:S(2)}, u32[]{:S(2)}) collective-permute-start(f32[264,128]{1,0:T(8,128)S(1)} %add.58), channel_id=1, source_target_pairs={{0,16},{8,24},{16,0},{24,8},{1,17},{9,25},{17,1},{25,9},{2,18},{10... | collective-permute-start | bytes 405512 | tf_op jit(solution)/shard_map/ppermute | solution.py:178
  28.2 3.9 %collective-permute-done.5 = f32[264,128]{1,0:T(8,128)S(1)} collective-permute-done((f32[264,128]{1,0:T(8,128)S(1)}, f32[264,128]{1,0:T(8,128)S(1)}, u32[]{:S(2)}, u32[]{:S(2)}) %collective-permute-start.5) | collective-permute-done | bytes 135200 | tf_op jit(solution)/shard_map/ppermute | solution.py:178
  32.2 1.3 collective-permute-done.6.rest_3_
  33.5 3.8 %shard_map.71 = (f32[512,128]{1,0:T(8,128)S(1)}, f32[8,128]{1,0:T(8,128)S(1)}, f32[128,128]{1,0:T(8,128)S(1)}, f32[136,128]{1,0:T(8,128)S(1)}) custom-call(s32[320]{0:T(512)S(1)} %copy-done, s32[320]{0:T(512)S(1)} %copy-done.1, s32[1,1]{1,0:T(1,128)S(6)} %copy.10.counts, bf16[160,256,128]{2,1,0:T(8,128)(2,1)S(1)} %shard_map.68.rest_0_, ...), custom_call_target="tpu_custom_call" | custom-call | tf_op jit(solution)/shard_map/pallas_call | solution.py:197
  37.3 8.5 %collective-permute-start.7 = (f32[136,128]{1,0:T(8,128)S(1)}, f32[136,128]{1,0:T(8,128)S(1)}, u32[]{:S(2)}, u32[]{:S(2)}) collective-permute-start(f32[136,128]{1,0:T(8,128)S(1)} %get-tuple-element.22), channel_id=1, source_target_pairs={{0,1},{1,0},{2,3},{3,2},{4,5},{5,4},{6,7},{7,6},{8,9},{9,8},{10,11... | collective-permute-start | bytes 208904 | tf_op jit(solution)/shard_map/ppermute | solution.py:178
  45.8 2.3 %collective-permute-done.7 = f32[136,128]{1,0:T(8,128)S(1)} collective-permute-done((f32[136,128]{1,0:T(8,128)S(1)}, f32[136,128]{1,0:T(8,128)S(1)}, u32[]{:S(2)}, u32[]{:S(2)}) %collective-permute-start.7) | collective-permute-done | bytes 69664 | tf_op jit(solution)/shard_map/ppermute | solution.py:178
  48.1 5.0 %collective-permute-done.8 = f32[136,128]{1,0:T(8,128)S(1)} collective-permute-done((f32[136,128]{1,0:T(8,128)S(1)}, f32[136,128]{1,0:T(8,128)S(1)}, u32[]{:S(2)}, u32[]{:S(2)}) %collective-permute-start.8) | collective-permute-done | bytes 69664 | tf_op jit(solution)/shard_map/ppermute | solution.py:178
  53.2 1.6 %collective-permute-start.9 = (f32[136,128]{1,0:T(8,128)S(1)}, f32[136,128]{1,0:T(8,128)S(1)}, u32[]{:S(2)}, u32[]{:S(2)}) collective-permute-start(f32[136,128]{1,0:T(8,128)S(1)} %add.61.rest_2_), channel_id=1, source_target_pairs={{0,4},{1,5},{2,6},{3,7},{4,0},{5,1},{6,2},{7,3},{8,12},{9,13},{10,... | collective-permute-start | bytes 208904 | tf_op jit(solution)/shard_map/ppermute | solution.py:178
  54.7 3.7 %collective-permute-done.9.rest_3_ = f32[136,128]{1,0:T(8,128)S(1)} collective-permute-done((f32[136,128]{1,0:T(8,128)S(1)}, f32[136,128]{1,0:T(8,128)S(1)}, u32[]{:S(2)}, u32[]{:S(2)}) %collective-permute-start.9) | collective-permute-done | bytes 69664 | tf_op jit(solution)/shard_map/ppermute | solution.py:178
  58.5 2.7 %shard_map.72 = (f32[128,128]{1,0:T(8,128)S(1)}, f32[8,128]{1,0:T(8,128)S(1)}, f32[264,128]{1,0:T(8,128)S(1)}, f32[264,128]{1,0:T(8,128)S(1)}) custom-call(s32[320]{0:T(512)S(1)} %copy-done, s32[320]{0:T(512)S(1)} %copy-done.1, s32[1,1]{1,0:T(1,128)S(6)} %copy.10.counts, bf16[160,256,128]{2,1,0:T(8,128)(2,1)S(1)} %shard_map.68.rest_0_, ...), custom_call_target="tpu_custom_call" | custom-call | tf_op jit(solution)/shard_map/pallas_call | solution.py:197
  61.3 1.3 collective-permute-done.10
  62.6 2.3 %collective-permute-start.11 = (f32[264,128]{1,0:T(8,128)S(1)}, f32[264,128]{1,0:T(8,128)S(1)}, u32[]{:S(2)}, u32[]{:S(2)}) collective-permute-start(f32[264,128]{1,0:T(8,128)S(1)} %add.62), channel_id=1, source_target_pairs={{0,16},{8,24},{16,0},{24,8},{1,17},{9,25},{17,1},{25,9},{2,18},{10... | collective-permute-start | bytes 405512 | tf_op jit(solution)/shard_map/ppermute | solution.py:178
  64.9 3.9 %collective-permute-done.11 = f32[264,128]{1,0:T(8,128)S(1)} collective-permute-done((f32[264,128]{1,0:T(8,128)S(1)}, f32[264,128]{1,0:T(8,128)S(1)}, u32[]{:S(2)}, u32[]{:S(2)}) %collective-permute-start.11) | collective-permute-done | bytes 135200 | tf_op jit(solution)/shard_map/ppermute | solution.py:178
  68.9 1.3 collective-permute-done.12.rest_3_
  70.3 3.8 %shard_map.73 = (f32[512,128]{1,0:T(8,128)S(1)}, f32[8,128]{1,0:T(8,128)S(1)}, f32[128,128]{1,0:T(8,128)S(1)}, f32[136,128]{1,0:T(8,128)S(1)}) custom-call(s32[320]{0:T(512)S(1)} %copy-done, s32[320]{0:T(512)S(1)} %copy-done.1, s32[1,1]{1,0:T(1,128)S(6)} %copy.10.counts, bf16[160,256,128]{2,1,0:T(8,128)(2,1)S(1)} %shard_map.68.rest_0_, ...), custom_call_target="tpu_custom_call" | custom-call | tf_op jit(solution)/shard_map/pallas_call | solution.py:197
  74.1 9.8 %collective-permute-start.13 = (f32[136,128]{1,0:T(8,128)S(1)}, f32[136,128]{1,0:T(8,128)S(1)}, u32[]{:S(2)}, u32[]{:S(2)}) collective-permute-start(f32[136,128]{1,0:T(8,128)S(1)} %get-tuple-element.31), channel_id=1, source_target_pairs={{0,1},{1,0},{2,3},{3,2},{4,5},{5,4},{6,7},{7,6},{8,9},{9,8},{10,11... | collective-permute-start | bytes 208904 | tf_op jit(solution)/shard_map/ppermute | solution.py:178
  83.8 2.3 %collective-permute-done.13 = f32[136,128]{1,0:T(8,128)S(1)} collective-permute-done((f32[136,128]{1,0:T(8,128)S(1)}, f32[136,128]{1,0:T(8,128)S(1)}, u32[]{:S(2)}, u32[]{:S(2)}) %collective-permute-start.13) | collective-permute-done | bytes 69664 | tf_op jit(solution)/shard_map/ppermute | solution.py:178
  86.2 4.6 %collective-permute-done.14 = f32[136,128]{1,0:T(8,128)S(1)} collective-permute-done((f32[136,128]{1,0:T(8,128)S(1)}, f32[136,128]{1,0:T(8,128)S(1)}, u32[]{:S(2)}, u32[]{:S(2)}) %collective-permute-start.14) | collective-permute-done | bytes 69664 | tf_op jit(solution)/shard_map/ppermute | solution.py:178
  90.8 1.5 %collective-permute-start.15 = (f32[136,128]{1,0:T(8,128)S(1)}, f32[136,128]{1,0:T(8,128)S(1)}, u32[]{:S(2)}, u32[]{:S(2)}) collective-permute-start(f32[136,128]{1,0:T(8,128)S(1)} %add.66.rest_2_), channel_id=1, source_target_pairs={{0,4},{1,5},{2,6},{3,7},{4,0},{5,1},{6,2},{7,3},{8,12},{9,13},{10,... | collective-permute-start | bytes 208904 | tf_op jit(solution)/shard_map/ppermute | solution.py:178
  92.3 3.8 %collective-permute-done.15.rest_3_ = f32[136,128]{1,0:T(8,128)S(1)} collective-permute-done((f32[136,128]{1,0:T(8,128)S(1)}, f32[136,128]{1,0:T(8,128)S(1)}, u32[]{:S(2)}, u32[]{:S(2)}) %collective-permute-start.15) | collective-permute-done | bytes 69664 | tf_op jit(solution)/shard_map/ppermute | solution.py:178
  96.1 3.4 %shard_map.74 = (f32[128,128]{1,0:T(8,128)}, f32[8,128]{1,0:T(8,128)S(1)}, f32[264,128]{1,0:T(8,128)S(1)}, f32[264,128]{1,0:T(8,128)S(1)}) custom-call(s32[320]{0:T(512)S(1)} %copy-done, s32[320]{0:T(512)S(1)} %copy-done.1, s32[1,1]{1,0:T(1,128)S(6)} %copy.10.counts, bf16[160,256,128]{2,1,0:T(8,128)(2,1)S(1)} %shard_map.68.rest_0_, ...), custom_call_target="tpu_custom_call" | custom-call | tf_op jit(solution)/shard_map/pallas_call | solution.py:197
  99.4 1.4 collective-permute-done.16
  100.8 2.4 %collective-permute-start.17 = (f32[264,128]{1,0:T(8,128)S(1)}, f32[264,128]{1,0:T(8,128)S(1)}, u32[]{:S(2)}, u32[]{:S(2)}) collective-permute-start(f32[264,128]{1,0:T(8,128)S(1)} %add.67), channel_id=1, source_target_pairs={{0,16},{8,24},{16,0},{24,8},{1,17},{9,25},{17,1},{25,9},{2,18},{10... | collective-permute-start | bytes 405512 | tf_op jit(solution)/shard_map/ppermute | solution.py:178
  103.2 0.6 slice.24
  103.8 3.3 %collective-permute-done.17 = f32[264,128]{1,0:T(8,128)S(1)} collective-permute-done((f32[264,128]{1,0:T(8,128)S(1)}, f32[264,128]{1,0:T(8,128)S(1)}, u32[]{:S(2)}, u32[]{:S(2)}) %collective-permute-start.17) | collective-permute-done | bytes 135200 | tf_op jit(solution)/shard_map/ppermute | solution.py:178
  107.2 0.5 slice.28
  108.4 0.7 fusion.1
  109.1 0.7 multiply_reduce_fusion
  109.7 0.6 broadcast_in_dim.3
  110.5 1.2 collective-permute-done.18
  111.6 0.6 broadcast_add_fusion
  112.3 4.7 %collective-permute-start.19 = (f32[8,128]{1,0:T(8,128)S(1)}, f32[8,128]{1,0:T(8,128)S(1)}, u32[]{:S(2)}, u32[]{:S(2)}) collective-permute-start(f32[8,128]{1,0:T(8,128)S(1)} %broadcast_add_fusion), channel_id=1, source_target_pairs={{0,1},{1,0},{2,3},{3,2},{4,5},{5,4},{6,7},{7,6},{8,9},{9,8},{10,11... | collective-permute-start | bytes 12296 | tf_op jit(solution)/shard_map/ppermute | solution.py:178
  117.0 1.6 %collective-permute-done.19 = f32[8,128]{1,0:T(8,128)S(1)} collective-permute-done((f32[8,128]{1,0:T(8,128)S(1)}, f32[8,128]{1,0:T(8,128)S(1)}, u32[]{:S(2)}, u32[]{:S(2)}) %collective-permute-start.19) | collective-permute-done | bytes 4128 | tf_op jit(solution)/shard_map/ppermute | solution.py:178
  118.5 0.6 fusion.3
  119.6 3.3 %collective-permute-done.20 = f32[8,128]{1,0:T(8,128)S(1)} collective-permute-done((f32[8,128]{1,0:T(8,128)S(1)}, f32[8,128]{1,0:T(8,128)S(1)}, u32[]{:S(2)}, u32[]{:S(2)}) %collective-permute-start.20) | collective-permute-done | bytes 4128 | tf_op jit(solution)/shard_map/ppermute | solution.py:178
  122.9 1.6 %collective-permute-start.21 = (f32[8,128]{1,0:T(8,128)S(1)}, f32[8,128]{1,0:T(8,128)S(1)}, u32[]{:S(2)}, u32[]{:S(2)}) collective-permute-start(f32[8,128]{1,0:T(8,128)S(1)} %add.75), channel_id=1, source_target_pairs={{0,4},{1,5},{2,6},{3,7},{4,0},{5,1},{6,2},{7,3},{8,12},{9,13},{10,... | collective-permute-start | bytes 12296 | tf_op jit(solution)/shard_map/ppermute | solution.py:178
  124.5 0.5 slice.23
  125.0 0.5 slice.21
  134.1 2.0 %multiply_subtract_fusion = (f32[128,128]{1,0:T(8,128)}, f32[128,128]{1,0:T(8,128)}) fusion(f32[256,128]{1,0:T(8,128)S(1)} %get-tuple-element.39, s32[]{:T(128)S(6)} %select_n.8, f32[]{:T(128)S(6)} %div.85, f32[]{:T(128)} %bitcast.7, f32[128,128]{1,0:T(8,128)S(1)} %get-tuple-element.30, f32[]{:T(128)} %bitcast, f32[]{:T(128)S(6)} %div.73, ...), kind=kLoop, calls=%fused_computation.5 | loop fusion | flops 163840 | bytes 327712 | tf_op jit(solution)/shard_map/sub | solution.py:303
  (33 shorter events, 2.1 us)
Async XLA Ops:
  0.6 4.9 %collective-permute-start = (f32[16,128]{1,0:T(8,128)}, f32[16,128]{1,0:T(8,128)S(1)}, u32[]{:S(2)}, u32[]{:S(2)}) collective-permute-start(f32[16,128]{1,0:T(8,128)} %param.9), channel_id=1, source_target_pairs={{0,1},{1,0},{2,3},{3,2},{4,5},{5,4},{6,7},{7,6},{8,9},{9,8},{10,11... | collective-permute-start | bytes 24584 | tf_op jit(solution)/shard_map/ppermute | solution.py:178
  5.5 14.9 %collective-permute-start.3 = (f32[32,128]{1,0:T(8,128)S(1)}, f32[32,128]{1,0:T(8,128)S(1)}, u32[]{:S(2)}, u32[]{:S(2)}) collective-permute-start(f32[32,128]{1,0:T(8,128)S(1)} %constant_dynamic-update-slice_fusion.rest_2_), channel_id=1, source_target_pairs={{0,6},{1,7},{2,4},{3,5},{4,2},{5,3},{6,0},{7,1},{8,14},{9,15},{10,... | collective-permute-start | bytes 49160 | tf_op jit(solution)/shard_map/ppermute | solution.py:178
  9.6 10.8 %collective-permute-start.2 = (f32[32,128]{1,0:T(8,128)S(1)}, f32[32,128]{1,0:T(8,128)S(1)}, u32[]{:S(2)}, u32[]{:S(2)}) collective-permute-start(f32[32,128]{1,0:T(8,128)S(1)} %constant_dynamic-update-slice_fusion.rest_2_), channel_id=1, source_target_pairs={{0,4},{1,5},{2,6},{3,7},{4,0},{5,1},{6,2},{7,3},{8,12},{9,13},{10,... | collective-permute-start | bytes 49160 | tf_op jit(solution)/shard_map/ppermute | solution.py:178
  9.6 10.8 %collective-permute-start.1 = (f32[32,128]{1,0:T(8,128)S(1)}, f32[32,128]{1,0:T(8,128)S(1)}, u32[]{:S(2)}, u32[]{:S(2)}) collective-permute-start(f32[32,128]{1,0:T(8,128)S(1)} %constant_dynamic-update-slice_fusion.rest_2_), channel_id=1, source_target_pairs={{0,2},{1,3},{2,0},{3,1},{4,6},{5,7},{6,4},{7,5},{8,10},{9,11},{10,... | collective-permute-start | bytes 49160 | tf_op jit(solution)/shard_map/ppermute | solution.py:178
  15.6 4.8 %copy-start = (s32[320]{0:T(512)S(1)}, s32[320]{0:T(512)}, u32[]{:S(2)}) copy-start(s32[320]{0:T(512)} %pick.9) | copy-start | bytes 3844
  15.6 4.8 %copy-start.1 = (s32[320]{0:T(512)S(1)}, s32[320]{0:T(512)}, u32[]{:S(2)}) copy-start(s32[320]{0:T(512)} %cell.9) | copy-start | bytes 3844
  23.2 1.4 %collective-permute-start.4 = (f32[264,128]{1,0:T(8,128)S(1)}, f32[264,128]{1,0:T(8,128)S(1)}, u32[]{:S(2)}, u32[]{:S(2)}) collective-permute-start(f32[264,128]{1,0:T(8,128)S(1)} %get-tuple-element.21), channel_id=1, source_target_pairs={{0,8},{8,0},{16,24},{24,16},{1,9},{9,1},{17,25},{25,17},{2,10},{10... | collective-permute-start | bytes 405512 | tf_op jit(solution)/shard_map/ppermute | solution.py:178
  24.6 7.5 %collective-permute-start.5 = (f32[264,128]{1,0:T(8,128)S(1)}, f32[264,128]{1,0:T(8,128)S(1)}, u32[]{:S(2)}, u32[]{:S(2)}) collective-permute-start(f32[264,128]{1,0:T(8,128)S(1)} %add.58), channel_id=1, source_target_pairs={{0,16},{8,24},{16,0},{24,8},{1,17},{9,25},{17,1},{25,9},{2,18},{10... | collective-permute-start | bytes 405512 | tf_op jit(solution)/shard_map/ppermute | solution.py:178
  32.1 1.4 %collective-permute-start.6 = (f32[264,128]{1,0:T(8,128)S(1)}, f32[264,128]{1,0:T(8,128)S(1)}, u32[]{:S(2)}, u32[]{:S(2)}) collective-permute-start(f32[264,128]{1,0:T(8,128)S(1)} %add.59.rest_2_), channel_id=1, source_target_pairs={{0,8},{8,0},{16,24},{24,16},{1,9},{9,1},{17,25},{25,17},{2,10},{10... | collective-permute-start | bytes 405512 | tf_op jit(solution)/shard_map/ppermute | solution.py:178
  37.3 10.7 %collective-permute-start.7 = (f32[136,128]{1,0:T(8,128)S(1)}, f32[136,128]{1,0:T(8,128)S(1)}, u32[]{:S(2)}, u32[]{:S(2)}) collective-permute-start(f32[136,128]{1,0:T(8,128)S(1)} %get-tuple-element.22), channel_id=1, source_target_pairs={{0,1},{1,0},{2,3},{3,2},{4,5},{5,4},{6,7},{7,6},{8,9},{9,8},{10,11... | collective-permute-start | bytes 208904 | tf_op jit(solution)/shard_map/ppermute | solution.py:178
  48.1 5.1 %collective-permute-start.8 = (f32[136,128]{1,0:T(8,128)S(1)}, f32[136,128]{1,0:T(8,128)S(1)}, u32[]{:S(2)}, u32[]{:S(2)}) collective-permute-start(f32[136,128]{1,0:T(8,128)S(1)} %add.60), channel_id=1, source_target_pairs={{0,2},{1,3},{2,0},{3,1},{4,6},{5,7},{6,4},{7,5},{8,10},{9,11},{10,... | collective-permute-start | bytes 208904 | tf_op jit(solution)/shard_map/ppermute | solution.py:178
  53.2 5.3 %collective-permute-start.9 = (f32[136,128]{1,0:T(8,128)S(1)}, f32[136,128]{1,0:T(8,128)S(1)}, u32[]{:S(2)}, u32[]{:S(2)}) collective-permute-start(f32[136,128]{1,0:T(8,128)S(1)} %add.61.rest_2_), channel_id=1, source_target_pairs={{0,4},{1,5},{2,6},{3,7},{4,0},{5,1},{6,2},{7,3},{8,12},{9,13},{10,... | collective-permute-start | bytes 208904 | tf_op jit(solution)/shard_map/ppermute | solution.py:178
  61.2 1.4 %collective-permute-start.10 = (f32[264,128]{1,0:T(8,128)S(1)}, f32[264,128]{1,0:T(8,128)S(1)}, u32[]{:S(2)}, u32[]{:S(2)}) collective-permute-start(f32[264,128]{1,0:T(8,128)S(1)} %get-tuple-element.27), channel_id=1, source_target_pairs={{0,8},{8,0},{16,24},{24,16},{1,9},{9,1},{17,25},{25,17},{2,10},{10... | collective-permute-start | bytes 405512 | tf_op jit(solution)/shard_map/ppermute | solution.py:178
  62.6 6.2 %collective-permute-start.11 = (f32[264,128]{1,0:T(8,128)S(1)}, f32[264,128]{1,0:T(8,128)S(1)}, u32[]{:S(2)}, u32[]{:S(2)}) collective-permute-start(f32[264,128]{1,0:T(8,128)S(1)} %add.62), channel_id=1, source_target_pairs={{0,16},{8,24},{16,0},{24,8},{1,17},{9,25},{17,1},{25,9},{2,18},{10... | collective-permute-start | bytes 405512 | tf_op jit(solution)/shard_map/ppermute | solution.py:178
  68.8 1.4 %collective-permute-start.12 = (f32[264,128]{1,0:T(8,128)S(1)}, f32[264,128]{1,0:T(8,128)S(1)}, u32[]{:S(2)}, u32[]{:S(2)}) collective-permute-start(f32[264,128]{1,0:T(8,128)S(1)} %add.63.rest_2_), channel_id=1, source_target_pairs={{0,8},{8,0},{16,24},{24,16},{1,9},{9,1},{17,25},{25,17},{2,10},{10... | collective-permute-start | bytes 405512 | tf_op jit(solution)/shard_map/ppermute | solution.py:178
  74.1 12.1 %collective-permute-start.13 = (f32[136,128]{1,0:T(8,128)S(1)}, f32[136,128]{1,0:T(8,128)S(1)}, u32[]{:S(2)}, u32[]{:S(2)}) collective-permute-start(f32[136,128]{1,0:T(8,128)S(1)} %get-tuple-element.31), channel_id=1, source_target_pairs={{0,1},{1,0},{2,3},{3,2},{4,5},{5,4},{6,7},{7,6},{8,9},{9,8},{10,11... | collective-permute-start | bytes 208904 | tf_op jit(solution)/shard_map/ppermute | solution.py:178
  86.1 4.7 %collective-permute-start.14 = (f32[136,128]{1,0:T(8,128)S(1)}, f32[136,128]{1,0:T(8,128)S(1)}, u32[]{:S(2)}, u32[]{:S(2)}) collective-permute-start(f32[136,128]{1,0:T(8,128)S(1)} %add.65), channel_id=1, source_target_pairs={{0,2},{1,3},{2,0},{3,1},{4,6},{5,7},{6,4},{7,5},{8,10},{9,11},{10,... | collective-permute-start | bytes 208904 | tf_op jit(solution)/shard_map/ppermute | solution.py:178
  90.8 5.3 %collective-permute-start.15 = (f32[136,128]{1,0:T(8,128)S(1)}, f32[136,128]{1,0:T(8,128)S(1)}, u32[]{:S(2)}, u32[]{:S(2)}) collective-permute-start(f32[136,128]{1,0:T(8,128)S(1)} %add.66.rest_2_), channel_id=1, source_target_pairs={{0,4},{1,5},{2,6},{3,7},{4,0},{5,1},{6,2},{7,3},{8,12},{9,13},{10,... | collective-permute-start | bytes 208904 | tf_op jit(solution)/shard_map/ppermute | solution.py:178
  99.4 1.4 collective-permute-start.16
  100.8 6.3 %collective-permute-start.17 = (f32[264,128]{1,0:T(8,128)S(1)}, f32[264,128]{1,0:T(8,128)S(1)}, u32[]{:S(2)}, u32[]{:S(2)}) collective-permute-start(f32[264,128]{1,0:T(8,128)S(1)} %add.67), channel_id=1, source_target_pairs={{0,16},{8,24},{16,0},{24,8},{1,17},{9,25},{17,1},{25,9},{2,18},{10... | collective-permute-start | bytes 405512 | tf_op jit(solution)/shard_map/ppermute | solution.py:178
  110.4 1.2 collective-permute-start.18
  112.3 6.3 %collective-permute-start.19 = (f32[8,128]{1,0:T(8,128)S(1)}, f32[8,128]{1,0:T(8,128)S(1)}, u32[]{:S(2)}, u32[]{:S(2)}) collective-permute-start(f32[8,128]{1,0:T(8,128)S(1)} %broadcast_add_fusion), channel_id=1, source_target_pairs={{0,1},{1,0},{2,3},{3,2},{4,5},{5,4},{6,7},{7,6},{8,9},{9,8},{10,11... | collective-permute-start | bytes 12296 | tf_op jit(solution)/shard_map/ppermute | solution.py:178
  119.2 3.7 %collective-permute-start.20 = (f32[8,128]{1,0:T(8,128)S(1)}, f32[8,128]{1,0:T(8,128)S(1)}, u32[]{:S(2)}, u32[]{:S(2)}) collective-permute-start(f32[8,128]{1,0:T(8,128)S(1)} %fusion.3), channel_id=1, source_target_pairs={{0,2},{1,3},{2,0},{3,1},{4,6},{5,7},{6,4},{7,5},{8,10},{9,11},{10,... | collective-permute-start | bytes 12296 | tf_op jit(solution)/shard_map/ppermute | solution.py:178
  122.9 9.9 %collective-permute-start.21 = (f32[8,128]{1,0:T(8,128)S(1)}, f32[8,128]{1,0:T(8,128)S(1)}, u32[]{:S(2)}, u32[]{:S(2)}) collective-permute-start(f32[8,128]{1,0:T(8,128)S(1)} %add.75), channel_id=1, source_target_pairs={{0,4},{1,5},{2,6},{3,7},{4,0},{5,1},{6,2},{7,3},{8,12},{9,13},{10,... | collective-permute-start | bytes 12296 | tf_op jit(solution)/shard_map/ppermute | solution.py:178

commit v3 on v2

v3 whole, which is shorter than its diff:
```python
import functools

import jax
import jax.numpy as jnp
from jax import lax
from jax.experimental import pallas as pl
from jax.experimental.pallas import tpu as pltpu
from jax.sharding import PartitionSpec as P

PBLK = 128
CBLK = 512
ITERS = 2
B = 128
SUB = 8
GROUP = 16
PARTS = 2
STEP = 16
BUFFERS = 4
TAIL = 8


def split(value):
    high = value.astype(jnp.bfloat16)
    return high, (value - high.astype(jnp.float32)).astype(jnp.bfloat16)


def split_tiles(start, tiles, data, out, data_out, held, arrived):
    steps = out.shape[0] // STEP
    data_out[...] = data[...]

    def copy(step, slot):
        return pltpu.make_async_copy(
            tiles.at[pl.ds(start + step * STEP, STEP)], held.at[slot], arrived.at[slot]
        )

    for step in range(min(BUFFERS - 1, steps)):
        copy(step, step).start()
    for step in range(steps):
        slot = step % BUFFERS
        ahead = step + BUFFERS - 1
        if ahead < steps:
            copy(ahead, ahead % BUFFERS).start()
        copy(step, slot).wait()

        def one(k, carry):
            high, low = split(held[slot, k])
            out[step * STEP + k, :B, :] = high
            out[step * STEP + k, B:, :] = low
            return carry

        lax.fori_loop(0, STEP, one, 0, unroll=4)


def rows_of(ref, start, blocks):
    return ref.at[pl.ds(start, blocks, stride=SUB), :]


def fill_table(table, value):
    high, low = split(value)
    blocks = value.shape[0]
    for start, term in enumerate((high, low, high, low)):
        rows_of(table, start, blocks)[...] = term.astype(jnp.float32)


def block_at(index):
    return pl.ds(pl.multiple_of(index * SUB, SUB), SUB)


def pair_transposed(tiles, one, two, first):
    row = jnp.where(first, one, two).astype(jnp.bfloat16)
    row = jnp.concatenate([row, row], axis=1)
    both = jnp.dot(row, tiles, preferred_element_type=jnp.float32)
    return both[:, :B], both[:, B:]


def pair_forward(tiles, one, two, first):
    zero = jnp.zeros_like(one)
    row = jnp.concatenate([jnp.where(first, one, zero), jnp.where(first, zero, two)], axis=1)
    both = lax.dot_general(
        row.astype(jnp.bfloat16),
        tiles,
        (((1,), (1,)), ((), ())),
        preferred_element_type=jnp.float32,
    )
    both = both[:, :B] + both[:, B:]
    return both, both


def over_tiles(parts, live, product, table, source, target, blocks, accs):
    places = [(accs[0], 0), (accs[0], 1), (accs[1], 2), (accs[1], 3)]
    for acc, start in places:
        rows_of(acc, start, blocks)[...] = jnp.zeros((blocks, B), jnp.float32)
    upper = lax.broadcasted_iota(jnp.int32, (SUB, B), 0) < 2
    first = 0
    for tiles in parts:
        size = tiles.shape[0]
        here = jnp.clip(live - first, 0, size)

        def some(group, carry, tiles=tiles, first=first):
            base = group * GROUP
            sums = []
            for k in range(0, GROUP, 2):
                slot = first + base + k
                pair = jnp.concatenate([tiles[base + k], tiles[base + k + 1]], axis=1)
                one, two = (table[block_at(source[slot + n]), :] for n in range(2))
                sums.append(product(pair, one, two, upper))
            for k in range(GROUP):
                slot = first + base + k
                place = block_at(jnp.where(slot < live, target[slot], blocks))
                accs[k % 2][place, :] += sums[k // 2][k % 2]
            return carry

        lax.fori_loop(0, (here + GROUP - 1) // GROUP, some, 0)
        first += size
    return sum(rows_of(acc, start, blocks)[...] for acc, start in places)


def halves(n_rows, cells):
    size = cells // n_rows
    return size, [range(core, n_rows, 2) for core in range(2)]


def adjoint_tail(n_rows, parts, pick, cell, counts, u, keep, send, table, *accs):
    fill_table(table, u)
    whole = over_tiles(parts, counts[0, 0], pair_transposed, table, pick, cell, CBLK, accs)
    square = jnp.full((TAIL, B), jnp.sum(u * u))
    size, _ = halves(n_rows, CBLK)
    core = lax.rem(lax.axis_index("rows"), 2)
    for block in range(n_rows):
        part = whole[block * size : (block + 1) * size]
        place = pl.ds(block // 2 * size, size)

        @pl.when(core == block % 2)
        def _():
            keep[place, :] = part

        @pl.when(core != block % 2)
        def _():
            send[place, :] = part

    keep[pl.ds(CBLK // 2, TAIL), :] = square
    send[pl.ds(CBLK // 2, TAIL), :] = square


def first_adjoint(n_rows, n_cols, pick, cell, counts, *rest):
    parts, pieces, (u_out, keep, send, table, *accs) = rest[:PARTS], rest[PARTS:-6], rest[-6:]
    me = lax.axis_index("cols")
    offset = 0
    for piece in pieces:
        rows = PBLK // n_cols
        for at in range(piece.shape[0] // rows):
            owner = jnp.bitwise_xor(me, offset)
            u_out[pl.ds(pl.multiple_of(owner * rows, rows), rows), :] = piece[pl.ds(at * rows, rows), :]
            offset += 1
    adjoint_tail(n_rows, parts, pick, cell, counts, u_out[...], keep, send, table, *accs)


def next_adjoint(n_rows, pick, cell, counts, *rest):
    parts = rest[:PARTS]
    mine, other, u_old, beta_old, u_out, alpha_out, keep, send, table, *accs = rest[PARTS:]
    total = mine[...] + other[...]
    alpha = jnp.sqrt(total[PBLK:])
    alpha_out[...] = alpha
    u = total[:PBLK] / alpha[:1] - alpha[:1] * (u_old[...] / beta_old[:1])
    u_out[...] = u
    adjoint_tail(n_rows, parts, pick, cell, counts, u, keep, send, table, *accs)


def cell_vector(n_rows, mine, other, v_old, alpha_old, v_out, beta_out, own_out):
    size, _ = halves(n_rows, CBLK)
    me = lax.axis_index("rows")
    core = lax.rem(me, 2)
    beta = jnp.sqrt(mine[pl.ds(CBLK // 2, TAIL), :])
    beta_out[...] = beta
    for block in range(n_rows):
        place = pl.ds(block // 2 * size, size)
        part = jnp.where(core == block % 2, mine[place, :], other[place, :]) / beta[:1]
        here = pl.ds(block * size, size)
        if v_old is not None:
            part = part - beta[:1] * (v_old[here, :] / alpha_old[:1])
        v_out[here, :] = part
    own_out[...] = v_out[pl.ds(pl.multiple_of(me * size, size), size), :]
    v = v_out[...]
    return v, jnp.full((TAIL, B), jnp.sum(v * v))


def forward(first, n_rows, pick, cell, counts, *rest):
    parts, rest = rest[:PARTS], rest[PARTS:]
    old = (None, None) if first else rest[2:4]
    v_out, beta_out, own_out, out, table, *accs = rest[-7:]
    v, square = cell_vector(n_rows, rest[0], rest[1], *old, v_out, beta_out, own_out)
    fill_table(table, v)
    out[:PBLK, :] = over_tiles(parts, counts[0, 0], pair_forward, table, cell, pick, PBLK, accs)
    out[pl.ds(PBLK, TAIL), :] = square


def last_vector(n_rows, mine, other, v_old, alpha_old, v_out, beta_out, own_out, square_out):
    _, square_out[...] = cell_vector(
        n_rows, mine, other, v_old, alpha_old, v_out, beta_out, own_out
    )


def finish(*refs):
    blocks, refs = refs[: ITERS + 1], refs[ITERS + 1 :]
    betas, refs = refs[: ITERS + 1], refs[ITERS + 1 :]
    alphas, refs = refs[:ITERS], refs[ITERS:]
    squares, (model_out, search_out) = refs[:-2], refs[-2:]
    betas = [ref[:1] for ref in betas]
    alphas = [ref[:1] for ref in alphas] + [jnp.sqrt(sum(ref[:1] for ref in squares))]
    phibar, rhobar = betas[0], alphas[0]
    search = blocks[0][...] / alphas[0]
    model = jnp.zeros_like(search)
    for step in range(ITERS):
        beta, alpha = betas[step + 1], alphas[step + 1]
        rho = jnp.sqrt(rhobar * rhobar + beta * beta)
        cosine = rhobar / rho
        sine = beta / rho
        theta = sine * alpha
        rhobar = -cosine * alpha
        phi = cosine * phibar
        phibar = sine * phibar
        model = model + phi / rho * search
        search = blocks[step + 1][...] / alpha - theta / rho * search
    model_out[...] = model
    search_out[...] = search


def swapped(block, axis, size, bit):
    return lax.ppermute(block, axis, [(i, i ^ bit) for i in range(size)])


def shape(*dims):
    return jax.ShapeDtypeStruct(dims, jnp.float32)


VECTOR = pl.BlockSpec(memory_space=pltpu.VMEM)
SCALAR = pl.BlockSpec(memory_space=pltpu.SMEM)


def call(kernel, outs, sources, targets, scalars, arrays):
    return pl.pallas_call(
        kernel,
        out_shape=outs,
        in_specs=[SCALAR] * len(scalars) + [VECTOR] * len(arrays),
        out_specs=[VECTOR] * len(outs),
        scratch_shapes=[
            pltpu.VMEM((sources * SUB, B), jnp.float32),
            pltpu.VMEM(((targets + 1) * SUB, B), jnp.float32),
            pltpu.VMEM(((targets + 1) * SUB, B), jnp.float32),
        ],
        compiler_params=pltpu.CompilerParams(vmem_limit_bytes=24 << 20),
    )(*scalars, *arrays)


def split_part(kernels, data, part):
    size = kernels.shape[0] // PARTS
    return pl.pallas_call(
        functools.partial(split_tiles, part * size),
        out_shape=[pltpu.VMEM((size, 2 * B, B), jnp.bfloat16), shape(*data.shape)],
        in_specs=[pl.BlockSpec(memory_space=pl.ANY), VECTOR],
        out_specs=[VECTOR, VECTOR],
        scratch_shapes=[
            pltpu.VMEM((BUFFERS, STEP, B, B), jnp.float32),
            pltpu.SemaphoreType.DMA((BUFFERS,)),
        ],
        cost_estimate=pl.CostEstimate(
            flops=4 * size * B * B, bytes_accessed=4 * size * B * B, transcendentals=0
        ),
        compiler_params=pltpu.CompilerParams(vmem_limit_bytes=24 << 20),
    )(kernels, data)


def simple_call(kernel, outs, arrays):
    return pl.pallas_call(
        kernel,
        out_shape=outs,
        in_specs=[VECTOR] * len(arrays),
        out_specs=[VECTOR] * len(outs),
    )(*arrays)


def per_device(n_rows, n_cols, kernels, pick_index, cell_index, counts, data):
    scalars = (pick_index, cell_index, counts)
    half = CBLK // 2 + TAIL
    own = CBLK // n_rows

    def sum_cells(keep, send):
        mine = keep + swapped(send, "rows", n_rows, 1)
        bit = 2
        while bit < n_rows:
            mine = mine + swapped(mine, "rows", n_rows, bit)
            bit *= 2
        return [mine, swapped(mine, "rows", n_rows, 1)]

    partner = swapped(data, "cols", n_cols, 1)
    tiles = [None] * PARTS
    tiles[0], passed = split_part(kernels, data, 0)
    for part in range(1, PARTS):
        tiles[part], _ = split_part(kernels, data, part)
    pair = jnp.concatenate([passed, partner], axis=0)
    pieces = [pair] + [swapped(pair, "cols", n_cols, bit) for bit in range(2, n_cols, 2)]
    upick, keep, send = call(
        functools.partial(first_adjoint, n_rows, n_cols),
        [shape(PBLK, B), shape(half, B), shape(half, B)],
        PBLK,
        CBLK,
        scalars,
        tiles + pieces,
    )
    old = []
    blocks, alphas, betas = [], [], []
    for step in range(ITERS):
        vcell, beta, block, product = call(
            functools.partial(forward, step == 0, n_rows),
            [shape(CBLK, B), shape(TAIL, B), shape(own, B), shape(PBLK + TAIL, B)],
            CBLK,
            PBLK,
            scalars,
            tiles + sum_cells(keep, send) + old,
        )
        blocks.append(block)
        betas.append(beta)
        bit = 1
        while 2 * bit < n_cols:
            product = product + swapped(product, "cols", n_cols, bit)
            bit *= 2
        upick, alpha, keep, send = call(
            functools.partial(next_adjoint, n_rows),
            [shape(PBLK, B), shape(TAIL, B), shape(half, B), shape(half, B)],
            PBLK,
            CBLK,
            scalars,
            tiles + [product, swapped(product, "cols", n_cols, bit), upick, beta],
        )
        alphas.append(alpha)
        old = [vcell, alpha]
    _, beta, block, square = simple_call(
        functools.partial(last_vector, n_rows),
        [shape(CBLK, B), shape(TAIL, B), shape(own, B), shape(TAIL, B)],
        sum_cells(keep, send) + old,
    )
    blocks.append(block)
    betas.append(beta)
    square = square + swapped(square, "cols", n_cols, 1)
    squares = [square] + [swapped(square, "cols", n_cols, bit) for bit in range(2, n_cols, 2)]
    model, search = simple_call(
        finish, [shape(own, B), shape(own, B)], blocks + betas + alphas + squares
    )
    return (model, search)


def solution(mesh):
    def run(*args):
        return per_device(mesh.shape["rows"], mesh.shape["cols"], *args)

    return jax.shard_map(
        run,
        mesh=mesh,
        in_specs=(
            P(("rows", "cols"), None, None),
            P(("rows", "cols")),
            P(("rows", "cols")),
            P("rows", "cols"),
            P("cols", "rows"),
        ),
        out_specs=(P("rows", "cols"), P("rows", "cols")),
        check_vma=False,
    )
```

time: 137 us -> 129 us (0.942)
  Pallas kernels: 25.9 us -> 46.2 us
  starting transfers between devices: 44.4 us -> 27.7 us
  between operations: 9.71 us -> 1.62 us
  other arithmetic: 4.81 us -> 0.84 us
  waiting for transfers between devices: 46.7 us -> 49.3 us
  local copies, waits for them, and re-layouts: 4.6 us -> 2.01 us
    ppermute x22 -> x23, starting transfers between devices: 44.4 us -> 27.7 us  [swapped(): return lax.ppermute(block, axis, [(i, i ^ bit) for i in range(size)])]
    pallas_call x5, Pallas kernels: 16.4 us -> 32.6 us  [call(): pl.pallas_call(kernel, out_shape=outs, in_specs=[SCALAR] * len(scalars) +...]
    pallas_call x2 -> x4, Pallas kernels: 9.54 us -> 13.6 us  [the longest x2 10 us: split_part(): pl.pallas_call(functools.partial(split_tiles, part * size), out_shape=[pl...]
    slice x6 -> x0, local copies, waits for them, and re-layouts: 3.21 us -> none  [the longest x2 1.12 us: per_device(): alphas.append(alpha[0, 0])]
    ppermute x22 -> x23, waiting for transfers between devices: 46.7 us -> 49.3 us  [swapped(): return lax.ppermute(block, axis, [(i, i ^ bit) for i in range(size)])]
    sub x1 -> x0, other arithmetic: 2 us -> none  [per_device(): search = blocks[step + 1] / alpha - theta / rho * search]
  transfers between devices with their start and end apart: 22 -> 23, of which waited for: 18 -> 18; matrix products, arithmetic and copies ran while one was open for 2% -> 0% of each run, Pallas kernels for 7% -> 8%
where the time goes in v3:
time: 129 us; the launch traced here: 128 us
  waiting for transfers between devices  49.3 us (38%)
  Pallas kernels  46.2 us (36%)
  starting transfers between devices  27.7 us (21%)
  local copies, waits for them, and re-layouts  2.01 us (2%)
  between operations  1.62 us (1%)
    ppermute x23, waiting for transfers between devices, swapped(): return lax.ppermute(block, axis, [(i, i ^ bit) for i in range(size)])  49.3 us
    pallas_call x5, Pallas kernels, call(): pl.pallas_call(kernel, out_shape=outs, in_specs=[SCALAR] * len(scalars) +...  32.6 us
    ppermute x23, starting transfers between devices, swapped(): return lax.ppermute(block, axis, [(i, i ^ bit) for i in range(size)])  27.7 us
    pallas_call x2, Pallas kernels, split_part(): pl.pallas_call(functools.partial(split_tiles, part * size), out_shape=[pl...  10 us
    pallas_call x2, Pallas kernels, simple_call(): pl.pallas_call(kernel, out_shape=outs, in_specs=[VECTOR] * len(arrays), o...  3.57 us
  transfers between devices with their start and end apart: 23, of which 18 were waited for; matrix products, arithmetic and copies ran while one was open for 0% of the time, Pallas kernels for 8%

profile of v3, /device:TPU:0, one launch (start us, length us, event | category | flops | bytes accessed | tf_op | source)
XLA Modules:
  0.0 127.6 jit_solution(18342637471965065559)
XLA Ops:
  0.6 3.0 %collective-permute-start = (f32[16,128]{1,0:T(8,128)}, f32[16,128]{1,0:T(8,128)S(1)}, u32[]{:S(2)}, u32[]{:S(2)}) collective-permute-start(f32[16,128]{1,0:T(8,128)} %data.3), channel_id=1, source_target_pairs={{0,1},{1,0},{2,3},{3,2},{4,5},{5,4},{6,7},{7,6},{8,9},{9,8},{10,11... | collective-permute-start | bytes 24584 | tf_op jit(solution)/shard_map/ppermute | solution.py:229
  3.7 0.7 copy-done.5
  4.4 4.7 %shard_map.68 = (bf16[160,256,128]{2,1,0:T(8,128)(2,1)S(1)}, f32[16,128]{1,0:T(8,128)S(1)}) custom-call(f32[320,128,128]{2,1,0:T(8,128)} %tiles.3, f32[16,128]{1,0:T(8,128)S(1)} %copy-done.5), custom_call_target="tpu_custom_call" | custom-call | flops 10485760 | bytes 10485760 | tf_op jit(solution)/shard_map/pallas_call | solution.py:257
  9.1 3.7 %collective-permute-start.3 = (f32[32,128]{1,0:T(8,128)S(1)}, f32[32,128]{1,0:T(8,128)S(1)}, u32[]{:S(2)}, u32[]{:S(2)}) collective-permute-start(f32[32,128]{1,0:T(8,128)S(1)} %constant_dynamic-update-slice_fusion.rest_2_), channel_id=1, source_target_pairs={{0,6},{1,7},{2,4},{3,5},{4,2},{5,3},{6,0},{7,1},{8,14},{9,15},{10,... | collective-permute-start | bytes 49160 | tf_op jit(solution)/shard_map/ppermute | solution.py:229
  12.8 0.8 collective-permute-start.1
  14.3 5.3 %shard_map.69 = (bf16[160,256,128]{2,1,0:T(8,128)(2,1)S(1)}, f32[16,128]{1,0:T(8,128)}) custom-call(f32[320,128,128]{2,1,0:T(8,128)} %tiles.3, f32[16,128]{1,0:T(8,128)S(1)} %copy-done.5), custom_call_target="tpu_custom_call" | custom-call | flops 10485760 | bytes 10485760 | tf_op jit(solution)/shard_map/pallas_call | solution.py:257
  19.6 5.5 %shard_map.70 = (f32[128,128]{1,0:T(8,128)S(1)}, f32[264,128]{1,0:T(8,128)S(1)}, f32[264,128]{1,0:T(8,128)S(1)}) custom-call(s32[320]{0:T(512)S(1)} %copy-done.3, s32[320]{0:T(512)S(1)} %copy-done.4, s32[1,1]{1,0:T(1,128)S(6)} %copy.8.counts, bf16[160,256,128]{2,1,0:T(8,128)(2,1)S(1)} %get-tuple-element.26.rest_0_, ...), custom_call_target="tpu_custom_call" | custom-call | tf_op jit(solution)/shard_map/pallas_call | solution.py:241
  25.1 0.1 collective-permute-start.4
  25.2 1.3 %collective-permute-done.4 = f32[264,128]{1,0:T(8,128)S(1)} collective-permute-done((f32[264,128]{1,0:T(8,128)S(1)}, f32[264,128]{1,0:T(8,128)S(1)}, u32[]{:S(2)}, u32[]{:S(2)}) %collective-permute-start.4) | collective-permute-done | bytes 135200 | tf_op jit(solution)/shard_map/ppermute | solution.py:229
  26.6 1.0 collective-permute-start.5
  27.6 4.7 %collective-permute-done.5 = f32[264,128]{1,0:T(8,128)S(1)} collective-permute-done((f32[264,128]{1,0:T(8,128)S(1)}, f32[264,128]{1,0:T(8,128)S(1)}, u32[]{:S(2)}, u32[]{:S(2)}) %collective-permute-start.5) | collective-permute-done | bytes 135200 | tf_op jit(solution)/shard_map/ppermute | solution.py:229
  32.4 1.3 %collective-permute-done.6.rest_3_ = f32[264,128]{1,0:T(8,128)S(1)} collective-permute-done((f32[264,128]{1,0:T(8,128)S(1)}, f32[264,128]{1,0:T(8,128)S(1)}, u32[]{:S(2)}, u32[]{:S(2)}) %collective-permute-start.6) | collective-permute-done | bytes 135200 | tf_op jit(solution)/shard_map/ppermute | solution.py:229
  33.7 7.7 %shard_map.71 = (f32[512,128]{1,0:T(8,128)S(1)}, f32[8,128]{1,0:T(8,128)S(1)}, f32[128,128]{1,0:T(8,128)S(1)}, f32[136,128]{1,0:T(8,128)S(1)}) custom-call(s32[320]{0:T(512)S(1)} %copy-done.3, s32[320]{0:T(512)S(1)} %copy-done.4, s32[1,1]{1,0:T(1,128)S(6)} %copy.8.counts, bf16[160,256,128]{2,1,0:T(8,128)(2,1)S(1)} %get-tuple-element.26.rest_0_, ...), custom_call_target="tpu_custom_call" | custom-call | tf_op jit(solution)/shard_map/pallas_call | solution.py:241
  41.6 4.3 %collective-permute-done.7 = f32[136,128]{1,0:T(8,128)S(1)} collective-permute-done((f32[136,128]{1,0:T(8,128)S(1)}, f32[136,128]{1,0:T(8,128)S(1)}, u32[]{:S(2)}, u32[]{:S(2)}) %collective-permute-start.7) | collective-permute-done | bytes 69664 | tf_op jit(solution)/shard_map/ppermute | solution.py:229
  45.9 2.0 %collective-permute-start.8 = (f32[136,128]{1,0:T(8,128)S(1)}, f32[136,128]{1,0:T(8,128)S(1)}, u32[]{:S(2)}, u32[]{:S(2)}) collective-permute-start(f32[136,128]{1,0:T(8,128)S(1)} %add.35), channel_id=1, source_target_pairs={{0,2},{1,3},{2,0},{3,1},{4,6},{5,7},{6,4},{7,5},{8,10},{9,11},{10,... | collective-permute-start | bytes 208904 | tf_op jit(solution)/shard_map/ppermute | solution.py:229
  47.8 2.4 %collective-permute-done.8 = f32[136,128]{1,0:T(8,128)S(1)} collective-permute-done((f32[136,128]{1,0:T(8,128)S(1)}, f32[136,128]{1,0:T(8,128)S(1)}, u32[]{:S(2)}, u32[]{:S(2)}) %collective-permute-start.8) | collective-permute-done | bytes 69664 | tf_op jit(solution)/shard_map/ppermute | solution.py:229
  50.3 2.8 %collective-permute-start.9 = (f32[136,128]{1,0:T(8,128)S(1)}, f32[136,128]{1,0:T(8,128)S(1)}, u32[]{:S(2)}, u32[]{:S(2)}) collective-permute-start(f32[136,128]{1,0:T(8,128)S(1)} %add.36.rest_2_), channel_id=1, source_target_pairs={{0,4},{1,5},{2,6},{3,7},{4,0},{5,1},{6,2},{7,3},{8,12},{9,13},{10,... | collective-permute-start | bytes 208904 | tf_op jit(solution)/shard_map/ppermute | solution.py:229
  53.1 2.5 %collective-permute-done.9.rest_3_ = f32[136,128]{1,0:T(8,128)S(1)} collective-permute-done((f32[136,128]{1,0:T(8,128)S(1)}, f32[136,128]{1,0:T(8,128)S(1)}, u32[]{:S(2)}, u32[]{:S(2)}) %collective-permute-start.9) | collective-permute-done | bytes 69664 | tf_op jit(solution)/shard_map/ppermute | solution.py:229
  55.5 5.5 %shard_map.72 = (f32[128,128]{1,0:T(8,128)S(1)}, f32[8,128]{1,0:T(8,128)S(1)}, f32[264,128]{1,0:T(8,128)S(1)}, f32[264,128]{1,0:T(8,128)S(1)}) custom-call(s32[320]{0:T(512)S(1)} %copy-done.3, s32[320]{0:T(512)S(1)} %copy-done.4, s32[1,1]{1,0:T(1,128)S(6)} %copy.8.counts, bf16[160,256,128]{2,1,0:T(8,128)(2,1)S(1)} %get-tuple-element.26.rest_0_, ...), custom_call_target="tpu_custom_call" | custom-call | tf_op jit(solution)/shard_map/pallas_call | solution.py:241
  61.1 0.1 collective-permute-start.10
  61.1 1.3 %collective-permute-done.10 = f32[264,128]{1,0:T(8,128)S(1)} collective-permute-done((f32[264,128]{1,0:T(8,128)S(1)}, f32[264,128]{1,0:T(8,128)S(1)}, u32[]{:S(2)}, u32[]{:S(2)}) %collective-permute-start.10) | collective-permute-done | bytes 135200 | tf_op jit(solution)/shard_map/ppermute | solution.py:229
  62.5 0.1 collective-permute-start.11
  62.6 5.6 %collective-permute-done.11 = f32[264,128]{1,0:T(8,128)S(1)} collective-permute-done((f32[264,128]{1,0:T(8,128)S(1)}, f32[264,128]{1,0:T(8,128)S(1)}, u32[]{:S(2)}, u32[]{:S(2)}) %collective-permute-start.11) | collective-permute-done | bytes 135200 | tf_op jit(solution)/shard_map/ppermute | solution.py:229
  68.3 1.3 %collective-permute-done.12.rest_3_ = f32[264,128]{1,0:T(8,128)S(1)} collective-permute-done((f32[264,128]{1,0:T(8,128)S(1)}, f32[264,128]{1,0:T(8,128)S(1)}, u32[]{:S(2)}, u32[]{:S(2)}) %collective-permute-start.12) | collective-permute-done | bytes 135200 | tf_op jit(solution)/shard_map/ppermute | solution.py:229
  69.6 7.7 %shard_map.73 = (f32[512,128]{1,0:T(8,128)S(1)}, f32[8,128]{1,0:T(8,128)S(1)}, f32[128,128]{1,0:T(8,128)S(1)}, f32[136,128]{1,0:T(8,128)S(1)}) custom-call(s32[320]{0:T(512)S(1)} %copy-done.3, s32[320]{0:T(512)S(1)} %copy-done.4, s32[1,1]{1,0:T(1,128)S(6)} %copy.8.counts, bf16[160,256,128]{2,1,0:T(8,128)(2,1)S(1)} %get-tuple-element.26.rest_0_, ...), custom_call_target="tpu_custom_call" | custom-call | tf_op jit(solution)/shard_map/pallas_call | solution.py:241
  77.4 0.1 collective-permute-start.13
  77.5 4.3 %collective-permute-done.13 = f32[136,128]{1,0:T(8,128)S(1)} collective-permute-done((f32[136,128]{1,0:T(8,128)S(1)}, f32[136,128]{1,0:T(8,128)S(1)}, u32[]{:S(2)}, u32[]{:S(2)}) %collective-permute-start.13) | collective-permute-done | bytes 69664 | tf_op jit(solution)/shard_map/ppermute | solution.py:229
  81.8 3.6 %collective-permute-start.14 = (f32[136,128]{1,0:T(8,128)S(1)}, f32[136,128]{1,0:T(8,128)S(1)}, u32[]{:S(2)}, u32[]{:S(2)}) collective-permute-start(f32[136,128]{1,0:T(8,128)S(1)} %add.39), channel_id=1, source_target_pairs={{0,2},{1,3},{2,0},{3,1},{4,6},{5,7},{6,4},{7,5},{8,10},{9,11},{10,... | collective-permute-start | bytes 208904 | tf_op jit(solution)/shard_map/ppermute | solution.py:229
  85.5 2.3 %collective-permute-done.14 = f32[136,128]{1,0:T(8,128)S(1)} collective-permute-done((f32[136,128]{1,0:T(8,128)S(1)}, f32[136,128]{1,0:T(8,128)S(1)}, u32[]{:S(2)}, u32[]{:S(2)}) %collective-permute-start.14) | collective-permute-done | bytes 69664 | tf_op jit(solution)/shard_map/ppermute | solution.py:229
  87.8 3.2 %collective-permute-start.15 = (f32[136,128]{1,0:T(8,128)S(1)}, f32[136,128]{1,0:T(8,128)S(1)}, u32[]{:S(2)}, u32[]{:S(2)}) collective-permute-start(f32[136,128]{1,0:T(8,128)S(1)} %add.40.rest_2_), channel_id=1, source_target_pairs={{0,4},{1,5},{2,6},{3,7},{4,0},{5,1},{6,2},{7,3},{8,12},{9,13},{10,... | collective-permute-start | bytes 208904 | tf_op jit(solution)/shard_map/ppermute | solution.py:229
  91.0 2.3 %collective-permute-done.15.rest_3_ = f32[136,128]{1,0:T(8,128)S(1)} collective-permute-done((f32[136,128]{1,0:T(8,128)S(1)}, f32[136,128]{1,0:T(8,128)S(1)}, u32[]{:S(2)}, u32[]{:S(2)}) %collective-permute-start.15) | collective-permute-done | bytes 69664 | tf_op jit(solution)/shard_map/ppermute | solution.py:229
  93.3 6.1 %shard_map.74 = (f32[128,128]{1,0:T(8,128)}, f32[8,128]{1,0:T(8,128)S(1)}, f32[264,128]{1,0:T(8,128)S(1)}, f32[264,128]{1,0:T(8,128)S(1)}) custom-call(s32[320]{0:T(512)S(1)} %copy-done.3, s32[320]{0:T(512)S(1)} %copy-done.4, s32[1,1]{1,0:T(1,128)S(6)} %copy.8.counts, bf16[160,256,128]{2,1,0:T(8,128)(2,1)S(1)} %get-tuple-element.26.rest_0_, ...), custom_call_target="tpu_custom_call" | custom-call | tf_op jit(solution)/shard_map/pallas_call | solution.py:241
  99.4 0.1 collective-permute-start.16
  99.5 1.3 %collective-permute-done.16 = f32[264,128]{1,0:T(8,128)S(1)} collective-permute-done((f32[264,128]{1,0:T(8,128)S(1)}, f32[264,128]{1,0:T(8,128)S(1)}, u32[]{:S(2)}, u32[]{:S(2)}) %collective-permute-start.16) | collective-permute-done | bytes 135200 | tf_op jit(solution)/shard_map/ppermute | solution.py:229
  100.9 0.1 collective-permute-start.17
  101.0 5.6 %collective-permute-done.17 = f32[264,128]{1,0:T(8,128)S(1)} collective-permute-done((f32[264,128]{1,0:T(8,128)S(1)}, f32[264,128]{1,0:T(8,128)S(1)}, u32[]{:S(2)}, u32[]{:S(2)}) %collective-permute-start.17) | collective-permute-done | bytes 135200 | tf_op jit(solution)/shard_map/ppermute | solution.py:229
  106.7 1.3 %collective-permute-done.18.other = f32[264,128]{1,0:T(8,128)S(1)} collective-permute-done((f32[264,128]{1,0:T(8,128)S(1)}, f32[264,128]{1,0:T(8,128)S(1)}, u32[]{:S(2)}, u32[]{:S(2)}) %collective-permute-start.18) | collective-permute-done | bytes 135200 | tf_op jit(solution)/shard_map/ppermute | solution.py:229
  108.0 0.6 copy-done.11
  108.7 1.9 %shard_map.75 = (f32[512,128]{1,0:T(8,128)}, f32[8,128]{1,0:T(8,128)}, f32[128,128]{1,0:T(8,128)}, f32[8,128]{1,0:T(8,128)}) custom-call(f32[264,128]{1,0:T(8,128)} %copy-done.10, f32[264,128]{1,0:T(8,128)} %copy-done.11, f32[512,128]{1,0:T(8,128)} %copy-done, f32[8,128]{1,0:T(8,128)} %copy-done.6), custom_call_target="tpu_custom_call" | custom-call | tf_op jit(solution)/shard_map/pallas_call | solution.py:274
  110.6 0.5 collective-permute-start.19
  111.1 3.3 %collective-permute-done.19 = f32[8,128]{1,0:T(8,128)S(1)} collective-permute-done((f32[8,128]{1,0:T(8,128)}, f32[8,128]{1,0:T(8,128)S(1)}, u32[]{:S(2)}, u32[]{:S(2)}) %collective-permute-start.19) | collective-permute-done | bytes 4128 | tf_op jit(solution)/shard_map/ppermute | solution.py:229
  114.5 0.7 add.43.refs_8_
  115.1 5.7 %collective-permute-start.22 = (f32[8,128]{1,0:T(8,128)S(1)}, f32[8,128]{1,0:T(8,128)S(1)}, u32[]{:S(2)}, u32[]{:S(2)}) collective-permute-start(f32[8,128]{1,0:T(8,128)S(1)} %add.43.refs_8_), channel_id=1, source_target_pairs={{0,6},{1,7},{2,4},{3,5},{4,2},{5,3},{6,0},{7,1},{8,14},{9,15},{10,... | collective-permute-start | bytes 12296 | tf_op jit(solution)/shard_map/ppermute | solution.py:229
  120.9 0.6 collective-permute-start.20
  121.4 1.0 collective-permute-done.22.refs_11_
  122.5 2.9 %collective-permute-done.21.refs_10_ = f32[8,128]{1,0:T(8,128)S(1)} collective-permute-done((f32[8,128]{1,0:T(8,128)S(1)}, f32[8,128]{1,0:T(8,128)S(1)}, u32[]{:S(2)}, u32[]{:S(2)}) %collective-permute-start.21) | collective-permute-done | bytes 4128 | tf_op jit(solution)/shard_map/ppermute | solution.py:229
  125.4 0.6 copy-done.14
  126.0 1.6 %shard_map.76 = (f32[128,128]{1,0:T(8,128)}, f32[128,128]{1,0:T(8,128)}) custom-call(f32[128,128]{1,0:T(8,128)} %copy-done.1, f32[128,128]{1,0:T(8,128)} %copy-done.2, f32[128,128]{1,0:T(8,128)} %get-tuple-element.47.refs_2_, f32[8,128]{1,0:T(8,128)} %copy-done.7, f32[8,128]{1,0:T(8,128)} %copy-done.9, f32[8,128]{1,0:T(8,128)} %get-tuple-element.48.refs_5_, ...), custom_call_target="tpu_custom_call" | custom-call | tf_op jit(solution)/shard_map/pallas_call | solution.py:274
  (52 shorter events, 0.5 us)
Async XLA Ops:
  0.6 8.5 %collective-permute-start = (f32[16,128]{1,0:T(8,128)}, f32[16,128]{1,0:T(8,128)S(1)}, u32[]{:S(2)}, u32[]{:S(2)}) collective-permute-start(f32[16,128]{1,0:T(8,128)} %data.3), channel_id=1, source_target_pairs={{0,1},{1,0},{2,3},{3,2},{4,5},{5,4},{6,7},{7,6},{8,9},{9,8},{10,11... | collective-permute-start | bytes 24584 | tf_op jit(solution)/shard_map/ppermute | solution.py:229
  3.7 0.7 copy-start.5
  9.1 10.4 %collective-permute-start.3 = (f32[32,128]{1,0:T(8,128)S(1)}, f32[32,128]{1,0:T(8,128)S(1)}, u32[]{:S(2)}, u32[]{:S(2)}) collective-permute-start(f32[32,128]{1,0:T(8,128)S(1)} %constant_dynamic-update-slice_fusion.rest_2_), channel_id=1, source_target_pairs={{0,6},{1,7},{2,4},{3,5},{4,2},{5,3},{6,0},{7,1},{8,14},{9,15},{10,... | collective-permute-start | bytes 49160 | tf_op jit(solution)/shard_map/ppermute | solution.py:229
  12.8 6.8 %collective-permute-start.2 = (f32[32,128]{1,0:T(8,128)S(1)}, f32[32,128]{1,0:T(8,128)S(1)}, u32[]{:S(2)}, u32[]{:S(2)}) collective-permute-start(f32[32,128]{1,0:T(8,128)S(1)} %constant_dynamic-update-slice_fusion.rest_2_), channel_id=1, source_target_pairs={{0,4},{1,5},{2,6},{3,7},{4,0},{5,1},{6,2},{7,3},{8,12},{9,13},{10,... | collective-permute-start | bytes 49160 | tf_op jit(solution)/shard_map/ppermute | solution.py:229
  12.8 6.8 %collective-permute-start.1 = (f32[32,128]{1,0:T(8,128)S(1)}, f32[32,128]{1,0:T(8,128)S(1)}, u32[]{:S(2)}, u32[]{:S(2)}) collective-permute-start(f32[32,128]{1,0:T(8,128)S(1)} %constant_dynamic-update-slice_fusion.rest_2_), channel_id=1, source_target_pairs={{0,2},{1,3},{2,0},{3,1},{4,6},{5,7},{6,4},{7,5},{8,10},{9,11},{10,... | collective-permute-start | bytes 49160 | tf_op jit(solution)/shard_map/ppermute | solution.py:229
  14.2 5.4 %copy-start.3 = (s32[320]{0:T(512)S(1)}, s32[320]{0:T(512)}, u32[]{:S(2)}) copy-start(s32[320]{0:T(512)} %pick.9) | copy-start | bytes 3844
  14.3 5.4 %copy-start.4 = (s32[320]{0:T(512)S(1)}, s32[320]{0:T(512)}, u32[]{:S(2)}) copy-start(s32[320]{0:T(512)} %cell.9) | copy-start | bytes 3844
  25.1 1.4 %collective-permute-start.4 = (f32[264,128]{1,0:T(8,128)S(1)}, f32[264,128]{1,0:T(8,128)S(1)}, u32[]{:S(2)}, u32[]{:S(2)}) collective-permute-start(f32[264,128]{1,0:T(8,128)S(1)} %get-tuple-element.30), channel_id=1, source_target_pairs={{0,8},{8,0},{16,24},{24,16},{1,9},{9,1},{17,25},{25,17},{2,10},{10... | collective-permute-start | bytes 405512 | tf_op jit(solution)/shard_map/ppermute | solution.py:229
  26.6 5.7 %collective-permute-start.5 = (f32[264,128]{1,0:T(8,128)S(1)}, f32[264,128]{1,0:T(8,128)S(1)}, u32[]{:S(2)}, u32[]{:S(2)}) collective-permute-start(f32[264,128]{1,0:T(8,128)S(1)} %add.33), channel_id=1, source_target_pairs={{0,16},{8,24},{16,0},{24,8},{1,17},{9,25},{17,1},{25,9},{2,18},{10... | collective-permute-start | bytes 405512 | tf_op jit(solution)/shard_map/ppermute | solution.py:229
  32.3 1.4 %collective-permute-start.6 = (f32[264,128]{1,0:T(8,128)S(1)}, f32[264,128]{1,0:T(8,128)S(1)}, u32[]{:S(2)}, u32[]{:S(2)}) collective-permute-start(f32[264,128]{1,0:T(8,128)S(1)} %add.34.rest_2_), channel_id=1, source_target_pairs={{0,8},{8,0},{16,24},{24,16},{1,9},{9,1},{17,25},{25,17},{2,10},{10... | collective-permute-start | bytes 405512 | tf_op jit(solution)/shard_map/ppermute | solution.py:229
  41.5 6.4 %copy-start.1 = (f32[128,128]{1,0:T(8,128)}, f32[128,128]{1,0:T(8,128)S(1)}, u32[]{:S(2)}) copy-start(f32[128,128]{1,0:T(8,128)S(1)} %get-tuple-element.31.refs_0_) | copy-start | bytes 196612
  41.5 19.6 %copy-start.7 = (f32[8,128]{1,0:T(8,128)}, f32[8,128]{1,0:T(8,128)S(1)}, u32[]{:S(2)}) copy-start(f32[8,128]{1,0:T(8,128)S(1)} %get-tuple-element.34.rest_5_.refs_3_) | copy-start | bytes 12292
  41.5 4.4 %collective-permute-start.7 = (f32[136,128]{1,0:T(8,128)S(1)}, f32[136,128]{1,0:T(8,128)S(1)}, u32[]{:S(2)}, u32[]{:S(2)}) collective-permute-start(f32[136,128]{1,0:T(8,128)S(1)} %get-tuple-element.32), channel_id=1, source_target_pairs={{0,1},{1,0},{2,3},{3,2},{4,5},{5,4},{6,7},{7,6},{8,9},{9,8},{10,11... | collective-permute-start | bytes 208904 | tf_op jit(solution)/shard_map/ppermute | solution.py:229
  45.9 4.4 %collective-permute-start.8 = (f32[136,128]{1,0:T(8,128)S(1)}, f32[136,128]{1,0:T(8,128)S(1)}, u32[]{:S(2)}, u32[]{:S(2)}) collective-permute-start(f32[136,128]{1,0:T(8,128)S(1)} %add.35), channel_id=1, source_target_pairs={{0,2},{1,3},{2,0},{3,1},{4,6},{5,7},{6,4},{7,5},{8,10},{9,11},{10,... | collective-permute-start | bytes 208904 | tf_op jit(solution)/shard_map/ppermute | solution.py:229
  50.3 5.3 %collective-permute-start.9 = (f32[136,128]{1,0:T(8,128)S(1)}, f32[136,128]{1,0:T(8,128)S(1)}, u32[]{:S(2)}, u32[]{:S(2)}) collective-permute-start(f32[136,128]{1,0:T(8,128)S(1)} %add.36.rest_2_), channel_id=1, source_target_pairs={{0,4},{1,5},{2,6},{3,7},{4,0},{5,1},{6,2},{7,3},{8,12},{9,13},{10,... | collective-permute-start | bytes 208904 | tf_op jit(solution)/shard_map/ppermute | solution.py:229
  61.0 16.4 %copy-start.8 = (f32[8,128]{1,0:T(8,128)}, f32[8,128]{1,0:T(8,128)S(1)}, u32[]{:S(2)}) copy-start(f32[8,128]{1,0:T(8,128)S(1)} %get-tuple-element.38.rest_5_.refs_6_) | copy-start | bytes 12292
  61.1 1.4 %collective-permute-start.10 = (f32[264,128]{1,0:T(8,128)S(1)}, f32[264,128]{1,0:T(8,128)S(1)}, u32[]{:S(2)}, u32[]{:S(2)}) collective-permute-start(f32[264,128]{1,0:T(8,128)S(1)} %get-tuple-element.36), channel_id=1, source_target_pairs={{0,8},{8,0},{16,24},{24,16},{1,9},{9,1},{17,25},{25,17},{2,10},{10... | collective-permute-start | bytes 405512 | tf_op jit(solution)/shard_map/ppermute | solution.py:229
  62.5 5.7 %collective-permute-start.11 = (f32[264,128]{1,0:T(8,128)S(1)}, f32[264,128]{1,0:T(8,128)S(1)}, u32[]{:S(2)}, u32[]{:S(2)}) collective-permute-start(f32[264,128]{1,0:T(8,128)S(1)} %add.37), channel_id=1, source_target_pairs={{0,16},{8,24},{16,0},{24,8},{1,17},{9,25},{17,1},{25,9},{2,18},{10... | collective-permute-start | bytes 405512 | tf_op jit(solution)/shard_map/ppermute | solution.py:229
  68.2 1.4 %collective-permute-start.12 = (f32[264,128]{1,0:T(8,128)S(1)}, f32[264,128]{1,0:T(8,128)S(1)}, u32[]{:S(2)}, u32[]{:S(2)}) collective-permute-start(f32[264,128]{1,0:T(8,128)S(1)} %add.38.rest_2_), channel_id=1, source_target_pairs={{0,8},{8,0},{16,24},{24,16},{1,9},{9,1},{17,25},{25,17},{2,10},{10... | collective-permute-start | bytes 405512 | tf_op jit(solution)/shard_map/ppermute | solution.py:229
  77.4 15.9 %copy-start = (f32[512,128]{1,0:T(8,128)}, f32[512,128]{1,0:T(8,128)S(1)}, u32[]{:S(2)}) copy-start(f32[512,128]{1,0:T(8,128)S(1)} %get-tuple-element.45.v_old) | copy-start | bytes 786436
  77.4 22.0 %copy-start.2 = (f32[128,128]{1,0:T(8,128)}, f32[128,128]{1,0:T(8,128)S(1)}, u32[]{:S(2)}) copy-start(f32[128,128]{1,0:T(8,128)S(1)} %get-tuple-element.39.refs_1_) | copy-start | bytes 196612
  77.4 22.0 %copy-start.9 = (f32[8,128]{1,0:T(8,128)}, f32[8,128]{1,0:T(8,128)S(1)}, u32[]{:S(2)}) copy-start(f32[8,128]{1,0:T(8,128)S(1)} %get-tuple-element.42.rest_5_.refs_4_) | copy-start | bytes 12292
  77.4 4.4 %collective-permute-start.13 = (f32[136,128]{1,0:T(8,128)S(1)}, f32[136,128]{1,0:T(8,128)S(1)}, u32[]{:S(2)}, u32[]{:S(2)}) collective-permute-start(f32[136,128]{1,0:T(8,128)S(1)} %get-tuple-element.40), channel_id=1, source_target_pairs={{0,1},{1,0},{2,3},{3,2},{4,5},{5,4},{6,7},{7,6},{8,9},{9,8},{10,11... | collective-permute-start | bytes 208904 | tf_op jit(solution)/shard_map/ppermute | solution.py:229
  81.8 6.0 %collective-permute-start.14 = (f32[136,128]{1,0:T(8,128)S(1)}, f32[136,128]{1,0:T(8,128)S(1)}, u32[]{:S(2)}, u32[]{:S(2)}) collective-permute-start(f32[136,128]{1,0:T(8,128)S(1)} %add.39), channel_id=1, source_target_pairs={{0,2},{1,3},{2,0},{3,1},{4,6},{5,7},{6,4},{7,5},{8,10},{9,11},{10,... | collective-permute-start | bytes 208904 | tf_op jit(solution)/shard_map/ppermute | solution.py:229
  87.8 5.5 %collective-permute-start.15 = (f32[136,128]{1,0:T(8,128)S(1)}, f32[136,128]{1,0:T(8,128)S(1)}, u32[]{:S(2)}, u32[]{:S(2)}) collective-permute-start(f32[136,128]{1,0:T(8,128)S(1)} %add.40.rest_2_), channel_id=1, source_target_pairs={{0,4},{1,5},{2,6},{3,7},{4,0},{5,1},{6,2},{7,3},{8,12},{9,13},{10,... | collective-permute-start | bytes 208904 | tf_op jit(solution)/shard_map/ppermute | solution.py:229
  99.4 1.4 %copy-start.6 = (f32[8,128]{1,0:T(8,128)}, f32[8,128]{1,0:T(8,128)S(1)}, u32[]{:S(2)}) copy-start(f32[8,128]{1,0:T(8,128)S(1)} %get-tuple-element.46.alpha_old.refs_7_) | copy-start | bytes 12292
  99.4 1.4 %collective-permute-start.16 = (f32[264,128]{1,0:T(8,128)S(1)}, f32[264,128]{1,0:T(8,128)S(1)}, u32[]{:S(2)}, u32[]{:S(2)}) collective-permute-start(f32[264,128]{1,0:T(8,128)S(1)} %get-tuple-element.44), channel_id=1, source_target_pairs={{0,8},{8,0},{16,24},{24,16},{1,9},{9,1},{17,25},{25,17},{2,10},{10... | collective-permute-start | bytes 405512 | tf_op jit(solution)/shard_map/ppermute | solution.py:229
  100.9 5.7 %collective-permute-start.17 = (f32[264,128]{1,0:T(8,128)S(1)}, f32[264,128]{1,0:T(8,128)S(1)}, u32[]{:S(2)}, u32[]{:S(2)}) collective-permute-start(f32[264,128]{1,0:T(8,128)S(1)} %add.41), channel_id=1, source_target_pairs={{0,16},{8,24},{16,0},{24,8},{1,17},{9,25},{17,1},{25,9},{2,18},{10... | collective-permute-start | bytes 405512 | tf_op jit(solution)/shard_map/ppermute | solution.py:229
  106.6 1.4 %copy-start.10 = (f32[264,128]{1,0:T(8,128)}, f32[264,128]{1,0:T(8,128)S(1)}, u32[]{:S(2)}) copy-start(f32[264,128]{1,0:T(8,128)S(1)} %add.42.mine) | copy-start | bytes 405508
  106.6 1.4 %collective-permute-start.18 = (f32[264,128]{1,0:T(8,128)S(1)}, f32[264,128]{1,0:T(8,128)S(1)}, u32[]{:S(2)}, u32[]{:S(2)}) collective-permute-start(f32[264,128]{1,0:T(8,128)S(1)} %add.42.mine), channel_id=1, source_target_pairs={{0,8},{8,0},{16,24},{24,16},{1,9},{9,1},{17,25},{25,17},{2,10},{10... | collective-permute-start | bytes 405512 | tf_op jit(solution)/shard_map/ppermute | solution.py:229
  108.0 0.7 copy-start.11
  110.6 3.8 %collective-permute-start.19 = (f32[8,128]{1,0:T(8,128)}, f32[8,128]{1,0:T(8,128)S(1)}, u32[]{:S(2)}, u32[]{:S(2)}) collective-permute-start(f32[8,128]{1,0:T(8,128)} %get-tuple-element.49), channel_id=1, source_target_pairs={{0,1},{1,0},{2,3},{3,2},{4,5},{5,4},{6,7},{7,6},{8,9},{9,8},{10,11... | collective-permute-start | bytes 12296 | tf_op jit(solution)/shard_map/ppermute | solution.py:229
  115.1 10.3 %copy-start.12 = (f32[8,128]{1,0:T(8,128)}, f32[8,128]{1,0:T(8,128)S(1)}, u32[]{:S(2)}) copy-start(f32[8,128]{1,0:T(8,128)S(1)} %add.43.refs_8_) | copy-start | bytes 12292
  115.1 7.3 %collective-permute-start.22 = (f32[8,128]{1,0:T(8,128)S(1)}, f32[8,128]{1,0:T(8,128)S(1)}, u32[]{:S(2)}, u32[]{:S(2)}) collective-permute-start(f32[8,128]{1,0:T(8,128)S(1)} %add.43.refs_8_), channel_id=1, source_target_pairs={{0,6},{1,7},{2,4},{3,5},{4,2},{5,3},{6,0},{7,1},{8,14},{9,15},{10,... | collective-permute-start | bytes 12296 | tf_op jit(solution)/shard_map/ppermute | solution.py:229
  120.9 4.5 %collective-permute-start.21 = (f32[8,128]{1,0:T(8,128)S(1)}, f32[8,128]{1,0:T(8,128)S(1)}, u32[]{:S(2)}, u32[]{:S(2)}) collective-permute-start(f32[8,128]{1,0:T(8,128)S(1)} %add.43.refs_8_), channel_id=1, source_target_pairs={{0,4},{1,5},{2,6},{3,7},{4,0},{5,1},{6,2},{7,3},{8,12},{9,13},{10,... | collective-permute-start | bytes 12296 | tf_op jit(solution)/shard_map/ppermute | solution.py:229
  120.9 4.5 %collective-permute-start.20 = (f32[8,128]{1,0:T(8,128)S(1)}, f32[8,128]{1,0:T(8,128)S(1)}, u32[]{:S(2)}, u32[]{:S(2)}) collective-permute-start(f32[8,128]{1,0:T(8,128)S(1)} %add.43.refs_8_), channel_id=1, source_target_pairs={{0,2},{1,3},{2,0},{3,1},{4,6},{5,7},{6,4},{7,5},{8,10},{9,11},{10,... | collective-permute-start | bytes 12296 | tf_op jit(solution)/shard_map/ppermute | solution.py:229
  122.5 2.9 %copy-start.13 = (f32[8,128]{1,0:T(8,128)}, f32[8,128]{1,0:T(8,128)S(1)}, u32[]{:S(2)}) copy-start(f32[8,128]{1,0:T(8,128)S(1)} %collective-permute-done.22.refs_11_) | copy-start | bytes 12292
  125.4 0.6 copy-start.14
  125.4 0.6 copy-start.15

commit v4 on v3

--- a/solution.py
+++ b/solution.py
@@ -14,9 +14,11 @@
 SUB = 8
 GROUP = 16
 PARTS = 2
-STEP = 16
-BUFFERS = 4
+STEP = 8
+BUFFERS = 6
+UNITS = 2
 TAIL = 8
+EXTRA = 3
 
 
 def split(value):
@@ -66,27 +68,23 @@
     return pl.ds(pl.multiple_of(index * SUB, SUB), SUB)
 
 
-def pair_transposed(tiles, one, two, first):
-    row = jnp.where(first, one, two).astype(jnp.bfloat16)
-    row = jnp.concatenate([row, row], axis=1)
-    both = jnp.dot(row, tiles, preferred_element_type=jnp.float32)
-    return both[:, :B], both[:, B:]
-
-
-def pair_forward(tiles, one, two, first):
+def twice(rows):
+    return jnp.concatenate([rows, rows], axis=0).astype(jnp.bfloat16)
+
+
+def pair_row_transposed(one, two, first):
+    row = twice(jnp.where(first, one, two))
+    return jnp.concatenate([row, row], axis=1)
+
+
+def pair_row_forward(one, two, first):
     zero = jnp.zeros_like(one)
-    row = jnp.concatenate([jnp.where(first, one, zero), jnp.where(first, zero, two)], axis=1)
-    both = lax.dot_general(
-        row.astype(jnp.bfloat16),
-        tiles,
-        (((1,), (1,)), ((), ())),
-        preferred_element_type=jnp.float32,
-    )
-    both = both[:, :B] + both[:, B:]
-    return both, both
-
-
-def over_tiles(parts, live, product, table, source, target, blocks, accs):
+    return jnp.concatenate(
+        [twice(jnp.where(first, one, zero)), twice(jnp.where(first, zero, two))], axis=1
+    )
+
+
+def over_tiles(parts, live, forward, table, source, target, blocks, accs):
     places = [(accs[0], 0), (accs[0], 1), (accs[1], 2), (accs[1], 3)]
     for acc, start in places:
         rows_of(acc, start, blocks)[...] = jnp.zeros((blocks, B), jnp.float32)
@@ -97,18 +95,32 @@
         here = jnp.clip(live - first, 0, size)
 
         def some(group, carry, tiles=tiles, first=first):
+            kinds = [pltpu.ACC(k % UNITS)((2 * SUB, 2 * B), jnp.float32) for k in range(GROUP // 2)]
+            pl.run_scoped(functools.partial(multiply, group, tiles, first), *kinds)
+            return carry
+
+        def multiply(group, tiles, first, *units):
             base = group * GROUP
             sums = []
             for k in range(0, GROUP, 2):
                 slot = first + base + k
+                at, unit = divmod(k // 2, UNITS)
                 pair = jnp.concatenate([tiles[base + k], tiles[base + k + 1]], axis=1)
+                pltpu.matmul_push_rhs(pair, at % 2, unit, transpose=forward)
                 one, two = (table[block_at(source[slot + n]), :] for n in range(2))
-                sums.append(product(pair, one, two, upper))
+                row = (pair_row_forward if forward else pair_row_transposed)(one, two, upper)
+                pltpu.matmul_acc_lhs(units[k // 2], row, load_staged_rhs=at % 2)
+            for k in range(0, GROUP, 2):
+                both = pltpu.matmul_pop(units[k // 2])[:SUB]
+                if forward:
+                    both = both[:, :B] + both[:, B:]
+                    sums.append((both, both))
+                else:
+                    sums.append((both[:, :B], both[:, B:]))
             for k in range(GROUP):
                 slot = first + base + k
                 place = block_at(jnp.where(slot < live, target[slot], blocks))
                 accs[k % 2][place, :] += sums[k // 2][k % 2]
-            return carry
 
         lax.fori_loop(0, (here + GROUP - 1) // GROUP, some, 0)
         first += size
@@ -122,7 +134,7 @@
 
 def adjoint_tail(n_rows, parts, pick, cell, counts, u, keep, send, table, *accs):
     fill_table(table, u)
-    whole = over_tiles(parts, counts[0, 0], pair_transposed, table, pick, cell, CBLK, accs)
+    whole = over_tiles(parts, counts[0, 0], False, table, pick, cell, CBLK, accs)
     square = jnp.full((TAIL, B), jnp.sum(u * u))
     size, _ = halves(n_rows, CBLK)
     core = lax.rem(lax.axis_index("rows"), 2)
@@ -143,7 +155,7 @@
 
 
 def first_adjoint(n_rows, n_cols, pick, cell, counts, *rest):
-    parts, pieces, (u_out, keep, send, table, *accs) = rest[:PARTS], rest[PARTS:-6], rest[-6:]
+    parts, pieces, (u_out, keep, send, table, *accs) = rest[:PARTS], rest[PARTS:-EXTRA - 3], rest[-EXTRA - 3 :]
     me = lax.axis_index("cols")
     offset = 0
     for piece in pieces:
@@ -187,10 +199,10 @@
 def forward(first, n_rows, pick, cell, counts, *rest):
     parts, rest = rest[:PARTS], rest[PARTS:]
     old = (None, None) if first else rest[2:4]
-    v_out, beta_out, own_out, out, table, *accs = rest[-7:]
+    v_out, beta_out, own_out, out, table, *accs = rest[-EXTRA - 4 :]
     v, square = cell_vector(n_rows, rest[0], rest[1], *old, v_out, beta_out, own_out)
     fill_table(table, v)
-    out[:PBLK, :] = over_tiles(parts, counts[0, 0], pair_forward, table, cell, pick, PBLK, accs)
+    out[:PBLK, :] = over_tiles(parts, counts[0, 0], True, table, cell, pick, PBLK, accs)
     out[pl.ds(PBLK, TAIL), :] = square
 
 

time: 129 us -> 129 us (level); the launches traced: 128 us -> 129 us
  starting transfers between devices: 27.7 us -> 38.9 us
  Pallas kernels: 46.2 us -> 37.5 us
    ppermute x23, starting transfers between devices: 27.7 us -> 38.9 us  [swapped(): return lax.ppermute(block, axis, [(i, i ^ bit) for i in range(size)])]
    pallas_call x5, Pallas kernels: 32.6 us -> 23.2 us  [call(): pl.pallas_call(kernel, out_shape=outs, in_specs=[SCALAR] * len(scalars) +...]
where the time goes in v4:
time: 129 us
  waiting for transfers between devices  48.4 us (38%)
  starting transfers between devices  38.9 us (30%)
  Pallas kernels  37.5 us (29%)
  local copies, waits for them, and re-layouts  2.01 us (2%)
  between operations  1.61 us (1%)
    ppermute x23, waiting for transfers between devices, swapped(): return lax.ppermute(block, axis, [(i, i ^ bit) for i in range(size)])  48.4 us
    ppermute x23, starting transfers between devices, swapped(): return lax.ppermute(block, axis, [(i, i ^ bit) for i in range(size)])  38.9 us
    pallas_call x5, Pallas kernels, call(): pl.pallas_call(kernel, out_shape=outs, in_specs=[SCALAR] * len(scalars) +...  23.2 us
    pallas_call x2, Pallas kernels, split_part(): pl.pallas_call(functools.partial(split_tiles, part * size), out_shape=[pl...  10.7 us
    pallas_call x2, Pallas kernels, simple_call(): pl.pallas_call(kernel, out_shape=outs, in_specs=[VECTOR] * len(arrays), o...  3.57 us
  transfers between devices with their start and end apart: 23, of which 18 were waited for; matrix products, arithmetic and copies ran while one was open for 0% of the time, Pallas kernels for 8%

profile of v4, /device:TPU:0, one launch (start us, length us, event | category | flops | bytes accessed | tf_op | source)
XLA Modules:
  0.0 129.3 jit_solution(13161394961094445752)
XLA Ops:
  0.6 3.0 %collective-permute-start = (f32[16,128]{1,0:T(8,128)}, f32[16,128]{1,0:T(8,128)S(1)}, u32[]{:S(2)}, u32[]{:S(2)}) collective-permute-start(f32[16,128]{1,0:T(8,128)} %data.3), channel_id=1, source_target_pairs={{0,1},{1,0},{2,3},{3,2},{4,5},{5,4},{6,7},{7,6},{8,9},{9,8},{10,11... | collective-permute-start | bytes 24584 | tf_op jit(solution)/shard_map/ppermute | solution.py:241
  3.7 0.7 copy-done.5
  4.4 5.1 %shard_map.68 = (bf16[160,256,128]{2,1,0:T(8,128)(2,1)S(1)}, f32[16,128]{1,0:T(8,128)S(1)}) custom-call(f32[320,128,128]{2,1,0:T(8,128)} %tiles.3, f32[16,128]{1,0:T(8,128)S(1)} %copy-done.5), custom_call_target="tpu_custom_call" | custom-call | flops 10485760 | bytes 10485760 | tf_op jit(solution)/shard_map/pallas_call | solution.py:269
  9.5 3.7 %collective-permute-start.3 = (f32[32,128]{1,0:T(8,128)S(1)}, f32[32,128]{1,0:T(8,128)S(1)}, u32[]{:S(2)}, u32[]{:S(2)}) collective-permute-start(f32[32,128]{1,0:T(8,128)S(1)} %constant_dynamic-update-slice_fusion.rest_2_), channel_id=1, source_target_pairs={{0,6},{1,7},{2,4},{3,5},{4,2},{5,3},{6,0},{7,1},{8,14},{9,15},{10,... | collective-permute-start | bytes 49160 | tf_op jit(solution)/shard_map/ppermute | solution.py:241
  13.2 0.8 collective-permute-start.1
  14.6 5.7 %shard_map.69 = (bf16[160,256,128]{2,1,0:T(8,128)(2,1)S(1)}, f32[16,128]{1,0:T(8,128)}) custom-call(f32[320,128,128]{2,1,0:T(8,128)} %tiles.3, f32[16,128]{1,0:T(8,128)S(1)} %copy-done.5), custom_call_target="tpu_custom_call" | custom-call | flops 10485760 | bytes 10485760 | tf_op jit(solution)/shard_map/pallas_call | solution.py:269
  20.4 4.0 %shard_map.70 = (f32[128,128]{1,0:T(8,128)S(1)}, f32[264,128]{1,0:T(8,128)S(1)}, f32[264,128]{1,0:T(8,128)S(1)}) custom-call(s32[320]{0:T(512)S(1)} %copy-done.3, s32[320]{0:T(512)S(1)} %copy-done.4, s32[1,1]{1,0:T(1,128)S(6)} %copy.8.counts, bf16[160,256,128]{2,1,0:T(8,128)(2,1)S(1)} %get-tuple-element.26.rest_0_, ...), custom_call_target="tpu_custom_call" | custom-call | tf_op jit(solution)/shard_map/pallas_call | solution.py:253
  24.4 1.3 %collective-permute-done.4 = f32[264,128]{1,0:T(8,128)S(1)} collective-permute-done((f32[264,128]{1,0:T(8,128)S(1)}, f32[264,128]{1,0:T(8,128)S(1)}, u32[]{:S(2)}, u32[]{:S(2)}) %collective-permute-start.4) | collective-permute-done | bytes 135200 | tf_op jit(solution)/shard_map/ppermute | solution.py:241
  25.8 0.8 collective-permute-start.5
  26.6 4.9 %collective-permute-done.5 = f32[264,128]{1,0:T(8,128)S(1)} collective-permute-done((f32[264,128]{1,0:T(8,128)S(1)}, f32[264,128]{1,0:T(8,128)S(1)}, u32[]{:S(2)}, u32[]{:S(2)}) %collective-permute-start.5) | collective-permute-done | bytes 135200 | tf_op jit(solution)/shard_map/ppermute | solution.py:241
  31.6 1.3 %collective-permute-done.6.rest_3_ = f32[264,128]{1,0:T(8,128)S(1)} collective-permute-done((f32[264,128]{1,0:T(8,128)S(1)}, f32[264,128]{1,0:T(8,128)S(1)}, u32[]{:S(2)}, u32[]{:S(2)}) %collective-permute-start.6) | collective-permute-done | bytes 135200 | tf_op jit(solution)/shard_map/ppermute | solution.py:241
  32.9 5.3 %shard_map.71 = (f32[512,128]{1,0:T(8,128)S(1)}, f32[8,128]{1,0:T(8,128)S(1)}, f32[128,128]{1,0:T(8,128)S(1)}, f32[136,128]{1,0:T(8,128)S(1)}) custom-call(s32[320]{0:T(512)S(1)} %copy-done.3, s32[320]{0:T(512)S(1)} %copy-done.4, s32[1,1]{1,0:T(1,128)S(6)} %copy.8.counts, bf16[160,256,128]{2,1,0:T(8,128)(2,1)S(1)} %get-tuple-element.26.rest_0_, ...), custom_call_target="tpu_custom_call" | custom-call | tf_op jit(solution)/shard_map/pallas_call | solution.py:253
  38.3 0.4 collective-permute-start.7
  38.7 3.9 %collective-permute-done.7 = f32[136,128]{1,0:T(8,128)S(1)} collective-permute-done((f32[136,128]{1,0:T(8,128)S(1)}, f32[136,128]{1,0:T(8,128)S(1)}, u32[]{:S(2)}, u32[]{:S(2)}) %collective-permute-start.7) | collective-permute-done | bytes 69664 | tf_op jit(solution)/shard_map/ppermute | solution.py:241
  42.6 4.2 %collective-permute-start.8 = (f32[136,128]{1,0:T(8,128)S(1)}, f32[136,128]{1,0:T(8,128)S(1)}, u32[]{:S(2)}, u32[]{:S(2)}) collective-permute-start(f32[136,128]{1,0:T(8,128)S(1)} %add.35), channel_id=1, source_target_pairs={{0,2},{1,3},{2,0},{3,1},{4,6},{5,7},{6,4},{7,5},{8,10},{9,11},{10,... | collective-permute-start | bytes 208904 | tf_op jit(solution)/shard_map/ppermute | solution.py:241
  46.9 2.3 %collective-permute-done.8 = f32[136,128]{1,0:T(8,128)S(1)} collective-permute-done((f32[136,128]{1,0:T(8,128)S(1)}, f32[136,128]{1,0:T(8,128)S(1)}, u32[]{:S(2)}, u32[]{:S(2)}) %collective-permute-start.8) | collective-permute-done | bytes 69664 | tf_op jit(solution)/shard_map/ppermute | solution.py:241
  49.2 5.9 %collective-permute-start.9 = (f32[136,128]{1,0:T(8,128)S(1)}, f32[136,128]{1,0:T(8,128)S(1)}, u32[]{:S(2)}, u32[]{:S(2)}) collective-permute-start(f32[136,128]{1,0:T(8,128)S(1)} %add.36.rest_2_), channel_id=1, source_target_pairs={{0,4},{1,5},{2,6},{3,7},{4,0},{5,1},{6,2},{7,3},{8,12},{9,13},{10,... | collective-permute-start | bytes 208904 | tf_op jit(solution)/shard_map/ppermute | solution.py:241
  55.1 2.3 %collective-permute-done.9.rest_3_ = f32[136,128]{1,0:T(8,128)S(1)} collective-permute-done((f32[136,128]{1,0:T(8,128)S(1)}, f32[136,128]{1,0:T(8,128)S(1)}, u32[]{:S(2)}, u32[]{:S(2)}) %collective-permute-start.9) | collective-permute-done | bytes 69664 | tf_op jit(solution)/shard_map/ppermute | solution.py:241
  57.4 4.0 %shard_map.72 = (f32[128,128]{1,0:T(8,128)S(1)}, f32[8,128]{1,0:T(8,128)S(1)}, f32[264,128]{1,0:T(8,128)S(1)}, f32[264,128]{1,0:T(8,128)S(1)}) custom-call(s32[320]{0:T(512)S(1)} %copy-done.3, s32[320]{0:T(512)S(1)} %copy-done.4, s32[1,1]{1,0:T(1,128)S(6)} %copy.8.counts, bf16[160,256,128]{2,1,0:T(8,128)(2,1)S(1)} %get-tuple-element.26.rest_0_, ...), custom_call_target="tpu_custom_call" | custom-call | tf_op jit(solution)/shard_map/pallas_call | solution.py:253
  61.4 1.3 %collective-permute-done.10 = f32[264,128]{1,0:T(8,128)S(1)} collective-permute-done((f32[264,128]{1,0:T(8,128)S(1)}, f32[264,128]{1,0:T(8,128)S(1)}, u32[]{:S(2)}, u32[]{:S(2)}) %collective-permute-start.10) | collective-permute-done | bytes 135200 | tf_op jit(solution)/shard_map/ppermute | solution.py:241
  62.8 0.1 collective-permute-start.11
  62.9 5.6 %collective-permute-done.11 = f32[264,128]{1,0:T(8,128)S(1)} collective-permute-done((f32[264,128]{1,0:T(8,128)S(1)}, f32[264,128]{1,0:T(8,128)S(1)}, u32[]{:S(2)}, u32[]{:S(2)}) %collective-permute-start.11) | collective-permute-done | bytes 135200 | tf_op jit(solution)/shard_map/ppermute | solution.py:241
  68.6 1.3 %collective-permute-done.12.rest_3_ = f32[264,128]{1,0:T(8,128)S(1)} collective-permute-done((f32[264,128]{1,0:T(8,128)S(1)}, f32[264,128]{1,0:T(8,128)S(1)}, u32[]{:S(2)}, u32[]{:S(2)}) %collective-permute-start.12) | collective-permute-done | bytes 135200 | tf_op jit(solution)/shard_map/ppermute | solution.py:241
  69.9 5.4 %shard_map.73 = (f32[512,128]{1,0:T(8,128)S(1)}, f32[8,128]{1,0:T(8,128)S(1)}, f32[128,128]{1,0:T(8,128)S(1)}, f32[136,128]{1,0:T(8,128)S(1)}) custom-call(s32[320]{0:T(512)S(1)} %copy-done.3, s32[320]{0:T(512)S(1)} %copy-done.4, s32[1,1]{1,0:T(1,128)S(6)} %copy.8.counts, bf16[160,256,128]{2,1,0:T(8,128)(2,1)S(1)} %get-tuple-element.26.rest_0_, ...), custom_call_target="tpu_custom_call" | custom-call | tf_op jit(solution)/shard_map/pallas_call | solution.py:253
  75.3 0.6 collective-permute-start.13
  75.9 3.8 %collective-permute-done.13 = f32[136,128]{1,0:T(8,128)S(1)} collective-permute-done((f32[136,128]{1,0:T(8,128)S(1)}, f32[136,128]{1,0:T(8,128)S(1)}, u32[]{:S(2)}, u32[]{:S(2)}) %collective-permute-start.13) | collective-permute-done | bytes 69664 | tf_op jit(solution)/shard_map/ppermute | solution.py:241
  79.7 5.1 %collective-permute-start.14 = (f32[136,128]{1,0:T(8,128)S(1)}, f32[136,128]{1,0:T(8,128)S(1)}, u32[]{:S(2)}, u32[]{:S(2)}) collective-permute-start(f32[136,128]{1,0:T(8,128)S(1)} %add.39), channel_id=1, source_target_pairs={{0,2},{1,3},{2,0},{3,1},{4,6},{5,7},{6,4},{7,5},{8,10},{9,11},{10,... | collective-permute-start | bytes 208904 | tf_op jit(solution)/shard_map/ppermute | solution.py:241
  84.8 2.3 %collective-permute-done.14 = f32[136,128]{1,0:T(8,128)S(1)} collective-permute-done((f32[136,128]{1,0:T(8,128)S(1)}, f32[136,128]{1,0:T(8,128)S(1)}, u32[]{:S(2)}, u32[]{:S(2)}) %collective-permute-start.14) | collective-permute-done | bytes 69664 | tf_op jit(solution)/shard_map/ppermute | solution.py:241
  87.1 6.0 %collective-permute-start.15 = (f32[136,128]{1,0:T(8,128)S(1)}, f32[136,128]{1,0:T(8,128)S(1)}, u32[]{:S(2)}, u32[]{:S(2)}) collective-permute-start(f32[136,128]{1,0:T(8,128)S(1)} %add.40.rest_2_), channel_id=1, source_target_pairs={{0,4},{1,5},{2,6},{3,7},{4,0},{5,1},{6,2},{7,3},{8,12},{9,13},{10,... | collective-permute-start | bytes 208904 | tf_op jit(solution)/shard_map/ppermute | solution.py:241
  93.1 2.3 %collective-permute-done.15.rest_3_ = f32[136,128]{1,0:T(8,128)S(1)} collective-permute-done((f32[136,128]{1,0:T(8,128)S(1)}, f32[136,128]{1,0:T(8,128)S(1)}, u32[]{:S(2)}, u32[]{:S(2)}) %collective-permute-start.15) | collective-permute-done | bytes 69664 | tf_op jit(solution)/shard_map/ppermute | solution.py:241
  95.4 4.6 %shard_map.74 = (f32[128,128]{1,0:T(8,128)}, f32[8,128]{1,0:T(8,128)S(1)}, f32[264,128]{1,0:T(8,128)S(1)}, f32[264,128]{1,0:T(8,128)S(1)}) custom-call(s32[320]{0:T(512)S(1)} %copy-done.3, s32[320]{0:T(512)S(1)} %copy-done.4, s32[1,1]{1,0:T(1,128)S(6)} %copy.8.counts, bf16[160,256,128]{2,1,0:T(8,128)(2,1)S(1)} %get-tuple-element.26.rest_0_, ...), custom_call_target="tpu_custom_call" | custom-call | tf_op jit(solution)/shard_map/pallas_call | solution.py:253
  100.0 0.1 collective-permute-start.16
  100.1 1.3 %collective-permute-done.16 = f32[264,128]{1,0:T(8,128)S(1)} collective-permute-done((f32[264,128]{1,0:T(8,128)S(1)}, f32[264,128]{1,0:T(8,128)S(1)}, u32[]{:S(2)}, u32[]{:S(2)}) %collective-permute-start.16) | collective-permute-done | bytes 135200 | tf_op jit(solution)/shard_map/ppermute | solution.py:241
  101.4 0.1 collective-permute-start.17
  101.5 5.6 %collective-permute-done.17 = f32[264,128]{1,0:T(8,128)S(1)} collective-permute-done((f32[264,128]{1,0:T(8,128)S(1)}, f32[264,128]{1,0:T(8,128)S(1)}, u32[]{:S(2)}, u32[]{:S(2)}) %collective-permute-start.17) | collective-permute-done | bytes 135200 | tf_op jit(solution)/shard_map/ppermute | solution.py:241
  107.2 0.1 collective-permute-start.18
  107.3 1.3 %collective-permute-done.18.other = f32[264,128]{1,0:T(8,128)S(1)} collective-permute-done((f32[264,128]{1,0:T(8,128)S(1)}, f32[264,128]{1,0:T(8,128)S(1)}, u32[]{:S(2)}, u32[]{:S(2)}) %collective-permute-start.18) | collective-permute-done | bytes 135200 | tf_op jit(solution)/shard_map/ppermute | solution.py:241
  108.6 0.6 copy-done.11
  109.3 1.9 %shard_map.75 = (f32[512,128]{1,0:T(8,128)}, f32[8,128]{1,0:T(8,128)}, f32[128,128]{1,0:T(8,128)}, f32[8,128]{1,0:T(8,128)}) custom-call(f32[264,128]{1,0:T(8,128)} %copy-done.10, f32[264,128]{1,0:T(8,128)} %copy-done.11, f32[512,128]{1,0:T(8,128)} %copy-done, f32[8,128]{1,0:T(8,128)} %copy-done.6), custom_call_target="tpu_custom_call" | custom-call | tf_op jit(solution)/shard_map/pallas_call | solution.py:286
  111.2 0.5 collective-permute-start.19
  111.7 3.3 %collective-permute-done.19 = f32[8,128]{1,0:T(8,128)S(1)} collective-permute-done((f32[8,128]{1,0:T(8,128)}, f32[8,128]{1,0:T(8,128)S(1)}, u32[]{:S(2)}, u32[]{:S(2)}) %collective-permute-start.19) | collective-permute-done | bytes 4128 | tf_op jit(solution)/shard_map/ppermute | solution.py:241
  115.0 0.7 add.43.refs_8_
  115.7 6.8 %collective-permute-start.22 = (f32[8,128]{1,0:T(8,128)S(1)}, f32[8,128]{1,0:T(8,128)S(1)}, u32[]{:S(2)}, u32[]{:S(2)}) collective-permute-start(f32[8,128]{1,0:T(8,128)S(1)} %add.43.refs_8_), channel_id=1, source_target_pairs={{0,6},{1,7},{2,4},{3,5},{4,2},{5,3},{6,0},{7,1},{8,14},{9,15},{10,... | collective-permute-start | bytes 12296 | tf_op jit(solution)/shard_map/ppermute | solution.py:241
  122.6 0.6 collective-permute-start.20
  123.1 1.0 collective-permute-done.22.refs_11_
  124.1 2.9 %collective-permute-done.21.refs_10_ = f32[8,128]{1,0:T(8,128)S(1)} collective-permute-done((f32[8,128]{1,0:T(8,128)S(1)}, f32[8,128]{1,0:T(8,128)S(1)}, u32[]{:S(2)}, u32[]{:S(2)}) %collective-permute-start.21) | collective-permute-done | bytes 4128 | tf_op jit(solution)/shard_map/ppermute | solution.py:241
  127.1 0.6 copy-done.14
  127.7 1.6 %shard_map.76 = (f32[128,128]{1,0:T(8,128)}, f32[128,128]{1,0:T(8,128)}) custom-call(f32[128,128]{1,0:T(8,128)} %copy-done.1, f32[128,128]{1,0:T(8,128)} %copy-done.2, f32[128,128]{1,0:T(8,128)} %get-tuple-element.47.refs_2_, f32[8,128]{1,0:T(8,128)} %copy-done.7, f32[8,128]{1,0:T(8,128)} %copy-done.9, f32[8,128]{1,0:T(8,128)} %get-tuple-element.48.refs_5_, ...), custom_call_target="tpu_custom_call" | custom-call | tf_op jit(solution)/shard_map/pallas_call | solution.py:286
  (52 shorter events, 0.5 us)
Async XLA Ops:
  0.6 8.9 %collective-permute-start = (f32[16,128]{1,0:T(8,128)}, f32[16,128]{1,0:T(8,128)S(1)}, u32[]{:S(2)}, u32[]{:S(2)}) collective-permute-start(f32[16,128]{1,0:T(8,128)} %data.3), channel_id=1, source_target_pairs={{0,1},{1,0},{2,3},{3,2},{4,5},{5,4},{6,7},{7,6},{8,9},{9,8},{10,11... | collective-permute-start | bytes 24584 | tf_op jit(solution)/shard_map/ppermute | solution.py:241
  3.7 0.7 copy-start.5
  9.5 10.8 %collective-permute-start.3 = (f32[32,128]{1,0:T(8,128)S(1)}, f32[32,128]{1,0:T(8,128)S(1)}, u32[]{:S(2)}, u32[]{:S(2)}) collective-permute-start(f32[32,128]{1,0:T(8,128)S(1)} %constant_dynamic-update-slice_fusion.rest_2_), channel_id=1, source_target_pairs={{0,6},{1,7},{2,4},{3,5},{4,2},{5,3},{6,0},{7,1},{8,14},{9,15},{10,... | collective-permute-start | bytes 49160 | tf_op jit(solution)/shard_map/ppermute | solution.py:241
  13.2 7.1 %collective-permute-start.2 = (f32[32,128]{1,0:T(8,128)S(1)}, f32[32,128]{1,0:T(8,128)S(1)}, u32[]{:S(2)}, u32[]{:S(2)}) collective-permute-start(f32[32,128]{1,0:T(8,128)S(1)} %constant_dynamic-update-slice_fusion.rest_2_), channel_id=1, source_target_pairs={{0,4},{1,5},{2,6},{3,7},{4,0},{5,1},{6,2},{7,3},{8,12},{9,13},{10,... | collective-permute-start | bytes 49160 | tf_op jit(solution)/shard_map/ppermute | solution.py:241
  13.2 7.2 %collective-permute-start.1 = (f32[32,128]{1,0:T(8,128)S(1)}, f32[32,128]{1,0:T(8,128)S(1)}, u32[]{:S(2)}, u32[]{:S(2)}) collective-permute-start(f32[32,128]{1,0:T(8,128)S(1)} %constant_dynamic-update-slice_fusion.rest_2_), channel_id=1, source_target_pairs={{0,2},{1,3},{2,0},{3,1},{4,6},{5,7},{6,4},{7,5},{8,10},{9,11},{10,... | collective-permute-start | bytes 49160 | tf_op jit(solution)/shard_map/ppermute | solution.py:241
  14.6 5.7 %copy-start.3 = (s32[320]{0:T(512)S(1)}, s32[320]{0:T(512)}, u32[]{:S(2)}) copy-start(s32[320]{0:T(512)} %pick.9) | copy-start | bytes 3844
  14.6 5.7 %copy-start.4 = (s32[320]{0:T(512)S(1)}, s32[320]{0:T(512)}, u32[]{:S(2)}) copy-start(s32[320]{0:T(512)} %cell.9) | copy-start | bytes 3844
  24.3 1.4 %collective-permute-start.4 = (f32[264,128]{1,0:T(8,128)S(1)}, f32[264,128]{1,0:T(8,128)S(1)}, u32[]{:S(2)}, u32[]{:S(2)}) collective-permute-start(f32[264,128]{1,0:T(8,128)S(1)} %get-tuple-element.30), channel_id=1, source_target_pairs={{0,8},{8,0},{16,24},{24,16},{1,9},{9,1},{17,25},{25,17},{2,10},{10... | collective-permute-start | bytes 405512 | tf_op jit(solution)/shard_map/ppermute | solution.py:241
  25.8 5.7 %collective-permute-start.5 = (f32[264,128]{1,0:T(8,128)S(1)}, f32[264,128]{1,0:T(8,128)S(1)}, u32[]{:S(2)}, u32[]{:S(2)}) collective-permute-start(f32[264,128]{1,0:T(8,128)S(1)} %add.33), channel_id=1, source_target_pairs={{0,16},{8,24},{16,0},{24,8},{1,17},{9,25},{17,1},{25,9},{2,18},{10... | collective-permute-start | bytes 405512 | tf_op jit(solution)/shard_map/ppermute | solution.py:241
  31.5 1.4 %collective-permute-start.6 = (f32[264,128]{1,0:T(8,128)S(1)}, f32[264,128]{1,0:T(8,128)S(1)}, u32[]{:S(2)}, u32[]{:S(2)}) collective-permute-start(f32[264,128]{1,0:T(8,128)S(1)} %add.34.rest_2_), channel_id=1, source_target_pairs={{0,8},{8,0},{16,24},{24,16},{1,9},{9,1},{17,25},{25,17},{2,10},{10... | collective-permute-start | bytes 405512 | tf_op jit(solution)/shard_map/ppermute | solution.py:241
  38.2 8.6 %copy-start.1 = (f32[128,128]{1,0:T(8,128)}, f32[128,128]{1,0:T(8,128)S(1)}, u32[]{:S(2)}) copy-start(f32[128,128]{1,0:T(8,128)S(1)} %get-tuple-element.31.refs_0_) | copy-start | bytes 196612
  38.2 23.1 %copy-start.7 = (f32[8,128]{1,0:T(8,128)}, f32[8,128]{1,0:T(8,128)S(1)}, u32[]{:S(2)}) copy-start(f32[8,128]{1,0:T(8,128)S(1)} %get-tuple-element.34.rest_5_.refs_3_) | copy-start | bytes 12292
  38.3 4.4 %collective-permute-start.7 = (f32[136,128]{1,0:T(8,128)S(1)}, f32[136,128]{1,0:T(8,128)S(1)}, u32[]{:S(2)}, u32[]{:S(2)}) collective-permute-start(f32[136,128]{1,0:T(8,128)S(1)} %get-tuple-element.32), channel_id=1, source_target_pairs={{0,1},{1,0},{2,3},{3,2},{4,5},{5,4},{6,7},{7,6},{8,9},{9,8},{10,11... | collective-permute-start | bytes 208904 | tf_op jit(solution)/shard_map/ppermute | solution.py:241
  42.6 6.5 %collective-permute-start.8 = (f32[136,128]{1,0:T(8,128)S(1)}, f32[136,128]{1,0:T(8,128)S(1)}, u32[]{:S(2)}, u32[]{:S(2)}) collective-permute-start(f32[136,128]{1,0:T(8,128)S(1)} %add.35), channel_id=1, source_target_pairs={{0,2},{1,3},{2,0},{3,1},{4,6},{5,7},{6,4},{7,5},{8,10},{9,11},{10,... | collective-permute-start | bytes 208904 | tf_op jit(solution)/shard_map/ppermute | solution.py:241
  49.2 8.2 %collective-permute-start.9 = (f32[136,128]{1,0:T(8,128)S(1)}, f32[136,128]{1,0:T(8,128)S(1)}, u32[]{:S(2)}, u32[]{:S(2)}) collective-permute-start(f32[136,128]{1,0:T(8,128)S(1)} %add.36.rest_2_), channel_id=1, source_target_pairs={{0,4},{1,5},{2,6},{3,7},{4,0},{5,1},{6,2},{7,3},{8,12},{9,13},{10,... | collective-permute-start | bytes 208904 | tf_op jit(solution)/shard_map/ppermute | solution.py:241
  61.3 14.0 %copy-start.8 = (f32[8,128]{1,0:T(8,128)}, f32[8,128]{1,0:T(8,128)S(1)}, u32[]{:S(2)}) copy-start(f32[8,128]{1,0:T(8,128)S(1)} %get-tuple-element.38.rest_5_.refs_6_) | copy-start | bytes 12292
  61.3 1.4 %collective-permute-start.10 = (f32[264,128]{1,0:T(8,128)S(1)}, f32[264,128]{1,0:T(8,128)S(1)}, u32[]{:S(2)}, u32[]{:S(2)}) collective-permute-start(f32[264,128]{1,0:T(8,128)S(1)} %get-tuple-element.36), channel_id=1, source_target_pairs={{0,8},{8,0},{16,24},{24,16},{1,9},{9,1},{17,25},{25,17},{2,10},{10... | collective-permute-start | bytes 405512 | tf_op jit(solution)/shard_map/ppermute | solution.py:241
  62.8 5.7 %collective-permute-start.11 = (f32[264,128]{1,0:T(8,128)S(1)}, f32[264,128]{1,0:T(8,128)S(1)}, u32[]{:S(2)}, u32[]{:S(2)}) collective-permute-start(f32[264,128]{1,0:T(8,128)S(1)} %add.37), channel_id=1, source_target_pairs={{0,16},{8,24},{16,0},{24,8},{1,17},{9,25},{17,1},{25,9},{2,18},{10... | collective-permute-start | bytes 405512 | tf_op jit(solution)/shard_map/ppermute | solution.py:241
  68.5 1.4 %collective-permute-start.12 = (f32[264,128]{1,0:T(8,128)S(1)}, f32[264,128]{1,0:T(8,128)S(1)}, u32[]{:S(2)}, u32[]{:S(2)}) collective-permute-start(f32[264,128]{1,0:T(8,128)S(1)} %add.38.rest_2_), channel_id=1, source_target_pairs={{0,8},{8,0},{16,24},{24,16},{1,9},{9,1},{17,25},{25,17},{2,10},{10... | collective-permute-start | bytes 405512 | tf_op jit(solution)/shard_map/ppermute | solution.py:241
  75.3 20.1 %copy-start = (f32[512,128]{1,0:T(8,128)}, f32[512,128]{1,0:T(8,128)S(1)}, u32[]{:S(2)}) copy-start(f32[512,128]{1,0:T(8,128)S(1)} %get-tuple-element.45.v_old) | copy-start | bytes 786436
  75.3 24.7 %copy-start.2 = (f32[128,128]{1,0:T(8,128)}, f32[128,128]{1,0:T(8,128)S(1)}, u32[]{:S(2)}) copy-start(f32[128,128]{1,0:T(8,128)S(1)} %get-tuple-element.39.refs_1_) | copy-start | bytes 196612
  75.3 24.7 %copy-start.9 = (f32[8,128]{1,0:T(8,128)}, f32[8,128]{1,0:T(8,128)S(1)}, u32[]{:S(2)}) copy-start(f32[8,128]{1,0:T(8,128)S(1)} %get-tuple-element.42.rest_5_.refs_4_) | copy-start | bytes 12292
  75.3 4.4 %collective-permute-start.13 = (f32[136,128]{1,0:T(8,128)S(1)}, f32[136,128]{1,0:T(8,128)S(1)}, u32[]{:S(2)}, u32[]{:S(2)}) collective-permute-start(f32[136,128]{1,0:T(8,128)S(1)} %get-tuple-element.40), channel_id=1, source_target_pairs={{0,1},{1,0},{2,3},{3,2},{4,5},{5,4},{6,7},{7,6},{8,9},{9,8},{10,11... | collective-permute-start | bytes 208904 | tf_op jit(solution)/shard_map/ppermute | solution.py:241
  79.7 7.4 %collective-permute-start.14 = (f32[136,128]{1,0:T(8,128)S(1)}, f32[136,128]{1,0:T(8,128)S(1)}, u32[]{:S(2)}, u32[]{:S(2)}) collective-permute-start(f32[136,128]{1,0:T(8,128)S(1)} %add.39), channel_id=1, source_target_pairs={{0,2},{1,3},{2,0},{3,1},{4,6},{5,7},{6,4},{7,5},{8,10},{9,11},{10,... | collective-permute-start | bytes 208904 | tf_op jit(solution)/shard_map/ppermute | solution.py:241
  87.1 8.2 %collective-permute-start.15 = (f32[136,128]{1,0:T(8,128)S(1)}, f32[136,128]{1,0:T(8,128)S(1)}, u32[]{:S(2)}, u32[]{:S(2)}) collective-permute-start(f32[136,128]{1,0:T(8,128)S(1)} %add.40.rest_2_), channel_id=1, source_target_pairs={{0,4},{1,5},{2,6},{3,7},{4,0},{5,1},{6,2},{7,3},{8,12},{9,13},{10,... | collective-permute-start | bytes 208904 | tf_op jit(solution)/shard_map/ppermute | solution.py:241
  100.0 1.4 %copy-start.6 = (f32[8,128]{1,0:T(8,128)}, f32[8,128]{1,0:T(8,128)S(1)}, u32[]{:S(2)}) copy-start(f32[8,128]{1,0:T(8,128)S(1)} %get-tuple-element.46.alpha_old.refs_7_) | copy-start | bytes 12292
  100.0 1.4 %collective-permute-start.16 = (f32[264,128]{1,0:T(8,128)S(1)}, f32[264,128]{1,0:T(8,128)S(1)}, u32[]{:S(2)}, u32[]{:S(2)}) collective-permute-start(f32[264,128]{1,0:T(8,128)S(1)} %get-tuple-element.44), channel_id=1, source_target_pairs={{0,8},{8,0},{16,24},{24,16},{1,9},{9,1},{17,25},{25,17},{2,10},{10... | collective-permute-start | bytes 405512 | tf_op jit(solution)/shard_map/ppermute | solution.py:241
  101.4 5.7 %collective-permute-start.17 = (f32[264,128]{1,0:T(8,128)S(1)}, f32[264,128]{1,0:T(8,128)S(1)}, u32[]{:S(2)}, u32[]{:S(2)}) collective-permute-start(f32[264,128]{1,0:T(8,128)S(1)} %add.41), channel_id=1, source_target_pairs={{0,16},{8,24},{16,0},{24,8},{1,17},{9,25},{17,1},{25,9},{2,18},{10... | collective-permute-start | bytes 405512 | tf_op jit(solution)/shard_map/ppermute | solution.py:241
  107.2 1.4 %copy-start.10 = (f32[264,128]{1,0:T(8,128)}, f32[264,128]{1,0:T(8,128)S(1)}, u32[]{:S(2)}) copy-start(f32[264,128]{1,0:T(8,128)S(1)} %add.42.mine) | copy-start | bytes 405508
  107.2 1.4 %collective-permute-start.18 = (f32[264,128]{1,0:T(8,128)S(1)}, f32[264,128]{1,0:T(8,128)S(1)}, u32[]{:S(2)}, u32[]{:S(2)}) collective-permute-start(f32[264,128]{1,0:T(8,128)S(1)} %add.42.mine), channel_id=1, source_target_pairs={{0,8},{8,0},{16,24},{24,16},{1,9},{9,1},{17,25},{25,17},{2,10},{10... | collective-permute-start | bytes 405512 | tf_op jit(solution)/shard_map/ppermute | solution.py:241
  108.6 0.7 copy-start.11
  111.2 3.8 %collective-permute-start.19 = (f32[8,128]{1,0:T(8,128)}, f32[8,128]{1,0:T(8,128)S(1)}, u32[]{:S(2)}, u32[]{:S(2)}) collective-permute-start(f32[8,128]{1,0:T(8,128)} %get-tuple-element.49), channel_id=1, source_target_pairs={{0,1},{1,0},{2,3},{3,2},{4,5},{5,4},{6,7},{7,6},{8,9},{9,8},{10,11... | collective-permute-start | bytes 12296 | tf_op jit(solution)/shard_map/ppermute | solution.py:241
  115.7 11.4 %copy-start.12 = (f32[8,128]{1,0:T(8,128)}, f32[8,128]{1,0:T(8,128)S(1)}, u32[]{:S(2)}) copy-start(f32[8,128]{1,0:T(8,128)S(1)} %add.43.refs_8_) | copy-start | bytes 12292
  115.7 8.4 %collective-permute-start.22 = (f32[8,128]{1,0:T(8,128)S(1)}, f32[8,128]{1,0:T(8,128)S(1)}, u32[]{:S(2)}, u32[]{:S(2)}) collective-permute-start(f32[8,128]{1,0:T(8,128)S(1)} %add.43.refs_8_), channel_id=1, source_target_pairs={{0,6},{1,7},{2,4},{3,5},{4,2},{5,3},{6,0},{7,1},{8,14},{9,15},{10,... | collective-permute-start | bytes 12296 | tf_op jit(solution)/shard_map/ppermute | solution.py:241
  122.5 4.5 %collective-permute-start.21 = (f32[8,128]{1,0:T(8,128)S(1)}, f32[8,128]{1,0:T(8,128)S(1)}, u32[]{:S(2)}, u32[]{:S(2)}) collective-permute-start(f32[8,128]{1,0:T(8,128)S(1)} %add.43.refs_8_), channel_id=1, source_target_pairs={{0,4},{1,5},{2,6},{3,7},{4,0},{5,1},{6,2},{7,3},{8,12},{9,13},{10,... | collective-permute-start | bytes 12296 | tf_op jit(solution)/shard_map/ppermute | solution.py:241
  122.6 4.5 %collective-permute-start.20 = (f32[8,128]{1,0:T(8,128)S(1)}, f32[8,128]{1,0:T(8,128)S(1)}, u32[]{:S(2)}, u32[]{:S(2)}) collective-permute-start(f32[8,128]{1,0:T(8,128)S(1)} %add.43.refs_8_), channel_id=1, source_target_pairs={{0,2},{1,3},{2,0},{3,1},{4,6},{5,7},{6,4},{7,5},{8,10},{9,11},{10,... | collective-permute-start | bytes 12296 | tf_op jit(solution)/shard_map/ppermute | solution.py:241
  124.1 2.9 %copy-start.13 = (f32[8,128]{1,0:T(8,128)}, f32[8,128]{1,0:T(8,128)S(1)}, u32[]{:S(2)}) copy-start(f32[8,128]{1,0:T(8,128)S(1)} %collective-permute-done.22.refs_11_) | copy-start | bytes 12292
  127.1 0.6 copy-start.14
  127.1 0.6 copy-start.15

commit v5 on v3

--- a/solution.py
+++ b/solution.py
@@ -12,10 +12,10 @@
 ITERS = 2
 B = 128
 SUB = 8
-GROUP = 16
+GROUP = 32
 PARTS = 2
-STEP = 16
-BUFFERS = 4
+STEP = 32
+BUFFERS = 3
 TAIL = 8
 
 
@@ -155,14 +155,17 @@
     adjoint_tail(n_rows, parts, pick, cell, counts, u_out[...], keep, send, table, *accs)
 
 
-def next_adjoint(n_rows, pick, cell, counts, *rest):
+def next_adjoint(last, n_rows, pick, cell, counts, *rest):
     parts = rest[:PARTS]
-    mine, other, u_old, beta_old, u_out, alpha_out, keep, send, table, *accs = rest[PARTS:]
+    mine, other, u_old, beta_old, *rest = rest[PARTS:]
+    u_out = None if last else rest.pop(0)
+    alpha_out, keep, send, table, *accs = rest
     total = mine[...] + other[...]
     alpha = jnp.sqrt(total[PBLK:])
     alpha_out[...] = alpha
     u = total[:PBLK] / alpha[:1] - alpha[:1] * (u_old[...] / beta_old[:1])
-    u_out[...] = u
+    if not last:
+        u_out[...] = u
     adjoint_tail(n_rows, parts, pick, cell, counts, u, keep, send, table, *accs)
 
 
@@ -194,10 +197,8 @@
     out[pl.ds(PBLK, TAIL), :] = square
 
 
-def last_vector(n_rows, mine, other, v_old, alpha_old, v_out, beta_out, own_out, square_out):
-    _, square_out[...] = cell_vector(
-        n_rows, mine, other, v_old, alpha_old, v_out, beta_out, own_out
-    )
+def last_vector(n_rows, mine, other, v_old, alpha_old, beta_out, own_out, square_out, v):
+    _, square_out[...] = cell_vector(n_rows, mine, other, v_old, alpha_old, v, beta_out, own_out)
 
 
 def finish(*refs):
@@ -270,12 +271,14 @@
     )(kernels, data)
 
 
-def simple_call(kernel, outs, arrays):
+def simple_call(kernel, outs, arrays, scratch=()):
     return pl.pallas_call(
         kernel,
         out_shape=outs,
         in_specs=[VECTOR] * len(arrays),
         out_specs=[VECTOR] * len(outs),
+        scratch_shapes=scratch,
+        compiler_params=pltpu.CompilerParams(vmem_limit_bytes=4 << 20),
     )(*arrays)
 
 
@@ -324,20 +327,23 @@
         while 2 * bit < n_cols:
             product = product + swapped(product, "cols", n_cols, bit)
             bit *= 2
-        upick, alpha, keep, send = call(
-            functools.partial(next_adjoint, n_rows),
-            [shape(PBLK, B), shape(TAIL, B), shape(half, B), shape(half, B)],
+        last = step == ITERS - 1
+        *passed, alpha, keep, send = call(
+            functools.partial(next_adjoint, last, n_rows),
+            [shape(PBLK, B)] * (not last) + [shape(TAIL, B), shape(half, B), shape(half, B)],
             PBLK,
             CBLK,
             scalars,
             tiles + [product, swapped(product, "cols", n_cols, bit), upick, beta],
         )
+        upick = passed[0] if passed else None
         alphas.append(alpha)
         old = [vcell, alpha]
-    _, beta, block, square = simple_call(
+    beta, block, square = simple_call(
         functools.partial(last_vector, n_rows),
-        [shape(CBLK, B), shape(TAIL, B), shape(own, B), shape(TAIL, B)],
+        [shape(TAIL, B), shape(own, B), shape(TAIL, B)],
         sum_cells(keep, send) + old,
+        [pltpu.VMEM((CBLK, B), jnp.float32)],
     )
     blocks.append(block)
     betas.append(beta)

time: 129 us -> 115 us (0.89)
  Pallas kernels: 46.2 us -> 31.4 us
  starting transfers between devices: 27.7 us -> 32.4 us
    pallas_call x5, Pallas kernels: 32.6 us -> 20.8 us  [call(): pl.pallas_call(kernel, out_shape=outs, in_specs=[SCALAR] * len(scalars) +...]
    ppermute x23, starting transfers between devices: 27.7 us -> 32.4 us  [swapped(): return lax.ppermute(block, axis, [(i, i ^ bit) for i in range(size)])]
    pallas_call x2, Pallas kernels: 3.57 us -> 0.95 us  [simple_call(): pl.pallas_call(kernel, out_shape=outs, in_specs=[VECTOR] * len(arrays), o...]
  transfers between devices with their start and end apart: 23 -> 23, of which waited for: 18 -> 19; matrix products, arithmetic and copies ran while one was open for 0% -> 0% of each run, Pallas kernels for 8% -> 8%
where the time goes in v5:
time: 115 us; the launch traced here: 114 us
  waiting for transfers between devices  48.2 us (42%)
  starting transfers between devices  32.4 us (28%)
  Pallas kernels  31.4 us (27%)
  between operations  1.53 us (1%)
    ppermute x23, waiting for transfers between devices, swapped(): return lax.ppermute(block, axis, [(i, i ^ bit) for i in range(size)])  48.2 us
    ppermute x23, starting transfers between devices, swapped(): return lax.ppermute(block, axis, [(i, i ^ bit) for i in range(size)])  32.4 us
    pallas_call x5, Pallas kernels, call(): pl.pallas_call(kernel, out_shape=outs, in_specs=[SCALAR] * len(scalars) +...  20.8 us
    pallas_call x2, Pallas kernels, split_part(): pl.pallas_call(functools.partial(split_tiles, part * size), out_shape=[pl...  9.62 us
  transfers between devices with their start and end apart: 23, of which 19 were waited for; matrix products, arithmetic and copies ran while one was open for 0% of the time, Pallas kernels for 8%

profile of v5, /device:TPU:0, one launch (start us, length us, event | category | flops | bytes accessed | tf_op | source)
XLA Modules:
  0.0 114.4 jit_solution(1026622271946014156)
XLA Ops:
  0.6 3.0 %collective-permute-start = (f32[16,128]{1,0:T(8,128)}, f32[16,128]{1,0:T(8,128)S(1)}, u32[]{:S(2)}, u32[]{:S(2)}) collective-permute-start(f32[16,128]{1,0:T(8,128)} %data.3), channel_id=1, source_target_pairs={{0,1},{1,0},{2,3},{3,2},{4,5},{5,4},{6,7},{7,6},{8,9},{9,8},{10,11... | collective-permute-start | bytes 24584 | tf_op jit(solution)/shard_map/ppermute | solution.py:230
  3.7 0.7 copy-done.2
  4.4 4.5 %shard_map.68 = (bf16[160,256,128]{2,1,0:T(8,128)(2,1)S(1)}, f32[16,128]{1,0:T(8,128)S(1)}) custom-call(f32[320,128,128]{2,1,0:T(8,128)} %tiles.3, f32[16,128]{1,0:T(8,128)S(1)} %copy-done.2), custom_call_target="tpu_custom_call" | custom-call | flops 10485760 | bytes 10485760 | tf_op jit(solution)/shard_map/pallas_call | solution.py:258
  8.9 3.7 %collective-permute-start.3 = (f32[32,128]{1,0:T(8,128)S(1)}, f32[32,128]{1,0:T(8,128)S(1)}, u32[]{:S(2)}, u32[]{:S(2)}) collective-permute-start(f32[32,128]{1,0:T(8,128)S(1)} %constant_dynamic-update-slice_fusion.rest_2_), channel_id=1, source_target_pairs={{0,6},{1,7},{2,4},{3,5},{4,2},{5,3},{6,0},{7,1},{8,14},{9,15},{10,... | collective-permute-start | bytes 49160 | tf_op jit(solution)/shard_map/ppermute | solution.py:230
  12.6 0.8 collective-permute-start.1
  14.1 5.1 %shard_map.69 = (bf16[160,256,128]{2,1,0:T(8,128)(2,1)S(1)}, f32[16,128]{1,0:T(8,128)}) custom-call(f32[320,128,128]{2,1,0:T(8,128)} %tiles.3, f32[16,128]{1,0:T(8,128)S(1)} %copy-done.2), custom_call_target="tpu_custom_call" | custom-call | flops 10485760 | bytes 10485760 | tf_op jit(solution)/shard_map/pallas_call | solution.py:258
  19.2 3.6 %shard_map.70 = (f32[128,128]{1,0:T(8,128)S(1)}, f32[264,128]{1,0:T(8,128)S(1)}, f32[264,128]{1,0:T(8,128)S(1)}) custom-call(s32[320]{0:T(512)S(1)} %copy-done, s32[320]{0:T(512)S(1)} %copy-done.1, s32[1,1]{1,0:T(1,128)S(6)} %copy.8.counts, bf16[160,256,128]{2,1,0:T(8,128)(2,1)S(1)} %get-tuple-element.26.rest_0_, ...), custom_call_target="tpu_custom_call" | custom-call | tf_op jit(solution)/shard_map/pallas_call | solution.py:242
  22.8 0.1 collective-permute-start.4
  22.9 1.3 %collective-permute-done.4 = f32[264,128]{1,0:T(8,128)S(1)} collective-permute-done((f32[264,128]{1,0:T(8,128)S(1)}, f32[264,128]{1,0:T(8,128)S(1)}, u32[]{:S(2)}, u32[]{:S(2)}) %collective-permute-start.4) | collective-permute-done | bytes 135200 | tf_op jit(solution)/shard_map/ppermute | solution.py:230
  24.2 1.2 %collective-permute-start.5 = (f32[264,128]{1,0:T(8,128)S(1)}, f32[264,128]{1,0:T(8,128)S(1)}, u32[]{:S(2)}, u32[]{:S(2)}) collective-permute-start(f32[264,128]{1,0:T(8,128)S(1)} %add.33), channel_id=1, source_target_pairs={{0,16},{8,24},{16,0},{24,8},{1,17},{9,25},{17,1},{25,9},{2,18},{10... | collective-permute-start | bytes 405512 | tf_op jit(solution)/shard_map/ppermute | solution.py:230
  25.5 4.5 %collective-permute-done.5 = f32[264,128]{1,0:T(8,128)S(1)} collective-permute-done((f32[264,128]{1,0:T(8,128)S(1)}, f32[264,128]{1,0:T(8,128)S(1)}, u32[]{:S(2)}, u32[]{:S(2)}) %collective-permute-start.5) | collective-permute-done | bytes 135200 | tf_op jit(solution)/shard_map/ppermute | solution.py:230
  30.1 1.3 %collective-permute-done.6.rest_3_ = f32[264,128]{1,0:T(8,128)S(1)} collective-permute-done((f32[264,128]{1,0:T(8,128)S(1)}, f32[264,128]{1,0:T(8,128)S(1)}, u32[]{:S(2)}, u32[]{:S(2)}) %collective-permute-start.6) | collective-permute-done | bytes 135200 | tf_op jit(solution)/shard_map/ppermute | solution.py:230
  31.4 5.0 %shard_map.71 = (f32[512,128]{1,0:T(8,128)S(1)}, f32[8,128]{1,0:T(8,128)S(1)}, f32[128,128]{1,0:T(8,128)S(1)}, f32[136,128]{1,0:T(8,128)S(1)}) custom-call(s32[320]{0:T(512)S(1)} %copy-done, s32[320]{0:T(512)S(1)} %copy-done.1, s32[1,1]{1,0:T(1,128)S(6)} %copy.8.counts, bf16[160,256,128]{2,1,0:T(8,128)(2,1)S(1)} %get-tuple-element.26.rest_0_, ...), custom_call_target="tpu_custom_call" | custom-call | tf_op jit(solution)/shard_map/pallas_call | solution.py:242
  36.4 0.1 collective-permute-start.7
  36.5 4.3 %collective-permute-done.7 = f32[136,128]{1,0:T(8,128)S(1)} collective-permute-done((f32[136,128]{1,0:T(8,128)S(1)}, f32[136,128]{1,0:T(8,128)S(1)}, u32[]{:S(2)}, u32[]{:S(2)}) %collective-permute-start.7) | collective-permute-done | bytes 69664 | tf_op jit(solution)/shard_map/ppermute | solution.py:230
  40.8 1.8 %collective-permute-start.8 = (f32[136,128]{1,0:T(8,128)S(1)}, f32[136,128]{1,0:T(8,128)S(1)}, u32[]{:S(2)}, u32[]{:S(2)}) collective-permute-start(f32[136,128]{1,0:T(8,128)S(1)} %add.35), channel_id=1, source_target_pairs={{0,2},{1,3},{2,0},{3,1},{4,6},{5,7},{6,4},{7,5},{8,10},{9,11},{10,... | collective-permute-start | bytes 208904 | tf_op jit(solution)/shard_map/ppermute | solution.py:230
  42.7 2.5 %collective-permute-done.8 = f32[136,128]{1,0:T(8,128)S(1)} collective-permute-done((f32[136,128]{1,0:T(8,128)S(1)}, f32[136,128]{1,0:T(8,128)S(1)}, u32[]{:S(2)}, u32[]{:S(2)}) %collective-permute-start.8) | collective-permute-done | bytes 69664 | tf_op jit(solution)/shard_map/ppermute | solution.py:230
  45.2 6.4 %collective-permute-start.9 = (f32[136,128]{1,0:T(8,128)S(1)}, f32[136,128]{1,0:T(8,128)S(1)}, u32[]{:S(2)}, u32[]{:S(2)}) collective-permute-start(f32[136,128]{1,0:T(8,128)S(1)} %add.36.rest_2_), channel_id=1, source_target_pairs={{0,4},{1,5},{2,6},{3,7},{4,0},{5,1},{6,2},{7,3},{8,12},{9,13},{10,... | collective-permute-start | bytes 208904 | tf_op jit(solution)/shard_map/ppermute | solution.py:230
  51.7 2.5 %collective-permute-done.9.rest_3_ = f32[136,128]{1,0:T(8,128)S(1)} collective-permute-done((f32[136,128]{1,0:T(8,128)S(1)}, f32[136,128]{1,0:T(8,128)S(1)}, u32[]{:S(2)}, u32[]{:S(2)}) %collective-permute-start.9) | collective-permute-done | bytes 69664 | tf_op jit(solution)/shard_map/ppermute | solution.py:230
  54.1 3.6 %shard_map.72 = (f32[128,128]{1,0:T(8,128)S(1)}, f32[8,128]{1,0:T(8,128)S(1)}, f32[264,128]{1,0:T(8,128)S(1)}, f32[264,128]{1,0:T(8,128)S(1)}) custom-call(s32[320]{0:T(512)S(1)} %copy-done, s32[320]{0:T(512)S(1)} %copy-done.1, s32[1,1]{1,0:T(1,128)S(6)} %copy.8.counts, bf16[160,256,128]{2,1,0:T(8,128)(2,1)S(1)} %get-tuple-element.26.rest_0_, ...), custom_call_target="tpu_custom_call" | custom-call | tf_op jit(solution)/shard_map/pallas_call | solution.py:242
  57.7 0.1 collective-permute-start.10
  57.8 1.3 %collective-permute-done.10 = f32[264,128]{1,0:T(8,128)S(1)} collective-permute-done((f32[264,128]{1,0:T(8,128)S(1)}, f32[264,128]{1,0:T(8,128)S(1)}, u32[]{:S(2)}, u32[]{:S(2)}) %collective-permute-start.10) | collective-permute-done | bytes 135200 | tf_op jit(solution)/shard_map/ppermute | solution.py:230
  59.1 0.2 collective-permute-start.11
  59.3 5.5 %collective-permute-done.11 = f32[264,128]{1,0:T(8,128)S(1)} collective-permute-done((f32[264,128]{1,0:T(8,128)S(1)}, f32[264,128]{1,0:T(8,128)S(1)}, u32[]{:S(2)}, u32[]{:S(2)}) %collective-permute-start.11) | collective-permute-done | bytes 135200 | tf_op jit(solution)/shard_map/ppermute | solution.py:230
  64.9 0.1 collective-permute-start.12
  64.9 1.3 %collective-permute-done.12.rest_3_ = f32[264,128]{1,0:T(8,128)S(1)} collective-permute-done((f32[264,128]{1,0:T(8,128)S(1)}, f32[264,128]{1,0:T(8,128)S(1)}, u32[]{:S(2)}, u32[]{:S(2)}) %collective-permute-start.12) | collective-permute-done | bytes 135200 | tf_op jit(solution)/shard_map/ppermute | solution.py:230
  66.3 5.1 %shard_map.73 = (f32[512,128]{1,0:T(8,128)S(1)}, f32[8,128]{1,0:T(8,128)S(1)}, f32[128,128]{1,0:T(8,128)S(1)}, f32[136,128]{1,0:T(8,128)S(1)}) custom-call(s32[320]{0:T(512)S(1)} %copy-done, s32[320]{0:T(512)S(1)} %copy-done.1, s32[1,1]{1,0:T(1,128)S(6)} %copy.8.counts, bf16[160,256,128]{2,1,0:T(8,128)(2,1)S(1)} %get-tuple-element.26.rest_0_, ...), custom_call_target="tpu_custom_call" | custom-call | tf_op jit(solution)/shard_map/pallas_call | solution.py:242
  71.4 4.3 %collective-permute-done.13 = f32[136,128]{1,0:T(8,128)S(1)} collective-permute-done((f32[136,128]{1,0:T(8,128)S(1)}, f32[136,128]{1,0:T(8,128)S(1)}, u32[]{:S(2)}, u32[]{:S(2)}) %collective-permute-start.13) | collective-permute-done | bytes 69664 | tf_op jit(solution)/shard_map/ppermute | solution.py:230
  75.8 2.8 %collective-permute-start.14 = (f32[136,128]{1,0:T(8,128)S(1)}, f32[136,128]{1,0:T(8,128)S(1)}, u32[]{:S(2)}, u32[]{:S(2)}) collective-permute-start(f32[136,128]{1,0:T(8,128)S(1)} %add.39), channel_id=1, source_target_pairs={{0,2},{1,3},{2,0},{3,1},{4,6},{5,7},{6,4},{7,5},{8,10},{9,11},{10,... | collective-permute-start | bytes 208904 | tf_op jit(solution)/shard_map/ppermute | solution.py:230
  78.5 2.3 %collective-permute-done.14 = f32[136,128]{1,0:T(8,128)S(1)} collective-permute-done((f32[136,128]{1,0:T(8,128)S(1)}, f32[136,128]{1,0:T(8,128)S(1)}, u32[]{:S(2)}, u32[]{:S(2)}) %collective-permute-start.14) | collective-permute-done | bytes 69664 | tf_op jit(solution)/shard_map/ppermute | solution.py:230
  80.9 6.3 %collective-permute-start.15 = (f32[136,128]{1,0:T(8,128)S(1)}, f32[136,128]{1,0:T(8,128)S(1)}, u32[]{:S(2)}, u32[]{:S(2)}) collective-permute-start(f32[136,128]{1,0:T(8,128)S(1)} %add.40.rest_2_), channel_id=1, source_target_pairs={{0,4},{1,5},{2,6},{3,7},{4,0},{5,1},{6,2},{7,3},{8,12},{9,13},{10,... | collective-permute-start | bytes 208904 | tf_op jit(solution)/shard_map/ppermute | solution.py:230
  87.2 2.5 %collective-permute-done.15.rest_3_ = f32[136,128]{1,0:T(8,128)S(1)} collective-permute-done((f32[136,128]{1,0:T(8,128)S(1)}, f32[136,128]{1,0:T(8,128)S(1)}, u32[]{:S(2)}, u32[]{:S(2)}) %collective-permute-start.15) | collective-permute-done | bytes 69664 | tf_op jit(solution)/shard_map/ppermute | solution.py:230
  89.7 3.6 %shard_map.74 = (f32[8,128]{1,0:T(8,128)S(1)}, f32[264,128]{1,0:T(8,128)S(1)}, f32[264,128]{1,0:T(8,128)S(1)}) custom-call(s32[320]{0:T(512)S(1)} %copy-done, s32[320]{0:T(512)S(1)} %copy-done.1, s32[1,1]{1,0:T(1,128)S(6)} %copy.8.counts, bf16[160,256,128]{2,1,0:T(8,128)(2,1)S(1)} %get-tuple-element.26.rest_0_, ...), custom_call_target="tpu_custom_call" | custom-call | tf_op jit(solution)/shard_map/pallas_call | solution.py:242
  93.2 0.1 collective-permute-start.16
  93.3 1.3 %collective-permute-done.16 = f32[264,128]{1,0:T(8,128)S(1)} collective-permute-done((f32[264,128]{1,0:T(8,128)S(1)}, f32[264,128]{1,0:T(8,128)S(1)}, u32[]{:S(2)}, u32[]{:S(2)}) %collective-permute-start.16) | collective-permute-done | bytes 135200 | tf_op jit(solution)/shard_map/ppermute | solution.py:230
  94.7 0.1 collective-permute-start.17
  94.8 5.6 %collective-permute-done.17 = f32[264,128]{1,0:T(8,128)S(1)} collective-permute-done((f32[264,128]{1,0:T(8,128)S(1)}, f32[264,128]{1,0:T(8,128)S(1)}, u32[]{:S(2)}, u32[]{:S(2)}) %collective-permute-start.17) | collective-permute-done | bytes 135200 | tf_op jit(solution)/shard_map/ppermute | solution.py:230
  100.5 1.3 %collective-permute-done.18.other = f32[264,128]{1,0:T(8,128)S(1)} collective-permute-done((f32[264,128]{1,0:T(8,128)S(1)}, f32[264,128]{1,0:T(8,128)S(1)}, u32[]{:S(2)}, u32[]{:S(2)}) %collective-permute-start.18) | collective-permute-done | bytes 135200 | tf_op jit(solution)/shard_map/ppermute | solution.py:230
  101.8 0.3 shard_map.75
  102.1 0.5 collective-permute-start.19
  102.6 3.2 %collective-permute-done.19 = f32[8,128]{1,0:T(8,128)S(1)} collective-permute-done((f32[8,128]{1,0:T(8,128)S(1)}, f32[8,128]{1,0:T(8,128)S(1)}, u32[]{:S(2)}, u32[]{:S(2)}) %collective-permute-start.19) | collective-permute-done | bytes 4128 | tf_op jit(solution)/shard_map/ppermute | solution.py:230
  105.7 3.2 %collective-permute-start.22 = (f32[8,128]{1,0:T(8,128)S(1)}, f32[8,128]{1,0:T(8,128)S(1)}, u32[]{:S(2)}, u32[]{:S(2)}) collective-permute-start(f32[8,128]{1,0:T(8,128)S(1)} %add.43.refs_8_), channel_id=1, source_target_pairs={{0,6},{1,7},{2,4},{3,5},{4,2},{5,3},{6,0},{7,1},{8,14},{9,15},{10,... | collective-permute-start | bytes 12296 | tf_op jit(solution)/shard_map/ppermute | solution.py:230
  108.9 1.1 collective-permute-start.21
  110.0 0.6 collective-permute-start.20
  110.6 0.5 collective-permute-done.22.refs_11_
  111.1 2.3 %collective-permute-done.21.refs_10_ = f32[8,128]{1,0:T(8,128)S(1)} collective-permute-done((f32[8,128]{1,0:T(8,128)S(1)}, f32[8,128]{1,0:T(8,128)S(1)}, u32[]{:S(2)}, u32[]{:S(2)}) %collective-permute-start.21) | collective-permute-done | bytes 4128 | tf_op jit(solution)/shard_map/ppermute | solution.py:230
  113.5 0.2 collective-permute-done.20.refs_9_
  113.6 0.7 shard_map.76
  (26 shorter events, 0.4 us)
Async XLA Ops:
  0.6 8.3 %collective-permute-start = (f32[16,128]{1,0:T(8,128)}, f32[16,128]{1,0:T(8,128)S(1)}, u32[]{:S(2)}, u32[]{:S(2)}) collective-permute-start(f32[16,128]{1,0:T(8,128)} %data.3), channel_id=1, source_target_pairs={{0,1},{1,0},{2,3},{3,2},{4,5},{5,4},{6,7},{7,6},{8,9},{9,8},{10,11... | collective-permute-start | bytes 24584 | tf_op jit(solution)/shard_map/ppermute | solution.py:230
  3.7 0.7 copy-start.2
  8.9 10.2 %collective-permute-start.3 = (f32[32,128]{1,0:T(8,128)S(1)}, f32[32,128]{1,0:T(8,128)S(1)}, u32[]{:S(2)}, u32[]{:S(2)}) collective-permute-start(f32[32,128]{1,0:T(8,128)S(1)} %constant_dynamic-update-slice_fusion.rest_2_), channel_id=1, source_target_pairs={{0,6},{1,7},{2,4},{3,5},{4,2},{5,3},{6,0},{7,1},{8,14},{9,15},{10,... | collective-permute-start | bytes 49160 | tf_op jit(solution)/shard_map/ppermute | solution.py:230
  12.6 6.6 %collective-permute-start.2 = (f32[32,128]{1,0:T(8,128)S(1)}, f32[32,128]{1,0:T(8,128)S(1)}, u32[]{:S(2)}, u32[]{:S(2)}) collective-permute-start(f32[32,128]{1,0:T(8,128)S(1)} %constant_dynamic-update-slice_fusion.rest_2_), channel_id=1, source_target_pairs={{0,4},{1,5},{2,6},{3,7},{4,0},{5,1},{6,2},{7,3},{8,12},{9,13},{10,... | collective-permute-start | bytes 49160 | tf_op jit(solution)/shard_map/ppermute | solution.py:230
  12.6 6.6 %collective-permute-start.1 = (f32[32,128]{1,0:T(8,128)S(1)}, f32[32,128]{1,0:T(8,128)S(1)}, u32[]{:S(2)}, u32[]{:S(2)}) collective-permute-start(f32[32,128]{1,0:T(8,128)S(1)} %constant_dynamic-update-slice_fusion.rest_2_), channel_id=1, source_target_pairs={{0,2},{1,3},{2,0},{3,1},{4,6},{5,7},{6,4},{7,5},{8,10},{9,11},{10,... | collective-permute-start | bytes 49160 | tf_op jit(solution)/shard_map/ppermute | solution.py:230
  14.0 5.2 %copy-start = (s32[320]{0:T(512)S(1)}, s32[320]{0:T(512)}, u32[]{:S(2)}) copy-start(s32[320]{0:T(512)} %pick.9) | copy-start | bytes 3844
  14.1 5.2 %copy-start.1 = (s32[320]{0:T(512)S(1)}, s32[320]{0:T(512)}, u32[]{:S(2)}) copy-start(s32[320]{0:T(512)} %cell.9) | copy-start | bytes 3844
  22.8 1.4 %collective-permute-start.4 = (f32[264,128]{1,0:T(8,128)S(1)}, f32[264,128]{1,0:T(8,128)S(1)}, u32[]{:S(2)}, u32[]{:S(2)}) collective-permute-start(f32[264,128]{1,0:T(8,128)S(1)} %get-tuple-element.30), channel_id=1, source_target_pairs={{0,8},{8,0},{16,24},{24,16},{1,9},{9,1},{17,25},{25,17},{2,10},{10... | collective-permute-start | bytes 405512 | tf_op jit(solution)/shard_map/ppermute | solution.py:230
  24.2 5.7 %collective-permute-start.5 = (f32[264,128]{1,0:T(8,128)S(1)}, f32[264,128]{1,0:T(8,128)S(1)}, u32[]{:S(2)}, u32[]{:S(2)}) collective-permute-start(f32[264,128]{1,0:T(8,128)S(1)} %add.33), channel_id=1, source_target_pairs={{0,16},{8,24},{16,0},{24,8},{1,17},{9,25},{17,1},{25,9},{2,18},{10... | collective-permute-start | bytes 405512 | tf_op jit(solution)/shard_map/ppermute | solution.py:230
  30.0 1.4 %collective-permute-start.6 = (f32[264,128]{1,0:T(8,128)S(1)}, f32[264,128]{1,0:T(8,128)S(1)}, u32[]{:S(2)}, u32[]{:S(2)}) collective-permute-start(f32[264,128]{1,0:T(8,128)S(1)} %add.34.rest_2_), channel_id=1, source_target_pairs={{0,8},{8,0},{16,24},{24,16},{1,9},{9,1},{17,25},{25,17},{2,10},{10... | collective-permute-start | bytes 405512 | tf_op jit(solution)/shard_map/ppermute | solution.py:230
  36.4 4.4 %collective-permute-start.7 = (f32[136,128]{1,0:T(8,128)S(1)}, f32[136,128]{1,0:T(8,128)S(1)}, u32[]{:S(2)}, u32[]{:S(2)}) collective-permute-start(f32[136,128]{1,0:T(8,128)S(1)} %get-tuple-element.32), channel_id=1, source_target_pairs={{0,1},{1,0},{2,3},{3,2},{4,5},{5,4},{6,7},{7,6},{8,9},{9,8},{10,11... | collective-permute-start | bytes 208904 | tf_op jit(solution)/shard_map/ppermute | solution.py:230
  40.8 4.4 %collective-permute-start.8 = (f32[136,128]{1,0:T(8,128)S(1)}, f32[136,128]{1,0:T(8,128)S(1)}, u32[]{:S(2)}, u32[]{:S(2)}) collective-permute-start(f32[136,128]{1,0:T(8,128)S(1)} %add.35), channel_id=1, source_target_pairs={{0,2},{1,3},{2,0},{3,1},{4,6},{5,7},{6,4},{7,5},{8,10},{9,11},{10,... | collective-permute-start | bytes 208904 | tf_op jit(solution)/shard_map/ppermute | solution.py:230
  45.2 8.9 %collective-permute-start.9 = (f32[136,128]{1,0:T(8,128)S(1)}, f32[136,128]{1,0:T(8,128)S(1)}, u32[]{:S(2)}, u32[]{:S(2)}) collective-permute-start(f32[136,128]{1,0:T(8,128)S(1)} %add.36.rest_2_), channel_id=1, source_target_pairs={{0,4},{1,5},{2,6},{3,7},{4,0},{5,1},{6,2},{7,3},{8,12},{9,13},{10,... | collective-permute-start | bytes 208904 | tf_op jit(solution)/shard_map/ppermute | solution.py:230
  57.7 1.4 %collective-permute-start.10 = (f32[264,128]{1,0:T(8,128)S(1)}, f32[264,128]{1,0:T(8,128)S(1)}, u32[]{:S(2)}, u32[]{:S(2)}) collective-permute-start(f32[264,128]{1,0:T(8,128)S(1)} %get-tuple-element.36), channel_id=1, source_target_pairs={{0,8},{8,0},{16,24},{24,16},{1,9},{9,1},{17,25},{25,17},{2,10},{10... | collective-permute-start | bytes 405512 | tf_op jit(solution)/shard_map/ppermute | solution.py:230
  59.1 5.7 %collective-permute-start.11 = (f32[264,128]{1,0:T(8,128)S(1)}, f32[264,128]{1,0:T(8,128)S(1)}, u32[]{:S(2)}, u32[]{:S(2)}) collective-permute-start(f32[264,128]{1,0:T(8,128)S(1)} %add.37), channel_id=1, source_target_pairs={{0,16},{8,24},{16,0},{24,8},{1,17},{9,25},{17,1},{25,9},{2,18},{10... | collective-permute-start | bytes 405512 | tf_op jit(solution)/shard_map/ppermute | solution.py:230
  64.9 1.4 %collective-permute-start.12 = (f32[264,128]{1,0:T(8,128)S(1)}, f32[264,128]{1,0:T(8,128)S(1)}, u32[]{:S(2)}, u32[]{:S(2)}) collective-permute-start(f32[264,128]{1,0:T(8,128)S(1)} %add.38.rest_2_), channel_id=1, source_target_pairs={{0,8},{8,0},{16,24},{24,16},{1,9},{9,1},{17,25},{25,17},{2,10},{10... | collective-permute-start | bytes 405512 | tf_op jit(solution)/shard_map/ppermute | solution.py:230
  71.4 4.4 %collective-permute-start.13 = (f32[136,128]{1,0:T(8,128)S(1)}, f32[136,128]{1,0:T(8,128)S(1)}, u32[]{:S(2)}, u32[]{:S(2)}) collective-permute-start(f32[136,128]{1,0:T(8,128)S(1)} %get-tuple-element.40), channel_id=1, source_target_pairs={{0,1},{1,0},{2,3},{3,2},{4,5},{5,4},{6,7},{7,6},{8,9},{9,8},{10,11... | collective-permute-start | bytes 208904 | tf_op jit(solution)/shard_map/ppermute | solution.py:230
  75.8 5.1 %collective-permute-start.14 = (f32[136,128]{1,0:T(8,128)S(1)}, f32[136,128]{1,0:T(8,128)S(1)}, u32[]{:S(2)}, u32[]{:S(2)}) collective-permute-start(f32[136,128]{1,0:T(8,128)S(1)} %add.39), channel_id=1, source_target_pairs={{0,2},{1,3},{2,0},{3,1},{4,6},{5,7},{6,4},{7,5},{8,10},{9,11},{10,... | collective-permute-start | bytes 208904 | tf_op jit(solution)/shard_map/ppermute | solution.py:230
  80.9 8.8 %collective-permute-start.15 = (f32[136,128]{1,0:T(8,128)S(1)}, f32[136,128]{1,0:T(8,128)S(1)}, u32[]{:S(2)}, u32[]{:S(2)}) collective-permute-start(f32[136,128]{1,0:T(8,128)S(1)} %add.40.rest_2_), channel_id=1, source_target_pairs={{0,4},{1,5},{2,6},{3,7},{4,0},{5,1},{6,2},{7,3},{8,12},{9,13},{10,... | collective-permute-start | bytes 208904 | tf_op jit(solution)/shard_map/ppermute | solution.py:230
  93.2 1.4 %collective-permute-start.16 = (f32[264,128]{1,0:T(8,128)S(1)}, f32[264,128]{1,0:T(8,128)S(1)}, u32[]{:S(2)}, u32[]{:S(2)}) collective-permute-start(f32[264,128]{1,0:T(8,128)S(1)} %get-tuple-element.44), channel_id=1, source_target_pairs={{0,8},{8,0},{16,24},{24,16},{1,9},{9,1},{17,25},{25,17},{2,10},{10... | collective-permute-start | bytes 405512 | tf_op jit(solution)/shard_map/ppermute | solution.py:230
  94.7 5.7 %collective-permute-start.17 = (f32[264,128]{1,0:T(8,128)S(1)}, f32[264,128]{1,0:T(8,128)S(1)}, u32[]{:S(2)}, u32[]{:S(2)}) collective-permute-start(f32[264,128]{1,0:T(8,128)S(1)} %add.41), channel_id=1, source_target_pairs={{0,16},{8,24},{16,0},{24,8},{1,17},{9,25},{17,1},{25,9},{2,18},{10... | collective-permute-start | bytes 405512 | tf_op jit(solution)/shard_map/ppermute | solution.py:230
  100.4 1.4 %collective-permute-start.18 = (f32[264,128]{1,0:T(8,128)S(1)}, f32[264,128]{1,0:T(8,128)S(1)}, u32[]{:S(2)}, u32[]{:S(2)}) collective-permute-start(f32[264,128]{1,0:T(8,128)S(1)} %add.42.mine), channel_id=1, source_target_pairs={{0,8},{8,0},{16,24},{24,16},{1,9},{9,1},{17,25},{25,17},{2,10},{10... | collective-permute-start | bytes 405512 | tf_op jit(solution)/shard_map/ppermute | solution.py:230
  102.1 3.7 %collective-permute-start.19 = (f32[8,128]{1,0:T(8,128)S(1)}, f32[8,128]{1,0:T(8,128)S(1)}, u32[]{:S(2)}, u32[]{:S(2)}) collective-permute-start(f32[8,128]{1,0:T(8,128)S(1)} %get-tuple-element.49), channel_id=1, source_target_pairs={{0,1},{1,0},{2,3},{3,2},{4,5},{5,4},{6,7},{7,6},{8,9},{9,8},{10,11... | collective-permute-start | bytes 12296 | tf_op jit(solution)/shard_map/ppermute | solution.py:230
  105.7 5.4 %collective-permute-start.22 = (f32[8,128]{1,0:T(8,128)S(1)}, f32[8,128]{1,0:T(8,128)S(1)}, u32[]{:S(2)}, u32[]{:S(2)}) collective-permute-start(f32[8,128]{1,0:T(8,128)S(1)} %add.43.refs_8_), channel_id=1, source_target_pairs={{0,6},{1,7},{2,4},{3,5},{4,2},{5,3},{6,0},{7,1},{8,14},{9,15},{10,... | collective-permute-start | bytes 12296 | tf_op jit(solution)/shard_map/ppermute | solution.py:230
  108.9 4.5 %collective-permute-start.21 = (f32[8,128]{1,0:T(8,128)S(1)}, f32[8,128]{1,0:T(8,128)S(1)}, u32[]{:S(2)}, u32[]{:S(2)}) collective-permute-start(f32[8,128]{1,0:T(8,128)S(1)} %add.43.refs_8_), channel_id=1, source_target_pairs={{0,4},{1,5},{2,6},{3,7},{4,0},{5,1},{6,2},{7,3},{8,12},{9,13},{10,... | collective-permute-start | bytes 12296 | tf_op jit(solution)/shard_map/ppermute | solution.py:230
  110.0 3.6 %collective-permute-start.20 = (f32[8,128]{1,0:T(8,128)S(1)}, f32[8,128]{1,0:T(8,128)S(1)}, u32[]{:S(2)}, u32[]{:S(2)}) collective-permute-start(f32[8,128]{1,0:T(8,128)S(1)} %add.43.refs_8_), channel_id=1, source_target_pairs={{0,2},{1,3},{2,0},{3,1},{4,6},{5,7},{6,4},{7,5},{8,10},{9,11},{10,... | collective-permute-start | bytes 12296 | tf_op jit(solution)/shard_map/ppermute | solution.py:230

commit v6 on v5

--- a/solution.py
+++ b/solution.py
@@ -12,7 +12,7 @@
 ITERS = 2
 B = 128
 SUB = 8
-GROUP = 32
+GROUP = 80
 PARTS = 2
 STEP = 32
 BUFFERS = 3
@@ -51,68 +51,66 @@
         lax.fori_loop(0, STEP, one, 0, unroll=4)
 
 
-def rows_of(ref, start, blocks):
-    return ref.at[pl.ds(start, blocks, stride=SUB), :]
-
-
 def fill_table(table, value):
-    high, low = split(value)
-    blocks = value.shape[0]
-    for start, term in enumerate((high, low, high, low)):
-        rows_of(table, start, blocks)[...] = term.astype(jnp.float32)
-
-
-def block_at(index):
-    return pl.ds(pl.multiple_of(index * SUB, SUB), SUB)
-
-
-def pair_transposed(tiles, one, two, first):
-    row = jnp.where(first, one, two).astype(jnp.bfloat16)
-    row = jnp.concatenate([row, row], axis=1)
-    both = jnp.dot(row, tiles, preferred_element_type=jnp.float32)
-    return both[:, :B], both[:, B:]
-
-
-def pair_forward(tiles, one, two, first):
-    zero = jnp.zeros_like(one)
-    row = jnp.concatenate([jnp.where(first, one, zero), jnp.where(first, zero, two)], axis=1)
-    both = lax.dot_general(
-        row.astype(jnp.bfloat16),
-        tiles,
-        (((1,), (1,)), ((), ())),
-        preferred_element_type=jnp.float32,
-    )
-    both = both[:, :B] + both[:, B:]
-    return both, both
-
-
-def over_tiles(parts, live, product, table, source, target, blocks, accs):
-    places = [(accs[0], 0), (accs[0], 1), (accs[1], 2), (accs[1], 3)]
-    for acc, start in places:
-        rows_of(acc, start, blocks)[...] = jnp.zeros((blocks, B), jnp.float32)
-    upper = lax.broadcasted_iota(jnp.int32, (SUB, B), 0) < 2
+    for index, term in enumerate(split(value)):
+        table[index] = term.astype(jnp.float32)
+
+
+def row_pair(table, source, slot, forward, at):
+    place = lax.broadcasted_iota(jnp.int32, (SUB, B), 0)
+
+    def term(n, index):
+        row = jnp.broadcast_to(table[index, pl.ds(source[slot + n], 1), :], (SUB, B))
+        return jnp.where(place == at + n, row, 0.0)
+
+    def both(*tiles):
+        terms = [sum(term(n, index) for n in tiles) for index in range(2)]
+        return jnp.concatenate(terms, axis=0).astype(jnp.bfloat16)
+
+    if forward:
+        return jnp.concatenate([both(0), both(1)], axis=1)
+    return jnp.concatenate([both(0, 1)] * 2, axis=1)
+
+
+def eight(tiles, base, table, source, slot, forward):
+    total = jnp.zeros((2 * SUB, 2 * B), jnp.float32)
+    over = ((1,), (1 if forward else 0,))
+    for k in range(0, SUB, 2):
+        pair = jnp.concatenate([tiles[base + k], tiles[base + k + 1]], axis=1)
+        row = row_pair(table, source, slot + k, forward, k)
+        total += lax.dot_general(row, pair, (over, ((), ())), preferred_element_type=jnp.float32)
+    total = total[:SUB] + total[SUB:]
+    if forward:
+        return total[:, :B] + total[:, B:]
+    odd = lax.rem(lax.broadcasted_iota(jnp.int32, (SUB, B), 0), 2) == 1
+    return jnp.where(odd, total[:, B:], total[:, :B])
+
+
+def over_tiles(parts, live, forward, table, source, targets, blocks, sums):
+    sums[...] = jnp.zeros_like(sums)
     first = 0
     for tiles in parts:
         size = tiles.shape[0]
         here = jnp.clip(live - first, 0, size)
 
         def some(group, carry, tiles=tiles, first=first):
-            base = group * GROUP
-            sums = []
-            for k in range(0, GROUP, 2):
-                slot = first + base + k
-                pair = jnp.concatenate([tiles[base + k], tiles[base + k + 1]], axis=1)
-                one, two = (table[block_at(source[slot + n]), :] for n in range(2))
-                sums.append(product(pair, one, two, upper))
-            for k in range(GROUP):
-                slot = first + base + k
-                place = block_at(jnp.where(slot < live, target[slot], blocks))
-                accs[k % 2][place, :] += sums[k // 2][k % 2]
+            for k in range(0, GROUP, SUB):
+                base = group * GROUP + k
+                slot = first + base
+                value = eight(tiles, base, table, source, slot, forward)
+                sums[pl.ds(pl.multiple_of(slot, SUB), SUB), :] = value
             return carry
 
         lax.fori_loop(0, (here + GROUP - 1) // GROUP, some, 0)
         first += size
-    return sum(rows_of(acc, start, blocks)[...] for acc, start in places)
+    slots = sums.shape[0]
+    block = lax.broadcasted_iota(jnp.int32, (blocks, slots), 0)
+    slot = lax.broadcasted_iota(jnp.int32, (1, slots), 1)
+    chosen = block == jnp.where(slot < live, targets[...], -1)
+    chosen = jnp.where(chosen, 1.0, 0.0).astype(jnp.bfloat16)
+    both = jnp.concatenate(split(sums[...]), axis=1)
+    total = jnp.dot(chosen, both, preferred_element_type=jnp.float32)
+    return total[:, :B] + total[:, B:]
 
 
 def halves(n_rows, cells):
@@ -120,9 +118,9 @@
     return size, [range(core, n_rows, 2) for core in range(2)]
 
 
-def adjoint_tail(n_rows, parts, pick, cell, counts, u, keep, send, table, *accs):
+def adjoint_tail(n_rows, parts, pick, cells, counts, u, keep, send, table, sums):
     fill_table(table, u)
-    whole = over_tiles(parts, counts[0, 0], pair_transposed, table, pick, cell, CBLK, accs)
+    whole = over_tiles(parts, counts[0, 0], False, table, pick, cells, CBLK, sums)
     square = jnp.full((TAIL, B), jnp.sum(u * u))
     size, _ = halves(n_rows, CBLK)
     core = lax.rem(lax.axis_index("rows"), 2)
@@ -142,8 +140,8 @@
     send[pl.ds(CBLK // 2, TAIL), :] = square
 
 
-def first_adjoint(n_rows, n_cols, pick, cell, counts, *rest):
-    parts, pieces, (u_out, keep, send, table, *accs) = rest[:PARTS], rest[PARTS:-6], rest[-6:]
+def first_adjoint(n_rows, n_cols, pick, counts, cells, *rest):
+    parts, pieces, (u_out, keep, send, table, sums) = rest[:PARTS], rest[PARTS:-5], rest[-5:]
     me = lax.axis_index("cols")
     offset = 0
     for piece in pieces:
@@ -152,21 +150,21 @@
             owner = jnp.bitwise_xor(me, offset)
             u_out[pl.ds(pl.multiple_of(owner * rows, rows), rows), :] = piece[pl.ds(at * rows, rows), :]
             offset += 1
-    adjoint_tail(n_rows, parts, pick, cell, counts, u_out[...], keep, send, table, *accs)
-
-
-def next_adjoint(last, n_rows, pick, cell, counts, *rest):
+    adjoint_tail(n_rows, parts, pick, cells, counts, u_out[...], keep, send, table, sums)
+
+
+def next_adjoint(last, n_rows, pick, counts, cells, *rest):
     parts = rest[:PARTS]
     mine, other, u_old, beta_old, *rest = rest[PARTS:]
     u_out = None if last else rest.pop(0)
-    alpha_out, keep, send, table, *accs = rest
+    alpha_out, keep, send, table, sums = rest
     total = mine[...] + other[...]
     alpha = jnp.sqrt(total[PBLK:])
     alpha_out[...] = alpha
     u = total[:PBLK] / alpha[:1] - alpha[:1] * (u_old[...] / beta_old[:1])
     if not last:
         u_out[...] = u
-    adjoint_tail(n_rows, parts, pick, cell, counts, u, keep, send, table, *accs)
+    adjoint_tail(n_rows, parts, pick, cells, counts, u, keep, send, table, sums)
 
 
 def cell_vector(n_rows, mine, other, v_old, alpha_old, v_out, beta_out, own_out):
@@ -187,13 +185,13 @@
     return v, jnp.full((TAIL, B), jnp.sum(v * v))
 
 
-def forward(first, n_rows, pick, cell, counts, *rest):
+def forward(first, n_rows, cell, counts, picks, *rest):
     parts, rest = rest[:PARTS], rest[PARTS:]
     old = (None, None) if first else rest[2:4]
-    v_out, beta_out, own_out, out, table, *accs = rest[-7:]
+    v_out, beta_out, own_out, out, table, sums = rest[-6:]
     v, square = cell_vector(n_rows, rest[0], rest[1], *old, v_out, beta_out, own_out)
     fill_table(table, v)
-    out[:PBLK, :] = over_tiles(parts, counts[0, 0], pair_forward, table, cell, pick, PBLK, accs)
+    out[:PBLK, :] = over_tiles(parts, counts[0, 0], True, table, cell, picks, PBLK, sums)
     out[pl.ds(PBLK, TAIL), :] = square
 
 
@@ -238,19 +236,19 @@
 SCALAR = pl.BlockSpec(memory_space=pltpu.SMEM)
 
 
-def call(kernel, outs, sources, targets, scalars, arrays):
+def call(kernel, outs, blocks, source, counts, targets, tiles, arrays):
+    slots = targets.shape[1]
     return pl.pallas_call(
         kernel,
         out_shape=outs,
-        in_specs=[SCALAR] * len(scalars) + [VECTOR] * len(arrays),
+        in_specs=[SCALAR] * 2 + [VECTOR] * (1 + len(tiles) + len(arrays)),
         out_specs=[VECTOR] * len(outs),
         scratch_shapes=[
-            pltpu.VMEM((sources * SUB, B), jnp.float32),
-            pltpu.VMEM(((targets + 1) * SUB, B), jnp.float32),
-            pltpu.VMEM(((targets + 1) * SUB, B), jnp.float32),
+            pltpu.VMEM((2, blocks, B), jnp.float32),
+            pltpu.VMEM((slots, B), jnp.float32),
         ],
-        compiler_params=pltpu.CompilerParams(vmem_limit_bytes=24 << 20),
-    )(*scalars, *arrays)
+        compiler_params=pltpu.CompilerParams(vmem_limit_bytes=16 << 20),
+    )(source, counts, targets, *tiles, *arrays)
 
 
 def split_part(kernels, data, part):
@@ -283,7 +281,9 @@
 
 
 def per_device(n_rows, n_cols, kernels, pick_index, cell_index, counts, data):
-    scalars = (pick_index, cell_index, counts)
+    slots = kernels.shape[0]
+    by_pick = (pick_index, counts, cell_index.reshape(1, slots))
+    by_cell = (cell_index, counts, pick_index.reshape(1, slots))
     half = CBLK // 2 + TAIL
     own = CBLK // n_rows
 
@@ -306,9 +306,9 @@
         functools.partial(first_adjoint, n_rows, n_cols),
         [shape(PBLK, B), shape(half, B), shape(half, B)],
         PBLK,
-        CBLK,
-        scalars,
-        tiles + pieces,
+        *by_pick,
+        tiles,
+        pieces,
     )
     old = []
     blocks, alphas, betas = [], [], []
@@ -317,9 +317,9 @@
             functools.partial(forward, step == 0, n_rows),
             [shape(CBLK, B), shape(TAIL, B), shape(own, B), shape(PBLK + TAIL, B)],
             CBLK,
-            PBLK,
-            scalars,
-            tiles + sum_cells(keep, send) + old,
+            *by_cell,
+            tiles,
+            sum_cells(keep, send) + old,
         )
         blocks.append(block)
         betas.append(beta)
@@ -332,9 +332,9 @@
             functools.partial(next_adjoint, last, n_rows),
             [shape(PBLK, B)] * (not last) + [shape(TAIL, B), shape(half, B), shape(half, B)],
             PBLK,
-            CBLK,
-            scalars,
-            tiles + [product, swapped(product, "cols", n_cols, bit), upick, beta],
+            *by_pick,
+            tiles,
+            [product, swapped(product, "cols", n_cols, bit), upick, beta],
         )
         upick = passed[0] if passed else None
         alphas.append(alpha)

time: 115 us -> 113 us (0.983)
  starting transfers between devices: 32.4 us -> 19.7 us
  waiting for transfers between devices: 48.2 us -> 54.6 us
  Pallas kernels: 31.4 us -> 36.7 us
    ppermute x23, starting transfers between devices: 32.4 us -> 19.7 us  [swapped(): return lax.ppermute(block, axis, [(i, i ^ bit) for i in range(size)])]
    ppermute x23, waiting for transfers between devices: 48.2 us -> 54.6 us  [swapped(): return lax.ppermute(block, axis, [(i, i ^ bit) for i in range(size)])]
    pallas_call x5, Pallas kernels: 20.8 us -> 26.2 us  [call(): pl.pallas_call(kernel, out_shape=outs, in_specs=[SCALAR] * 2 + [VECTOR] *...]
  transfers between devices with their start and end apart: 23 -> 23, of which waited for: 19 -> 18; matrix products, arithmetic and copies ran while one was open for 0% -> 0% of each run, Pallas kernels for 8% -> 8%
where the time goes in v6:
time: 113 us
  waiting for transfers between devices  54.6 us (48%)
  Pallas kernels  36.7 us (32%)
  starting transfers between devices  19.7 us (17%)
  between operations  1.58 us (1%)
    ppermute x23, waiting for transfers between devices, swapped(): return lax.ppermute(block, axis, [(i, i ^ bit) for i in range(size)])  54.6 us
    pallas_call x5, Pallas kernels, call(): pl.pallas_call(kernel, out_shape=outs, in_specs=[SCALAR] * 2 + [VECTOR] *...  26.2 us
    ppermute x23, starting transfers between devices, swapped(): return lax.ppermute(block, axis, [(i, i ^ bit) for i in range(size)])  19.7 us
    pallas_call x2, Pallas kernels, split_part(): pl.pallas_call(functools.partial(split_tiles, part * size), out_shape=[pl...  9.62 us
  transfers between devices with their start and end apart: 23, of which 18 were waited for; matrix products, arithmetic and copies ran while one was open for 0% of the time, Pallas kernels for 8%

profile of v6, /device:TPU:0, one launch (start us, length us, event | category | flops | bytes accessed | tf_op | source)
XLA Modules:
  0.0 113.4 jit_solution(950491317196245432)
XLA Ops:
  0.6 3.0 %collective-permute-start = (f32[16,128]{1,0:T(8,128)}, f32[16,128]{1,0:T(8,128)S(1)}, u32[]{:S(2)}, u32[]{:S(2)}) collective-permute-start(f32[16,128]{1,0:T(8,128)} %data.3), channel_id=1, source_target_pairs={{0,1},{1,0},{2,3},{3,2},{4,5},{5,4},{6,7},{7,6},{8,9},{9,8},{10,11... | collective-permute-start | bytes 24584 | tf_op jit(solution)/shard_map/ppermute | solution.py:228
  3.7 0.7 copy-done
  4.4 4.5 %shard_map.68 = (bf16[160,256,128]{2,1,0:T(8,128)(2,1)S(1)}, f32[16,128]{1,0:T(8,128)S(1)}) custom-call(f32[320,128,128]{2,1,0:T(8,128)} %tiles.3, f32[16,128]{1,0:T(8,128)S(1)} %copy-done), custom_call_target="tpu_custom_call" | custom-call | flops 10485760 | bytes 10485760 | tf_op jit(solution)/shard_map/pallas_call | solution.py:256
  9.0 3.7 %collective-permute-start.3 = (f32[32,128]{1,0:T(8,128)S(1)}, f32[32,128]{1,0:T(8,128)S(1)}, u32[]{:S(2)}, u32[]{:S(2)}) collective-permute-start(f32[32,128]{1,0:T(8,128)S(1)} %constant_dynamic-update-slice_fusion.rest_2_), channel_id=1, source_target_pairs={{0,6},{1,7},{2,4},{3,5},{4,2},{5,3},{6,0},{7,1},{8,14},{9,15},{10,... | collective-permute-start | bytes 49160 | tf_op jit(solution)/shard_map/ppermute | solution.py:228
  12.6 0.8 collective-permute-start.1
  14.1 5.1 %shard_map.69 = (bf16[160,256,128]{2,1,0:T(8,128)(2,1)S(1)}, f32[16,128]{1,0:T(8,128)}) custom-call(f32[320,128,128]{2,1,0:T(8,128)} %tiles.3, f32[16,128]{1,0:T(8,128)S(1)} %copy-done), custom_call_target="tpu_custom_call" | custom-call | flops 10485760 | bytes 10485760 | tf_op jit(solution)/shard_map/pallas_call | solution.py:256
  19.2 4.1 %shard_map.70 = (f32[128,128]{1,0:T(8,128)S(1)}, f32[264,128]{1,0:T(8,128)S(1)}, f32[264,128]{1,0:T(8,128)S(1)}) custom-call(s32[320]{0:T(512)S(1)} %copy-done.1, s32[1,1]{1,0:T(1,128)S(6)} %copy.8.counts, s32[1,320]{1,0:T(1,128)S(1)} %reshape.11.cells, bf16[160,256,128]{2,1,0:T(8,128)(2,1)S(1)} %get-tuple-element.26.rest_0_, ...), custom_call_target="tpu_custom_call" | custom-call | tf_op jit(solution)/shard_map/pallas_call | solution.py:241
  23.4 0.1 collective-permute-start.4
  23.5 1.3 %collective-permute-done.4 = f32[264,128]{1,0:T(8,128)S(1)} collective-permute-done((f32[264,128]{1,0:T(8,128)S(1)}, f32[264,128]{1,0:T(8,128)S(1)}, u32[]{:S(2)}, u32[]{:S(2)}) %collective-permute-start.4) | collective-permute-done | bytes 135200 | tf_op jit(solution)/shard_map/ppermute | solution.py:228
  24.8 0.1 collective-permute-start.5
  24.9 5.6 %collective-permute-done.5 = f32[264,128]{1,0:T(8,128)S(1)} collective-permute-done((f32[264,128]{1,0:T(8,128)S(1)}, f32[264,128]{1,0:T(8,128)S(1)}, u32[]{:S(2)}, u32[]{:S(2)}) %collective-permute-start.5) | collective-permute-done | bytes 135200 | tf_op jit(solution)/shard_map/ppermute | solution.py:228
  30.6 0.1 collective-permute-start.6
  30.6 1.3 %collective-permute-done.6.rest_3_ = f32[264,128]{1,0:T(8,128)S(1)} collective-permute-done((f32[264,128]{1,0:T(8,128)S(1)}, f32[264,128]{1,0:T(8,128)S(1)}, u32[]{:S(2)}, u32[]{:S(2)}) %collective-permute-start.6) | collective-permute-done | bytes 135200 | tf_op jit(solution)/shard_map/ppermute | solution.py:228
  32.0 6.9 %shard_map.71 = (f32[512,128]{1,0:T(8,128)S(1)}, f32[8,128]{1,0:T(8,128)S(1)}, f32[128,128]{1,0:T(8,128)S(1)}, f32[136,128]{1,0:T(8,128)S(1)}) custom-call(s32[320]{0:T(512)S(1)} %copy-done.2, s32[1,1]{1,0:T(1,128)S(6)} %copy.8.counts, s32[1,320]{1,0:T(1,128)S(1)} %reshape.10.picks, bf16[160,256,128]{2,1,0:T(8,128)(2,1)S(1)} %get-tuple-element.26.rest_0_, ...), custom_call_target="tpu_custom_call" | custom-call | tf_op jit(solution)/shard_map/pallas_call | solution.py:241
  38.9 0.1 collective-permute-start.7
  38.9 4.3 %collective-permute-done.7 = f32[136,128]{1,0:T(8,128)S(1)} collective-permute-done((f32[136,128]{1,0:T(8,128)S(1)}, f32[136,128]{1,0:T(8,128)S(1)}, u32[]{:S(2)}, u32[]{:S(2)}) %collective-permute-start.7) | collective-permute-done | bytes 69664 | tf_op jit(solution)/shard_map/ppermute | solution.py:228
  43.2 0.1 collective-permute-start.8
  43.3 4.3 %collective-permute-done.8 = f32[136,128]{1,0:T(8,128)S(1)} collective-permute-done((f32[136,128]{1,0:T(8,128)S(1)}, f32[136,128]{1,0:T(8,128)S(1)}, u32[]{:S(2)}, u32[]{:S(2)}) %collective-permute-start.8) | collective-permute-done | bytes 69664 | tf_op jit(solution)/shard_map/ppermute | solution.py:228
  47.6 2.7 %collective-permute-start.9 = (f32[136,128]{1,0:T(8,128)S(1)}, f32[136,128]{1,0:T(8,128)S(1)}, u32[]{:S(2)}, u32[]{:S(2)}) collective-permute-start(f32[136,128]{1,0:T(8,128)S(1)} %add.36.rest_2_), channel_id=1, source_target_pairs={{0,4},{1,5},{2,6},{3,7},{4,0},{5,1},{6,2},{7,3},{8,12},{9,13},{10,... | collective-permute-start | bytes 208904 | tf_op jit(solution)/shard_map/ppermute | solution.py:228
  50.3 2.6 %collective-permute-done.9.rest_3_ = f32[136,128]{1,0:T(8,128)S(1)} collective-permute-done((f32[136,128]{1,0:T(8,128)S(1)}, f32[136,128]{1,0:T(8,128)S(1)}, u32[]{:S(2)}, u32[]{:S(2)}) %collective-permute-start.9) | collective-permute-done | bytes 69664 | tf_op jit(solution)/shard_map/ppermute | solution.py:228
  52.9 4.1 %shard_map.72 = (f32[128,128]{1,0:T(8,128)S(1)}, f32[8,128]{1,0:T(8,128)S(1)}, f32[264,128]{1,0:T(8,128)S(1)}, f32[264,128]{1,0:T(8,128)S(1)}) custom-call(s32[320]{0:T(512)S(1)} %copy-done.1, s32[1,1]{1,0:T(1,128)S(6)} %copy.8.counts, s32[1,320]{1,0:T(1,128)S(1)} %reshape.11.cells, bf16[160,256,128]{2,1,0:T(8,128)(2,1)S(1)} %get-tuple-element.26.rest_0_, ...), custom_call_target="tpu_custom_call" | custom-call | tf_op jit(solution)/shard_map/pallas_call | solution.py:241
  57.0 0.1 collective-permute-start.10
  57.1 1.3 %collective-permute-done.10 = f32[264,128]{1,0:T(8,128)S(1)} collective-permute-done((f32[264,128]{1,0:T(8,128)S(1)}, f32[264,128]{1,0:T(8,128)S(1)}, u32[]{:S(2)}, u32[]{:S(2)}) %collective-permute-start.10) | collective-permute-done | bytes 135200 | tf_op jit(solution)/shard_map/ppermute | solution.py:228
  58.5 0.1 collective-permute-start.11
  58.6 5.6 %collective-permute-done.11 = f32[264,128]{1,0:T(8,128)S(1)} collective-permute-done((f32[264,128]{1,0:T(8,128)S(1)}, f32[264,128]{1,0:T(8,128)S(1)}, u32[]{:S(2)}, u32[]{:S(2)}) %collective-permute-start.11) | collective-permute-done | bytes 135200 | tf_op jit(solution)/shard_map/ppermute | solution.py:228
  64.2 0.1 collective-permute-start.12
  64.3 1.3 %collective-permute-done.12.rest_3_ = f32[264,128]{1,0:T(8,128)S(1)} collective-permute-done((f32[264,128]{1,0:T(8,128)S(1)}, f32[264,128]{1,0:T(8,128)S(1)}, u32[]{:S(2)}, u32[]{:S(2)}) %collective-permute-start.12) | collective-permute-done | bytes 135200 | tf_op jit(solution)/shard_map/ppermute | solution.py:228
  65.6 6.9 %shard_map.73 = (f32[512,128]{1,0:T(8,128)S(1)}, f32[8,128]{1,0:T(8,128)S(1)}, f32[128,128]{1,0:T(8,128)S(1)}, f32[136,128]{1,0:T(8,128)S(1)}) custom-call(s32[320]{0:T(512)S(1)} %copy-done.2, s32[1,1]{1,0:T(1,128)S(6)} %copy.8.counts, s32[1,320]{1,0:T(1,128)S(1)} %reshape.10.picks, bf16[160,256,128]{2,1,0:T(8,128)(2,1)S(1)} %get-tuple-element.26.rest_0_, ...), custom_call_target="tpu_custom_call" | custom-call | tf_op jit(solution)/shard_map/pallas_call | solution.py:241
  72.5 0.1 collective-permute-start.13
  72.6 4.3 %collective-permute-done.13 = f32[136,128]{1,0:T(8,128)S(1)} collective-permute-done((f32[136,128]{1,0:T(8,128)S(1)}, f32[136,128]{1,0:T(8,128)S(1)}, u32[]{:S(2)}, u32[]{:S(2)}) %collective-permute-start.13) | collective-permute-done | bytes 69664 | tf_op jit(solution)/shard_map/ppermute | solution.py:228
  76.9 0.1 collective-permute-start.14
  77.0 4.3 %collective-permute-done.14 = f32[136,128]{1,0:T(8,128)S(1)} collective-permute-done((f32[136,128]{1,0:T(8,128)S(1)}, f32[136,128]{1,0:T(8,128)S(1)}, u32[]{:S(2)}, u32[]{:S(2)}) %collective-permute-start.14) | collective-permute-done | bytes 69664 | tf_op jit(solution)/shard_map/ppermute | solution.py:228
  81.3 3.5 %collective-permute-start.15 = (f32[136,128]{1,0:T(8,128)S(1)}, f32[136,128]{1,0:T(8,128)S(1)}, u32[]{:S(2)}, u32[]{:S(2)}) collective-permute-start(f32[136,128]{1,0:T(8,128)S(1)} %add.40.rest_2_), channel_id=1, source_target_pairs={{0,4},{1,5},{2,6},{3,7},{4,0},{5,1},{6,2},{7,3},{8,12},{9,13},{10,... | collective-permute-start | bytes 208904 | tf_op jit(solution)/shard_map/ppermute | solution.py:228
  84.8 2.3 %collective-permute-done.15.rest_3_ = f32[136,128]{1,0:T(8,128)S(1)} collective-permute-done((f32[136,128]{1,0:T(8,128)S(1)}, f32[136,128]{1,0:T(8,128)S(1)}, u32[]{:S(2)}, u32[]{:S(2)}) %collective-permute-start.15) | collective-permute-done | bytes 69664 | tf_op jit(solution)/shard_map/ppermute | solution.py:228
  87.1 4.1 %shard_map.74 = (f32[8,128]{1,0:T(8,128)S(1)}, f32[264,128]{1,0:T(8,128)S(1)}, f32[264,128]{1,0:T(8,128)S(1)}) custom-call(s32[320]{0:T(512)S(1)} %copy-done.1, s32[1,1]{1,0:T(1,128)S(6)} %copy.8.counts, s32[1,320]{1,0:T(1,128)S(1)} %reshape.11.cells, bf16[160,256,128]{2,1,0:T(8,128)(2,1)S(1)} %get-tuple-element.26.rest_0_, ...), custom_call_target="tpu_custom_call" | custom-call | tf_op jit(solution)/shard_map/pallas_call | solution.py:241
  91.2 0.1 collective-permute-start.16
  91.3 1.3 %collective-permute-done.16 = f32[264,128]{1,0:T(8,128)S(1)} collective-permute-done((f32[264,128]{1,0:T(8,128)S(1)}, f32[264,128]{1,0:T(8,128)S(1)}, u32[]{:S(2)}, u32[]{:S(2)}) %collective-permute-start.16) | collective-permute-done | bytes 135200 | tf_op jit(solution)/shard_map/ppermute | solution.py:228
  92.7 0.1 collective-permute-start.17
  92.8 5.6 %collective-permute-done.17 = f32[264,128]{1,0:T(8,128)S(1)} collective-permute-done((f32[264,128]{1,0:T(8,128)S(1)}, f32[264,128]{1,0:T(8,128)S(1)}, u32[]{:S(2)}, u32[]{:S(2)}) %collective-permute-start.17) | collective-permute-done | bytes 135200 | tf_op jit(solution)/shard_map/ppermute | solution.py:228
  98.4 0.1 collective-permute-start.18
  98.5 1.3 %collective-permute-done.18.other = f32[264,128]{1,0:T(8,128)S(1)} collective-permute-done((f32[264,128]{1,0:T(8,128)S(1)}, f32[264,128]{1,0:T(8,128)S(1)}, u32[]{:S(2)}, u32[]{:S(2)}) %collective-permute-start.18) | collective-permute-done | bytes 135200 | tf_op jit(solution)/shard_map/ppermute | solution.py:228
  99.8 0.3 shard_map.75
  100.2 3.6 %collective-permute-done.19 = f32[8,128]{1,0:T(8,128)S(1)} collective-permute-done((f32[8,128]{1,0:T(8,128)S(1)}, f32[8,128]{1,0:T(8,128)S(1)}, u32[]{:S(2)}, u32[]{:S(2)}) %collective-permute-start.19) | collective-permute-done | bytes 4128 | tf_op jit(solution)/shard_map/ppermute | solution.py:228
  103.8 4.5 %collective-permute-start.22 = (f32[8,128]{1,0:T(8,128)S(1)}, f32[8,128]{1,0:T(8,128)S(1)}, u32[]{:S(2)}, u32[]{:S(2)}) collective-permute-start(f32[8,128]{1,0:T(8,128)S(1)} %add.43.refs_8_), channel_id=1, source_target_pairs={{0,6},{1,7},{2,4},{3,5},{4,2},{5,3},{6,0},{7,1},{8,14},{9,15},{10,... | collective-permute-start | bytes 12296 | tf_op jit(solution)/shard_map/ppermute | solution.py:228
  108.2 0.6 collective-permute-start.20
  108.8 1.0 collective-permute-done.22.refs_11_
  109.8 2.9 %collective-permute-done.21.refs_10_ = f32[8,128]{1,0:T(8,128)S(1)} collective-permute-done((f32[8,128]{1,0:T(8,128)S(1)}, f32[8,128]{1,0:T(8,128)S(1)}, u32[]{:S(2)}, u32[]{:S(2)}) %collective-permute-start.21) | collective-permute-done | bytes 4128 | tf_op jit(solution)/shard_map/ppermute | solution.py:228
  112.7 0.7 shard_map.76
  (28 shorter events, 0.3 us)
Async XLA Ops:
  0.6 8.3 %collective-permute-start = (f32[16,128]{1,0:T(8,128)}, f32[16,128]{1,0:T(8,128)S(1)}, u32[]{:S(2)}, u32[]{:S(2)}) collective-permute-start(f32[16,128]{1,0:T(8,128)} %data.3), channel_id=1, source_target_pairs={{0,1},{1,0},{2,3},{3,2},{4,5},{5,4},{6,7},{7,6},{8,9},{9,8},{10,11... | collective-permute-start | bytes 24584 | tf_op jit(solution)/shard_map/ppermute | solution.py:228
  3.7 0.7 copy-start
  4.4 9.7 %copy-start.2 = (s32[320]{0:T(512)S(1)}, s32[320]{0:T(512)}, u32[]{:S(2)}) copy-start(s32[320]{0:T(512)} %cell.3) | copy-start | bytes 3844
  9.0 10.3 %collective-permute-start.3 = (f32[32,128]{1,0:T(8,128)S(1)}, f32[32,128]{1,0:T(8,128)S(1)}, u32[]{:S(2)}, u32[]{:S(2)}) collective-permute-start(f32[32,128]{1,0:T(8,128)S(1)} %constant_dynamic-update-slice_fusion.rest_2_), channel_id=1, source_target_pairs={{0,6},{1,7},{2,4},{3,5},{4,2},{5,3},{6,0},{7,1},{8,14},{9,15},{10,... | collective-permute-start | bytes 49160 | tf_op jit(solution)/shard_map/ppermute | solution.py:228
  12.6 6.6 %collective-permute-start.2 = (f32[32,128]{1,0:T(8,128)S(1)}, f32[32,128]{1,0:T(8,128)S(1)}, u32[]{:S(2)}, u32[]{:S(2)}) collective-permute-start(f32[32,128]{1,0:T(8,128)S(1)} %constant_dynamic-update-slice_fusion.rest_2_), channel_id=1, source_target_pairs={{0,4},{1,5},{2,6},{3,7},{4,0},{5,1},{6,2},{7,3},{8,12},{9,13},{10,... | collective-permute-start | bytes 49160 | tf_op jit(solution)/shard_map/ppermute | solution.py:228
  12.6 6.6 %collective-permute-start.1 = (f32[32,128]{1,0:T(8,128)S(1)}, f32[32,128]{1,0:T(8,128)S(1)}, u32[]{:S(2)}, u32[]{:S(2)}) collective-permute-start(f32[32,128]{1,0:T(8,128)S(1)} %constant_dynamic-update-slice_fusion.rest_2_), channel_id=1, source_target_pairs={{0,2},{1,3},{2,0},{3,1},{4,6},{5,7},{6,4},{7,5},{8,10},{9,11},{10,... | collective-permute-start | bytes 49160 | tf_op jit(solution)/shard_map/ppermute | solution.py:228
  14.1 5.2 %copy-start.1 = (s32[320]{0:T(512)S(1)}, s32[320]{0:T(512)}, u32[]{:S(2)}) copy-start(s32[320]{0:T(512)} %pick.5) | copy-start | bytes 3844
  23.4 1.4 %collective-permute-start.4 = (f32[264,128]{1,0:T(8,128)S(1)}, f32[264,128]{1,0:T(8,128)S(1)}, u32[]{:S(2)}, u32[]{:S(2)}) collective-permute-start(f32[264,128]{1,0:T(8,128)S(1)} %get-tuple-element.30), channel_id=1, source_target_pairs={{0,8},{8,0},{16,24},{24,16},{1,9},{9,1},{17,25},{25,17},{2,10},{10... | collective-permute-start | bytes 405512 | tf_op jit(solution)/shard_map/ppermute | solution.py:228
  24.8 5.7 %collective-permute-start.5 = (f32[264,128]{1,0:T(8,128)S(1)}, f32[264,128]{1,0:T(8,128)S(1)}, u32[]{:S(2)}, u32[]{:S(2)}) collective-permute-start(f32[264,128]{1,0:T(8,128)S(1)} %add.33), channel_id=1, source_target_pairs={{0,16},{8,24},{16,0},{24,8},{1,17},{9,25},{17,1},{25,9},{2,18},{10... | collective-permute-start | bytes 405512 | tf_op jit(solution)/shard_map/ppermute | solution.py:228
  30.6 1.4 %collective-permute-start.6 = (f32[264,128]{1,0:T(8,128)S(1)}, f32[264,128]{1,0:T(8,128)S(1)}, u32[]{:S(2)}, u32[]{:S(2)}) collective-permute-start(f32[264,128]{1,0:T(8,128)S(1)} %add.34.rest_2_), channel_id=1, source_target_pairs={{0,8},{8,0},{16,24},{24,16},{1,9},{9,1},{17,25},{25,17},{2,10},{10... | collective-permute-start | bytes 405512 | tf_op jit(solution)/shard_map/ppermute | solution.py:228
  38.9 4.4 %collective-permute-start.7 = (f32[136,128]{1,0:T(8,128)S(1)}, f32[136,128]{1,0:T(8,128)S(1)}, u32[]{:S(2)}, u32[]{:S(2)}) collective-permute-start(f32[136,128]{1,0:T(8,128)S(1)} %get-tuple-element.32), channel_id=1, source_target_pairs={{0,1},{1,0},{2,3},{3,2},{4,5},{5,4},{6,7},{7,6},{8,9},{9,8},{10,11... | collective-permute-start | bytes 208904 | tf_op jit(solution)/shard_map/ppermute | solution.py:228
  43.2 4.4 %collective-permute-start.8 = (f32[136,128]{1,0:T(8,128)S(1)}, f32[136,128]{1,0:T(8,128)S(1)}, u32[]{:S(2)}, u32[]{:S(2)}) collective-permute-start(f32[136,128]{1,0:T(8,128)S(1)} %add.35), channel_id=1, source_target_pairs={{0,2},{1,3},{2,0},{3,1},{4,6},{5,7},{6,4},{7,5},{8,10},{9,11},{10,... | collective-permute-start | bytes 208904 | tf_op jit(solution)/shard_map/ppermute | solution.py:228
  47.6 5.3 %collective-permute-start.9 = (f32[136,128]{1,0:T(8,128)S(1)}, f32[136,128]{1,0:T(8,128)S(1)}, u32[]{:S(2)}, u32[]{:S(2)}) collective-permute-start(f32[136,128]{1,0:T(8,128)S(1)} %add.36.rest_2_), channel_id=1, source_target_pairs={{0,4},{1,5},{2,6},{3,7},{4,0},{5,1},{6,2},{7,3},{8,12},{9,13},{10,... | collective-permute-start | bytes 208904 | tf_op jit(solution)/shard_map/ppermute | solution.py:228
  57.0 1.4 %collective-permute-start.10 = (f32[264,128]{1,0:T(8,128)S(1)}, f32[264,128]{1,0:T(8,128)S(1)}, u32[]{:S(2)}, u32[]{:S(2)}) collective-permute-start(f32[264,128]{1,0:T(8,128)S(1)} %get-tuple-element.36), channel_id=1, source_target_pairs={{0,8},{8,0},{16,24},{24,16},{1,9},{9,1},{17,25},{25,17},{2,10},{10... | collective-permute-start | bytes 405512 | tf_op jit(solution)/shard_map/ppermute | solution.py:228
  58.5 5.7 %collective-permute-start.11 = (f32[264,128]{1,0:T(8,128)S(1)}, f32[264,128]{1,0:T(8,128)S(1)}, u32[]{:S(2)}, u32[]{:S(2)}) collective-permute-start(f32[264,128]{1,0:T(8,128)S(1)} %add.37), channel_id=1, source_target_pairs={{0,16},{8,24},{16,0},{24,8},{1,17},{9,25},{17,1},{25,9},{2,18},{10... | collective-permute-start | bytes 405512 | tf_op jit(solution)/shard_map/ppermute | solution.py:228
  64.2 1.4 %collective-permute-start.12 = (f32[264,128]{1,0:T(8,128)S(1)}, f32[264,128]{1,0:T(8,128)S(1)}, u32[]{:S(2)}, u32[]{:S(2)}) collective-permute-start(f32[264,128]{1,0:T(8,128)S(1)} %add.38.rest_2_), channel_id=1, source_target_pairs={{0,8},{8,0},{16,24},{24,16},{1,9},{9,1},{17,25},{25,17},{2,10},{10... | collective-permute-start | bytes 405512 | tf_op jit(solution)/shard_map/ppermute | solution.py:228
  72.5 4.4 %collective-permute-start.13 = (f32[136,128]{1,0:T(8,128)S(1)}, f32[136,128]{1,0:T(8,128)S(1)}, u32[]{:S(2)}, u32[]{:S(2)}) collective-permute-start(f32[136,128]{1,0:T(8,128)S(1)} %get-tuple-element.40), channel_id=1, source_target_pairs={{0,1},{1,0},{2,3},{3,2},{4,5},{5,4},{6,7},{7,6},{8,9},{9,8},{10,11... | collective-permute-start | bytes 208904 | tf_op jit(solution)/shard_map/ppermute | solution.py:228
  76.9 4.4 %collective-permute-start.14 = (f32[136,128]{1,0:T(8,128)S(1)}, f32[136,128]{1,0:T(8,128)S(1)}, u32[]{:S(2)}, u32[]{:S(2)}) collective-permute-start(f32[136,128]{1,0:T(8,128)S(1)} %add.39), channel_id=1, source_target_pairs={{0,2},{1,3},{2,0},{3,1},{4,6},{5,7},{6,4},{7,5},{8,10},{9,11},{10,... | collective-permute-start | bytes 208904 | tf_op jit(solution)/shard_map/ppermute | solution.py:228
  81.3 5.8 %collective-permute-start.15 = (f32[136,128]{1,0:T(8,128)S(1)}, f32[136,128]{1,0:T(8,128)S(1)}, u32[]{:S(2)}, u32[]{:S(2)}) collective-permute-start(f32[136,128]{1,0:T(8,128)S(1)} %add.40.rest_2_), channel_id=1, source_target_pairs={{0,4},{1,5},{2,6},{3,7},{4,0},{5,1},{6,2},{7,3},{8,12},{9,13},{10,... | collective-permute-start | bytes 208904 | tf_op jit(solution)/shard_map/ppermute | solution.py:228
  91.2 1.4 %collective-permute-start.16 = (f32[264,128]{1,0:T(8,128)S(1)}, f32[264,128]{1,0:T(8,128)S(1)}, u32[]{:S(2)}, u32[]{:S(2)}) collective-permute-start(f32[264,128]{1,0:T(8,128)S(1)} %get-tuple-element.44), channel_id=1, source_target_pairs={{0,8},{8,0},{16,24},{24,16},{1,9},{9,1},{17,25},{25,17},{2,10},{10... | collective-permute-start | bytes 405512 | tf_op jit(solution)/shard_map/ppermute | solution.py:228
  92.7 5.7 %collective-permute-start.17 = (f32[264,128]{1,0:T(8,128)S(1)}, f32[264,128]{1,0:T(8,128)S(1)}, u32[]{:S(2)}, u32[]{:S(2)}) collective-permute-start(f32[264,128]{1,0:T(8,128)S(1)} %add.41), channel_id=1, source_target_pairs={{0,16},{8,24},{16,0},{24,8},{1,17},{9,25},{17,1},{25,9},{2,18},{10... | collective-permute-start | bytes 405512 | tf_op jit(solution)/shard_map/ppermute | solution.py:228
  98.4 1.4 %collective-permute-start.18 = (f32[264,128]{1,0:T(8,128)S(1)}, f32[264,128]{1,0:T(8,128)S(1)}, u32[]{:S(2)}, u32[]{:S(2)}) collective-permute-start(f32[264,128]{1,0:T(8,128)S(1)} %add.42.mine), channel_id=1, source_target_pairs={{0,8},{8,0},{16,24},{24,16},{1,9},{9,1},{17,25},{25,17},{2,10},{10... | collective-permute-start | bytes 405512 | tf_op jit(solution)/shard_map/ppermute | solution.py:228
  100.1 3.7 %collective-permute-start.19 = (f32[8,128]{1,0:T(8,128)S(1)}, f32[8,128]{1,0:T(8,128)S(1)}, u32[]{:S(2)}, u32[]{:S(2)}) collective-permute-start(f32[8,128]{1,0:T(8,128)S(1)} %get-tuple-element.49), channel_id=1, source_target_pairs={{0,1},{1,0},{2,3},{3,2},{4,5},{5,4},{6,7},{7,6},{8,9},{9,8},{10,11... | collective-permute-start | bytes 12296 | tf_op jit(solution)/shard_map/ppermute | solution.py:228
  103.8 6.0 %collective-permute-start.22 = (f32[8,128]{1,0:T(8,128)S(1)}, f32[8,128]{1,0:T(8,128)S(1)}, u32[]{:S(2)}, u32[]{:S(2)}) collective-permute-start(f32[8,128]{1,0:T(8,128)S(1)} %add.43.refs_8_), channel_id=1, source_target_pairs={{0,6},{1,7},{2,4},{3,5},{4,2},{5,3},{6,0},{7,1},{8,14},{9,15},{10,... | collective-permute-start | bytes 12296 | tf_op jit(solution)/shard_map/ppermute | solution.py:228
  108.2 4.5 %collective-permute-start.21 = (f32[8,128]{1,0:T(8,128)S(1)}, f32[8,128]{1,0:T(8,128)S(1)}, u32[]{:S(2)}, u32[]{:S(2)}) collective-permute-start(f32[8,128]{1,0:T(8,128)S(1)} %add.43.refs_8_), channel_id=1, source_target_pairs={{0,4},{1,5},{2,6},{3,7},{4,0},{5,1},{6,2},{7,3},{8,12},{9,13},{10,... | collective-permute-start | bytes 12296 | tf_op jit(solution)/shard_map/ppermute | solution.py:228
  108.2 4.5 %collective-permute-start.20 = (f32[8,128]{1,0:T(8,128)S(1)}, f32[8,128]{1,0:T(8,128)S(1)}, u32[]{:S(2)}, u32[]{:S(2)}) collective-permute-start(f32[8,128]{1,0:T(8,128)S(1)} %add.43.refs_8_), channel_id=1, source_target_pairs={{0,2},{1,3},{2,0},{3,1},{4,6},{5,7},{6,4},{7,5},{8,10},{9,11},{10,... | collective-permute-start | bytes 12296 | tf_op jit(solution)/shard_map/ppermute | solution.py:228

commit v7 on v6

--- a/solution.py
+++ b/solution.py
@@ -13,9 +13,12 @@
 B = 128
 SUB = 8
 GROUP = 80
-PARTS = 2
-STEP = 32
-BUFFERS = 3
+SHARES = (1, 1, 2)
+PARTS = len(SHARES)
+TURNED = 2
+STEP = 16
+BUFFERS = 4
+CHUNK = 32
 TAIL = 8
 
 
@@ -24,9 +27,10 @@
     return high, (value - high.astype(jnp.float32)).astype(jnp.bfloat16)
 
 
-def split_tiles(start, tiles, data, out, data_out, held, arrived):
+def split_tiles(start, tiles, data, out, data_out, held, arrived, passed):
     steps = out.shape[0] // STEP
-    data_out[...] = data[...]
+    through = pltpu.make_async_copy(data, data_out, passed)
+    through.start()
 
     def copy(step, slot):
         return pltpu.make_async_copy(
@@ -43,12 +47,28 @@
         copy(step, slot).wait()
 
         def one(k, carry):
-            high, low = split(held[slot, k])
-            out[step * STEP + k, :B, :] = high
-            out[step * STEP + k, B:, :] = low
+            for row in range(0, B, CHUNK):
+                high, low = split(held[slot, k, pl.ds(row, CHUNK), :])
+                out[step * STEP + k, pl.ds(row, CHUNK), :] = high
+                out[step * STEP + k, pl.ds(B + row, CHUNK), :] = low
             return carry
 
         lax.fori_loop(0, STEP, one, 0, unroll=4)
+    through.wait()
+
+
+def turn_tiles(*refs):
+    through = pltpu.make_async_copy(refs[TURNED], refs[TURNED + 1], refs[-1])
+    through.start()
+    for tiles, out in zip(refs[:TURNED], refs[TURNED + 2 : -1]):
+
+        def one(k, carry, tiles=tiles, out=out):
+            out[k, :B, :] = tiles[k, :B, :].T
+            out[k, B:, :] = tiles[k, B:, :].T
+            return carry
+
+        lax.fori_loop(0, tiles.shape[0], one, 0, unroll=4)
+    through.wait()
 
 
 def fill_table(table, value):
@@ -56,7 +76,7 @@
         table[index] = term.astype(jnp.float32)
 
 
-def row_pair(table, source, slot, forward, at):
+def row_pair(table, source, slot, at, turned):
     place = lax.broadcasted_iota(jnp.int32, (SUB, B), 0)
 
     def term(n, index):
@@ -67,37 +87,38 @@
         terms = [sum(term(n, index) for n in tiles) for index in range(2)]
         return jnp.concatenate(terms, axis=0).astype(jnp.bfloat16)
 
-    if forward:
+    if turned:
         return jnp.concatenate([both(0), both(1)], axis=1)
     return jnp.concatenate([both(0, 1)] * 2, axis=1)
 
 
-def eight(tiles, base, table, source, slot, forward):
+def eight(tiles, base, table, source, slot, turned):
     total = jnp.zeros((2 * SUB, 2 * B), jnp.float32)
-    over = ((1,), (1 if forward else 0,))
+    over = ((1,), (1 if turned else 0,))
     for k in range(0, SUB, 2):
         pair = jnp.concatenate([tiles[base + k], tiles[base + k + 1]], axis=1)
-        row = row_pair(table, source, slot + k, forward, k)
+        row = row_pair(table, source, slot + k, k, turned)
         total += lax.dot_general(row, pair, (over, ((), ())), preferred_element_type=jnp.float32)
     total = total[:SUB] + total[SUB:]
-    if forward:
+    if turned:
         return total[:, :B] + total[:, B:]
     odd = lax.rem(lax.broadcasted_iota(jnp.int32, (SUB, B), 0), 2) == 1
     return jnp.where(odd, total[:, B:], total[:, :B])
 
 
-def over_tiles(parts, live, forward, table, source, targets, blocks, sums):
+def over_tiles(parts, live, table, source, targets, blocks, sums, turned=0):
     sums[...] = jnp.zeros_like(sums)
     first = 0
-    for tiles in parts:
+    for part, tiles in enumerate(parts):
         size = tiles.shape[0]
+        turn = part >= len(parts) - turned
         here = jnp.clip(live - first, 0, size)
 
-        def some(group, carry, tiles=tiles, first=first):
+        def some(group, carry, tiles=tiles, first=first, turn=turn):
             for k in range(0, GROUP, SUB):
                 base = group * GROUP + k
                 slot = first + base
-                value = eight(tiles, base, table, source, slot, forward)
+                value = eight(tiles, base, table, source, slot, turn)
                 sums[pl.ds(pl.multiple_of(slot, SUB), SUB), :] = value
             return carry
 
@@ -120,7 +141,7 @@
 
 def adjoint_tail(n_rows, parts, pick, cells, counts, u, keep, send, table, sums):
     fill_table(table, u)
-    whole = over_tiles(parts, counts[0, 0], False, table, pick, cells, CBLK, sums)
+    whole = over_tiles(parts, counts[0, 0], table, pick, cells, CBLK, sums)
     square = jnp.full((TAIL, B), jnp.sum(u * u))
     size, _ = halves(n_rows, CBLK)
     core = lax.rem(lax.axis_index("rows"), 2)
@@ -191,7 +212,7 @@
     v_out, beta_out, own_out, out, table, sums = rest[-6:]
     v, square = cell_vector(n_rows, rest[0], rest[1], *old, v_out, beta_out, own_out)
     fill_table(table, v)
-    out[:PBLK, :] = over_tiles(parts, counts[0, 0], True, table, cell, picks, PBLK, sums)
+    out[:PBLK, :] = over_tiles(parts, counts[0, 0], table, cell, picks, PBLK, sums, PARTS - TURNED)
     out[pl.ds(PBLK, TAIL), :] = square
 
 
@@ -247,26 +268,44 @@
             pltpu.VMEM((2, blocks, B), jnp.float32),
             pltpu.VMEM((slots, B), jnp.float32),
         ],
-        compiler_params=pltpu.CompilerParams(vmem_limit_bytes=16 << 20),
+        compiler_params=pltpu.CompilerParams(vmem_limit_bytes=12 << 20),
     )(source, counts, targets, *tiles, *arrays)
 
 
-def split_part(kernels, data, part):
-    size = kernels.shape[0] // PARTS
+def split_part(kernels, data, start, size):
+    if start == 0:
+        data = pltpu.with_memory_space_constraint(data, pltpu.HBM)
     return pl.pallas_call(
-        functools.partial(split_tiles, part * size),
+        functools.partial(split_tiles, start),
         out_shape=[pltpu.VMEM((size, 2 * B, B), jnp.bfloat16), shape(*data.shape)],
-        in_specs=[pl.BlockSpec(memory_space=pl.ANY), VECTOR],
+        in_specs=[pl.BlockSpec(memory_space=pltpu.HBM), pl.BlockSpec(memory_space=pl.ANY)],
         out_specs=[VECTOR, VECTOR],
         scratch_shapes=[
             pltpu.VMEM((BUFFERS, STEP, B, B), jnp.float32),
             pltpu.SemaphoreType.DMA((BUFFERS,)),
+            pltpu.SemaphoreType.DMA,
         ],
         cost_estimate=pl.CostEstimate(
             flops=4 * size * B * B, bytes_accessed=4 * size * B * B, transcendentals=0
         ),
-        compiler_params=pltpu.CompilerParams(vmem_limit_bytes=24 << 20),
+        compiler_params=pltpu.CompilerParams(vmem_limit_bytes=12 << 20),
     )(kernels, data)
+
+
+def turned(tiles, data):
+    total = sum(part.shape[0] for part in tiles)
+    data, *out = pl.pallas_call(
+        turn_tiles,
+        out_shape=[shape(*data.shape)] + [pltpu.VMEM(part.shape, part.dtype) for part in tiles],
+        in_specs=[VECTOR] * TURNED + [pl.BlockSpec(memory_space=pl.ANY)],
+        out_specs=[VECTOR] * (TURNED + 1),
+        scratch_shapes=[pltpu.SemaphoreType.DMA],
+        cost_estimate=pl.CostEstimate(
+            flops=0, bytes_accessed=2 * total * B * B, transcendentals=0
+        ),
+        compiler_params=pltpu.CompilerParams(vmem_limit_bytes=4 << 20),
+    )(*tiles, data)
+    return data, out
 
 
 def simple_call(kernel, outs, arrays, scratch=()):
@@ -287,21 +326,40 @@
     half = CBLK // 2 + TAIL
     own = CBLK // n_rows
 
+    transposed = []
+
     def sum_cells(keep, send):
         mine = keep + swapped(send, "rows", n_rows, 1)
         bit = 2
         while bit < n_rows:
-            mine = mine + swapped(mine, "rows", n_rows, bit)
+            other = swapped(mine, "rows", n_rows, bit)
+            if not transposed:
+                mine, parts = turned(tiles[:TURNED], mine)
+                transposed.extend(parts + tiles[TURNED:])
+            mine = mine + other
             bit *= 2
         return [mine, swapped(mine, "rows", n_rows, 1)]
 
-    partner = swapped(data, "cols", n_cols, 1)
-    tiles = [None] * PARTS
-    tiles[0], passed = split_part(kernels, data, 0)
-    for part in range(1, PARTS):
-        tiles[part], _ = split_part(kernels, data, part)
-    pair = jnp.concatenate([passed, partner], axis=0)
-    pieces = [pair] + [swapped(pair, "cols", n_cols, bit) for bit in range(2, n_cols, 2)]
+    kernels = pltpu.with_memory_space_constraint(kernels, pltpu.HBM)
+    tiles = []
+    held = data
+    partner = None
+    bit = 1
+    for share in SHARES:
+        if bit < n_cols:
+            held = held if partner is None else jnp.concatenate([held, partner], axis=0)
+            partner = swapped(held, "cols", n_cols, bit)
+            bit *= 2
+        start = sum(part.shape[0] for part in tiles)
+        part, passed = split_part(kernels, held, start, slots * share // sum(SHARES))
+        tiles.append(part)
+        if bit < n_cols:
+            held = passed
+    while bit < n_cols:
+        held = jnp.concatenate([held, partner], axis=0)
+        partner = swapped(held, "cols", n_cols, bit)
+        bit *= 2
+    pieces = [held, partner]
     upick, keep, send = call(
         functools.partial(first_adjoint, n_rows, n_cols),
         [shape(PBLK, B), shape(half, B), shape(half, B)],
@@ -313,13 +371,14 @@
     old = []
     blocks, alphas, betas = [], [], []
     for step in range(ITERS):
+        sums = sum_cells(keep, send)
         vcell, beta, block, product = call(
             functools.partial(forward, step == 0, n_rows),
             [shape(CBLK, B), shape(TAIL, B), shape(own, B), shape(PBLK + TAIL, B)],
             CBLK,
             *by_cell,
-            tiles,
-            sum_cells(keep, send) + old,
+            transposed,
+            sums + old,
         )
         blocks.append(block)
         betas.append(beta)

time: 113 us -> 110 us (0.973)
  waiting for transfers between devices: 54.6 us -> 42.7 us
  starting transfers between devices: 19.7 us -> 29.9 us
  Pallas kernels: 36.7 us -> 35.5 us
    ppermute x23 -> x22, waiting for transfers between devices: 54.6 us -> 42.7 us  [swapped(): return lax.ppermute(block, axis, [(i, i ^ bit) for i in range(size)])]
    ppermute x23 -> x22, starting transfers between devices: 19.7 us -> 29.9 us  [swapped(): return lax.ppermute(block, axis, [(i, i ^ bit) for i in range(size)])]
    pallas_call x5, Pallas kernels: 26.2 us -> 18.3 us  [call(): pl.pallas_call(kernel, out_shape=outs, in_specs=[SCALAR] * 2 + [VECTOR] *...]
    pallas_call x2 -> x4, Pallas kernels: 9.62 us -> 16.3 us  [the longest x3 11.2 us: split_part(): pl.pallas_call(functools.partial(split_tiles, start), out_shape=[pltpu.VM...]
  transfers between devices with their start and end apart: 23 -> 22, of which waited for: 18 -> 18; matrix products, arithmetic and copies ran while one was open for 0% -> 0% of each run, Pallas kernels for 8% -> 15%
where the time goes in v7:
time: 110 us
  waiting for transfers between devices  42.7 us (39%)
  Pallas kernels  35.5 us (32%)
  starting transfers between devices  29.9 us (27%)
  between operations  1.57 us (1%)
    ppermute x22, waiting for transfers between devices, swapped(): return lax.ppermute(block, axis, [(i, i ^ bit) for i in range(size)])  42.7 us
    ppermute x22, starting transfers between devices, swapped(): return lax.ppermute(block, axis, [(i, i ^ bit) for i in range(size)])  29.9 us
    pallas_call x5, Pallas kernels, call(): pl.pallas_call(kernel, out_shape=outs, in_specs=[SCALAR] * 2 + [VECTOR] *...  18.3 us
    pallas_call x3, Pallas kernels, split_part(): pl.pallas_call(functools.partial(split_tiles, start), out_shape=[pltpu.VM...  11.2 us
    pallas_call x1, Pallas kernels, turned(): pl.pallas_call(turn_tiles, out_shape=[shape(*data.shape)] + [pltpu.VMEM(p...  5.04 us
  transfers between devices with their start and end apart: 22, of which 18 were waited for; matrix products, arithmetic and copies ran while one was open for 0% of the time, Pallas kernels for 15%

profile of v7, /device:TPU:0, one launch (start us, length us, event | category | flops | bytes accessed | tf_op | source)
XLA Modules:
  0.0 109.9 jit_solution(14124602174749178756)
XLA Ops:
  0.6 3.0 %collective-permute-start = (f32[16,128]{1,0:T(8,128)}, f32[16,128]{1,0:T(8,128)S(1)}, u32[]{:S(2)}, u32[]{:S(2)}) collective-permute-start(f32[16,128]{1,0:T(8,128)} %data.1), channel_id=1, source_target_pairs={{0,1},{1,0},{2,3},{3,2},{4,5},{5,4},{6,7},{7,6},{8,9},{9,8},{10,11... | collective-permute-start | bytes 24584 | tf_op jit(solution)/shard_map/ppermute | solution.py:249
  3.7 2.9 %shard_map.68 = (bf16[80,256,128]{2,1,0:T(8,128)(2,1)S(1)}, f32[16,128]{1,0:T(8,128)S(1)}) custom-call(f32[320,128,128]{2,1,0:T(8,128)} %tiles.5, f32[16,128]{1,0:T(8,128)} %data.1), custom_call_target="tpu_custom_call" | custom-call | flops 5242880 | bytes 5242880 | tf_op jit(solution)/shard_map/pallas_call | solution.py:278
  6.6 1.6 %collective-permute-start.1 = (f32[32,128]{1,0:T(8,128)S(1)}, f32[32,128]{1,0:T(8,128)S(1)}, u32[]{:S(2)}, u32[]{:S(2)}) collective-permute-start(f32[32,128]{1,0:T(8,128)S(1)} %constant_dynamic-update-slice_fusion.data), channel_id=1, source_target_pairs={{0,2},{1,3},{2,0},{3,1},{4,6},{5,7},{6,4},{7,5},{8,10},{9,11},{10,... | collective-permute-start | bytes 49160 | tf_op jit(solution)/shard_map/ppermute | solution.py:249
  8.3 2.9 %shard_map.69 = (bf16[80,256,128]{2,1,0:T(8,128)(2,1)S(1)}, f32[32,128]{1,0:T(8,128)S(1)}) custom-call(f32[320,128,128]{2,1,0:T(8,128)} %tiles.5, f32[32,128]{1,0:T(8,128)S(1)} %constant_dynamic-update-slice_fusion.data), custom_call_target="tpu_custom_call" | custom-call | flops 5242880 | bytes 5242880 | tf_op jit(solution)/shard_map/pallas_call | solution.py:278
  11.3 2.7 %collective-permute-start.2 = (f32[64,128]{1,0:T(8,128)S(1)}, f32[64,128]{1,0:T(8,128)S(1)}, u32[]{:S(2)}, u32[]{:S(2)}) collective-permute-start(f32[64,128]{1,0:T(8,128)S(1)} %constant_dynamic-update-slice_fusion.2.data.rest_3_), channel_id=1, source_target_pairs={{0,4},{1,5},{2,6},{3,7},{4,0},{5,1},{6,2},{7,3},{8,12},{9,13},{10,... | collective-permute-start | bytes 98312 | tf_op jit(solution)/shard_map/ppermute | solution.py:249
  14.6 5.4 %shard_map.70 = (bf16[160,256,128]{2,1,0:T(8,128)(2,1)S(1)}, f32[64,128]{1,0:T(8,128)}) custom-call(f32[320,128,128]{2,1,0:T(8,128)} %tiles.5, f32[64,128]{1,0:T(8,128)S(1)} %constant_dynamic-update-slice_fusion.2.data.rest_3_), custom_call_target="tpu_custom_call" | custom-call | flops 10485760 | bytes 10485760 | tf_op jit(solution)/shard_map/pallas_call | solution.py:278
  20.0 3.3 %shard_map.71 = (f32[128,128]{1,0:T(8,128)S(1)}, f32[264,128]{1,0:T(8,128)S(1)}, f32[264,128]{1,0:T(8,128)S(1)}) custom-call(s32[320]{0:T(512)S(1)} %copy-done, s32[1,1]{1,0:T(1,128)S(6)} %copy.9.counts, s32[1,320]{1,0:T(1,128)S(1)} %reshape.11.cells, bf16[80,256,128]{2,1,0:T(8,128)(2,1)S(1)} %get-tuple-element.31.rest_0_.refs_0_, ...), custom_call_target="tpu_custom_call" | custom-call | tf_op jit(solution)/shard_map/pallas_call | solution.py:262
  23.4 1.3 %collective-permute-done.3 = f32[264,128]{1,0:T(8,128)S(1)} collective-permute-done((f32[264,128]{1,0:T(8,128)S(1)}, f32[264,128]{1,0:T(8,128)S(1)}, u32[]{:S(2)}, u32[]{:S(2)}) %collective-permute-start.3) | collective-permute-done | bytes 135200 | tf_op jit(solution)/shard_map/ppermute | solution.py:249
  24.8 1.6 %collective-permute-start.4 = (f32[264,128]{1,0:T(8,128)S(1)}, f32[264,128]{1,0:T(8,128)S(1)}, u32[]{:S(2)}, u32[]{:S(2)}) collective-permute-start(f32[264,128]{1,0:T(8,128)S(1)} %add.33.refs_2_), channel_id=1, source_target_pairs={{0,16},{8,24},{16,0},{24,8},{1,17},{9,25},{17,1},{25,9},{2,18},{10... | collective-permute-start | bytes 405512 | tf_op jit(solution)/shard_map/ppermute | solution.py:249
  26.3 5.0 %shard_map.72 = (f32[264,128]{1,0:T(8,128)S(1)}, bf16[80,256,128]{2,1,0:T(8,128)(2,1)S(1)}, bf16[80,256,128]{2,1,0:T(8,128)(2,1)S(1)}) custom-call(bf16[80,256,128]{2,1,0:T(8,128)(2,1)S(1)} %get-tuple-element.31.rest_0_.refs_0_, bf16[80,256,128]{2,1,0:T(8,128)(2,1)S(1)} %get-tuple-element.33.rest_1_.refs_1_, f32[264,128]{1,0:T(8,128)S(1)} %add.33.refs_2_), custom_call_target="tpu_custom_call" | custom-call | bytes 5242880 | tf_op jit(solution)/shard_map/pallas_call | solution.py:297
  31.4 0.1 collective-permute-start.5
  31.5 1.3 %collective-permute-done.5.rest_4_ = f32[264,128]{1,0:T(8,128)S(1)} collective-permute-done((f32[264,128]{1,0:T(8,128)S(1)}, f32[264,128]{1,0:T(8,128)S(1)}, u32[]{:S(2)}, u32[]{:S(2)}) %collective-permute-start.5) | collective-permute-done | bytes 135200 | tf_op jit(solution)/shard_map/ppermute | solution.py:249
  32.8 4.1 %shard_map.73 = (f32[512,128]{1,0:T(8,128)S(1)}, f32[8,128]{1,0:T(8,128)S(1)}, f32[128,128]{1,0:T(8,128)S(1)}, f32[136,128]{1,0:T(8,128)S(1)}) custom-call(s32[320]{0:T(512)S(1)} %copy-done.1, s32[1,1]{1,0:T(1,128)S(6)} %copy.9.counts, s32[1,320]{1,0:T(1,128)S(1)} %reshape.10.picks, bf16[80,256,128]{2,1,0:T(8,128)(2,1)S(1)} %get-tuple-element.38.rest_0_, ...), custom_call_target="tpu_custom_call" | custom-call | tf_op jit(solution)/shard_map/pallas_call | solution.py:262
  36.9 2.2 %collective-permute-start.6 = (f32[136,128]{1,0:T(8,128)S(1)}, f32[136,128]{1,0:T(8,128)S(1)}, u32[]{:S(2)}, u32[]{:S(2)}) collective-permute-start(f32[136,128]{1,0:T(8,128)S(1)} %get-tuple-element.42), channel_id=1, source_target_pairs={{0,1},{1,0},{2,3},{3,2},{4,5},{5,4},{6,7},{7,6},{8,9},{9,8},{10,11... | collective-permute-start | bytes 208904 | tf_op jit(solution)/shard_map/ppermute | solution.py:249
  39.1 2.5 %collective-permute-done.6 = f32[136,128]{1,0:T(8,128)S(1)} collective-permute-done((f32[136,128]{1,0:T(8,128)S(1)}, f32[136,128]{1,0:T(8,128)S(1)}, u32[]{:S(2)}, u32[]{:S(2)}) %collective-permute-start.6) | collective-permute-done | bytes 69664 | tf_op jit(solution)/shard_map/ppermute | solution.py:249
  41.7 2.7 %collective-permute-start.7 = (f32[136,128]{1,0:T(8,128)S(1)}, f32[136,128]{1,0:T(8,128)S(1)}, u32[]{:S(2)}, u32[]{:S(2)}) collective-permute-start(f32[136,128]{1,0:T(8,128)S(1)} %add.35), channel_id=1, source_target_pairs={{0,2},{1,3},{2,0},{3,1},{4,6},{5,7},{6,4},{7,5},{8,10},{9,11},{10,... | collective-permute-start | bytes 208904 | tf_op jit(solution)/shard_map/ppermute | solution.py:249
  44.3 2.3 %collective-permute-done.7 = f32[136,128]{1,0:T(8,128)S(1)} collective-permute-done((f32[136,128]{1,0:T(8,128)S(1)}, f32[136,128]{1,0:T(8,128)S(1)}, u32[]{:S(2)}, u32[]{:S(2)}) %collective-permute-start.7) | collective-permute-done | bytes 69664 | tf_op jit(solution)/shard_map/ppermute | solution.py:249
  46.6 0.3 collective-permute-start.8
  46.9 5.0 %collective-permute-done.8.rest_4_ = f32[136,128]{1,0:T(8,128)S(1)} collective-permute-done((f32[136,128]{1,0:T(8,128)S(1)}, f32[136,128]{1,0:T(8,128)S(1)}, u32[]{:S(2)}, u32[]{:S(2)}) %collective-permute-start.8) | collective-permute-done | bytes 69664 | tf_op jit(solution)/shard_map/ppermute | solution.py:249
  51.9 3.3 %shard_map.74 = (f32[128,128]{1,0:T(8,128)S(1)}, f32[8,128]{1,0:T(8,128)S(1)}, f32[264,128]{1,0:T(8,128)S(1)}, f32[264,128]{1,0:T(8,128)S(1)}) custom-call(s32[320]{0:T(512)S(1)} %copy-done, s32[1,1]{1,0:T(1,128)S(6)} %copy.9.counts, s32[1,320]{1,0:T(1,128)S(1)} %reshape.11.cells, bf16[80,256,128]{2,1,0:T(8,128)(2,1)S(1)} %get-tuple-element.31.rest_0_.refs_0_, ...), custom_call_target="tpu_custom_call" | custom-call | tf_op jit(solution)/shard_map/pallas_call | solution.py:262
  55.2 0.1 collective-permute-start.9
  55.3 1.3 %collective-permute-done.9 = f32[264,128]{1,0:T(8,128)S(1)} collective-permute-done((f32[264,128]{1,0:T(8,128)S(1)}, f32[264,128]{1,0:T(8,128)S(1)}, u32[]{:S(2)}, u32[]{:S(2)}) %collective-permute-start.9) | collective-permute-done | bytes 135200 | tf_op jit(solution)/shard_map/ppermute | solution.py:249
  56.7 0.8 collective-permute-start.10
  57.5 4.9 %collective-permute-done.10 = f32[264,128]{1,0:T(8,128)S(1)} collective-permute-done((f32[264,128]{1,0:T(8,128)S(1)}, f32[264,128]{1,0:T(8,128)S(1)}, u32[]{:S(2)}, u32[]{:S(2)}) %collective-permute-start.10) | collective-permute-done | bytes 135200 | tf_op jit(solution)/shard_map/ppermute | solution.py:249
  62.5 1.3 %collective-permute-done.11.rest_4_ = f32[264,128]{1,0:T(8,128)S(1)} collective-permute-done((f32[264,128]{1,0:T(8,128)S(1)}, f32[264,128]{1,0:T(8,128)S(1)}, u32[]{:S(2)}, u32[]{:S(2)}) %collective-permute-start.11) | collective-permute-done | bytes 135200 | tf_op jit(solution)/shard_map/ppermute | solution.py:249
  63.8 4.1 %shard_map.75 = (f32[512,128]{1,0:T(8,128)S(1)}, f32[8,128]{1,0:T(8,128)S(1)}, f32[128,128]{1,0:T(8,128)S(1)}, f32[136,128]{1,0:T(8,128)S(1)}) custom-call(s32[320]{0:T(512)S(1)} %copy-done.1, s32[1,1]{1,0:T(1,128)S(6)} %copy.9.counts, s32[1,320]{1,0:T(1,128)S(1)} %reshape.10.picks, bf16[80,256,128]{2,1,0:T(8,128)(2,1)S(1)} %get-tuple-element.38.rest_0_, ...), custom_call_target="tpu_custom_call" | custom-call | tf_op jit(solution)/shard_map/pallas_call | solution.py:262
  67.9 4.3 %collective-permute-start.12 = (f32[136,128]{1,0:T(8,128)S(1)}, f32[136,128]{1,0:T(8,128)S(1)}, u32[]{:S(2)}, u32[]{:S(2)}) collective-permute-start(f32[136,128]{1,0:T(8,128)S(1)} %get-tuple-element.50), channel_id=1, source_target_pairs={{0,1},{1,0},{2,3},{3,2},{4,5},{5,4},{6,7},{7,6},{8,9},{9,8},{10,11... | collective-permute-start | bytes 208904 | tf_op jit(solution)/shard_map/ppermute | solution.py:249
  72.2 2.5 %collective-permute-done.12 = f32[136,128]{1,0:T(8,128)S(1)} collective-permute-done((f32[136,128]{1,0:T(8,128)S(1)}, f32[136,128]{1,0:T(8,128)S(1)}, u32[]{:S(2)}, u32[]{:S(2)}) %collective-permute-start.12) | collective-permute-done | bytes 69664 | tf_op jit(solution)/shard_map/ppermute | solution.py:249
  74.7 2.2 %collective-permute-start.13 = (f32[136,128]{1,0:T(8,128)S(1)}, f32[136,128]{1,0:T(8,128)S(1)}, u32[]{:S(2)}, u32[]{:S(2)}) collective-permute-start(f32[136,128]{1,0:T(8,128)S(1)} %add.39), channel_id=1, source_target_pairs={{0,2},{1,3},{2,0},{3,1},{4,6},{5,7},{6,4},{7,5},{8,10},{9,11},{10,... | collective-permute-start | bytes 208904 | tf_op jit(solution)/shard_map/ppermute | solution.py:249
  77.0 2.5 %collective-permute-done.13 = f32[136,128]{1,0:T(8,128)S(1)} collective-permute-done((f32[136,128]{1,0:T(8,128)S(1)}, f32[136,128]{1,0:T(8,128)S(1)}, u32[]{:S(2)}, u32[]{:S(2)}) %collective-permute-start.13) | collective-permute-done | bytes 69664 | tf_op jit(solution)/shard_map/ppermute | solution.py:249
  79.5 0.1 collective-permute-start.14
  79.6 5.2 %collective-permute-done.14.rest_4_ = f32[136,128]{1,0:T(8,128)S(1)} collective-permute-done((f32[136,128]{1,0:T(8,128)S(1)}, f32[136,128]{1,0:T(8,128)S(1)}, u32[]{:S(2)}, u32[]{:S(2)}) %collective-permute-start.14) | collective-permute-done | bytes 69664 | tf_op jit(solution)/shard_map/ppermute | solution.py:249
  84.8 3.5 %shard_map.76 = (f32[8,128]{1,0:T(8,128)S(1)}, f32[264,128]{1,0:T(8,128)S(1)}, f32[264,128]{1,0:T(8,128)S(1)}) custom-call(s32[320]{0:T(512)S(1)} %copy-done, s32[1,1]{1,0:T(1,128)S(6)} %copy.9.counts, s32[1,320]{1,0:T(1,128)S(1)} %reshape.11.cells, bf16[80,256,128]{2,1,0:T(8,128)(2,1)S(1)} %get-tuple-element.31.rest_0_.refs_0_, ...), custom_call_target="tpu_custom_call" | custom-call | tf_op jit(solution)/shard_map/pallas_call | solution.py:262
  88.3 0.1 collective-permute-start.15
  88.4 1.3 %collective-permute-done.15 = f32[264,128]{1,0:T(8,128)S(1)} collective-permute-done((f32[264,128]{1,0:T(8,128)S(1)}, f32[264,128]{1,0:T(8,128)S(1)}, u32[]{:S(2)}, u32[]{:S(2)}) %collective-permute-start.15) | collective-permute-done | bytes 135200 | tf_op jit(solution)/shard_map/ppermute | solution.py:249
  89.7 0.8 collective-permute-start.16
  90.5 4.9 %collective-permute-done.16 = f32[264,128]{1,0:T(8,128)S(1)} collective-permute-done((f32[264,128]{1,0:T(8,128)S(1)}, f32[264,128]{1,0:T(8,128)S(1)}, u32[]{:S(2)}, u32[]{:S(2)}) %collective-permute-start.16) | collective-permute-done | bytes 135200 | tf_op jit(solution)/shard_map/ppermute | solution.py:249
  95.5 1.3 %collective-permute-done.17.other = f32[264,128]{1,0:T(8,128)S(1)} collective-permute-done((f32[264,128]{1,0:T(8,128)S(1)}, f32[264,128]{1,0:T(8,128)S(1)}, u32[]{:S(2)}, u32[]{:S(2)}) %collective-permute-start.17) | collective-permute-done | bytes 135200 | tf_op jit(solution)/shard_map/ppermute | solution.py:249
  96.9 0.3 shard_map.77
  97.1 2.8 %collective-permute-start.18 = (f32[8,128]{1,0:T(8,128)S(1)}, f32[8,128]{1,0:T(8,128)S(1)}, u32[]{:S(2)}, u32[]{:S(2)}) collective-permute-start(f32[8,128]{1,0:T(8,128)S(1)} %get-tuple-element.59), channel_id=1, source_target_pairs={{0,1},{1,0},{2,3},{3,2},{4,5},{5,4},{6,7},{7,6},{8,9},{9,8},{10,11... | collective-permute-start | bytes 12296 | tf_op jit(solution)/shard_map/ppermute | solution.py:249
  100.0 1.6 %collective-permute-done.18 = f32[8,128]{1,0:T(8,128)S(1)} collective-permute-done((f32[8,128]{1,0:T(8,128)S(1)}, f32[8,128]{1,0:T(8,128)S(1)}, u32[]{:S(2)}, u32[]{:S(2)}) %collective-permute-start.18) | collective-permute-done | bytes 4128 | tf_op jit(solution)/shard_map/ppermute | solution.py:249
  101.6 1.2 %collective-permute-start.21 = (f32[8,128]{1,0:T(8,128)S(1)}, f32[8,128]{1,0:T(8,128)S(1)}, u32[]{:S(2)}, u32[]{:S(2)}) collective-permute-start(f32[8,128]{1,0:T(8,128)S(1)} %add.43.refs_8_), channel_id=1, source_target_pairs={{0,6},{1,7},{2,4},{3,5},{4,2},{5,3},{6,0},{7,1},{8,14},{9,15},{10,... | collective-permute-start | bytes 12296 | tf_op jit(solution)/shard_map/ppermute | solution.py:249
  102.8 2.8 %collective-permute-start.20 = (f32[8,128]{1,0:T(8,128)S(1)}, f32[8,128]{1,0:T(8,128)S(1)}, u32[]{:S(2)}, u32[]{:S(2)}) collective-permute-start(f32[8,128]{1,0:T(8,128)S(1)} %add.43.refs_8_), channel_id=1, source_target_pairs={{0,4},{1,5},{2,6},{3,7},{4,0},{5,1},{6,2},{7,3},{8,12},{9,13},{10,... | collective-permute-start | bytes 12296 | tf_op jit(solution)/shard_map/ppermute | solution.py:249
  105.6 0.4 collective-permute-start.19
  106.0 1.0 collective-permute-done.21.refs_11_
  107.0 0.3 collective-permute-done.20.refs_10_
  107.3 1.9 %collective-permute-done.19.refs_9_ = f32[8,128]{1,0:T(8,128)S(1)} collective-permute-done((f32[8,128]{1,0:T(8,128)S(1)}, f32[8,128]{1,0:T(8,128)S(1)}, u32[]{:S(2)}, u32[]{:S(2)}) %collective-permute-start.19) | collective-permute-done | bytes 4128 | tf_op jit(solution)/shard_map/ppermute | solution.py:249
  109.2 0.7 shard_map.78
  (28 shorter events, 0.4 us)
Async XLA Ops:
  0.6 6.0 %collective-permute-start = (f32[16,128]{1,0:T(8,128)}, f32[16,128]{1,0:T(8,128)S(1)}, u32[]{:S(2)}, u32[]{:S(2)}) collective-permute-start(f32[16,128]{1,0:T(8,128)} %data.1), channel_id=1, source_target_pairs={{0,1},{1,0},{2,3},{3,2},{4,5},{5,4},{6,7},{7,6},{8,9},{9,8},{10,11... | collective-permute-start | bytes 24584 | tf_op jit(solution)/shard_map/ppermute | solution.py:249
  6.6 7.9 %copy-start.1 = (s32[320]{0:T(512)S(1)}, s32[320]{0:T(512)}, u32[]{:S(2)}) copy-start(s32[320]{0:T(512)} %cell.3) | copy-start | bytes 3844
  6.6 4.6 %collective-permute-start.1 = (f32[32,128]{1,0:T(8,128)S(1)}, f32[32,128]{1,0:T(8,128)S(1)}, u32[]{:S(2)}, u32[]{:S(2)}) collective-permute-start(f32[32,128]{1,0:T(8,128)S(1)} %constant_dynamic-update-slice_fusion.data), channel_id=1, source_target_pairs={{0,2},{1,3},{2,0},{3,1},{4,6},{5,7},{6,4},{7,5},{8,10},{9,11},{10,... | collective-permute-start | bytes 49160 | tf_op jit(solution)/shard_map/ppermute | solution.py:249
  11.3 8.7 %collective-permute-start.2 = (f32[64,128]{1,0:T(8,128)S(1)}, f32[64,128]{1,0:T(8,128)S(1)}, u32[]{:S(2)}, u32[]{:S(2)}) collective-permute-start(f32[64,128]{1,0:T(8,128)S(1)} %constant_dynamic-update-slice_fusion.2.data.rest_3_), channel_id=1, source_target_pairs={{0,4},{1,5},{2,6},{3,7},{4,0},{5,1},{6,2},{7,3},{8,12},{9,13},{10,... | collective-permute-start | bytes 98312 | tf_op jit(solution)/shard_map/ppermute | solution.py:249
  14.6 5.4 %copy-start = (s32[320]{0:T(512)S(1)}, s32[320]{0:T(512)}, u32[]{:S(2)}) copy-start(s32[320]{0:T(512)} %pick.5) | copy-start | bytes 3844
  23.3 1.4 %collective-permute-start.3 = (f32[264,128]{1,0:T(8,128)S(1)}, f32[264,128]{1,0:T(8,128)S(1)}, u32[]{:S(2)}, u32[]{:S(2)}) collective-permute-start(f32[264,128]{1,0:T(8,128)S(1)} %get-tuple-element.37), channel_id=1, source_target_pairs={{0,8},{8,0},{16,24},{24,16},{1,9},{9,1},{17,25},{25,17},{2,10},{10... | collective-permute-start | bytes 405512 | tf_op jit(solution)/shard_map/ppermute | solution.py:249
  24.8 6.6 %collective-permute-start.4 = (f32[264,128]{1,0:T(8,128)S(1)}, f32[264,128]{1,0:T(8,128)S(1)}, u32[]{:S(2)}, u32[]{:S(2)}) collective-permute-start(f32[264,128]{1,0:T(8,128)S(1)} %add.33.refs_2_), channel_id=1, source_target_pairs={{0,16},{8,24},{16,0},{24,8},{1,17},{9,25},{17,1},{25,9},{2,18},{10... | collective-permute-start | bytes 405512 | tf_op jit(solution)/shard_map/ppermute | solution.py:249
  31.4 1.4 %collective-permute-start.5 = (f32[264,128]{1,0:T(8,128)S(1)}, f32[264,128]{1,0:T(8,128)S(1)}, u32[]{:S(2)}, u32[]{:S(2)}) collective-permute-start(f32[264,128]{1,0:T(8,128)S(1)} %add.34.rest_3_), channel_id=1, source_target_pairs={{0,8},{8,0},{16,24},{24,16},{1,9},{9,1},{17,25},{25,17},{2,10},{10... | collective-permute-start | bytes 405512 | tf_op jit(solution)/shard_map/ppermute | solution.py:249
  36.9 4.7 %collective-permute-start.6 = (f32[136,128]{1,0:T(8,128)S(1)}, f32[136,128]{1,0:T(8,128)S(1)}, u32[]{:S(2)}, u32[]{:S(2)}) collective-permute-start(f32[136,128]{1,0:T(8,128)S(1)} %get-tuple-element.42), channel_id=1, source_target_pairs={{0,1},{1,0},{2,3},{3,2},{4,5},{5,4},{6,7},{7,6},{8,9},{9,8},{10,11... | collective-permute-start | bytes 208904 | tf_op jit(solution)/shard_map/ppermute | solution.py:249
  41.7 5.0 %collective-permute-start.7 = (f32[136,128]{1,0:T(8,128)S(1)}, f32[136,128]{1,0:T(8,128)S(1)}, u32[]{:S(2)}, u32[]{:S(2)}) collective-permute-start(f32[136,128]{1,0:T(8,128)S(1)} %add.35), channel_id=1, source_target_pairs={{0,2},{1,3},{2,0},{3,1},{4,6},{5,7},{6,4},{7,5},{8,10},{9,11},{10,... | collective-permute-start | bytes 208904 | tf_op jit(solution)/shard_map/ppermute | solution.py:249
  46.6 5.3 %collective-permute-start.8 = (f32[136,128]{1,0:T(8,128)S(1)}, f32[136,128]{1,0:T(8,128)S(1)}, u32[]{:S(2)}, u32[]{:S(2)}) collective-permute-start(f32[136,128]{1,0:T(8,128)S(1)} %add.36.rest_3_), channel_id=1, source_target_pairs={{0,4},{1,5},{2,6},{3,7},{4,0},{5,1},{6,2},{7,3},{8,12},{9,13},{10,... | collective-permute-start | bytes 208904 | tf_op jit(solution)/shard_map/ppermute | solution.py:249
  55.2 1.4 %collective-permute-start.9 = (f32[264,128]{1,0:T(8,128)S(1)}, f32[264,128]{1,0:T(8,128)S(1)}, u32[]{:S(2)}, u32[]{:S(2)}) collective-permute-start(f32[264,128]{1,0:T(8,128)S(1)} %get-tuple-element.46), channel_id=1, source_target_pairs={{0,8},{8,0},{16,24},{24,16},{1,9},{9,1},{17,25},{25,17},{2,10},{10... | collective-permute-start | bytes 405512 | tf_op jit(solution)/shard_map/ppermute | solution.py:249
  56.7 5.7 %collective-permute-start.10 = (f32[264,128]{1,0:T(8,128)S(1)}, f32[264,128]{1,0:T(8,128)S(1)}, u32[]{:S(2)}, u32[]{:S(2)}) collective-permute-start(f32[264,128]{1,0:T(8,128)S(1)} %add.37), channel_id=1, source_target_pairs={{0,16},{8,24},{16,0},{24,8},{1,17},{9,25},{17,1},{25,9},{2,18},{10... | collective-permute-start | bytes 405512 | tf_op jit(solution)/shard_map/ppermute | solution.py:249
  62.4 1.4 %collective-permute-start.11 = (f32[264,128]{1,0:T(8,128)S(1)}, f32[264,128]{1,0:T(8,128)S(1)}, u32[]{:S(2)}, u32[]{:S(2)}) collective-permute-start(f32[264,128]{1,0:T(8,128)S(1)} %add.38.rest_3_), channel_id=1, source_target_pairs={{0,8},{8,0},{16,24},{24,16},{1,9},{9,1},{17,25},{25,17},{2,10},{10... | collective-permute-start | bytes 405512 | tf_op jit(solution)/shard_map/ppermute | solution.py:249
  67.9 6.8 %collective-permute-start.12 = (f32[136,128]{1,0:T(8,128)S(1)}, f32[136,128]{1,0:T(8,128)S(1)}, u32[]{:S(2)}, u32[]{:S(2)}) collective-permute-start(f32[136,128]{1,0:T(8,128)S(1)} %get-tuple-element.50), channel_id=1, source_target_pairs={{0,1},{1,0},{2,3},{3,2},{4,5},{5,4},{6,7},{7,6},{8,9},{9,8},{10,11... | collective-permute-start | bytes 208904 | tf_op jit(solution)/shard_map/ppermute | solution.py:249
  74.7 4.8 %collective-permute-start.13 = (f32[136,128]{1,0:T(8,128)S(1)}, f32[136,128]{1,0:T(8,128)S(1)}, u32[]{:S(2)}, u32[]{:S(2)}) collective-permute-start(f32[136,128]{1,0:T(8,128)S(1)} %add.39), channel_id=1, source_target_pairs={{0,2},{1,3},{2,0},{3,1},{4,6},{5,7},{6,4},{7,5},{8,10},{9,11},{10,... | collective-permute-start | bytes 208904 | tf_op jit(solution)/shard_map/ppermute | solution.py:249
  79.5 5.3 %collective-permute-start.14 = (f32[136,128]{1,0:T(8,128)S(1)}, f32[136,128]{1,0:T(8,128)S(1)}, u32[]{:S(2)}, u32[]{:S(2)}) collective-permute-start(f32[136,128]{1,0:T(8,128)S(1)} %add.40.rest_3_), channel_id=1, source_target_pairs={{0,4},{1,5},{2,6},{3,7},{4,0},{5,1},{6,2},{7,3},{8,12},{9,13},{10,... | collective-permute-start | bytes 208904 | tf_op jit(solution)/shard_map/ppermute | solution.py:249
  88.3 1.4 %collective-permute-start.15 = (f32[264,128]{1,0:T(8,128)S(1)}, f32[264,128]{1,0:T(8,128)S(1)}, u32[]{:S(2)}, u32[]{:S(2)}) collective-permute-start(f32[264,128]{1,0:T(8,128)S(1)} %get-tuple-element.54), channel_id=1, source_target_pairs={{0,8},{8,0},{16,24},{24,16},{1,9},{9,1},{17,25},{25,17},{2,10},{10... | collective-permute-start | bytes 405512 | tf_op jit(solution)/shard_map/ppermute | solution.py:249
  89.7 5.7 %collective-permute-start.16 = (f32[264,128]{1,0:T(8,128)S(1)}, f32[264,128]{1,0:T(8,128)S(1)}, u32[]{:S(2)}, u32[]{:S(2)}) collective-permute-start(f32[264,128]{1,0:T(8,128)S(1)} %add.41), channel_id=1, source_target_pairs={{0,16},{8,24},{16,0},{24,8},{1,17},{9,25},{17,1},{25,9},{2,18},{10... | collective-permute-start | bytes 405512 | tf_op jit(solution)/shard_map/ppermute | solution.py:249
  95.5 1.4 %collective-permute-start.17 = (f32[264,128]{1,0:T(8,128)S(1)}, f32[264,128]{1,0:T(8,128)S(1)}, u32[]{:S(2)}, u32[]{:S(2)}) collective-permute-start(f32[264,128]{1,0:T(8,128)S(1)} %add.42.mine), channel_id=1, source_target_pairs={{0,8},{8,0},{16,24},{24,16},{1,9},{9,1},{17,25},{25,17},{2,10},{10... | collective-permute-start | bytes 405512 | tf_op jit(solution)/shard_map/ppermute | solution.py:249
  97.1 4.4 %collective-permute-start.18 = (f32[8,128]{1,0:T(8,128)S(1)}, f32[8,128]{1,0:T(8,128)S(1)}, u32[]{:S(2)}, u32[]{:S(2)}) collective-permute-start(f32[8,128]{1,0:T(8,128)S(1)} %get-tuple-element.59), channel_id=1, source_target_pairs={{0,1},{1,0},{2,3},{3,2},{4,5},{5,4},{6,7},{7,6},{8,9},{9,8},{10,11... | collective-permute-start | bytes 12296 | tf_op jit(solution)/shard_map/ppermute | solution.py:249
  101.6 5.4 %collective-permute-start.21 = (f32[8,128]{1,0:T(8,128)S(1)}, f32[8,128]{1,0:T(8,128)S(1)}, u32[]{:S(2)}, u32[]{:S(2)}) collective-permute-start(f32[8,128]{1,0:T(8,128)S(1)} %add.43.refs_8_), channel_id=1, source_target_pairs={{0,6},{1,7},{2,4},{3,5},{4,2},{5,3},{6,0},{7,1},{8,14},{9,15},{10,... | collective-permute-start | bytes 12296 | tf_op jit(solution)/shard_map/ppermute | solution.py:249
  102.8 4.5 %collective-permute-start.20 = (f32[8,128]{1,0:T(8,128)S(1)}, f32[8,128]{1,0:T(8,128)S(1)}, u32[]{:S(2)}, u32[]{:S(2)}) collective-permute-start(f32[8,128]{1,0:T(8,128)S(1)} %add.43.refs_8_), channel_id=1, source_target_pairs={{0,4},{1,5},{2,6},{3,7},{4,0},{5,1},{6,2},{7,3},{8,12},{9,13},{10,... | collective-permute-start | bytes 12296 | tf_op jit(solution)/shard_map/ppermute | solution.py:249
  105.6 3.6 %collective-permute-start.19 = (f32[8,128]{1,0:T(8,128)S(1)}, f32[8,128]{1,0:T(8,128)S(1)}, u32[]{:S(2)}, u32[]{:S(2)}) collective-permute-start(f32[8,128]{1,0:T(8,128)S(1)} %add.43.refs_8_), channel_id=1, source_target_pairs={{0,2},{1,3},{2,0},{3,1},{4,6},{5,7},{6,4},{7,5},{8,10},{9,11},{10,... | collective-permute-start | bytes 12296 | tf_op jit(solution)/shard_map/ppermute | solution.py:249

commit v8 on v7

--- a/solution.py
+++ b/solution.py
@@ -27,34 +27,41 @@
     return high, (value - high.astype(jnp.float32)).astype(jnp.bfloat16)
 
 
-def split_tiles(start, tiles, data, out, data_out, held, arrived, passed):
+def split_tiles(start, passes, tiles, *rest):
+    if passes:
+        data, out, data_out, held, arrived, passed = rest
+        through = pltpu.make_async_copy(data, data_out, passed)
+        through.start()
+    else:
+        out, held, arrived = rest
     steps = out.shape[0] // STEP
-    through = pltpu.make_async_copy(data, data_out, passed)
-    through.start()
-
-    def copy(step, slot):
+
+    def copy(step):
+        slot = lax.rem(step, BUFFERS)
         return pltpu.make_async_copy(
             tiles.at[pl.ds(start + step * STEP, STEP)], held.at[slot], arrived.at[slot]
         )
 
     for step in range(min(BUFFERS - 1, steps)):
-        copy(step, step).start()
-    for step in range(steps):
-        slot = step % BUFFERS
-        ahead = step + BUFFERS - 1
-        if ahead < steps:
-            copy(ahead, ahead % BUFFERS).start()
-        copy(step, slot).wait()
-
-        def one(k, carry):
+        copy(jnp.int32(step)).start()
+
+    def one(step, carry):
+        @pl.when(step + BUFFERS - 1 < steps)
+        def _():
+            copy(step + BUFFERS - 1).start()
+
+        copy(step).wait()
+        slot = lax.rem(step, BUFFERS)
+        for k in range(STEP):
             for row in range(0, B, CHUNK):
                 high, low = split(held[slot, k, pl.ds(row, CHUNK), :])
                 out[step * STEP + k, pl.ds(row, CHUNK), :] = high
                 out[step * STEP + k, pl.ds(B + row, CHUNK), :] = low
-            return carry
-
-        lax.fori_loop(0, STEP, one, 0, unroll=4)
-    through.wait()
+        return carry
+
+    lax.fori_loop(0, steps, one, 0)
+    if passes:
+        through.wait()
 
 
 def turn_tiles(*refs):
@@ -67,7 +74,7 @@
             out[k, B:, :] = tiles[k, B:, :].T
             return carry
 
-        lax.fori_loop(0, tiles.shape[0], one, 0, unroll=4)
+        lax.fori_loop(0, tiles.shape[0], one, 0, unroll=8)
     through.wait()
 
 
@@ -273,23 +280,26 @@
 
 
 def split_part(kernels, data, start, size):
-    if start == 0:
+    passes = data is not None
+    if start == 0 and passes:
         data = pltpu.with_memory_space_constraint(data, pltpu.HBM)
-    return pl.pallas_call(
-        functools.partial(split_tiles, start),
-        out_shape=[pltpu.VMEM((size, 2 * B, B), jnp.bfloat16), shape(*data.shape)],
-        in_specs=[pl.BlockSpec(memory_space=pltpu.HBM), pl.BlockSpec(memory_space=pl.ANY)],
-        out_specs=[VECTOR, VECTOR],
+    out = pl.pallas_call(
+        functools.partial(split_tiles, start, passes),
+        out_shape=[pltpu.VMEM((size, 2 * B, B), jnp.bfloat16)]
+        + ([shape(*data.shape)] if passes else []),
+        in_specs=[pl.BlockSpec(memory_space=pltpu.HBM)] + [pl.BlockSpec(memory_space=pl.ANY)] * passes,
+        out_specs=[VECTOR] * (1 + passes),
         scratch_shapes=[
             pltpu.VMEM((BUFFERS, STEP, B, B), jnp.float32),
             pltpu.SemaphoreType.DMA((BUFFERS,)),
-            pltpu.SemaphoreType.DMA,
-        ],
+        ]
+        + [pltpu.SemaphoreType.DMA] * passes,
         cost_estimate=pl.CostEstimate(
             flops=4 * size * B * B, bytes_accessed=4 * size * B * B, transcendentals=0
         ),
         compiler_params=pltpu.CompilerParams(vmem_limit_bytes=12 << 20),
-    )(kernels, data)
+    )(*([kernels, data] if passes else [kernels]))
+    return out if passes else (out[0], None)
 
 
 def turned(tiles, data):
@@ -351,9 +361,12 @@
             partner = swapped(held, "cols", n_cols, bit)
             bit *= 2
         start = sum(part.shape[0] for part in tiles)
-        part, passed = split_part(kernels, held, start, slots * share // sum(SHARES))
+        more = bit < n_cols
+        part, passed = split_part(
+            kernels, held if more else None, start, slots * share // sum(SHARES)
+        )
         tiles.append(part)
-        if bit < n_cols:
+        if more:
             held = passed
     while bit < n_cols:
         held = jnp.concatenate([held, partner], axis=0)

time: 110 us -> 108 us (0.982)
  Pallas kernels: 35.5 us -> 28.2 us
  waiting for transfers between devices: 42.7 us -> 47.6 us
    pallas_call x5, Pallas kernels: 18.3 us -> 12.8 us  [call(): pl.pallas_call(kernel, out_shape=outs, in_specs=[SCALAR] * 2 + [VECTOR] *...]
    ppermute x22, waiting for transfers between devices: 42.7 us -> 47.6 us  [swapped(): return lax.ppermute(block, axis, [(i, i ^ bit) for i in range(size)])]
  transfers between devices with their start and end apart: 22 -> 22, of which waited for: 18 -> 17; matrix products, arithmetic and copies ran while one was open for 0% -> 0% of each run, Pallas kernels for 15% -> 13%
where the time goes in v8:
time: 108 us
  waiting for transfers between devices  47.6 us (44%)
  starting transfers between devices  30.6 us (28%)
  Pallas kernels  28.2 us (26%)
  between operations  1.57 us (1%)
    ppermute x22, waiting for transfers between devices, swapped(): return lax.ppermute(block, axis, [(i, i ^ bit) for i in range(size)])  47.6 us
    ppermute x22, starting transfers between devices, swapped(): return lax.ppermute(block, axis, [(i, i ^ bit) for i in range(size)])  30.6 us
    pallas_call x5, Pallas kernels, call(): pl.pallas_call(kernel, out_shape=outs, in_specs=[SCALAR] * 2 + [VECTOR] *...  12.8 us
    pallas_call x3, Pallas kernels, split_part(): pl.pallas_call(functools.partial(split_tiles, start, passes), out_shape=[...  10.5 us
    pallas_call x1, Pallas kernels, turned(): pl.pallas_call(turn_tiles, out_shape=[shape(*data.shape)] + [pltpu.VMEM(p...  3.94 us
  transfers between devices with their start and end apart: 22, of which 17 were waited for; matrix products, arithmetic and copies ran while one was open for 0% of the time, Pallas kernels for 13%

profile of v8, /device:TPU:0, one launch (start us, length us, event | category | flops | bytes accessed | tf_op | source)
XLA Modules:
  0.0 108.1 jit_solution(1436966763277075711)
XLA Ops:
  0.6 3.0 %collective-permute-start = (f32[16,128]{1,0:T(8,128)}, f32[16,128]{1,0:T(8,128)S(1)}, u32[]{:S(2)}, u32[]{:S(2)}) collective-permute-start(f32[16,128]{1,0:T(8,128)} %rest_0_.1), channel_id=1, source_target_pairs={{0,1},{1,0},{2,3},{3,2},{4,5},{5,4},{6,7},{7,6},{8,9},{9,8},{10,11... | collective-permute-start | bytes 24584 | tf_op jit(solution)/shard_map/ppermute | solution.py:256
  3.7 2.9 %shard_map.68 = (bf16[80,256,128]{2,1,0:T(8,128)(2,1)S(1)}, f32[16,128]{1,0:T(8,128)S(1)}) custom-call(f32[320,128,128]{2,1,0:T(8,128)} %tiles.5, f32[16,128]{1,0:T(8,128)} %rest_0_.1), custom_call_target="tpu_custom_call" | custom-call | flops 5242880 | bytes 5242880 | tf_op jit(solution)/shard_map/pallas_call | solution.py:286
  6.6 1.6 %collective-permute-start.1 = (f32[32,128]{1,0:T(8,128)S(1)}, f32[32,128]{1,0:T(8,128)S(1)}, u32[]{:S(2)}, u32[]{:S(2)}) collective-permute-start(f32[32,128]{1,0:T(8,128)S(1)} %constant_dynamic-update-slice_fusion.rest_0_), channel_id=1, source_target_pairs={{0,2},{1,3},{2,0},{3,1},{4,6},{5,7},{6,4},{7,5},{8,10},{9,11},{10,... | collective-permute-start | bytes 49160 | tf_op jit(solution)/shard_map/ppermute | solution.py:256
  8.3 2.9 %shard_map.69 = (bf16[80,256,128]{2,1,0:T(8,128)(2,1)S(1)}, f32[32,128]{1,0:T(8,128)S(1)}) custom-call(f32[320,128,128]{2,1,0:T(8,128)} %tiles.5, f32[32,128]{1,0:T(8,128)S(1)} %constant_dynamic-update-slice_fusion.rest_0_), custom_call_target="tpu_custom_call" | custom-call | flops 5242880 | bytes 5242880 | tf_op jit(solution)/shard_map/pallas_call | solution.py:286
  11.2 2.7 %collective-permute-start.2 = (f32[64,128]{1,0:T(8,128)S(1)}, f32[64,128]{1,0:T(8,128)S(1)}, u32[]{:S(2)}, u32[]{:S(2)}) collective-permute-start(f32[64,128]{1,0:T(8,128)S(1)} %constant_dynamic-update-slice_fusion.2.rest_3_), channel_id=1, source_target_pairs={{0,4},{1,5},{2,6},{3,7},{4,0},{5,1},{6,2},{7,3},{8,12},{9,13},{10,... | collective-permute-start | bytes 98312 | tf_op jit(solution)/shard_map/ppermute | solution.py:256
  14.6 4.7 %shard_map.70.rest_2_ = bf16[160,256,128]{2,1,0:T(8,128)(2,1)S(1)} custom-call(f32[320,128,128]{2,1,0:T(8,128)} %tiles.5), custom_call_target="tpu_custom_call" | custom-call | flops 10485760 | bytes 10485760 | tf_op jit(solution)/shard_map/pallas_call | solution.py:286
  19.3 2.5 %shard_map.71 = (f32[128,128]{1,0:T(8,128)S(1)}, f32[264,128]{1,0:T(8,128)S(1)}, f32[264,128]{1,0:T(8,128)S(1)}) custom-call(s32[320]{0:T(512)S(1)} %copy-done, s32[1,1]{1,0:T(1,128)S(6)} %copy.9.counts, s32[1,320]{1,0:T(1,128)S(1)} %reshape.11.cells, bf16[80,256,128]{2,1,0:T(8,128)(2,1)S(1)} %get-tuple-element.30.rest_0_.refs_0_, ...), custom_call_target="tpu_custom_call" | custom-call | tf_op jit(solution)/shard_map/pallas_call | solution.py:269
  21.8 0.7 collective-permute-start.3
  22.5 1.0 collective-permute-done.3
  23.5 2.9 %collective-permute-start.4 = (f32[264,128]{1,0:T(8,128)S(1)}, f32[264,128]{1,0:T(8,128)S(1)}, u32[]{:S(2)}, u32[]{:S(2)}) collective-permute-start(f32[264,128]{1,0:T(8,128)S(1)} %add.33.refs_2_), channel_id=1, source_target_pairs={{0,16},{8,24},{16,0},{24,8},{1,17},{9,25},{17,1},{25,9},{2,18},{10... | collective-permute-start | bytes 405512 | tf_op jit(solution)/shard_map/ppermute | solution.py:256
  26.4 3.9 %shard_map.72 = (f32[264,128]{1,0:T(8,128)S(1)}, bf16[80,256,128]{2,1,0:T(8,128)(2,1)S(1)}, bf16[80,256,128]{2,1,0:T(8,128)(2,1)S(1)}) custom-call(bf16[80,256,128]{2,1,0:T(8,128)(2,1)S(1)} %get-tuple-element.30.rest_0_.refs_0_, bf16[80,256,128]{2,1,0:T(8,128)(2,1)S(1)} %get-tuple-element.32.rest_1_.refs_1_, f32[264,128]{1,0:T(8,128)S(1)} %add.33.refs_2_), custom_call_target="tpu_custom_call" | custom-call | bytes 5242880 | tf_op jit(solution)/shard_map/pallas_call | solution.py:307
  30.4 0.1 collective-permute-start.5
  30.5 1.3 %collective-permute-done.5.rest_4_ = f32[264,128]{1,0:T(8,128)S(1)} collective-permute-done((f32[264,128]{1,0:T(8,128)S(1)}, f32[264,128]{1,0:T(8,128)S(1)}, u32[]{:S(2)}, u32[]{:S(2)}) %collective-permute-start.5) | collective-permute-done | bytes 135200 | tf_op jit(solution)/shard_map/ppermute | solution.py:256
  31.8 2.6 %shard_map.73 = (f32[512,128]{1,0:T(8,128)S(1)}, f32[8,128]{1,0:T(8,128)S(1)}, f32[128,128]{1,0:T(8,128)S(1)}, f32[136,128]{1,0:T(8,128)S(1)}) custom-call(s32[320]{0:T(512)S(1)} %copy-done.1, s32[1,1]{1,0:T(1,128)S(6)} %copy.9.counts, s32[1,320]{1,0:T(1,128)S(1)} %reshape.10.picks, bf16[80,256,128]{2,1,0:T(8,128)(2,1)S(1)} %get-tuple-element.36.rest_0_, ...), custom_call_target="tpu_custom_call" | custom-call | tf_op jit(solution)/shard_map/pallas_call | solution.py:269
  34.4 0.1 collective-permute-start.6
  34.5 4.3 %collective-permute-done.6 = f32[136,128]{1,0:T(8,128)S(1)} collective-permute-done((f32[136,128]{1,0:T(8,128)S(1)}, f32[136,128]{1,0:T(8,128)S(1)}, u32[]{:S(2)}, u32[]{:S(2)}) %collective-permute-start.6) | collective-permute-done | bytes 69664 | tf_op jit(solution)/shard_map/ppermute | solution.py:256
  38.8 1.6 %collective-permute-start.7 = (f32[136,128]{1,0:T(8,128)S(1)}, f32[136,128]{1,0:T(8,128)S(1)}, u32[]{:S(2)}, u32[]{:S(2)}) collective-permute-start(f32[136,128]{1,0:T(8,128)S(1)} %add.35), channel_id=1, source_target_pairs={{0,2},{1,3},{2,0},{3,1},{4,6},{5,7},{6,4},{7,5},{8,10},{9,11},{10,... | collective-permute-start | bytes 208904 | tf_op jit(solution)/shard_map/ppermute | solution.py:256
  40.5 2.7 %collective-permute-done.7 = f32[136,128]{1,0:T(8,128)S(1)} collective-permute-done((f32[136,128]{1,0:T(8,128)S(1)}, f32[136,128]{1,0:T(8,128)S(1)}, u32[]{:S(2)}, u32[]{:S(2)}) %collective-permute-start.7) | collective-permute-done | bytes 69664 | tf_op jit(solution)/shard_map/ppermute | solution.py:256
  43.2 1.3 %collective-permute-start.8 = (f32[136,128]{1,0:T(8,128)S(1)}, f32[136,128]{1,0:T(8,128)S(1)}, u32[]{:S(2)}, u32[]{:S(2)}) collective-permute-start(f32[136,128]{1,0:T(8,128)S(1)} %add.36.rest_3_), channel_id=1, source_target_pairs={{0,4},{1,5},{2,6},{3,7},{4,0},{5,1},{6,2},{7,3},{8,12},{9,13},{10,... | collective-permute-start | bytes 208904 | tf_op jit(solution)/shard_map/ppermute | solution.py:256
  44.5 6.1 %collective-permute-done.8.rest_4_ = f32[136,128]{1,0:T(8,128)S(1)} collective-permute-done((f32[136,128]{1,0:T(8,128)S(1)}, f32[136,128]{1,0:T(8,128)S(1)}, u32[]{:S(2)}, u32[]{:S(2)}) %collective-permute-start.8) | collective-permute-done | bytes 69664 | tf_op jit(solution)/shard_map/ppermute | solution.py:256
  50.5 2.5 %shard_map.74 = (f32[128,128]{1,0:T(8,128)S(1)}, f32[8,128]{1,0:T(8,128)S(1)}, f32[264,128]{1,0:T(8,128)S(1)}, f32[264,128]{1,0:T(8,128)S(1)}) custom-call(s32[320]{0:T(512)S(1)} %copy-done, s32[1,1]{1,0:T(1,128)S(6)} %copy.9.counts, s32[1,320]{1,0:T(1,128)S(1)} %reshape.11.cells, bf16[80,256,128]{2,1,0:T(8,128)(2,1)S(1)} %get-tuple-element.30.rest_0_.refs_0_, ...), custom_call_target="tpu_custom_call" | custom-call | tf_op jit(solution)/shard_map/pallas_call | solution.py:269
  53.1 1.6 %collective-permute-start.9 = (f32[264,128]{1,0:T(8,128)S(1)}, f32[264,128]{1,0:T(8,128)S(1)}, u32[]{:S(2)}, u32[]{:S(2)}) collective-permute-start(f32[264,128]{1,0:T(8,128)S(1)} %get-tuple-element.44), channel_id=1, source_target_pairs={{0,8},{8,0},{16,24},{24,16},{1,9},{9,1},{17,25},{25,17},{2,10},{10... | collective-permute-start | bytes 405512 | tf_op jit(solution)/shard_map/ppermute | solution.py:256
  54.7 1.0 collective-permute-done.9
  55.7 3.5 %collective-permute-start.10 = (f32[264,128]{1,0:T(8,128)S(1)}, f32[264,128]{1,0:T(8,128)S(1)}, u32[]{:S(2)}, u32[]{:S(2)}) collective-permute-start(f32[264,128]{1,0:T(8,128)S(1)} %add.37), channel_id=1, source_target_pairs={{0,16},{8,24},{16,0},{24,8},{1,17},{9,25},{17,1},{25,9},{2,18},{10... | collective-permute-start | bytes 405512 | tf_op jit(solution)/shard_map/ppermute | solution.py:256
  59.2 3.9 %collective-permute-done.10 = f32[264,128]{1,0:T(8,128)S(1)} collective-permute-done((f32[264,128]{1,0:T(8,128)S(1)}, f32[264,128]{1,0:T(8,128)S(1)}, u32[]{:S(2)}, u32[]{:S(2)}) %collective-permute-start.10) | collective-permute-done | bytes 135200 | tf_op jit(solution)/shard_map/ppermute | solution.py:256
  63.1 0.1 collective-permute-start.11
  63.2 1.3 %collective-permute-done.11.rest_4_ = f32[264,128]{1,0:T(8,128)S(1)} collective-permute-done((f32[264,128]{1,0:T(8,128)S(1)}, f32[264,128]{1,0:T(8,128)S(1)}, u32[]{:S(2)}, u32[]{:S(2)}) %collective-permute-start.11) | collective-permute-done | bytes 135200 | tf_op jit(solution)/shard_map/ppermute | solution.py:256
  64.5 2.6 %shard_map.75 = (f32[512,128]{1,0:T(8,128)S(1)}, f32[8,128]{1,0:T(8,128)S(1)}, f32[128,128]{1,0:T(8,128)S(1)}, f32[136,128]{1,0:T(8,128)S(1)}) custom-call(s32[320]{0:T(512)S(1)} %copy-done.1, s32[1,1]{1,0:T(1,128)S(6)} %copy.9.counts, s32[1,320]{1,0:T(1,128)S(1)} %reshape.10.picks, bf16[80,256,128]{2,1,0:T(8,128)(2,1)S(1)} %get-tuple-element.36.rest_0_, ...), custom_call_target="tpu_custom_call" | custom-call | tf_op jit(solution)/shard_map/pallas_call | solution.py:269
  67.2 0.1 collective-permute-start.12
  67.2 4.3 %collective-permute-done.12 = f32[136,128]{1,0:T(8,128)S(1)} collective-permute-done((f32[136,128]{1,0:T(8,128)S(1)}, f32[136,128]{1,0:T(8,128)S(1)}, u32[]{:S(2)}, u32[]{:S(2)}) %collective-permute-start.12) | collective-permute-done | bytes 69664 | tf_op jit(solution)/shard_map/ppermute | solution.py:256
  71.5 0.1 collective-permute-start.13
  71.6 4.3 %collective-permute-done.13 = f32[136,128]{1,0:T(8,128)S(1)} collective-permute-done((f32[136,128]{1,0:T(8,128)S(1)}, f32[136,128]{1,0:T(8,128)S(1)}, u32[]{:S(2)}, u32[]{:S(2)}) %collective-permute-start.13) | collective-permute-done | bytes 69664 | tf_op jit(solution)/shard_map/ppermute | solution.py:256
  75.9 1.2 %collective-permute-start.14 = (f32[136,128]{1,0:T(8,128)S(1)}, f32[136,128]{1,0:T(8,128)S(1)}, u32[]{:S(2)}, u32[]{:S(2)}) collective-permute-start(f32[136,128]{1,0:T(8,128)S(1)} %add.40.rest_3_), channel_id=1, source_target_pairs={{0,4},{1,5},{2,6},{3,7},{4,0},{5,1},{6,2},{7,3},{8,12},{9,13},{10,... | collective-permute-start | bytes 208904 | tf_op jit(solution)/shard_map/ppermute | solution.py:256
  77.1 5.9 %collective-permute-done.14.rest_4_ = f32[136,128]{1,0:T(8,128)S(1)} collective-permute-done((f32[136,128]{1,0:T(8,128)S(1)}, f32[136,128]{1,0:T(8,128)S(1)}, u32[]{:S(2)}, u32[]{:S(2)}) %collective-permute-start.14) | collective-permute-done | bytes 69664 | tf_op jit(solution)/shard_map/ppermute | solution.py:256
  83.0 2.5 %shard_map.76 = (f32[8,128]{1,0:T(8,128)S(1)}, f32[264,128]{1,0:T(8,128)S(1)}, f32[264,128]{1,0:T(8,128)S(1)}) custom-call(s32[320]{0:T(512)S(1)} %copy-done, s32[1,1]{1,0:T(1,128)S(6)} %copy.9.counts, s32[1,320]{1,0:T(1,128)S(1)} %reshape.11.cells, bf16[80,256,128]{2,1,0:T(8,128)(2,1)S(1)} %get-tuple-element.30.rest_0_.refs_0_, ...), custom_call_target="tpu_custom_call" | custom-call | tf_op jit(solution)/shard_map/pallas_call | solution.py:269
  85.5 1.8 %collective-permute-start.15 = (f32[264,128]{1,0:T(8,128)S(1)}, f32[264,128]{1,0:T(8,128)S(1)}, u32[]{:S(2)}, u32[]{:S(2)}) collective-permute-start(f32[264,128]{1,0:T(8,128)S(1)} %get-tuple-element.52), channel_id=1, source_target_pairs={{0,8},{8,0},{16,24},{24,16},{1,9},{9,1},{17,25},{25,17},{2,10},{10... | collective-permute-start | bytes 405512 | tf_op jit(solution)/shard_map/ppermute | solution.py:256
  87.3 1.0 collective-permute-done.15
  88.3 3.8 %collective-permute-start.16 = (f32[264,128]{1,0:T(8,128)S(1)}, f32[264,128]{1,0:T(8,128)S(1)}, u32[]{:S(2)}, u32[]{:S(2)}) collective-permute-start(f32[264,128]{1,0:T(8,128)S(1)} %add.41), channel_id=1, source_target_pairs={{0,16},{8,24},{16,0},{24,8},{1,17},{9,25},{17,1},{25,9},{2,18},{10... | collective-permute-start | bytes 405512 | tf_op jit(solution)/shard_map/ppermute | solution.py:256
  92.1 3.9 %collective-permute-done.16 = f32[264,128]{1,0:T(8,128)S(1)} collective-permute-done((f32[264,128]{1,0:T(8,128)S(1)}, f32[264,128]{1,0:T(8,128)S(1)}, u32[]{:S(2)}, u32[]{:S(2)}) %collective-permute-start.16) | collective-permute-done | bytes 135200 | tf_op jit(solution)/shard_map/ppermute | solution.py:256
  96.1 0.1 collective-permute-start.17
  96.1 1.3 %collective-permute-done.17.other = f32[264,128]{1,0:T(8,128)S(1)} collective-permute-done((f32[264,128]{1,0:T(8,128)S(1)}, f32[264,128]{1,0:T(8,128)S(1)}, u32[]{:S(2)}, u32[]{:S(2)}) %collective-permute-start.17) | collective-permute-done | bytes 135200 | tf_op jit(solution)/shard_map/ppermute | solution.py:256
  97.5 0.3 shard_map.77
  97.7 0.1 collective-permute-start.18
  97.8 3.6 %collective-permute-done.18 = f32[8,128]{1,0:T(8,128)S(1)} collective-permute-done((f32[8,128]{1,0:T(8,128)S(1)}, f32[8,128]{1,0:T(8,128)S(1)}, u32[]{:S(2)}, u32[]{:S(2)}) %collective-permute-start.18) | collective-permute-done | bytes 4128 | tf_op jit(solution)/shard_map/ppermute | solution.py:256
  101.4 4.4 %collective-permute-start.19 = (f32[8,128]{1,0:T(8,128)S(1)}, f32[8,128]{1,0:T(8,128)S(1)}, u32[]{:S(2)}, u32[]{:S(2)}) collective-permute-start(f32[8,128]{1,0:T(8,128)S(1)} %add.43.refs_8_), channel_id=1, source_target_pairs={{0,2},{1,3},{2,0},{3,1},{4,6},{5,7},{6,4},{7,5},{8,10},{9,11},{10,... | collective-permute-start | bytes 12296 | tf_op jit(solution)/shard_map/ppermute | solution.py:256
  105.8 1.0 collective-permute-done.21.refs_11_
  106.8 0.6 collective-permute-done.19.refs_9_
  107.4 0.7 shard_map.78
  (28 shorter events, 0.2 us)
Async XLA Ops:
  0.6 6.0 %collective-permute-start = (f32[16,128]{1,0:T(8,128)}, f32[16,128]{1,0:T(8,128)S(1)}, u32[]{:S(2)}, u32[]{:S(2)}) collective-permute-start(f32[16,128]{1,0:T(8,128)} %rest_0_.1), channel_id=1, source_target_pairs={{0,1},{1,0},{2,3},{3,2},{4,5},{5,4},{6,7},{7,6},{8,9},{9,8},{10,11... | collective-permute-start | bytes 24584 | tf_op jit(solution)/shard_map/ppermute | solution.py:256
  6.6 7.9 %copy-start.1 = (s32[320]{0:T(512)S(1)}, s32[320]{0:T(512)}, u32[]{:S(2)}) copy-start(s32[320]{0:T(512)} %cell.3) | copy-start | bytes 3844
  6.6 4.6 %collective-permute-start.1 = (f32[32,128]{1,0:T(8,128)S(1)}, f32[32,128]{1,0:T(8,128)S(1)}, u32[]{:S(2)}, u32[]{:S(2)}) collective-permute-start(f32[32,128]{1,0:T(8,128)S(1)} %constant_dynamic-update-slice_fusion.rest_0_), channel_id=1, source_target_pairs={{0,2},{1,3},{2,0},{3,1},{4,6},{5,7},{6,4},{7,5},{8,10},{9,11},{10,... | collective-permute-start | bytes 49160 | tf_op jit(solution)/shard_map/ppermute | solution.py:256
  11.2 8.1 %collective-permute-start.2 = (f32[64,128]{1,0:T(8,128)S(1)}, f32[64,128]{1,0:T(8,128)S(1)}, u32[]{:S(2)}, u32[]{:S(2)}) collective-permute-start(f32[64,128]{1,0:T(8,128)S(1)} %constant_dynamic-update-slice_fusion.2.rest_3_), channel_id=1, source_target_pairs={{0,4},{1,5},{2,6},{3,7},{4,0},{5,1},{6,2},{7,3},{8,12},{9,13},{10,... | collective-permute-start | bytes 98312 | tf_op jit(solution)/shard_map/ppermute | solution.py:256
  14.6 4.7 %copy-start = (s32[320]{0:T(512)S(1)}, s32[320]{0:T(512)}, u32[]{:S(2)}) copy-start(s32[320]{0:T(512)} %pick.5) | copy-start | bytes 3844
  21.8 1.7 %collective-permute-start.3 = (f32[264,128]{1,0:T(8,128)S(1)}, f32[264,128]{1,0:T(8,128)S(1)}, u32[]{:S(2)}, u32[]{:S(2)}) collective-permute-start(f32[264,128]{1,0:T(8,128)S(1)} %get-tuple-element.35), channel_id=1, source_target_pairs={{0,8},{8,0},{16,24},{24,16},{1,9},{9,1},{17,25},{25,17},{2,10},{10... | collective-permute-start | bytes 405512 | tf_op jit(solution)/shard_map/ppermute | solution.py:256
  23.5 6.9 %collective-permute-start.4 = (f32[264,128]{1,0:T(8,128)S(1)}, f32[264,128]{1,0:T(8,128)S(1)}, u32[]{:S(2)}, u32[]{:S(2)}) collective-permute-start(f32[264,128]{1,0:T(8,128)S(1)} %add.33.refs_2_), channel_id=1, source_target_pairs={{0,16},{8,24},{16,0},{24,8},{1,17},{9,25},{17,1},{25,9},{2,18},{10... | collective-permute-start | bytes 405512 | tf_op jit(solution)/shard_map/ppermute | solution.py:256
  30.4 1.4 %collective-permute-start.5 = (f32[264,128]{1,0:T(8,128)S(1)}, f32[264,128]{1,0:T(8,128)S(1)}, u32[]{:S(2)}, u32[]{:S(2)}) collective-permute-start(f32[264,128]{1,0:T(8,128)S(1)} %add.34.rest_3_), channel_id=1, source_target_pairs={{0,8},{8,0},{16,24},{24,16},{1,9},{9,1},{17,25},{25,17},{2,10},{10... | collective-permute-start | bytes 405512 | tf_op jit(solution)/shard_map/ppermute | solution.py:256
  34.4 4.4 %collective-permute-start.6 = (f32[136,128]{1,0:T(8,128)S(1)}, f32[136,128]{1,0:T(8,128)S(1)}, u32[]{:S(2)}, u32[]{:S(2)}) collective-permute-start(f32[136,128]{1,0:T(8,128)S(1)} %get-tuple-element.40), channel_id=1, source_target_pairs={{0,1},{1,0},{2,3},{3,2},{4,5},{5,4},{6,7},{7,6},{8,9},{9,8},{10,11... | collective-permute-start | bytes 208904 | tf_op jit(solution)/shard_map/ppermute | solution.py:256
  38.8 4.4 %collective-permute-start.7 = (f32[136,128]{1,0:T(8,128)S(1)}, f32[136,128]{1,0:T(8,128)S(1)}, u32[]{:S(2)}, u32[]{:S(2)}) collective-permute-start(f32[136,128]{1,0:T(8,128)S(1)} %add.35), channel_id=1, source_target_pairs={{0,2},{1,3},{2,0},{3,1},{4,6},{5,7},{6,4},{7,5},{8,10},{9,11},{10,... | collective-permute-start | bytes 208904 | tf_op jit(solution)/shard_map/ppermute | solution.py:256
  43.2 7.3 %collective-permute-start.8 = (f32[136,128]{1,0:T(8,128)S(1)}, f32[136,128]{1,0:T(8,128)S(1)}, u32[]{:S(2)}, u32[]{:S(2)}) collective-permute-start(f32[136,128]{1,0:T(8,128)S(1)} %add.36.rest_3_), channel_id=1, source_target_pairs={{0,4},{1,5},{2,6},{3,7},{4,0},{5,1},{6,2},{7,3},{8,12},{9,13},{10,... | collective-permute-start | bytes 208904 | tf_op jit(solution)/shard_map/ppermute | solution.py:256
  53.1 2.6 %collective-permute-start.9 = (f32[264,128]{1,0:T(8,128)S(1)}, f32[264,128]{1,0:T(8,128)S(1)}, u32[]{:S(2)}, u32[]{:S(2)}) collective-permute-start(f32[264,128]{1,0:T(8,128)S(1)} %get-tuple-element.44), channel_id=1, source_target_pairs={{0,8},{8,0},{16,24},{24,16},{1,9},{9,1},{17,25},{25,17},{2,10},{10... | collective-permute-start | bytes 405512 | tf_op jit(solution)/shard_map/ppermute | solution.py:256
  55.7 7.4 %collective-permute-start.10 = (f32[264,128]{1,0:T(8,128)S(1)}, f32[264,128]{1,0:T(8,128)S(1)}, u32[]{:S(2)}, u32[]{:S(2)}) collective-permute-start(f32[264,128]{1,0:T(8,128)S(1)} %add.37), channel_id=1, source_target_pairs={{0,16},{8,24},{16,0},{24,8},{1,17},{9,25},{17,1},{25,9},{2,18},{10... | collective-permute-start | bytes 405512 | tf_op jit(solution)/shard_map/ppermute | solution.py:256
  63.1 1.4 %collective-permute-start.11 = (f32[264,128]{1,0:T(8,128)S(1)}, f32[264,128]{1,0:T(8,128)S(1)}, u32[]{:S(2)}, u32[]{:S(2)}) collective-permute-start(f32[264,128]{1,0:T(8,128)S(1)} %add.38.rest_3_), channel_id=1, source_target_pairs={{0,8},{8,0},{16,24},{24,16},{1,9},{9,1},{17,25},{25,17},{2,10},{10... | collective-permute-start | bytes 405512 | tf_op jit(solution)/shard_map/ppermute | solution.py:256
  67.2 4.4 %collective-permute-start.12 = (f32[136,128]{1,0:T(8,128)S(1)}, f32[136,128]{1,0:T(8,128)S(1)}, u32[]{:S(2)}, u32[]{:S(2)}) collective-permute-start(f32[136,128]{1,0:T(8,128)S(1)} %get-tuple-element.48), channel_id=1, source_target_pairs={{0,1},{1,0},{2,3},{3,2},{4,5},{5,4},{6,7},{7,6},{8,9},{9,8},{10,11... | collective-permute-start | bytes 208904 | tf_op jit(solution)/shard_map/ppermute | solution.py:256
  71.5 4.4 %collective-permute-start.13 = (f32[136,128]{1,0:T(8,128)S(1)}, f32[136,128]{1,0:T(8,128)S(1)}, u32[]{:S(2)}, u32[]{:S(2)}) collective-permute-start(f32[136,128]{1,0:T(8,128)S(1)} %add.39), channel_id=1, source_target_pairs={{0,2},{1,3},{2,0},{3,1},{4,6},{5,7},{6,4},{7,5},{8,10},{9,11},{10,... | collective-permute-start | bytes 208904 | tf_op jit(solution)/shard_map/ppermute | solution.py:256
  75.9 7.1 %collective-permute-start.14 = (f32[136,128]{1,0:T(8,128)S(1)}, f32[136,128]{1,0:T(8,128)S(1)}, u32[]{:S(2)}, u32[]{:S(2)}) collective-permute-start(f32[136,128]{1,0:T(8,128)S(1)} %add.40.rest_3_), channel_id=1, source_target_pairs={{0,4},{1,5},{2,6},{3,7},{4,0},{5,1},{6,2},{7,3},{8,12},{9,13},{10,... | collective-permute-start | bytes 208904 | tf_op jit(solution)/shard_map/ppermute | solution.py:256
  85.5 2.8 %collective-permute-start.15 = (f32[264,128]{1,0:T(8,128)S(1)}, f32[264,128]{1,0:T(8,128)S(1)}, u32[]{:S(2)}, u32[]{:S(2)}) collective-permute-start(f32[264,128]{1,0:T(8,128)S(1)} %get-tuple-element.52), channel_id=1, source_target_pairs={{0,8},{8,0},{16,24},{24,16},{1,9},{9,1},{17,25},{25,17},{2,10},{10... | collective-permute-start | bytes 405512 | tf_op jit(solution)/shard_map/ppermute | solution.py:256
  88.3 7.7 %collective-permute-start.16 = (f32[264,128]{1,0:T(8,128)S(1)}, f32[264,128]{1,0:T(8,128)S(1)}, u32[]{:S(2)}, u32[]{:S(2)}) collective-permute-start(f32[264,128]{1,0:T(8,128)S(1)} %add.41), channel_id=1, source_target_pairs={{0,16},{8,24},{16,0},{24,8},{1,17},{9,25},{17,1},{25,9},{2,18},{10... | collective-permute-start | bytes 405512 | tf_op jit(solution)/shard_map/ppermute | solution.py:256
  96.1 1.4 %collective-permute-start.17 = (f32[264,128]{1,0:T(8,128)S(1)}, f32[264,128]{1,0:T(8,128)S(1)}, u32[]{:S(2)}, u32[]{:S(2)}) collective-permute-start(f32[264,128]{1,0:T(8,128)S(1)} %add.42.mine), channel_id=1, source_target_pairs={{0,8},{8,0},{16,24},{24,16},{1,9},{9,1},{17,25},{25,17},{2,10},{10... | collective-permute-start | bytes 405512 | tf_op jit(solution)/shard_map/ppermute | solution.py:256
  97.7 3.7 %collective-permute-start.18 = (f32[8,128]{1,0:T(8,128)S(1)}, f32[8,128]{1,0:T(8,128)S(1)}, u32[]{:S(2)}, u32[]{:S(2)}) collective-permute-start(f32[8,128]{1,0:T(8,128)S(1)} %get-tuple-element.57), channel_id=1, source_target_pairs={{0,1},{1,0},{2,3},{3,2},{4,5},{5,4},{6,7},{7,6},{8,9},{9,8},{10,11... | collective-permute-start | bytes 12296 | tf_op jit(solution)/shard_map/ppermute | solution.py:256
  101.4 5.4 %collective-permute-start.21 = (f32[8,128]{1,0:T(8,128)S(1)}, f32[8,128]{1,0:T(8,128)S(1)}, u32[]{:S(2)}, u32[]{:S(2)}) collective-permute-start(f32[8,128]{1,0:T(8,128)S(1)} %add.43.refs_8_), channel_id=1, source_target_pairs={{0,6},{1,7},{2,4},{3,5},{4,2},{5,3},{6,0},{7,1},{8,14},{9,15},{10,... | collective-permute-start | bytes 12296 | tf_op jit(solution)/shard_map/ppermute | solution.py:256
  101.4 5.4 %collective-permute-start.20 = (f32[8,128]{1,0:T(8,128)S(1)}, f32[8,128]{1,0:T(8,128)S(1)}, u32[]{:S(2)}, u32[]{:S(2)}) collective-permute-start(f32[8,128]{1,0:T(8,128)S(1)} %add.43.refs_8_), channel_id=1, source_target_pairs={{0,4},{1,5},{2,6},{3,7},{4,0},{5,1},{6,2},{7,3},{8,12},{9,13},{10,... | collective-permute-start | bytes 12296 | tf_op jit(solution)/shard_map/ppermute | solution.py:256
  101.4 6.0 %collective-permute-start.19 = (f32[8,128]{1,0:T(8,128)S(1)}, f32[8,128]{1,0:T(8,128)S(1)}, u32[]{:S(2)}, u32[]{:S(2)}) collective-permute-start(f32[8,128]{1,0:T(8,128)S(1)} %add.43.refs_8_), channel_id=1, source_target_pairs={{0,2},{1,3},{2,0},{3,1},{4,6},{5,7},{6,4},{7,5},{8,10},{9,11},{10,... | collective-permute-start | bytes 12296 | tf_op jit(solution)/shard_map/ppermute | solution.py:256

commit v9 on v8

--- a/solution.py
+++ b/solution.py
@@ -13,11 +13,10 @@
 B = 128
 SUB = 8
 GROUP = 80
-SHARES = (1, 1, 2)
-PARTS = len(SHARES)
-TURNED = 2
-STEP = 16
-BUFFERS = 4
+PARTS = 2
+TURNED = 1
+STEP = 8
+BUFFERS = 8
 CHUNK = 32
 TAIL = 8
 
@@ -223,8 +222,18 @@
     out[pl.ds(PBLK, TAIL), :] = square
 
 
-def last_vector(n_rows, mine, other, v_old, alpha_old, beta_out, own_out, square_out, v):
-    _, square_out[...] = cell_vector(n_rows, mine, other, v_old, alpha_old, v, beta_out, own_out)
+def last_vector(n_rows, mine, v_old, alpha_old, beta_out, own_out, square_out, v):
+    size, _ = halves(n_rows, CBLK)
+    me = lax.axis_index("rows")
+    beta = jnp.sqrt(mine[pl.ds(CBLK // 2, TAIL), :])
+    beta_out[...] = beta
+    for block in range(n_rows // 2):
+        here = pl.ds(block * size, size)
+        whole = pl.ds(pl.multiple_of((2 * block + lax.rem(me, 2)) * size, size), size)
+        v[here, :] = mine[here, :] / beta[:1] - beta[:1] * (v_old[whole, :] / alpha_old[:1])
+    own_out[...] = v[pl.ds(pl.multiple_of(lax.div(me, 2) * size, size), size), :]
+    half = v[...]
+    square_out[...] = jnp.full((TAIL, B), jnp.sum(half * half))
 
 
 def finish(*refs):
@@ -338,7 +347,7 @@
 
     transposed = []
 
-    def sum_cells(keep, send):
+    def sum_half(keep, send):
         mine = keep + swapped(send, "rows", n_rows, 1)
         bit = 2
         while bit < n_rows:
@@ -348,31 +357,20 @@
                 transposed.extend(parts + tiles[TURNED:])
             mine = mine + other
             bit *= 2
+        return mine
+
+    def sum_cells(keep, send):
+        mine = sum_half(keep, send)
         return [mine, swapped(mine, "rows", n_rows, 1)]
 
     kernels = pltpu.with_memory_space_constraint(kernels, pltpu.HBM)
-    tiles = []
-    held = data
-    partner = None
-    bit = 1
-    for share in SHARES:
-        if bit < n_cols:
-            held = held if partner is None else jnp.concatenate([held, partner], axis=0)
-            partner = swapped(held, "cols", n_cols, bit)
-            bit *= 2
-        start = sum(part.shape[0] for part in tiles)
-        more = bit < n_cols
-        part, passed = split_part(
-            kernels, held if more else None, start, slots * share // sum(SHARES)
-        )
-        tiles.append(part)
-        if more:
-            held = passed
-    while bit < n_cols:
-        held = jnp.concatenate([held, partner], axis=0)
-        partner = swapped(held, "cols", n_cols, bit)
-        bit *= 2
-    pieces = [held, partner]
+    half_slots = slots // 2
+    partner = swapped(data, "cols", n_cols, 1)
+    first, passed = split_part(kernels, data, 0, half_slots)
+    second, _ = split_part(kernels, None, half_slots, slots - half_slots)
+    tiles = [first, second]
+    pair = jnp.concatenate([passed, partner], axis=0)
+    pieces = [pair] + [swapped(pair, "cols", n_cols, bit) for bit in range(2, n_cols, 2)]
     upick, keep, send = call(
         functools.partial(first_adjoint, n_rows, n_cols),
         [shape(PBLK, B), shape(half, B), shape(half, B)],
@@ -414,12 +412,17 @@
     beta, block, square = simple_call(
         functools.partial(last_vector, n_rows),
         [shape(TAIL, B), shape(own, B), shape(TAIL, B)],
-        sum_cells(keep, send) + old,
-        [pltpu.VMEM((CBLK, B), jnp.float32)],
+        [sum_half(keep, send)] + old,
+        [pltpu.VMEM((CBLK // 2, B), jnp.float32)],
     )
     blocks.append(block)
     betas.append(beta)
-    square = square + swapped(square, "cols", n_cols, 1)
+    both = [
+        (r * n_cols + c, (r ^ 1) * n_cols + (c ^ 1)) for r in range(n_rows) for c in range(n_cols)
+    ]
+    square = (square + swapped(square, "rows", n_rows, 1)) + (
+        swapped(square, "cols", n_cols, 1) + lax.ppermute(square, ("rows", "cols"), both)
+    )
     squares = [square] + [swapped(square, "cols", n_cols, bit) for bit in range(2, n_cols, 2)]
     model, search = simple_call(
         finish, [shape(own, B), shape(own, B)], blocks + betas + alphas + squares

time: 108 us -> 108 us (level)
  waiting for transfers between devices: 47.6 us -> 38.5 us
  starting transfers between devices: 30.6 us -> 35.5 us
  Pallas kernels: 28.2 us -> 31.8 us
    ppermute x22 -> x23, waiting for transfers between devices: 47.6 us -> 38.4 us  [swapped(): return lax.ppermute(block, axis, [(i, i ^ bit) for i in range(size)])]
    pallas_call x5, Pallas kernels: 12.8 us -> 18.1 us  [call(): pl.pallas_call(kernel, out_shape=outs, in_specs=[SCALAR] * 2 + [VECTOR] *...]
    ppermute x22 -> x23, starting transfers between devices: 30.6 us -> 33.7 us  [swapped(): return lax.ppermute(block, axis, [(i, i ^ bit) for i in range(size)])]
    ppermute x0 -> x1, starting transfers between devices: none -> 1.77 us  [per_device(): lax.ppermute(square, ('rows', 'cols'), both)]
    pallas_call x3 -> x2, Pallas kernels: 10.5 us -> 8.84 us  [split_part(): pl.pallas_call(functools.partial(split_tiles, start, passes), out_shape=[...]
  transfers between devices with their start and end apart: 22 -> 24, of which waited for: 17 -> 18; matrix products, arithmetic and copies ran while one was open for 0% -> 0% of each run, Pallas kernels for 13% -> 12%
where the time goes in v9:
time: 108 us
  waiting for transfers between devices  38.5 us (36%)
  starting transfers between devices  35.5 us (33%)
  Pallas kernels  31.8 us (29%)
  between operations  1.53 us (1%)
    ppermute x23, waiting for transfers between devices, swapped(): return lax.ppermute(block, axis, [(i, i ^ bit) for i in range(size)])  38.4 us
    ppermute x23, starting transfers between devices, swapped(): return lax.ppermute(block, axis, [(i, i ^ bit) for i in range(size)])  33.7 us
    pallas_call x5, Pallas kernels, call(): pl.pallas_call(kernel, out_shape=outs, in_specs=[SCALAR] * 2 + [VECTOR] *...  18.1 us
    pallas_call x2, Pallas kernels, split_part(): pl.pallas_call(functools.partial(split_tiles, start, passes), out_shape=[...  8.84 us
    pallas_call x1, Pallas kernels, turned(): pl.pallas_call(turn_tiles, out_shape=[shape(*data.shape)] + [pltpu.VMEM(p...  3.94 us
  transfers between devices with their start and end apart: 24, of which 18 were waited for; matrix products, arithmetic and copies ran while one was open for 0% of the time, Pallas kernels for 12%

profile of v9, /device:TPU:0, one launch (start us, length us, event | category | flops | bytes accessed | tf_op | source)
XLA Modules:
  0.0 107.5 jit_solution(787364734844202078)
XLA Ops:
  0.6 3.0 %collective-permute-start = (f32[16,128]{1,0:T(8,128)}, f32[16,128]{1,0:T(8,128)S(1)}, u32[]{:S(2)}, u32[]{:S(2)}) collective-permute-start(f32[16,128]{1,0:T(8,128)} %rest_0_.1), channel_id=1, source_target_pairs={{0,1},{1,0},{2,3},{3,2},{4,5},{5,4},{6,7},{7,6},{8,9},{9,8},{10,11... | collective-permute-start | bytes 24584 | tf_op jit(solution)/shard_map/ppermute | solution.py:265
  3.7 4.4 %shard_map.68 = (bf16[160,256,128]{2,1,0:T(8,128)(2,1)S(1)}, f32[16,128]{1,0:T(8,128)S(1)}) custom-call(f32[320,128,128]{2,1,0:T(8,128)} %tiles.3, f32[16,128]{1,0:T(8,128)} %rest_0_.1), custom_call_target="tpu_custom_call" | custom-call | flops 10485760 | bytes 10485760 | tf_op jit(solution)/shard_map/pallas_call | solution.py:295
  8.1 3.7 %collective-permute-start.3 = (f32[32,128]{1,0:T(8,128)S(1)}, f32[32,128]{1,0:T(8,128)S(1)}, u32[]{:S(2)}, u32[]{:S(2)}) collective-permute-start(f32[32,128]{1,0:T(8,128)S(1)} %constant_dynamic-update-slice_fusion.rest_2_), channel_id=1, source_target_pairs={{0,6},{1,7},{2,4},{3,5},{4,2},{5,3},{6,0},{7,1},{8,14},{9,15},{10,... | collective-permute-start | bytes 49160 | tf_op jit(solution)/shard_map/ppermute | solution.py:265
  11.8 0.8 collective-permute-start.1
  13.3 4.4 %shard_map.69.rest_1_ = bf16[160,256,128]{2,1,0:T(8,128)(2,1)S(1)} custom-call(f32[320,128,128]{2,1,0:T(8,128)} %tiles.3), custom_call_target="tpu_custom_call" | custom-call | flops 10485760 | bytes 10485760 | tf_op jit(solution)/shard_map/pallas_call | solution.py:295
  17.7 3.3 %shard_map.70 = (f32[128,128]{1,0:T(8,128)S(1)}, f32[264,128]{1,0:T(8,128)S(1)}, f32[264,128]{1,0:T(8,128)S(1)}) custom-call(s32[320]{0:T(512)S(1)} %copy-done, s32[1,1]{1,0:T(1,128)S(6)} %copy.8.counts, s32[1,320]{1,0:T(1,128)S(1)} %reshape.11.cells, bf16[160,256,128]{2,1,0:T(8,128)(2,1)S(1)} %get-tuple-element.27.rest_0_.refs_0_, ...), custom_call_target="tpu_custom_call" | custom-call | tf_op jit(solution)/shard_map/pallas_call | solution.py:278
  21.1 0.1 collective-permute-start.4
  21.2 1.3 %collective-permute-done.4 = f32[264,128]{1,0:T(8,128)S(1)} collective-permute-done((f32[264,128]{1,0:T(8,128)S(1)}, f32[264,128]{1,0:T(8,128)S(1)}, u32[]{:S(2)}, u32[]{:S(2)}) %collective-permute-start.4) | collective-permute-done | bytes 135200 | tf_op jit(solution)/shard_map/ppermute | solution.py:265
  22.5 0.9 collective-permute-start.5
  23.4 3.9 %shard_map.71 = (f32[264,128]{1,0:T(8,128)S(1)}, bf16[160,256,128]{2,1,0:T(8,128)(2,1)S(1)}) custom-call(bf16[160,256,128]{2,1,0:T(8,128)(2,1)S(1)} %get-tuple-element.27.rest_0_.refs_0_, f32[264,128]{1,0:T(8,128)S(1)} %add.39.refs_1_), custom_call_target="tpu_custom_call" | custom-call | bytes 5242880 | tf_op jit(solution)/shard_map/pallas_call | solution.py:316
  27.3 0.9 collective-permute-done.5
  28.2 0.1 collective-permute-start.6
  28.3 1.3 %collective-permute-done.6.rest_3_ = f32[264,128]{1,0:T(8,128)S(1)} collective-permute-done((f32[264,128]{1,0:T(8,128)S(1)}, f32[264,128]{1,0:T(8,128)S(1)}, u32[]{:S(2)}, u32[]{:S(2)}) %collective-permute-start.6) | collective-permute-done | bytes 135200 | tf_op jit(solution)/shard_map/ppermute | solution.py:265
  29.7 4.1 %shard_map.72 = (f32[512,128]{1,0:T(8,128)S(1)}, f32[8,128]{1,0:T(8,128)S(1)}, f32[128,128]{1,0:T(8,128)S(1)}, f32[136,128]{1,0:T(8,128)S(1)}) custom-call(s32[320]{0:T(512)S(1)} %copy-done.1, s32[1,1]{1,0:T(1,128)S(6)} %copy.8.counts, s32[1,320]{1,0:T(1,128)S(1)} %reshape.10.picks, bf16[160,256,128]{2,1,0:T(8,128)(2,1)S(1)} %get-tuple-element.31.rest_0_, ...), custom_call_target="tpu_custom_call" | custom-call | tf_op jit(solution)/shard_map/pallas_call | solution.py:278
  33.7 2.7 %collective-permute-start.7 = (f32[136,128]{1,0:T(8,128)S(1)}, f32[136,128]{1,0:T(8,128)S(1)}, u32[]{:S(2)}, u32[]{:S(2)}) collective-permute-start(f32[136,128]{1,0:T(8,128)S(1)} %get-tuple-element.34), channel_id=1, source_target_pairs={{0,1},{1,0},{2,3},{3,2},{4,5},{5,4},{6,7},{7,6},{8,9},{9,8},{10,11... | collective-permute-start | bytes 208904 | tf_op jit(solution)/shard_map/ppermute | solution.py:265
  36.4 2.5 %collective-permute-done.7 = f32[136,128]{1,0:T(8,128)S(1)} collective-permute-done((f32[136,128]{1,0:T(8,128)S(1)}, f32[136,128]{1,0:T(8,128)S(1)}, u32[]{:S(2)}, u32[]{:S(2)}) %collective-permute-start.7) | collective-permute-done | bytes 69664 | tf_op jit(solution)/shard_map/ppermute | solution.py:265
  38.9 2.8 %collective-permute-start.8 = (f32[136,128]{1,0:T(8,128)S(1)}, f32[136,128]{1,0:T(8,128)S(1)}, u32[]{:S(2)}, u32[]{:S(2)}) collective-permute-start(f32[136,128]{1,0:T(8,128)S(1)} %add.41), channel_id=1, source_target_pairs={{0,2},{1,3},{2,0},{3,1},{4,6},{5,7},{6,4},{7,5},{8,10},{9,11},{10,... | collective-permute-start | bytes 208904 | tf_op jit(solution)/shard_map/ppermute | solution.py:265
  41.7 2.3 %collective-permute-done.8 = f32[136,128]{1,0:T(8,128)S(1)} collective-permute-done((f32[136,128]{1,0:T(8,128)S(1)}, f32[136,128]{1,0:T(8,128)S(1)}, u32[]{:S(2)}, u32[]{:S(2)}) %collective-permute-start.8) | collective-permute-done | bytes 69664 | tf_op jit(solution)/shard_map/ppermute | solution.py:265
  44.0 2.1 %collective-permute-start.9 = (f32[136,128]{1,0:T(8,128)S(1)}, f32[136,128]{1,0:T(8,128)S(1)}, u32[]{:S(2)}, u32[]{:S(2)}) collective-permute-start(f32[136,128]{1,0:T(8,128)S(1)} %add.42.rest_2_), channel_id=1, source_target_pairs={{0,4},{1,5},{2,6},{3,7},{4,0},{5,1},{6,2},{7,3},{8,12},{9,13},{10,... | collective-permute-start | bytes 208904 | tf_op jit(solution)/shard_map/ppermute | solution.py:265
  46.1 3.2 %collective-permute-done.9.rest_3_ = f32[136,128]{1,0:T(8,128)S(1)} collective-permute-done((f32[136,128]{1,0:T(8,128)S(1)}, f32[136,128]{1,0:T(8,128)S(1)}, u32[]{:S(2)}, u32[]{:S(2)}) %collective-permute-start.9) | collective-permute-done | bytes 69664 | tf_op jit(solution)/shard_map/ppermute | solution.py:265
  49.3 3.3 %shard_map.73 = (f32[128,128]{1,0:T(8,128)S(1)}, f32[8,128]{1,0:T(8,128)S(1)}, f32[264,128]{1,0:T(8,128)S(1)}, f32[264,128]{1,0:T(8,128)S(1)}) custom-call(s32[320]{0:T(512)S(1)} %copy-done, s32[1,1]{1,0:T(1,128)S(6)} %copy.8.counts, s32[1,320]{1,0:T(1,128)S(1)} %reshape.11.cells, bf16[160,256,128]{2,1,0:T(8,128)(2,1)S(1)} %get-tuple-element.27.rest_0_.refs_0_, ...), custom_call_target="tpu_custom_call" | custom-call | tf_op jit(solution)/shard_map/pallas_call | solution.py:278
  52.6 0.1 collective-permute-start.10
  52.7 1.3 %collective-permute-done.10 = f32[264,128]{1,0:T(8,128)S(1)} collective-permute-done((f32[264,128]{1,0:T(8,128)S(1)}, f32[264,128]{1,0:T(8,128)S(1)}, u32[]{:S(2)}, u32[]{:S(2)}) %collective-permute-start.10) | collective-permute-done | bytes 135200 | tf_op jit(solution)/shard_map/ppermute | solution.py:265
  54.1 1.0 collective-permute-start.11
  55.1 4.7 %collective-permute-done.11 = f32[264,128]{1,0:T(8,128)S(1)} collective-permute-done((f32[264,128]{1,0:T(8,128)S(1)}, f32[264,128]{1,0:T(8,128)S(1)}, u32[]{:S(2)}, u32[]{:S(2)}) %collective-permute-start.11) | collective-permute-done | bytes 135200 | tf_op jit(solution)/shard_map/ppermute | solution.py:265
  59.8 0.1 collective-permute-start.12
  59.9 1.3 %collective-permute-done.12.rest_3_ = f32[264,128]{1,0:T(8,128)S(1)} collective-permute-done((f32[264,128]{1,0:T(8,128)S(1)}, f32[264,128]{1,0:T(8,128)S(1)}, u32[]{:S(2)}, u32[]{:S(2)}) %collective-permute-start.12) | collective-permute-done | bytes 135200 | tf_op jit(solution)/shard_map/ppermute | solution.py:265
  61.2 4.1 %shard_map.74 = (f32[512,128]{1,0:T(8,128)S(1)}, f32[8,128]{1,0:T(8,128)S(1)}, f32[128,128]{1,0:T(8,128)S(1)}, f32[136,128]{1,0:T(8,128)S(1)}) custom-call(s32[320]{0:T(512)S(1)} %copy-done.1, s32[1,1]{1,0:T(1,128)S(6)} %copy.8.counts, s32[1,320]{1,0:T(1,128)S(1)} %reshape.10.picks, bf16[160,256,128]{2,1,0:T(8,128)(2,1)S(1)} %get-tuple-element.31.rest_0_, ...), custom_call_target="tpu_custom_call" | custom-call | tf_op jit(solution)/shard_map/pallas_call | solution.py:278
  65.3 4.1 %collective-permute-start.13 = (f32[136,128]{1,0:T(8,128)S(1)}, f32[136,128]{1,0:T(8,128)S(1)}, u32[]{:S(2)}, u32[]{:S(2)}) collective-permute-start(f32[136,128]{1,0:T(8,128)S(1)} %get-tuple-element.42), channel_id=1, source_target_pairs={{0,1},{1,0},{2,3},{3,2},{4,5},{5,4},{6,7},{7,6},{8,9},{9,8},{10,11... | collective-permute-start | bytes 208904 | tf_op jit(solution)/shard_map/ppermute | solution.py:265
  69.4 2.5 %collective-permute-done.13 = f32[136,128]{1,0:T(8,128)S(1)} collective-permute-done((f32[136,128]{1,0:T(8,128)S(1)}, f32[136,128]{1,0:T(8,128)S(1)}, u32[]{:S(2)}, u32[]{:S(2)}) %collective-permute-start.13) | collective-permute-done | bytes 69664 | tf_op jit(solution)/shard_map/ppermute | solution.py:265
  71.9 2.6 %collective-permute-start.14 = (f32[136,128]{1,0:T(8,128)S(1)}, f32[136,128]{1,0:T(8,128)S(1)}, u32[]{:S(2)}, u32[]{:S(2)}) collective-permute-start(f32[136,128]{1,0:T(8,128)S(1)} %add.45), channel_id=1, source_target_pairs={{0,2},{1,3},{2,0},{3,1},{4,6},{5,7},{6,4},{7,5},{8,10},{9,11},{10,... | collective-permute-start | bytes 208904 | tf_op jit(solution)/shard_map/ppermute | solution.py:265
  74.5 2.3 %collective-permute-done.14 = f32[136,128]{1,0:T(8,128)S(1)} collective-permute-done((f32[136,128]{1,0:T(8,128)S(1)}, f32[136,128]{1,0:T(8,128)S(1)}, u32[]{:S(2)}, u32[]{:S(2)}) %collective-permute-start.14) | collective-permute-done | bytes 69664 | tf_op jit(solution)/shard_map/ppermute | solution.py:265
  76.8 2.1 %collective-permute-start.15 = (f32[136,128]{1,0:T(8,128)S(1)}, f32[136,128]{1,0:T(8,128)S(1)}, u32[]{:S(2)}, u32[]{:S(2)}) collective-permute-start(f32[136,128]{1,0:T(8,128)S(1)} %add.46.rest_2_), channel_id=1, source_target_pairs={{0,4},{1,5},{2,6},{3,7},{4,0},{5,1},{6,2},{7,3},{8,12},{9,13},{10,... | collective-permute-start | bytes 208904 | tf_op jit(solution)/shard_map/ppermute | solution.py:265
  79.0 3.2 %collective-permute-done.15.rest_3_ = f32[136,128]{1,0:T(8,128)S(1)} collective-permute-done((f32[136,128]{1,0:T(8,128)S(1)}, f32[136,128]{1,0:T(8,128)S(1)}, u32[]{:S(2)}, u32[]{:S(2)}) %collective-permute-start.15) | collective-permute-done | bytes 69664 | tf_op jit(solution)/shard_map/ppermute | solution.py:265
  82.2 3.3 %shard_map.75 = (f32[8,128]{1,0:T(8,128)S(1)}, f32[264,128]{1,0:T(8,128)S(1)}, f32[264,128]{1,0:T(8,128)S(1)}) custom-call(s32[320]{0:T(512)S(1)} %copy-done, s32[1,1]{1,0:T(1,128)S(6)} %copy.8.counts, s32[1,320]{1,0:T(1,128)S(1)} %reshape.11.cells, bf16[160,256,128]{2,1,0:T(8,128)(2,1)S(1)} %get-tuple-element.27.rest_0_.refs_0_, ...), custom_call_target="tpu_custom_call" | custom-call | tf_op jit(solution)/shard_map/pallas_call | solution.py:278
  85.6 1.3 %collective-permute-done.16 = f32[264,128]{1,0:T(8,128)S(1)} collective-permute-done((f32[264,128]{1,0:T(8,128)S(1)}, f32[264,128]{1,0:T(8,128)S(1)}, u32[]{:S(2)}, u32[]{:S(2)}) %collective-permute-start.16) | collective-permute-done | bytes 135200 | tf_op jit(solution)/shard_map/ppermute | solution.py:265
  86.9 1.7 %collective-permute-start.17 = (f32[264,128]{1,0:T(8,128)S(1)}, f32[264,128]{1,0:T(8,128)S(1)}, u32[]{:S(2)}, u32[]{:S(2)}) collective-permute-start(f32[264,128]{1,0:T(8,128)S(1)} %add.47), channel_id=1, source_target_pairs={{0,16},{8,24},{16,0},{24,8},{1,17},{9,25},{17,1},{25,9},{2,18},{10... | collective-permute-start | bytes 405512 | tf_op jit(solution)/shard_map/ppermute | solution.py:265
  88.6 4.0 %collective-permute-done.17 = f32[264,128]{1,0:T(8,128)S(1)} collective-permute-done((f32[264,128]{1,0:T(8,128)S(1)}, f32[264,128]{1,0:T(8,128)S(1)}, u32[]{:S(2)}, u32[]{:S(2)}) %collective-permute-start.17) | collective-permute-done | bytes 135200 | tf_op jit(solution)/shard_map/ppermute | solution.py:265
  92.7 0.2 shard_map.76
  92.9 1.8 %collective-permute-start.20 = (f32[8,128]{1,0:T(8,128)S(1)}, f32[8,128]{1,0:T(8,128)S(1)}, u32[]{:S(2)}, u32[]{:S(2)}) collective-permute-start(f32[8,128]{1,0:T(8,128)S(1)} %get-tuple-element.51), channel_id=1, source_target_pairs={{0,9},{1,8},{2,11},{3,10},{4,13},{5,12},{6,15},{7,14},{8,1},{9,0},... | collective-permute-start | bytes 12296 | tf_op jit(solution)/shard_map/ppermute | solution.py:424
  94.6 1.1 %collective-permute-start.19 = (f32[8,128]{1,0:T(8,128)S(1)}, f32[8,128]{1,0:T(8,128)S(1)}, u32[]{:S(2)}, u32[]{:S(2)}) collective-permute-start(f32[8,128]{1,0:T(8,128)S(1)} %get-tuple-element.51), channel_id=1, source_target_pairs={{0,1},{1,0},{2,3},{3,2},{4,5},{5,4},{6,7},{7,6},{8,9},{9,8},{10,11... | collective-permute-start | bytes 12296 | tf_op jit(solution)/shard_map/ppermute | solution.py:265
  95.8 0.1 collective-permute-done.20
  96.0 2.3 %collective-permute-done.19 = f32[8,128]{1,0:T(8,128)S(1)} collective-permute-done((f32[8,128]{1,0:T(8,128)S(1)}, f32[8,128]{1,0:T(8,128)S(1)}, u32[]{:S(2)}, u32[]{:S(2)}) %collective-permute-start.19) | collective-permute-done | bytes 4128 | tf_op jit(solution)/shard_map/ppermute | solution.py:265
  98.3 4.1 %collective-permute-start.23 = (f32[8,128]{1,0:T(8,128)S(1)}, f32[8,128]{1,0:T(8,128)S(1)}, u32[]{:S(2)}, u32[]{:S(2)}) collective-permute-start(f32[8,128]{1,0:T(8,128)S(1)} %add_add_fusion.refs_8_), channel_id=1, source_target_pairs={{0,6},{1,7},{2,4},{3,5},{4,2},{5,3},{6,0},{7,1},{8,14},{9,15},{10,... | collective-permute-start | bytes 12296 | tf_op jit(solution)/shard_map/ppermute | solution.py:265
  102.3 0.6 collective-permute-start.21
  103.0 0.9 collective-permute-done.23.refs_11_
  103.9 2.9 %collective-permute-done.22.refs_10_ = f32[8,128]{1,0:T(8,128)S(1)} collective-permute-done((f32[8,128]{1,0:T(8,128)S(1)}, f32[8,128]{1,0:T(8,128)S(1)}, u32[]{:S(2)}, u32[]{:S(2)}) %collective-permute-start.22) | collective-permute-done | bytes 4128 | tf_op jit(solution)/shard_map/ppermute | solution.py:265
  106.8 0.7 shard_map.77
  (29 shorter events, 0.3 us)
Async XLA Ops:
  0.6 12.6 %copy-start.1 = (s32[320]{0:T(512)S(1)}, s32[320]{0:T(512)}, u32[]{:S(2)}) copy-start(s32[320]{0:T(512)} %cell.3) | copy-start | bytes 3844
  0.6 7.5 %collective-permute-start = (f32[16,128]{1,0:T(8,128)}, f32[16,128]{1,0:T(8,128)S(1)}, u32[]{:S(2)}, u32[]{:S(2)}) collective-permute-start(f32[16,128]{1,0:T(8,128)} %rest_0_.1), channel_id=1, source_target_pairs={{0,1},{1,0},{2,3},{3,2},{4,5},{5,4},{6,7},{7,6},{8,9},{9,8},{10,11... | collective-permute-start | bytes 24584 | tf_op jit(solution)/shard_map/ppermute | solution.py:265
  8.1 9.6 %collective-permute-start.3 = (f32[32,128]{1,0:T(8,128)S(1)}, f32[32,128]{1,0:T(8,128)S(1)}, u32[]{:S(2)}, u32[]{:S(2)}) collective-permute-start(f32[32,128]{1,0:T(8,128)S(1)} %constant_dynamic-update-slice_fusion.rest_2_), channel_id=1, source_target_pairs={{0,6},{1,7},{2,4},{3,5},{4,2},{5,3},{6,0},{7,1},{8,14},{9,15},{10,... | collective-permute-start | bytes 49160 | tf_op jit(solution)/shard_map/ppermute | solution.py:265
  11.8 5.9 %collective-permute-start.2 = (f32[32,128]{1,0:T(8,128)S(1)}, f32[32,128]{1,0:T(8,128)S(1)}, u32[]{:S(2)}, u32[]{:S(2)}) collective-permute-start(f32[32,128]{1,0:T(8,128)S(1)} %constant_dynamic-update-slice_fusion.rest_2_), channel_id=1, source_target_pairs={{0,4},{1,5},{2,6},{3,7},{4,0},{5,1},{6,2},{7,3},{8,12},{9,13},{10,... | collective-permute-start | bytes 49160 | tf_op jit(solution)/shard_map/ppermute | solution.py:265
  11.8 5.9 %collective-permute-start.1 = (f32[32,128]{1,0:T(8,128)S(1)}, f32[32,128]{1,0:T(8,128)S(1)}, u32[]{:S(2)}, u32[]{:S(2)}) collective-permute-start(f32[32,128]{1,0:T(8,128)S(1)} %constant_dynamic-update-slice_fusion.rest_2_), channel_id=1, source_target_pairs={{0,2},{1,3},{2,0},{3,1},{4,6},{5,7},{6,4},{7,5},{8,10},{9,11},{10,... | collective-permute-start | bytes 49160 | tf_op jit(solution)/shard_map/ppermute | solution.py:265
  13.3 4.5 %copy-start = (s32[320]{0:T(512)S(1)}, s32[320]{0:T(512)}, u32[]{:S(2)}) copy-start(s32[320]{0:T(512)} %pick.5) | copy-start | bytes 3844
  21.1 1.4 %collective-permute-start.4 = (f32[264,128]{1,0:T(8,128)S(1)}, f32[264,128]{1,0:T(8,128)S(1)}, u32[]{:S(2)}, u32[]{:S(2)}) collective-permute-start(f32[264,128]{1,0:T(8,128)S(1)} %get-tuple-element.30), channel_id=1, source_target_pairs={{0,8},{8,0},{16,24},{24,16},{1,9},{9,1},{17,25},{25,17},{2,10},{10... | collective-permute-start | bytes 405512 | tf_op jit(solution)/shard_map/ppermute | solution.py:265
  22.5 5.7 %collective-permute-start.5 = (f32[264,128]{1,0:T(8,128)S(1)}, f32[264,128]{1,0:T(8,128)S(1)}, u32[]{:S(2)}, u32[]{:S(2)}) collective-permute-start(f32[264,128]{1,0:T(8,128)S(1)} %add.39.refs_1_), channel_id=1, source_target_pairs={{0,16},{8,24},{16,0},{24,8},{1,17},{9,25},{17,1},{25,9},{2,18},{10... | collective-permute-start | bytes 405512 | tf_op jit(solution)/shard_map/ppermute | solution.py:265
  28.2 1.4 %collective-permute-start.6 = (f32[264,128]{1,0:T(8,128)S(1)}, f32[264,128]{1,0:T(8,128)S(1)}, u32[]{:S(2)}, u32[]{:S(2)}) collective-permute-start(f32[264,128]{1,0:T(8,128)S(1)} %add.40.rest_2_), channel_id=1, source_target_pairs={{0,8},{8,0},{16,24},{24,16},{1,9},{9,1},{17,25},{25,17},{2,10},{10... | collective-permute-start | bytes 405512 | tf_op jit(solution)/shard_map/ppermute | solution.py:265
  33.7 5.2 %collective-permute-start.7 = (f32[136,128]{1,0:T(8,128)S(1)}, f32[136,128]{1,0:T(8,128)S(1)}, u32[]{:S(2)}, u32[]{:S(2)}) collective-permute-start(f32[136,128]{1,0:T(8,128)S(1)} %get-tuple-element.34), channel_id=1, source_target_pairs={{0,1},{1,0},{2,3},{3,2},{4,5},{5,4},{6,7},{7,6},{8,9},{9,8},{10,11... | collective-permute-start | bytes 208904 | tf_op jit(solution)/shard_map/ppermute | solution.py:265
  38.9 5.1 %collective-permute-start.8 = (f32[136,128]{1,0:T(8,128)S(1)}, f32[136,128]{1,0:T(8,128)S(1)}, u32[]{:S(2)}, u32[]{:S(2)}) collective-permute-start(f32[136,128]{1,0:T(8,128)S(1)} %add.41), channel_id=1, source_target_pairs={{0,2},{1,3},{2,0},{3,1},{4,6},{5,7},{6,4},{7,5},{8,10},{9,11},{10,... | collective-permute-start | bytes 208904 | tf_op jit(solution)/shard_map/ppermute | solution.py:265
  44.0 5.3 %collective-permute-start.9 = (f32[136,128]{1,0:T(8,128)S(1)}, f32[136,128]{1,0:T(8,128)S(1)}, u32[]{:S(2)}, u32[]{:S(2)}) collective-permute-start(f32[136,128]{1,0:T(8,128)S(1)} %add.42.rest_2_), channel_id=1, source_target_pairs={{0,4},{1,5},{2,6},{3,7},{4,0},{5,1},{6,2},{7,3},{8,12},{9,13},{10,... | collective-permute-start | bytes 208904 | tf_op jit(solution)/shard_map/ppermute | solution.py:265
  52.6 1.4 %collective-permute-start.10 = (f32[264,128]{1,0:T(8,128)S(1)}, f32[264,128]{1,0:T(8,128)S(1)}, u32[]{:S(2)}, u32[]{:S(2)}) collective-permute-start(f32[264,128]{1,0:T(8,128)S(1)} %get-tuple-element.38), channel_id=1, source_target_pairs={{0,8},{8,0},{16,24},{24,16},{1,9},{9,1},{17,25},{25,17},{2,10},{10... | collective-permute-start | bytes 405512 | tf_op jit(solution)/shard_map/ppermute | solution.py:265
  54.1 5.7 %collective-permute-start.11 = (f32[264,128]{1,0:T(8,128)S(1)}, f32[264,128]{1,0:T(8,128)S(1)}, u32[]{:S(2)}, u32[]{:S(2)}) collective-permute-start(f32[264,128]{1,0:T(8,128)S(1)} %add.43), channel_id=1, source_target_pairs={{0,16},{8,24},{16,0},{24,8},{1,17},{9,25},{17,1},{25,9},{2,18},{10... | collective-permute-start | bytes 405512 | tf_op jit(solution)/shard_map/ppermute | solution.py:265
  59.8 1.4 %collective-permute-start.12 = (f32[264,128]{1,0:T(8,128)S(1)}, f32[264,128]{1,0:T(8,128)S(1)}, u32[]{:S(2)}, u32[]{:S(2)}) collective-permute-start(f32[264,128]{1,0:T(8,128)S(1)} %add.44.rest_2_), channel_id=1, source_target_pairs={{0,8},{8,0},{16,24},{24,16},{1,9},{9,1},{17,25},{25,17},{2,10},{10... | collective-permute-start | bytes 405512 | tf_op jit(solution)/shard_map/ppermute | solution.py:265
  65.3 6.6 %collective-permute-start.13 = (f32[136,128]{1,0:T(8,128)S(1)}, f32[136,128]{1,0:T(8,128)S(1)}, u32[]{:S(2)}, u32[]{:S(2)}) collective-permute-start(f32[136,128]{1,0:T(8,128)S(1)} %get-tuple-element.42), channel_id=1, source_target_pairs={{0,1},{1,0},{2,3},{3,2},{4,5},{5,4},{6,7},{7,6},{8,9},{9,8},{10,11... | collective-permute-start | bytes 208904 | tf_op jit(solution)/shard_map/ppermute | solution.py:265
  71.9 4.9 %collective-permute-start.14 = (f32[136,128]{1,0:T(8,128)S(1)}, f32[136,128]{1,0:T(8,128)S(1)}, u32[]{:S(2)}, u32[]{:S(2)}) collective-permute-start(f32[136,128]{1,0:T(8,128)S(1)} %add.45), channel_id=1, source_target_pairs={{0,2},{1,3},{2,0},{3,1},{4,6},{5,7},{6,4},{7,5},{8,10},{9,11},{10,... | collective-permute-start | bytes 208904 | tf_op jit(solution)/shard_map/ppermute | solution.py:265
  76.8 5.3 %collective-permute-start.15 = (f32[136,128]{1,0:T(8,128)S(1)}, f32[136,128]{1,0:T(8,128)S(1)}, u32[]{:S(2)}, u32[]{:S(2)}) collective-permute-start(f32[136,128]{1,0:T(8,128)S(1)} %add.46.rest_2_), channel_id=1, source_target_pairs={{0,4},{1,5},{2,6},{3,7},{4,0},{5,1},{6,2},{7,3},{8,12},{9,13},{10,... | collective-permute-start | bytes 208904 | tf_op jit(solution)/shard_map/ppermute | solution.py:265
  85.5 1.4 %collective-permute-start.16 = (f32[264,128]{1,0:T(8,128)S(1)}, f32[264,128]{1,0:T(8,128)S(1)}, u32[]{:S(2)}, u32[]{:S(2)}) collective-permute-start(f32[264,128]{1,0:T(8,128)S(1)} %get-tuple-element.46), channel_id=1, source_target_pairs={{0,8},{8,0},{16,24},{24,16},{1,9},{9,1},{17,25},{25,17},{2,10},{10... | collective-permute-start | bytes 405512 | tf_op jit(solution)/shard_map/ppermute | solution.py:265
  86.9 5.7 %collective-permute-start.17 = (f32[264,128]{1,0:T(8,128)S(1)}, f32[264,128]{1,0:T(8,128)S(1)}, u32[]{:S(2)}, u32[]{:S(2)}) collective-permute-start(f32[264,128]{1,0:T(8,128)S(1)} %add.47), channel_id=1, source_target_pairs={{0,16},{8,24},{16,0},{24,8},{1,17},{9,25},{17,1},{25,9},{2,18},{10... | collective-permute-start | bytes 405512 | tf_op jit(solution)/shard_map/ppermute | solution.py:265
  92.9 3.1 %collective-permute-start.20 = (f32[8,128]{1,0:T(8,128)S(1)}, f32[8,128]{1,0:T(8,128)S(1)}, u32[]{:S(2)}, u32[]{:S(2)}) collective-permute-start(f32[8,128]{1,0:T(8,128)S(1)} %get-tuple-element.51), channel_id=1, source_target_pairs={{0,9},{1,8},{2,11},{3,10},{4,13},{5,12},{6,15},{7,14},{8,1},{9,0},... | collective-permute-start | bytes 12296 | tf_op jit(solution)/shard_map/ppermute | solution.py:424
  94.6 3.6 %collective-permute-start.19 = (f32[8,128]{1,0:T(8,128)S(1)}, f32[8,128]{1,0:T(8,128)S(1)}, u32[]{:S(2)}, u32[]{:S(2)}) collective-permute-start(f32[8,128]{1,0:T(8,128)S(1)} %get-tuple-element.51), channel_id=1, source_target_pairs={{0,1},{1,0},{2,3},{3,2},{4,5},{5,4},{6,7},{7,6},{8,9},{9,8},{10,11... | collective-permute-start | bytes 12296 | tf_op jit(solution)/shard_map/ppermute | solution.py:265
  95.8 2.5 %collective-permute-start.18 = (f32[8,128]{1,0:T(8,128)S(1)}, f32[8,128]{1,0:T(8,128)S(1)}, u32[]{:S(2)}, u32[]{:S(2)}) collective-permute-start(f32[8,128]{1,0:T(8,128)S(1)} %get-tuple-element.51), channel_id=1, source_target_pairs={{0,8},{8,0},{16,24},{24,16},{1,9},{9,1},{17,25},{25,17},{2,10},{10... | collective-permute-start | bytes 12296 | tf_op jit(solution)/shard_map/ppermute | solution.py:265
  98.3 5.6 %collective-permute-start.23 = (f32[8,128]{1,0:T(8,128)S(1)}, f32[8,128]{1,0:T(8,128)S(1)}, u32[]{:S(2)}, u32[]{:S(2)}) collective-permute-start(f32[8,128]{1,0:T(8,128)S(1)} %add_add_fusion.refs_8_), channel_id=1, source_target_pairs={{0,6},{1,7},{2,4},{3,5},{4,2},{5,3},{6,0},{7,1},{8,14},{9,15},{10,... | collective-permute-start | bytes 12296 | tf_op jit(solution)/shard_map/ppermute | solution.py:265
  102.3 4.5 %collective-permute-start.22 = (f32[8,128]{1,0:T(8,128)S(1)}, f32[8,128]{1,0:T(8,128)S(1)}, u32[]{:S(2)}, u32[]{:S(2)}) collective-permute-start(f32[8,128]{1,0:T(8,128)S(1)} %add_add_fusion.refs_8_), channel_id=1, source_target_pairs={{0,4},{1,5},{2,6},{3,7},{4,0},{5,1},{6,2},{7,3},{8,12},{9,13},{10,... | collective-permute-start | bytes 12296 | tf_op jit(solution)/shard_map/ppermute | solution.py:265
  102.3 4.5 %collective-permute-start.21 = (f32[8,128]{1,0:T(8,128)S(1)}, f32[8,128]{1,0:T(8,128)S(1)}, u32[]{:S(2)}, u32[]{:S(2)}) collective-permute-start(f32[8,128]{1,0:T(8,128)S(1)} %add_add_fusion.refs_8_), channel_id=1, source_target_pairs={{0,2},{1,3},{2,0},{3,1},{4,6},{5,7},{6,4},{7,5},{8,10},{9,11},{10,... | collective-permute-start | bytes 12296 | tf_op jit(solution)/shard_map/ppermute | solution.py:265

commit v10 on v9

--- a/solution.py
+++ b/solution.py
@@ -12,7 +12,7 @@
 ITERS = 2
 B = 128
 SUB = 8
-GROUP = 80
+GROUP = 160
 PARTS = 2
 TURNED = 1
 STEP = 8

time: 108 us -> 106 us (0.981)
  starting transfers between devices: 35.5 us -> 25.9 us
  waiting for transfers between devices: 38.5 us -> 42.8 us
  Pallas kernels: 31.8 us -> 36 us
    ppermute x23, starting transfers between devices: 33.7 us -> 25.8 us  [swapped(): return lax.ppermute(block, axis, [(i, i ^ bit) for i in range(size)])]
    pallas_call x5, Pallas kernels: 18.1 us -> 22.4 us  [call(): pl.pallas_call(kernel, out_shape=outs, in_specs=[SCALAR] * 2 + [VECTOR] *...]
    ppermute x23, waiting for transfers between devices: 38.4 us -> 41.6 us  [swapped(): return lax.ppermute(block, axis, [(i, i ^ bit) for i in range(size)])]
    ppermute x1, starting transfers between devices: 1.77 us -> 0.07 us  [per_device(): lax.ppermute(square, ('rows', 'cols'), both)]
where the time goes in v10:
time: 106 us
  waiting for transfers between devices  42.8 us (40%)
  Pallas kernels  36 us (34%)
  starting transfers between devices  25.9 us (24%)
  between operations  1.55 us (1%)
    ppermute x23, waiting for transfers between devices, swapped(): return lax.ppermute(block, axis, [(i, i ^ bit) for i in range(size)])  41.6 us
    ppermute x23, starting transfers between devices, swapped(): return lax.ppermute(block, axis, [(i, i ^ bit) for i in range(size)])  25.8 us
    pallas_call x5, Pallas kernels, call(): pl.pallas_call(kernel, out_shape=outs, in_specs=[SCALAR] * 2 + [VECTOR] *...  22.4 us
    pallas_call x2, Pallas kernels, split_part(): pl.pallas_call(functools.partial(split_tiles, start, passes), out_shape=[...  8.84 us
    pallas_call x1, Pallas kernels, turned(): pl.pallas_call(turn_tiles, out_shape=[shape(*data.shape)] + [pltpu.VMEM(p...  3.94 us
  transfers between devices with their start and end apart: 24, of which 18 were waited for; matrix products, arithmetic and copies ran while one was open for 0% of the time, Pallas kernels for 12%

profile of v10, /device:TPU:0, one launch (start us, length us, event | category | flops | bytes accessed | tf_op | source)
XLA Modules:
  0.0 106.5 jit_solution(1962468036395749599)
XLA Ops:
  0.6 3.0 %collective-permute-start = (f32[16,128]{1,0:T(8,128)}, f32[16,128]{1,0:T(8,128)S(1)}, u32[]{:S(2)}, u32[]{:S(2)}) collective-permute-start(f32[16,128]{1,0:T(8,128)} %rest_0_.1), channel_id=1, source_target_pairs={{0,1},{1,0},{2,3},{3,2},{4,5},{5,4},{6,7},{7,6},{8,9},{9,8},{10,11... | collective-permute-start | bytes 24584 | tf_op jit(solution)/shard_map/ppermute | solution.py:265
  3.7 4.4 %shard_map.68 = (bf16[160,256,128]{2,1,0:T(8,128)(2,1)S(1)}, f32[16,128]{1,0:T(8,128)S(1)}) custom-call(f32[320,128,128]{2,1,0:T(8,128)} %tiles.3, f32[16,128]{1,0:T(8,128)} %rest_0_.1), custom_call_target="tpu_custom_call" | custom-call | flops 10485760 | bytes 10485760 | tf_op jit(solution)/shard_map/pallas_call | solution.py:295
  8.1 3.7 %collective-permute-start.3 = (f32[32,128]{1,0:T(8,128)S(1)}, f32[32,128]{1,0:T(8,128)S(1)}, u32[]{:S(2)}, u32[]{:S(2)}) collective-permute-start(f32[32,128]{1,0:T(8,128)S(1)} %constant_dynamic-update-slice_fusion.rest_2_), channel_id=1, source_target_pairs={{0,6},{1,7},{2,4},{3,5},{4,2},{5,3},{6,0},{7,1},{8,14},{9,15},{10,... | collective-permute-start | bytes 49160 | tf_op jit(solution)/shard_map/ppermute | solution.py:265
  11.8 0.8 collective-permute-start.1
  13.3 4.4 %shard_map.69.rest_1_ = bf16[160,256,128]{2,1,0:T(8,128)(2,1)S(1)} custom-call(f32[320,128,128]{2,1,0:T(8,128)} %tiles.3), custom_call_target="tpu_custom_call" | custom-call | flops 10485760 | bytes 10485760 | tf_op jit(solution)/shard_map/pallas_call | solution.py:295
  17.7 3.9 %shard_map.70 = (f32[128,128]{1,0:T(8,128)S(1)}, f32[264,128]{1,0:T(8,128)S(1)}, f32[264,128]{1,0:T(8,128)S(1)}) custom-call(s32[320]{0:T(512)S(1)} %copy-done, s32[1,1]{1,0:T(1,128)S(6)} %copy.8.counts, s32[1,320]{1,0:T(1,128)S(1)} %reshape.11.cells, bf16[160,256,128]{2,1,0:T(8,128)(2,1)S(1)} %get-tuple-element.27.rest_0_.refs_0_, ...), custom_call_target="tpu_custom_call" | custom-call | tf_op jit(solution)/shard_map/pallas_call | solution.py:278
  21.6 0.1 collective-permute-start.4
  21.7 1.3 %collective-permute-done.4 = f32[264,128]{1,0:T(8,128)S(1)} collective-permute-done((f32[264,128]{1,0:T(8,128)S(1)}, f32[264,128]{1,0:T(8,128)S(1)}, u32[]{:S(2)}, u32[]{:S(2)}) %collective-permute-start.4) | collective-permute-done | bytes 135200 | tf_op jit(solution)/shard_map/ppermute | solution.py:265
  23.1 1.6 %collective-permute-start.5 = (f32[264,128]{1,0:T(8,128)S(1)}, f32[264,128]{1,0:T(8,128)S(1)}, u32[]{:S(2)}, u32[]{:S(2)}) collective-permute-start(f32[264,128]{1,0:T(8,128)S(1)} %add.39.refs_1_), channel_id=1, source_target_pairs={{0,16},{8,24},{16,0},{24,8},{1,17},{9,25},{17,1},{25,9},{2,18},{10... | collective-permute-start | bytes 405512 | tf_op jit(solution)/shard_map/ppermute | solution.py:265
  24.6 3.9 %shard_map.71 = (f32[264,128]{1,0:T(8,128)S(1)}, bf16[160,256,128]{2,1,0:T(8,128)(2,1)S(1)}) custom-call(bf16[160,256,128]{2,1,0:T(8,128)(2,1)S(1)} %get-tuple-element.27.rest_0_.refs_0_, f32[264,128]{1,0:T(8,128)S(1)} %add.39.refs_1_), custom_call_target="tpu_custom_call" | custom-call | bytes 5242880 | tf_op jit(solution)/shard_map/pallas_call | solution.py:316
  28.6 0.2 collective-permute-done.5
  28.8 0.1 collective-permute-start.6
  28.9 1.3 %collective-permute-done.6.rest_3_ = f32[264,128]{1,0:T(8,128)S(1)} collective-permute-done((f32[264,128]{1,0:T(8,128)S(1)}, f32[264,128]{1,0:T(8,128)S(1)}, u32[]{:S(2)}, u32[]{:S(2)}) %collective-permute-start.6) | collective-permute-done | bytes 135200 | tf_op jit(solution)/shard_map/ppermute | solution.py:265
  30.2 5.3 %shard_map.72 = (f32[512,128]{1,0:T(8,128)S(1)}, f32[8,128]{1,0:T(8,128)S(1)}, f32[128,128]{1,0:T(8,128)S(1)}, f32[136,128]{1,0:T(8,128)S(1)}) custom-call(s32[320]{0:T(512)S(1)} %copy-done.1, s32[1,1]{1,0:T(1,128)S(6)} %copy.8.counts, s32[1,320]{1,0:T(1,128)S(1)} %reshape.10.picks, bf16[160,256,128]{2,1,0:T(8,128)(2,1)S(1)} %get-tuple-element.31.rest_0_, ...), custom_call_target="tpu_custom_call" | custom-call | tf_op jit(solution)/shard_map/pallas_call | solution.py:278
  35.5 0.4 collective-permute-start.7
  36.0 3.9 %collective-permute-done.7 = f32[136,128]{1,0:T(8,128)S(1)} collective-permute-done((f32[136,128]{1,0:T(8,128)S(1)}, f32[136,128]{1,0:T(8,128)S(1)}, u32[]{:S(2)}, u32[]{:S(2)}) %collective-permute-start.7) | collective-permute-done | bytes 69664 | tf_op jit(solution)/shard_map/ppermute | solution.py:265
  39.9 0.1 collective-permute-start.8
  40.0 4.3 %collective-permute-done.8 = f32[136,128]{1,0:T(8,128)S(1)} collective-permute-done((f32[136,128]{1,0:T(8,128)S(1)}, f32[136,128]{1,0:T(8,128)S(1)}, u32[]{:S(2)}, u32[]{:S(2)}) %collective-permute-start.8) | collective-permute-done | bytes 69664 | tf_op jit(solution)/shard_map/ppermute | solution.py:265
  44.3 2.2 %collective-permute-start.9 = (f32[136,128]{1,0:T(8,128)S(1)}, f32[136,128]{1,0:T(8,128)S(1)}, u32[]{:S(2)}, u32[]{:S(2)}) collective-permute-start(f32[136,128]{1,0:T(8,128)S(1)} %add.42.rest_2_), channel_id=1, source_target_pairs={{0,4},{1,5},{2,6},{3,7},{4,0},{5,1},{6,2},{7,3},{8,12},{9,13},{10,... | collective-permute-start | bytes 208904 | tf_op jit(solution)/shard_map/ppermute | solution.py:265
  46.5 3.1 %collective-permute-done.9.rest_3_ = f32[136,128]{1,0:T(8,128)S(1)} collective-permute-done((f32[136,128]{1,0:T(8,128)S(1)}, f32[136,128]{1,0:T(8,128)S(1)}, u32[]{:S(2)}, u32[]{:S(2)}) %collective-permute-start.9) | collective-permute-done | bytes 69664 | tf_op jit(solution)/shard_map/ppermute | solution.py:265
  49.6 3.9 %shard_map.73 = (f32[128,128]{1,0:T(8,128)S(1)}, f32[8,128]{1,0:T(8,128)S(1)}, f32[264,128]{1,0:T(8,128)S(1)}, f32[264,128]{1,0:T(8,128)S(1)}) custom-call(s32[320]{0:T(512)S(1)} %copy-done, s32[1,1]{1,0:T(1,128)S(6)} %copy.8.counts, s32[1,320]{1,0:T(1,128)S(1)} %reshape.11.cells, bf16[160,256,128]{2,1,0:T(8,128)(2,1)S(1)} %get-tuple-element.27.rest_0_.refs_0_, ...), custom_call_target="tpu_custom_call" | custom-call | tf_op jit(solution)/shard_map/pallas_call | solution.py:278
  53.5 0.1 collective-permute-start.10
  53.6 1.3 %collective-permute-done.10 = f32[264,128]{1,0:T(8,128)S(1)} collective-permute-done((f32[264,128]{1,0:T(8,128)S(1)}, f32[264,128]{1,0:T(8,128)S(1)}, u32[]{:S(2)}, u32[]{:S(2)}) %collective-permute-start.10) | collective-permute-done | bytes 135200 | tf_op jit(solution)/shard_map/ppermute | solution.py:265
  54.9 1.5 %collective-permute-start.11 = (f32[264,128]{1,0:T(8,128)S(1)}, f32[264,128]{1,0:T(8,128)S(1)}, u32[]{:S(2)}, u32[]{:S(2)}) collective-permute-start(f32[264,128]{1,0:T(8,128)S(1)} %add.43), channel_id=1, source_target_pairs={{0,16},{8,24},{16,0},{24,8},{1,17},{9,25},{17,1},{25,9},{2,18},{10... | collective-permute-start | bytes 405512 | tf_op jit(solution)/shard_map/ppermute | solution.py:265
  56.5 4.2 %collective-permute-done.11 = f32[264,128]{1,0:T(8,128)S(1)} collective-permute-done((f32[264,128]{1,0:T(8,128)S(1)}, f32[264,128]{1,0:T(8,128)S(1)}, u32[]{:S(2)}, u32[]{:S(2)}) %collective-permute-start.11) | collective-permute-done | bytes 135200 | tf_op jit(solution)/shard_map/ppermute | solution.py:265
  60.7 0.1 collective-permute-start.12
  60.7 1.3 %collective-permute-done.12.rest_3_ = f32[264,128]{1,0:T(8,128)S(1)} collective-permute-done((f32[264,128]{1,0:T(8,128)S(1)}, f32[264,128]{1,0:T(8,128)S(1)}, u32[]{:S(2)}, u32[]{:S(2)}) %collective-permute-start.12) | collective-permute-done | bytes 135200 | tf_op jit(solution)/shard_map/ppermute | solution.py:265
  62.1 5.4 %shard_map.74 = (f32[512,128]{1,0:T(8,128)S(1)}, f32[8,128]{1,0:T(8,128)S(1)}, f32[128,128]{1,0:T(8,128)S(1)}, f32[136,128]{1,0:T(8,128)S(1)}) custom-call(s32[320]{0:T(512)S(1)} %copy-done.1, s32[1,1]{1,0:T(1,128)S(6)} %copy.8.counts, s32[1,320]{1,0:T(1,128)S(1)} %reshape.10.picks, bf16[160,256,128]{2,1,0:T(8,128)(2,1)S(1)} %get-tuple-element.31.rest_0_, ...), custom_call_target="tpu_custom_call" | custom-call | tf_op jit(solution)/shard_map/pallas_call | solution.py:278
  67.5 0.4 collective-permute-start.13
  67.9 4.0 %collective-permute-done.13 = f32[136,128]{1,0:T(8,128)S(1)} collective-permute-done((f32[136,128]{1,0:T(8,128)S(1)}, f32[136,128]{1,0:T(8,128)S(1)}, u32[]{:S(2)}, u32[]{:S(2)}) %collective-permute-start.13) | collective-permute-done | bytes 69664 | tf_op jit(solution)/shard_map/ppermute | solution.py:265
  71.9 0.1 collective-permute-start.14
  71.9 4.3 %collective-permute-done.14 = f32[136,128]{1,0:T(8,128)S(1)} collective-permute-done((f32[136,128]{1,0:T(8,128)S(1)}, f32[136,128]{1,0:T(8,128)S(1)}, u32[]{:S(2)}, u32[]{:S(2)}) %collective-permute-start.14) | collective-permute-done | bytes 69664 | tf_op jit(solution)/shard_map/ppermute | solution.py:265
  76.3 2.7 %collective-permute-start.15 = (f32[136,128]{1,0:T(8,128)S(1)}, f32[136,128]{1,0:T(8,128)S(1)}, u32[]{:S(2)}, u32[]{:S(2)}) collective-permute-start(f32[136,128]{1,0:T(8,128)S(1)} %add.46.rest_2_), channel_id=1, source_target_pairs={{0,4},{1,5},{2,6},{3,7},{4,0},{5,1},{6,2},{7,3},{8,12},{9,13},{10,... | collective-permute-start | bytes 208904 | tf_op jit(solution)/shard_map/ppermute | solution.py:265
  78.9 2.6 %collective-permute-done.15.rest_3_ = f32[136,128]{1,0:T(8,128)S(1)} collective-permute-done((f32[136,128]{1,0:T(8,128)S(1)}, f32[136,128]{1,0:T(8,128)S(1)}, u32[]{:S(2)}, u32[]{:S(2)}) %collective-permute-start.15) | collective-permute-done | bytes 69664 | tf_op jit(solution)/shard_map/ppermute | solution.py:265
  81.5 3.9 %shard_map.75 = (f32[8,128]{1,0:T(8,128)S(1)}, f32[264,128]{1,0:T(8,128)S(1)}, f32[264,128]{1,0:T(8,128)S(1)}) custom-call(s32[320]{0:T(512)S(1)} %copy-done, s32[1,1]{1,0:T(1,128)S(6)} %copy.8.counts, s32[1,320]{1,0:T(1,128)S(1)} %reshape.11.cells, bf16[160,256,128]{2,1,0:T(8,128)(2,1)S(1)} %get-tuple-element.27.rest_0_.refs_0_, ...), custom_call_target="tpu_custom_call" | custom-call | tf_op jit(solution)/shard_map/pallas_call | solution.py:278
  85.5 1.3 %collective-permute-done.16 = f32[264,128]{1,0:T(8,128)S(1)} collective-permute-done((f32[264,128]{1,0:T(8,128)S(1)}, f32[264,128]{1,0:T(8,128)S(1)}, u32[]{:S(2)}, u32[]{:S(2)}) %collective-permute-start.16) | collective-permute-done | bytes 135200 | tf_op jit(solution)/shard_map/ppermute | solution.py:265
  86.9 1.8 %collective-permute-start.17 = (f32[264,128]{1,0:T(8,128)S(1)}, f32[264,128]{1,0:T(8,128)S(1)}, u32[]{:S(2)}, u32[]{:S(2)}) collective-permute-start(f32[264,128]{1,0:T(8,128)S(1)} %add.47), channel_id=1, source_target_pairs={{0,16},{8,24},{16,0},{24,8},{1,17},{9,25},{17,1},{25,9},{2,18},{10... | collective-permute-start | bytes 405512 | tf_op jit(solution)/shard_map/ppermute | solution.py:265
  88.7 3.9 %collective-permute-done.17 = f32[264,128]{1,0:T(8,128)S(1)} collective-permute-done((f32[264,128]{1,0:T(8,128)S(1)}, f32[264,128]{1,0:T(8,128)S(1)}, u32[]{:S(2)}, u32[]{:S(2)}) %collective-permute-start.17) | collective-permute-done | bytes 135200 | tf_op jit(solution)/shard_map/ppermute | solution.py:265
  92.6 0.2 shard_map.76
  92.9 1.0 collective-permute-start.19
  93.8 0.9 collective-permute-start.18
  94.7 1.2 %collective-permute-done.20 = f32[8,128]{1,0:T(8,128)S(1)} collective-permute-done((f32[8,128]{1,0:T(8,128)S(1)}, f32[8,128]{1,0:T(8,128)S(1)}, u32[]{:S(2)}, u32[]{:S(2)}) %collective-permute-start.20) | collective-permute-done | bytes 4128 | tf_op jit(solution)/shard_map/ppermute | solution.py:424
  95.9 0.7 collective-permute-done.19
  96.6 4.7 %collective-permute-start.23 = (f32[8,128]{1,0:T(8,128)S(1)}, f32[8,128]{1,0:T(8,128)S(1)}, u32[]{:S(2)}, u32[]{:S(2)}) collective-permute-start(f32[8,128]{1,0:T(8,128)S(1)} %add_add_fusion.refs_8_), channel_id=1, source_target_pairs={{0,6},{1,7},{2,4},{3,5},{4,2},{5,3},{6,0},{7,1},{8,14},{9,15},{10,... | collective-permute-start | bytes 12296 | tf_op jit(solution)/shard_map/ppermute | solution.py:265
  101.3 0.6 collective-permute-start.21
  101.9 0.9 collective-permute-done.23.refs_11_
  102.8 2.9 %collective-permute-done.22.refs_10_ = f32[8,128]{1,0:T(8,128)S(1)} collective-permute-done((f32[8,128]{1,0:T(8,128)S(1)}, f32[8,128]{1,0:T(8,128)S(1)}, u32[]{:S(2)}, u32[]{:S(2)}) %collective-permute-start.22) | collective-permute-done | bytes 4128 | tf_op jit(solution)/shard_map/ppermute | solution.py:265
  105.8 0.7 shard_map.77
  (29 shorter events, 0.3 us)
Async XLA Ops:
  0.6 12.6 %copy-start.1 = (s32[320]{0:T(512)S(1)}, s32[320]{0:T(512)}, u32[]{:S(2)}) copy-start(s32[320]{0:T(512)} %cell.3) | copy-start | bytes 3844
  0.6 7.5 %collective-permute-start = (f32[16,128]{1,0:T(8,128)}, f32[16,128]{1,0:T(8,128)S(1)}, u32[]{:S(2)}, u32[]{:S(2)}) collective-permute-start(f32[16,128]{1,0:T(8,128)} %rest_0_.1), channel_id=1, source_target_pairs={{0,1},{1,0},{2,3},{3,2},{4,5},{5,4},{6,7},{7,6},{8,9},{9,8},{10,11... | collective-permute-start | bytes 24584 | tf_op jit(solution)/shard_map/ppermute | solution.py:265
  8.1 9.6 %collective-permute-start.3 = (f32[32,128]{1,0:T(8,128)S(1)}, f32[32,128]{1,0:T(8,128)S(1)}, u32[]{:S(2)}, u32[]{:S(2)}) collective-permute-start(f32[32,128]{1,0:T(8,128)S(1)} %constant_dynamic-update-slice_fusion.rest_2_), channel_id=1, source_target_pairs={{0,6},{1,7},{2,4},{3,5},{4,2},{5,3},{6,0},{7,1},{8,14},{9,15},{10,... | collective-permute-start | bytes 49160 | tf_op jit(solution)/shard_map/ppermute | solution.py:265
  11.8 5.9 %collective-permute-start.2 = (f32[32,128]{1,0:T(8,128)S(1)}, f32[32,128]{1,0:T(8,128)S(1)}, u32[]{:S(2)}, u32[]{:S(2)}) collective-permute-start(f32[32,128]{1,0:T(8,128)S(1)} %constant_dynamic-update-slice_fusion.rest_2_), channel_id=1, source_target_pairs={{0,4},{1,5},{2,6},{3,7},{4,0},{5,1},{6,2},{7,3},{8,12},{9,13},{10,... | collective-permute-start | bytes 49160 | tf_op jit(solution)/shard_map/ppermute | solution.py:265
  11.8 5.9 %collective-permute-start.1 = (f32[32,128]{1,0:T(8,128)S(1)}, f32[32,128]{1,0:T(8,128)S(1)}, u32[]{:S(2)}, u32[]{:S(2)}) collective-permute-start(f32[32,128]{1,0:T(8,128)S(1)} %constant_dynamic-update-slice_fusion.rest_2_), channel_id=1, source_target_pairs={{0,2},{1,3},{2,0},{3,1},{4,6},{5,7},{6,4},{7,5},{8,10},{9,11},{10,... | collective-permute-start | bytes 49160 | tf_op jit(solution)/shard_map/ppermute | solution.py:265
  13.3 4.5 %copy-start = (s32[320]{0:T(512)S(1)}, s32[320]{0:T(512)}, u32[]{:S(2)}) copy-start(s32[320]{0:T(512)} %pick.5) | copy-start | bytes 3844
  21.6 1.4 %collective-permute-start.4 = (f32[264,128]{1,0:T(8,128)S(1)}, f32[264,128]{1,0:T(8,128)S(1)}, u32[]{:S(2)}, u32[]{:S(2)}) collective-permute-start(f32[264,128]{1,0:T(8,128)S(1)} %get-tuple-element.30), channel_id=1, source_target_pairs={{0,8},{8,0},{16,24},{24,16},{1,9},{9,1},{17,25},{25,17},{2,10},{10... | collective-permute-start | bytes 405512 | tf_op jit(solution)/shard_map/ppermute | solution.py:265
  23.1 5.7 %collective-permute-start.5 = (f32[264,128]{1,0:T(8,128)S(1)}, f32[264,128]{1,0:T(8,128)S(1)}, u32[]{:S(2)}, u32[]{:S(2)}) collective-permute-start(f32[264,128]{1,0:T(8,128)S(1)} %add.39.refs_1_), channel_id=1, source_target_pairs={{0,16},{8,24},{16,0},{24,8},{1,17},{9,25},{17,1},{25,9},{2,18},{10... | collective-permute-start | bytes 405512 | tf_op jit(solution)/shard_map/ppermute | solution.py:265
  28.8 1.4 %collective-permute-start.6 = (f32[264,128]{1,0:T(8,128)S(1)}, f32[264,128]{1,0:T(8,128)S(1)}, u32[]{:S(2)}, u32[]{:S(2)}) collective-permute-start(f32[264,128]{1,0:T(8,128)S(1)} %add.40.rest_2_), channel_id=1, source_target_pairs={{0,8},{8,0},{16,24},{24,16},{1,9},{9,1},{17,25},{25,17},{2,10},{10... | collective-permute-start | bytes 405512 | tf_op jit(solution)/shard_map/ppermute | solution.py:265
  35.5 4.4 %collective-permute-start.7 = (f32[136,128]{1,0:T(8,128)S(1)}, f32[136,128]{1,0:T(8,128)S(1)}, u32[]{:S(2)}, u32[]{:S(2)}) collective-permute-start(f32[136,128]{1,0:T(8,128)S(1)} %get-tuple-element.34), channel_id=1, source_target_pairs={{0,1},{1,0},{2,3},{3,2},{4,5},{5,4},{6,7},{7,6},{8,9},{9,8},{10,11... | collective-permute-start | bytes 208904 | tf_op jit(solution)/shard_map/ppermute | solution.py:265
  39.9 4.4 %collective-permute-start.8 = (f32[136,128]{1,0:T(8,128)S(1)}, f32[136,128]{1,0:T(8,128)S(1)}, u32[]{:S(2)}, u32[]{:S(2)}) collective-permute-start(f32[136,128]{1,0:T(8,128)S(1)} %add.41), channel_id=1, source_target_pairs={{0,2},{1,3},{2,0},{3,1},{4,6},{5,7},{6,4},{7,5},{8,10},{9,11},{10,... | collective-permute-start | bytes 208904 | tf_op jit(solution)/shard_map/ppermute | solution.py:265
  44.3 5.3 %collective-permute-start.9 = (f32[136,128]{1,0:T(8,128)S(1)}, f32[136,128]{1,0:T(8,128)S(1)}, u32[]{:S(2)}, u32[]{:S(2)}) collective-permute-start(f32[136,128]{1,0:T(8,128)S(1)} %add.42.rest_2_), channel_id=1, source_target_pairs={{0,4},{1,5},{2,6},{3,7},{4,0},{5,1},{6,2},{7,3},{8,12},{9,13},{10,... | collective-permute-start | bytes 208904 | tf_op jit(solution)/shard_map/ppermute | solution.py:265
  53.5 1.4 %collective-permute-start.10 = (f32[264,128]{1,0:T(8,128)S(1)}, f32[264,128]{1,0:T(8,128)S(1)}, u32[]{:S(2)}, u32[]{:S(2)}) collective-permute-start(f32[264,128]{1,0:T(8,128)S(1)} %get-tuple-element.38), channel_id=1, source_target_pairs={{0,8},{8,0},{16,24},{24,16},{1,9},{9,1},{17,25},{25,17},{2,10},{10... | collective-permute-start | bytes 405512 | tf_op jit(solution)/shard_map/ppermute | solution.py:265
  54.9 5.7 %collective-permute-start.11 = (f32[264,128]{1,0:T(8,128)S(1)}, f32[264,128]{1,0:T(8,128)S(1)}, u32[]{:S(2)}, u32[]{:S(2)}) collective-permute-start(f32[264,128]{1,0:T(8,128)S(1)} %add.43), channel_id=1, source_target_pairs={{0,16},{8,24},{16,0},{24,8},{1,17},{9,25},{17,1},{25,9},{2,18},{10... | collective-permute-start | bytes 405512 | tf_op jit(solution)/shard_map/ppermute | solution.py:265
  60.7 1.4 %collective-permute-start.12 = (f32[264,128]{1,0:T(8,128)S(1)}, f32[264,128]{1,0:T(8,128)S(1)}, u32[]{:S(2)}, u32[]{:S(2)}) collective-permute-start(f32[264,128]{1,0:T(8,128)S(1)} %add.44.rest_2_), channel_id=1, source_target_pairs={{0,8},{8,0},{16,24},{24,16},{1,9},{9,1},{17,25},{25,17},{2,10},{10... | collective-permute-start | bytes 405512 | tf_op jit(solution)/shard_map/ppermute | solution.py:265
  67.5 4.4 %collective-permute-start.13 = (f32[136,128]{1,0:T(8,128)S(1)}, f32[136,128]{1,0:T(8,128)S(1)}, u32[]{:S(2)}, u32[]{:S(2)}) collective-permute-start(f32[136,128]{1,0:T(8,128)S(1)} %get-tuple-element.42), channel_id=1, source_target_pairs={{0,1},{1,0},{2,3},{3,2},{4,5},{5,4},{6,7},{7,6},{8,9},{9,8},{10,11... | collective-permute-start | bytes 208904 | tf_op jit(solution)/shard_map/ppermute | solution.py:265
  71.9 4.4 %collective-permute-start.14 = (f32[136,128]{1,0:T(8,128)S(1)}, f32[136,128]{1,0:T(8,128)S(1)}, u32[]{:S(2)}, u32[]{:S(2)}) collective-permute-start(f32[136,128]{1,0:T(8,128)S(1)} %add.45), channel_id=1, source_target_pairs={{0,2},{1,3},{2,0},{3,1},{4,6},{5,7},{6,4},{7,5},{8,10},{9,11},{10,... | collective-permute-start | bytes 208904 | tf_op jit(solution)/shard_map/ppermute | solution.py:265
  76.3 5.3 %collective-permute-start.15 = (f32[136,128]{1,0:T(8,128)S(1)}, f32[136,128]{1,0:T(8,128)S(1)}, u32[]{:S(2)}, u32[]{:S(2)}) collective-permute-start(f32[136,128]{1,0:T(8,128)S(1)} %add.46.rest_2_), channel_id=1, source_target_pairs={{0,4},{1,5},{2,6},{3,7},{4,0},{5,1},{6,2},{7,3},{8,12},{9,13},{10,... | collective-permute-start | bytes 208904 | tf_op jit(solution)/shard_map/ppermute | solution.py:265
  85.4 1.4 %collective-permute-start.16 = (f32[264,128]{1,0:T(8,128)S(1)}, f32[264,128]{1,0:T(8,128)S(1)}, u32[]{:S(2)}, u32[]{:S(2)}) collective-permute-start(f32[264,128]{1,0:T(8,128)S(1)} %get-tuple-element.46), channel_id=1, source_target_pairs={{0,8},{8,0},{16,24},{24,16},{1,9},{9,1},{17,25},{25,17},{2,10},{10... | collective-permute-start | bytes 405512 | tf_op jit(solution)/shard_map/ppermute | solution.py:265
  86.9 5.7 %collective-permute-start.17 = (f32[264,128]{1,0:T(8,128)S(1)}, f32[264,128]{1,0:T(8,128)S(1)}, u32[]{:S(2)}, u32[]{:S(2)}) collective-permute-start(f32[264,128]{1,0:T(8,128)S(1)} %add.47), channel_id=1, source_target_pairs={{0,16},{8,24},{16,0},{24,8},{1,17},{9,25},{17,1},{25,9},{2,18},{10... | collective-permute-start | bytes 405512 | tf_op jit(solution)/shard_map/ppermute | solution.py:265
  92.8 3.1 %collective-permute-start.20 = (f32[8,128]{1,0:T(8,128)S(1)}, f32[8,128]{1,0:T(8,128)S(1)}, u32[]{:S(2)}, u32[]{:S(2)}) collective-permute-start(f32[8,128]{1,0:T(8,128)S(1)} %get-tuple-element.51), channel_id=1, source_target_pairs={{0,9},{1,8},{2,11},{3,10},{4,13},{5,12},{6,15},{7,14},{8,1},{9,0},... | collective-permute-start | bytes 12296 | tf_op jit(solution)/shard_map/ppermute | solution.py:424
  92.9 3.7 %collective-permute-start.19 = (f32[8,128]{1,0:T(8,128)S(1)}, f32[8,128]{1,0:T(8,128)S(1)}, u32[]{:S(2)}, u32[]{:S(2)}) collective-permute-start(f32[8,128]{1,0:T(8,128)S(1)} %get-tuple-element.51), channel_id=1, source_target_pairs={{0,1},{1,0},{2,3},{3,2},{4,5},{5,4},{6,7},{7,6},{8,9},{9,8},{10,11... | collective-permute-start | bytes 12296 | tf_op jit(solution)/shard_map/ppermute | solution.py:265
  93.8 2.7 %collective-permute-start.18 = (f32[8,128]{1,0:T(8,128)S(1)}, f32[8,128]{1,0:T(8,128)S(1)}, u32[]{:S(2)}, u32[]{:S(2)}) collective-permute-start(f32[8,128]{1,0:T(8,128)S(1)} %get-tuple-element.51), channel_id=1, source_target_pairs={{0,8},{8,0},{16,24},{24,16},{1,9},{9,1},{17,25},{25,17},{2,10},{10... | collective-permute-start | bytes 12296 | tf_op jit(solution)/shard_map/ppermute | solution.py:265
  96.6 6.3 %collective-permute-start.23 = (f32[8,128]{1,0:T(8,128)S(1)}, f32[8,128]{1,0:T(8,128)S(1)}, u32[]{:S(2)}, u32[]{:S(2)}) collective-permute-start(f32[8,128]{1,0:T(8,128)S(1)} %add_add_fusion.refs_8_), channel_id=1, source_target_pairs={{0,6},{1,7},{2,4},{3,5},{4,2},{5,3},{6,0},{7,1},{8,14},{9,15},{10,... | collective-permute-start | bytes 12296 | tf_op jit(solution)/shard_map/ppermute | solution.py:265
  101.2 4.5 %collective-permute-start.22 = (f32[8,128]{1,0:T(8,128)S(1)}, f32[8,128]{1,0:T(8,128)S(1)}, u32[]{:S(2)}, u32[]{:S(2)}) collective-permute-start(f32[8,128]{1,0:T(8,128)S(1)} %add_add_fusion.refs_8_), channel_id=1, source_target_pairs={{0,4},{1,5},{2,6},{3,7},{4,0},{5,1},{6,2},{7,3},{8,12},{9,13},{10,... | collective-permute-start | bytes 12296 | tf_op jit(solution)/shard_map/ppermute | solution.py:265
  101.3 4.5 %collective-permute-start.21 = (f32[8,128]{1,0:T(8,128)S(1)}, f32[8,128]{1,0:T(8,128)S(1)}, u32[]{:S(2)}, u32[]{:S(2)}) collective-permute-start(f32[8,128]{1,0:T(8,128)S(1)} %add_add_fusion.refs_8_), channel_id=1, source_target_pairs={{0,2},{1,3},{2,0},{3,1},{4,6},{5,7},{6,4},{7,5},{8,10},{9,11},{10,... | collective-permute-start | bytes 12296 | tf_op jit(solution)/shard_map/ppermute | solution.py:265
